TPU v7x, 256 devices: a whole 4x4x8 slice. The times are simulated.
256 devices in a mesh: ctx: 128 (over z, x, y), head: 2 (over core).
Axes of the slice: x: 4, y: 4, z: 8, core: 2. Of those that a mesh axis runs over, the one named last changes fastest.
Arguments:
- context_query_array: bfloat16 [32768, 8192], P('ctx', 'head'), may hold values from -6.5 to 6.5
- context_key_array: bfloat16 [32768, 1024], P('ctx', 'head'), may hold values from -6 to 6
- context_value_array: bfloat16 [32768, 1024], P('ctx', 'head'), may hold values from -12 to 12
- block_lengths: int32 [128], P('ctx'), may hold values from 1 to 256, 24576 in all
- pending_request_queries: bfloat16 [4096, 8192], P(('ctx', 'head')), may hold values from -6.5 to 6.5
- pending_request_keys: bfloat16 [4096, 1024], P('ctx', 'head'), may hold values from -6 to 6
- pending_request_values: bfloat16 [4096, 1024], P('ctx', 'head'), may hold values from -6 to 6
- query_owner: int32 [1], replicated, may hold values from 0 to 127
Outputs:
- context_output: bfloat16 [32768, 8192], P('ctx', 'head')
- request_output: bfloat16 [4096, 8192], P('ctx', 'head')
Inputs may be any that keep to these rules, and one draw needn't show every extreme that they name: `block_lengths`: they sum to 24576 and the largest is 256.
All inputs are finite; a program needn't handle non-finite values. No bound on the sum of `block_lengths` on one device may be relied on, other than what follows from the above.
Results may differ from a plain program's by a relative error of at most 0.0085.
Values may be sent and summed in bfloat16 or wider, within the bound.
No kernel may reach another device: no remote copies, remote signals or barrier semaphores. Data moves between devices by JAX's collectives and lax.ppermute only.
A program may use at most 320 MiB of HBM per device.

v0:
```python
import jax
import jax.numpy as jnp
from jax import lax
from jax.sharding import PartitionSpec as P

QUERY_HEADS = 64
KEY_VALUE_HEADS = 8
HEAD_SIZE = 128


def from_root(value, axis, source):
    kept = jnp.where(lax.axis_index(axis) == source, value, 0).astype(value.dtype)
    return lax.psum(kept, axis)


def softmax_part(queries, key_rows, value_rows, usable):
    score_scale = queries.shape[-1] ** (-0.5)
    scores = (
        jnp.einsum("rhgd,khd->hgrk", queries, key_rows, preferred_element_type=jnp.float32)
        * score_scale
    )
    scores = jnp.where(usable[None, None], scores, -jnp.inf)
    row_max = jnp.max(scores, axis=3)
    weights = jnp.exp(scores - row_max[..., None]).astype(jnp.bfloat16)
    row_total = jnp.sum(weights.astype(jnp.float32), axis=3)
    weighted = jnp.einsum("hgrk,khd->hgrd", weights, value_rows, preferred_element_type=jnp.float32)
    return (row_max, row_total, weighted)


def combine(first, second):
    max_a, total_a, acc_a = first
    max_b, total_b, acc_b = second
    peak = jnp.maximum(max_a, max_b)
    factor_a = jnp.exp(max_a - peak)
    factor_b = jnp.exp(max_b - peak)
    return (
        peak,
        total_a * factor_a + total_b * factor_b,
        acc_a * factor_a[..., None] + acc_b * factor_b[..., None],
    )


def local(
    context_query_array,
    context_key_array,
    context_value_array,
    block_lengths,
    pending_request_queries,
    pending_request_keys,
    pending_request_values,
    query_owner,
):
    group_index = QUERY_HEADS // KEY_VALUE_HEADS
    half_group = group_index // 2
    block_rows = context_key_array.shape[0]
    heads_kv = context_key_array.shape[1] // HEAD_SIZE
    request_rows = pending_request_keys.shape[0]
    ctx_index = lax.axis_index("ctx")
    owner_id = query_owner[0]
    own_len = block_lengths[0]
    anchor_keys, anchor_values, anchor_lengths = (
        from_root(context_key_array, "ctx", 0),
        from_root(context_value_array, "ctx", 0),
        from_root(block_lengths, "ctx", 0),
    )
    row_ids = jnp.arange(block_rows, dtype=jnp.int32)
    sees_anchor = (row_ids[None, :] < anchor_lengths[0]) & (ctx_index > 0)
    usable = jnp.concatenate(
        [
            jnp.broadcast_to(sees_anchor, (block_rows, block_rows)),
            row_ids[None, :] <= row_ids[:, None],
        ],
        axis=1,
    )
    local_queries = context_query_array.reshape(block_rows, heads_kv, group_index, HEAD_SIZE)
    joined_keys = jnp.concatenate([anchor_keys, context_key_array], axis=0).reshape(
        2 * block_rows, heads_kv, HEAD_SIZE
    )
    joined_values = jnp.concatenate([anchor_values, context_value_array], axis=0).reshape(
        2 * block_rows, heads_kv, HEAD_SIZE
    )

    def local_piece(index):
        head = index // 2
        first_query = index % 2 * half_group
        queries = lax.dynamic_slice(
            local_queries, (0, head, first_query, 0), (block_rows, 1, half_group, HEAD_SIZE)
        )
        part = softmax_part(
            queries,
            lax.dynamic_slice_in_dim(joined_keys, head, 1, 1),
            lax.dynamic_slice_in_dim(joined_values, head, 1, 1),
            usable,
        )
        return part[2][0] / part[1][0][..., None]

    per_piece = lax.map(local_piece, jnp.arange(2 * heads_kv, dtype=jnp.int32))
    per_head = per_piece.reshape(heads_kv, group_index, block_rows, HEAD_SIZE)
    context_result = per_head.transpose(2, 0, 1, 3).reshape(
        block_rows, heads_kv * group_index * HEAD_SIZE
    )
    context_output = jnp.where((row_ids < own_len)[:, None], context_result, 0.0).astype(
        jnp.bfloat16
    )
    early_rows = from_root(pending_request_queries, "ctx", owner_id)
    asked_flat = lax.all_to_all(early_rows, "head", split_axis=1, concat_axis=0, tiled=True)
    asked_rows = asked_flat.reshape(request_rows, heads_kv, group_index, HEAD_SIZE)
    block_usable = jnp.broadcast_to(row_ids[None, :] < own_len, (request_rows, block_rows))
    query_ids = jnp.arange(request_rows, dtype=jnp.int32)
    self_usable = query_ids[None, :] <= query_ids[:, None]
    block_keys = context_key_array.reshape(block_rows, heads_kv, HEAD_SIZE)
    block_values = context_value_array.reshape(block_rows, heads_kv, HEAD_SIZE)
    request_keys = pending_request_keys.reshape(request_rows, heads_kv, HEAD_SIZE)
    request_values = pending_request_values.reshape(request_rows, heads_kv, HEAD_SIZE)
    is_owner = ctx_index == owner_id

    def request_head(head):
        queries = lax.dynamic_slice_in_dim(asked_rows, head, 1, 1)
        context_part = softmax_part(
            queries,
            lax.dynamic_slice_in_dim(block_keys, head, 1, 1),
            lax.dynamic_slice_in_dim(block_values, head, 1, 1),
            block_usable,
        )
        self_max, self_total, self_acc = softmax_part(
            queries,
            lax.dynamic_slice_in_dim(request_keys, head, 1, 1),
            lax.dynamic_slice_in_dim(request_values, head, 1, 1),
            self_usable,
        )
        self_max = jnp.where(is_owner, self_max, -jnp.inf)
        joined = combine(context_part, (self_max, self_total, self_acc))
        return (joined[0][0], joined[1][0], joined[2][0])

    local_max, local_total, local_acc = lax.map(request_head, jnp.arange(heads_kv, dtype=jnp.int32))
    global_max = lax.pmax(local_max, "ctx")
    factor = jnp.exp(local_max - global_max)
    full_total, full_acc = lax.psum((local_total * factor, local_acc * factor[..., None]), "ctx")
    answer = (
        (full_acc / full_total[..., None])
        .transpose(2, 0, 1, 3)
        .reshape(request_rows, heads_kv * group_index * HEAD_SIZE)
    )
    request_output = jnp.where(is_owner, answer, 0.0).astype(jnp.bfloat16)
    return (context_output, request_output)


def solution(mesh):
    in_specs = (
        P("ctx", "head"),
        P("ctx", "head"),
        P("ctx", "head"),
        P("ctx"),
        P(("ctx", "head"), None),
        P("ctx", "head"),
        P("ctx", "head"),
        P(),
    )
    out_specs = (P("ctx", "head"), P("ctx", "head"))
    return jax.shard_map(local, mesh=mesh, in_specs=in_specs, out_specs=out_specs, check_vma=False)
```

profile of v0, /device:TPU:2, one launch (start us, length us, event | category | flops | bytes accessed | tf_op | source)
XLA Modules:
  0.0 1689.7 jit_solution(12361680409677273629)
XLA Ops:
  7.2 1.1 copy.16
  8.3 1.1 copy.19
  10.1 0.7 copy.61
  10.8 0.8 broadcast_select_fusion.1
  12.4 31.0 %psum.42 = s32[]{:T(128)} all-reduce(s32[]{:T(128)} %bitcast.12), channel_id=1, replica_groups=mesh['ctx'=128,'head'=2] {'ctx'}, use_global_device_ids=true, to_apply=%region_2.3 | all-reduce | flops 1 | bytes 8 | tf_op jit(solution)/shard_map/psum | solution.py:13
  43.4 3.3 copy.18
  46.7 0.6 compare_and_fusion
  47.6 189.7 %all-reduce.6.cloned.1.call-done = (bf16[256,512]{0,1:T(8,128)(2,1)}, bf16[256,512]{0,1:T(8,128)(2,1)}, bf16[16,2,4096]{2,0,1:T(8,128)(2,1)}) async-done(((bf16[256,512]{0,1:T(8,128)(2,1)}, bf16[256,512]{0,1:T(8,128)(2,1)}, bf16[16,2,4096]{2,0,1:T(8,128)(2,1)}), (bf16[256,512]{0,1:T(8,128)(2,1)}, bf16[256,512]{0,1:T(8,128)(2,1)}, bf16[16,2,4096]{2,0,1:T(8,128)(2,1)})) %all-reduce.6.cloned.1.call-update) | async-done | bytes 786448 | tf_op jit(solution)/shard_map/psum | solution.py:13
  237.3 5.0 all_to_all.16
  242.3 17.9 %while.30 = (s32[]{:T(128)}, f32[4,8,32]{2,1,0:T(8,128)S(1)}, f32[4,8,32]{2,1,0:T(8,128)S(1)}, f32[4,8,32,128]{3,2,1,0:T(8,128)}, s32[4]{0:T(128)S(1)}, /*index=...) while((s32[]{:T(128)}, f32[4,8,32]{2,1,0:T(8,128)S(1)}, ...), condition=%wide.region_13.14_spmd.clone.clone, body=%wide.region_8.13_spmd.clone.sunk.clone | while | flops 38513412 | bytes 1843389 | solution.py:135
  245.6 0.9 fusion.90
  250.1 0.9 fusion.90
  254.6 0.9 fusion.90
  259.0 0.9 fusion.90
  260.2 676.3 %pmax.7 = f32[4,8,32]{2,1,0:T(8,128)S(1)} all-reduce(f32[4,8,32]{2,1,0:T(8,128)S(1)} %get-tuple-element.165), channel_id=1, replica_groups=mesh['ctx'=128,'head'=2] {'ctx'}, use_global_device_ids=true, to_apply=%region_14.15 | all-reduce | flops 1024 | bytes 8192 | tf_op jit(solution)/shard_map/pmax | solution.py:136
  936.5 2.1 broadcast_multiply_fusion
  938.6 681.6 %psum.47 = f32[4,8,32]{2,1,0:T(8,128)S(1)} all-reduce(f32[4,8,32]{2,1,0:T(8,128)S(1)} %get-tuple-element.255), channel_id=1, replica_groups=mesh['ctx'=128,'head'=2] {'ctx'}, use_global_device_ids=true, to_apply=%region_16.17 | all-reduce | flops 1024 | bytes 8192 | tf_op jit(solution)/shard_map/psum | solution.py:138
  1620.1 1.0 pad_maximum_fusion
  1621.1 1.8 pad_maximum_fusion.1
  1622.9 52.4 %while.29 = (s32[]{:T(128)}, bf16[8,4,256,128]{3,2,1,0:T(8,128)(2,1)}, pred[256,512]{0,1:T(8,128)(4,1)S(1)}, s32[8]{0:T(128)S(1)}, bf16[512,4,128]{0,2,1:T(8,128...) while((s32[]{:T(128)}, bf16[8,4,256,128]{3,2,1,0:T(8,128)(2,1)}, ...), condition=%wide.region_6.7_spmd.clone, body=%wide.region_3.6_spmd.sunk.clone | while | flops 275380256 | bytes 7756136 | solution.py:97
  1627.1 2.4 fusion.81
  1633.7 2.4 fusion.81
  1640.2 2.4 fusion.81
  1646.8 2.4 fusion.81
  1653.3 2.4 fusion.81
  1659.9 2.4 fusion.81
  1666.5 2.4 fusion.81
  1673.0 2.4 fusion.81
  1675.4 2.9 copy.24
  1678.3 2.4 fusion.45
  1680.7 1.2 fusion.46
  1682.1 0.8 copy.60
  (88 shorter events, 19.3 us)
Async XLA Ops:
  7.2 40.2 %copy-start = (bf16[32,512]{1,0:T(8,128)(2,1)S(1)}, bf16[32,512]{1,0:T(8,128)(2,1)}, u32[]{:S(2)}) copy-start(bf16[32,512]{1,0:T(8,128)(2,1)} %param.17) | copy-start | bytes 98308
  7.2 230.1 %all-reduce.6.cloned.1.call-start = ((), (), s32[]{:S(2)}) async-start(), calls=%async_computation.2 | async-start | bytes 1572864 | tf_op jit(solution)/shard_map/psum | solution.py:13
  11.7 1669.0 %all-reduce.4.cloned.1.call-start = ((), (), s32[]{:S(2)}) async-start(), calls=%async_computation.1 | async-start | bytes 1048576 | tf_op jit(solution)/shard_map/psum | solution.py:138
  43.4 4.0 copy-start.1
Sparse Core Ops, SparseCore 0:
  14.2 222.9 all-reduce.5
  938.7 220.1 all-reduce.3
where the time goes:
time: 1700 us; the launch traced here: 1690 us
  blocking collectives  1390 us (82%)
  waiting for transfers between devices  190 us (11%)
  matrix products  29.3 us (2%)
  loops' own time  29.1 us (2%)
  local copies, waits for them, and re-layouts  17.2 us (1%)
    psum x1, blocking collectives, local(): lax.psum((local_total * factor, local_acc * factor[..., None]), 'ctx')  682 us
    pmax x1, blocking collectives, local(): global_max = lax.pmax(local_max, 'ctx')  676 us
    psum x1, waiting for transfers between devices, from_root(): return lax.psum(kept, axis)  190 us
  transfers between devices with their start and end apart: 2, of which 1 were waited for; matrix products, arithmetic and copies ran while one was open for 3% of the time, Pallas kernels for 0%

commit v1 on v0

v1 whole, which is shorter than its diff:
```python
import functools

import jax
import jax.numpy as jnp
from jax import lax
from jax.experimental import pallas as pl
from jax.experimental.pallas import tpu as pltpu
from jax.sharding import PartitionSpec as P

HEAD_SIZE = 128
GROUP = 8
SCALE = HEAD_SIZE**-0.5
LOG2E = 1.4426950408889634
LN2 = 0.6931471805599453
MARK = 1024.0
VMEM_LIMIT = 32 * 1024 * 1024


def dot_nt(a, b):
    return lax.dot_general(a, b, (((1,), (1,)), ((), ())), preferred_element_type=jnp.float32)


def dot_nn(a, b):
    return lax.dot_general(a, b, (((1,), (0,)), ((), ())), preferred_element_type=jnp.float32)


def context_kernel(count, len_ref, root_ref, q_ref, k_ref, v_ref, *refs):
    ak_refs, av_refs = refs[:count], refs[count : 2 * count]
    o_ref, va_ref, vo_ref = refs[-3:]
    rows = k_ref.shape[0]
    half = rows // 2
    own_len = len_ref[0]
    root = root_ref[0] > 0
    ak = jnp.concatenate([ref[...] for ref in ak_refs], axis=0)
    ak = jnp.where(root, jnp.broadcast_to(k_ref[0:1, :], ak.shape), ak)
    av = jnp.concatenate([ref[...] for ref in av_refs], axis=0)
    hidden = (av > 100.0) | root
    va_ref[:, :HEAD_SIZE] = jnp.where(hidden, jnp.zeros_like(av), av)
    va_ref[:, HEAD_SIZE:] = jnp.where(hidden, jnp.zeros_like(av), jnp.ones_like(av))
    vo_ref[:, :HEAD_SIZE] = v_ref[...]
    vo_ref[:, HEAD_SIZE:] = jnp.ones((rows, HEAD_SIZE), jnp.bfloat16)
    c = SCALE * LOG2E
    for top in (0, half):
        keys = top + half
        row = top + lax.broadcasted_iota(jnp.int32, (half, keys), 0)
        col = lax.broadcasted_iota(jnp.int32, (half, keys), 1)
        causal = jnp.where(col <= row, 0.0, -jnp.inf).astype(jnp.float32)
        live = (top + lax.broadcasted_iota(jnp.int32, (half, HEAD_SIZE), 0)) < own_len
        for g in range(GROUP):
            lanes = slice(g * HEAD_SIZE, (g + 1) * HEAD_SIZE)
            q = q_ref[top : top + half, lanes]
            sa = dot_nt(q, ak)
            so = dot_nt(q, k_ref[0:keys, :]) + causal
            peak = jnp.maximum(
                jnp.max(sa, axis=1, keepdims=True), jnp.max(so, axis=1, keepdims=True)
            )
            wa = jnp.exp2((sa - peak) * c).astype(jnp.bfloat16)
            wo = jnp.exp2((so - peak) * c).astype(jnp.bfloat16)
            acc = dot_nn(wa, va_ref[...]) + dot_nn(wo, vo_ref[0:keys, :])
            out = acc[:, :HEAD_SIZE] / acc[:, HEAD_SIZE:]
            o_ref[top : top + half, lanes] = jnp.where(live, out, 0.0).astype(jnp.bfloat16)


def context_attention(own_len, is_root, q, k, v, anchor, head, done):
    rows, width = q.shape
    heads = k.shape[1] // HEAD_SIZE
    wide = GROUP * HEAD_SIZE
    smem = pl.BlockSpec(memory_space=pltpu.SMEM)
    kv_spec = pl.BlockSpec((rows, HEAD_SIZE), lambda i: (0, head))
    wide_spec = pl.BlockSpec((rows, wide), lambda i: (0, head))
    count = len(anchor)
    slab = anchor[0].shape[0]
    operands = [own_len, is_root, q, k, v] + anchor + anchor
    specs = [smem, smem, wide_spec, kv_spec, kv_spec]
    specs += [pl.BlockSpec((slab, HEAD_SIZE), lambda i: (0, head))] * count
    specs += [pl.BlockSpec((slab, HEAD_SIZE), lambda i: (0, heads + head))] * count
    alias = {}
    if done is not None:
        alias = {len(operands): 0}
        operands, specs = operands + [done], specs + [pl.BlockSpec(memory_space=pl.ANY)]
    return pl.pallas_call(
        functools.partial(context_kernel, count),
        grid=(1,),
        out_shape=jax.ShapeDtypeStruct((rows, width), jnp.bfloat16),
        in_specs=specs,
        out_specs=wide_spec,
        input_output_aliases=alias,
        scratch_shapes=[
            pltpu.VMEM((rows, 2 * HEAD_SIZE), jnp.bfloat16),
            pltpu.VMEM((rows, 2 * HEAD_SIZE), jnp.bfloat16),
        ],
        compiler_params=pltpu.CompilerParams(vmem_limit_bytes=VMEM_LIMIT),
        cost_estimate=pl.CostEstimate(
            flops=8 * rows * wide * rows, bytes_accessed=5 * 2**18, transcendentals=2 * rows * rows * GROUP
        ),
        name="context_attention",
    )(*operands)


def mark_kernel(len_ref, k_ref, v_ref, *o_refs):
    rows, width = k_ref.shape
    slab = rows // len(o_refs)
    first = jnp.broadcast_to(k_ref[0:1, :], (slab, width))
    for i, o_ref in enumerate(o_refs):
        span = slice(i * slab, (i + 1) * slab)
        valid = (i * slab + lax.broadcasted_iota(jnp.int32, first.shape, 0)) < len_ref[0]
        o_ref[:, :width] = jnp.where(valid, k_ref[span, :], first)
        o_ref[:, width:] = jnp.where(valid, v_ref[span, :], jnp.full_like(first, MARK))


def mark(own_len, k, v, pieces):
    rows, width = k.shape
    vmem = pl.BlockSpec(memory_space=pltpu.VMEM)
    shape = jax.ShapeDtypeStruct((rows // pieces, 2 * width), k.dtype)
    return pl.pallas_call(
        mark_kernel,
        out_shape=[shape] * pieces,
        in_specs=[pl.BlockSpec(memory_space=pltpu.SMEM), vmem, vmem],
        out_specs=[vmem] * pieces,
        compiler_params=pltpu.CompilerParams(vmem_limit_bytes=VMEM_LIMIT),
        cost_estimate=pl.CostEstimate(flops=2**18, bytes_accessed=2**20, transcendentals=0),
        name="mark",
    )(own_len, k, v)


def pack_kernel(rq_ref, o_ref):
    own, width = rq_ref.shape
    slabs = o_ref.shape[0] // 2
    some = o_ref.shape[1] // own
    for j in range(slabs):
        for c in range(2):
            for i in range(some):
                lane = c * (width // 2) + (some * j + i) * HEAD_SIZE
                o_ref[2 * j + c, i * own : (i + 1) * own, :] = rq_ref[:, lane : lane + HEAD_SIZE]


def pack(rq, slabs):
    vmem = pl.BlockSpec(memory_space=pltpu.VMEM)
    height = rq.size // (2 * slabs * HEAD_SIZE)
    return pl.pallas_call(
        pack_kernel,
        out_shape=jax.ShapeDtypeStruct((2 * slabs, height, HEAD_SIZE), jnp.bfloat16),
        in_specs=[vmem],
        out_specs=vmem,
        compiler_params=pltpu.CompilerParams(vmem_limit_bytes=56 * 1024 * 1024),
        cost_estimate=pl.CostEstimate(flops=2**18, bytes_accessed=2**19, transcendentals=0),
        name="pack",
    )(rq)


def plane_kernel(slab_ref, x_ref, o_ref):
    own = 16
    source = 2 * slab_ref[0]
    parts = []
    for i in range(x_ref.shape[1] // own):
        pick = slice(i * own, (i + 1) * own)
        parts += [x_ref[source, pick, :], x_ref[source + 1, pick, :]]
    part = jnp.concatenate(parts, axis=0)
    for z in range(o_ref.shape[0]):
        o_ref[z] = part


def slab_kernel(plane_ref, x_ref, o_ref):
    part = x_ref[plane_ref[0]]
    for j in range(o_ref.shape[0]):
        o_ref[j] = part


def choose(kernel, index, x, shape):
    vmem = pl.BlockSpec(memory_space=pltpu.VMEM)
    return pl.pallas_call(
        kernel,
        out_shape=jax.ShapeDtypeStruct(shape, x.dtype),
        in_specs=[pl.BlockSpec(memory_space=pltpu.SMEM), vmem],
        out_specs=vmem,
        compiler_params=pltpu.CompilerParams(vmem_limit_bytes=VMEM_LIMIT),
        cost_estimate=pl.CostEstimate(flops=2**18, bytes_accessed=3 * 2**19, transcendentals=0),
        name="choose",
    )(index, x)


def split3(x):
    high = x.astype(jnp.bfloat16).astype(jnp.float32)
    rest = x - high
    mid = rest.astype(jnp.bfloat16).astype(jnp.float32)
    low = (rest - mid).astype(jnp.bfloat16).astype(jnp.float32)
    return high, mid, low


def code_rows(pair, last, height):
    row = lax.broadcasted_iota(jnp.int32, (height, HEAD_SIZE), 0)
    return jnp.where(row == 0, pair, jnp.where(row == 1, last, 0.0)).astype(jnp.bfloat16)


def request_kernel(len_ref, own_ref, q_ref, k_ref, v_ref, rk_ref, rv_ref, o_ref, vb_ref, vr_ref):
    count, height, _ = o_ref.shape
    piece = height - 16
    n = count * piece
    keys = k_ref.shape[0]
    own = rk_ref.shape[0]
    c = SCALE * LOG2E
    vb_ref[:, :HEAD_SIZE] = v_ref[...]
    vb_ref[:, HEAD_SIZE:] = jnp.ones((keys, HEAD_SIZE), jnp.bfloat16)
    vr_ref[:, :HEAD_SIZE] = rv_ref[...]
    vr_ref[:, HEAD_SIZE:] = jnp.ones((own, HEAD_SIZE), jnp.bfloat16)
    q = q_ref[:, 0:piece, :].reshape(n, HEAD_SIZE)
    seen = lax.broadcasted_iota(jnp.int32, (n, keys), 1) < len_ref[0]
    sb = jnp.where(seen, dot_nt(q, k_ref[...]), -jnp.inf)
    row = lax.rem(lax.broadcasted_iota(jnp.int32, (n, own), 0), own)
    col = lax.broadcasted_iota(jnp.int32, (n, own), 1)
    seen_own = (col <= row) & (own_ref[0] > 0)
    sr = jnp.where(seen_own, dot_nt(q, rk_ref[...]), -jnp.inf)
    peak = jnp.maximum(jnp.max(sb, axis=1, keepdims=True), jnp.max(sr, axis=1, keepdims=True))
    wb = jnp.exp2((sb - peak) * c).astype(jnp.bfloat16)
    wr = jnp.exp2((sr - peak) * c).astype(jnp.bfloat16)
    acc = dot_nn(wb, vb_ref[...]) + dot_nn(wr, vr_ref[...])
    total = acc[:, HEAD_SIZE:]
    out = (acc[:, :HEAD_SIZE] / total).astype(jnp.bfloat16)
    lse = peak * SCALE + jnp.log(total)
    high, mid, low = split3(lse)
    row = lax.broadcasted_iota(jnp.int32, (piece, HEAD_SIZE), 0)
    lane = lax.broadcasted_iota(jnp.int32, (piece, HEAD_SIZE), 1)
    for p in range(count):
        part = slice(p * piece, (p + 1) * piece)
        pair = jnp.where(row == lane, high[part], jnp.where(row + piece == lane, mid[part], 0.0))
        last = jnp.where(row == lane, low[part], 0.0)
        o_ref[p, 0:piece, :] = out[part]
        o_ref[p, piece:height, :] = code_rows(
            jnp.sum(pair, axis=0, keepdims=True), jnp.sum(last, axis=0, keepdims=True), height - piece
        )


def request_partials(own_len, is_owner, moved, k, v, rk, rv):
    pieces = moved.shape[0]
    heads = k.shape[1] // HEAD_SIZE
    keys, own = k.shape[0], rk.shape[0]
    rows = heads * GROUP * own
    height = rows // pieces + 16
    smem = pl.BlockSpec(memory_space=pltpu.SMEM)
    kv_spec = pl.BlockSpec((keys, HEAD_SIZE), lambda h: (0, h))
    own_spec = pl.BlockSpec((own, HEAD_SIZE), lambda h: (0, h))
    return pl.pallas_call(
        request_kernel,
        grid=(heads,),
        out_shape=jax.ShapeDtypeStruct((pieces, height, HEAD_SIZE), jnp.bfloat16),
        in_specs=[
            smem,
            smem,
            pl.BlockSpec((pieces // heads,) + moved.shape[1:], lambda h: (h, 0, 0)),
            kv_spec,
            kv_spec,
            own_spec,
            own_spec,
        ],
        out_specs=pl.BlockSpec((pieces // heads, height, HEAD_SIZE), lambda h: (h, 0, 0)),
        scratch_shapes=[
            pltpu.VMEM((keys, 2 * HEAD_SIZE), jnp.bfloat16),
            pltpu.VMEM((own, 2 * HEAD_SIZE), jnp.bfloat16),
        ],
        compiler_params=pltpu.CompilerParams(vmem_limit_bytes=VMEM_LIMIT),
        cost_estimate=pl.CostEstimate(
            flops=4 * rows * HEAD_SIZE * (keys + own), bytes_accessed=3 * 2**20, transcendentals=rows * (keys + own)
        ),
        name="request_partials",
    )(own_len, is_owner, moved, k, v, rk, rv)


def join_kernel(keep_code, x_ref, o_ref):
    height = x_ref.shape[1]
    piece = height - 16
    code = x_ref[:, piece:height, :].astype(jnp.float32)
    pair, last = code[:, 0, :], code[:, 1, :]
    lse = pair + pltpu.roll(pair, piece, 1) + last
    lse = jnp.where(lax.broadcasted_iota(jnp.int32, lse.shape, 1) < piece, lse, 0.0)
    peak = jnp.max(lse, axis=0, keepdims=True)
    weight = jnp.exp(lse - peak)
    total = jnp.sum(weight, axis=0, keepdims=True)
    column = jnp.transpose(weight / total)
    out = jnp.zeros((piece, HEAD_SIZE), jnp.float32)
    for i in range(x_ref.shape[0]):
        out = out + column[0:piece, i : i + 1] * x_ref[i, 0:piece, :].astype(jnp.float32)
    copies = o_ref.shape[0]
    o_ref[:, 0:piece, :] = jnp.broadcast_to(out.astype(jnp.bfloat16)[None], (copies, piece, HEAD_SIZE))
    if keep_code:
        high, mid, low = split3(peak + jnp.log(total))
        lane = lax.broadcasted_iota(jnp.int32, high.shape, 1)
        pair = jnp.where(lane < piece, high, pltpu.roll(mid, piece, 1))
        rows = code_rows(pair, low, 16)
        o_ref[:, piece:height, :] = jnp.broadcast_to(rows[None], (copies, 16, HEAD_SIZE))


def join(x, copies, keep_code):
    height = x.shape[1] if keep_code else x.shape[1] - 16
    return pl.pallas_call(
        functools.partial(join_kernel, keep_code),
        out_shape=jax.ShapeDtypeStruct((copies, height, HEAD_SIZE), jnp.bfloat16),
        compiler_params=pltpu.CompilerParams(vmem_limit_bytes=VMEM_LIMIT),
        cost_estimate=pl.CostEstimate(flops=2**20, bytes_accessed=2**19, transcendentals=1024),
        name="join_pieces",
    )(x)


def exchange(x, axis):
    return lax.all_to_all(x, axis, split_axis=0, concat_axis=0, tiled=True)


def local(n_z, n_xy, q, k, v, block_lengths, rq, rk, rv, query_owner):
    z, xy = lax.axis_index("z"), lax.axis_index("xy")
    owner = query_owner[0]
    owner_z, owner_xy = owner // n_xy, owner % n_xy
    own_len = block_lengths
    mine = (z == owner_z) & (xy == owner_xy)
    is_owner = mine.astype(jnp.int32).reshape(1)
    is_root = ((z == 0) & (xy == 0)).astype(jnp.int32).reshape(1)
    heads = q.shape[1] // HEAD_SIZE
    own_rows = rk.shape[0]

    moved = exchange(pack(rq, n_xy), ("xy", "head"))
    moved = choose(plane_kernel, owner_xy.reshape(1), moved, (n_z, 2 * moved.shape[1], HEAD_SIZE))
    moved = exchange(moved, "z")
    moved = choose(slab_kernel, owner_z.reshape(1), moved, (n_xy,) + moved.shape[1:])
    moved = exchange(moved, "xy")

    def move(x, pairs):
        return lax.ppermute(x, ("z", "xy"), pairs)

    n_x = 4
    n_y = n_xy // n_x
    x, y = xy // n_y, xy % n_y
    pieces = mark(own_len, k, v, n_x)
    held = [move(pieces[i], [(0, i * n_y)]) for i in range(1, n_x)]
    held = jnp.where(x == 0, pieces[0], held[0] + held[1] + held[2])
    rows_x = [i * n_y for i in range(n_x)]
    got = [move(held, [(p, p + i) for p in rows_x]) for i in range(1, n_y)]
    held = jnp.where(y == 0, held, got[0] + got[1] + got[2])
    plane = range(n_xy)
    got = [move(held, [(p, to * n_xy + p) for p in plane]) for to in (3, 5)]
    held = jnp.where(z == 0, held, got[0] + got[1])
    steps = (((0, 1), (3, 4), (5, 6)), ((0, 7), (3, 2)))
    got = [move(held, [(a * n_xy + p, b * n_xy + p) for a, b in step for p in plane]) for step in steps]
    held = jnp.where((z == 0) | (z == 3) | (z == 5), held, got[0] + got[1])
    anchor = [held]
    for i in range(1, n_x):
        pairs = []
        for a in range(n_z * n_x):
            there = a // n_x * n_x + (a + i) % n_x
            pairs += [(a * n_y + p, there * n_y + p) for p in range(n_y)]
        anchor.append(move(held, pairs))

    partials = request_partials(own_len, is_owner, moved, k, v, rk, rv)
    planes = join(exchange(partials, "xy"), n_z, True)
    joined = exchange(planes, "z")
    context_output = context_attention(own_len, is_root, q, k, v, anchor, 0, None)
    context_output = context_attention(own_len, is_root, q, k, v, anchor, 1, context_output)
    answer = exchange(join(joined, n_xy, False), "xy")
    for head in range(2, k.shape[1] // HEAD_SIZE):
        context_output = context_attention(own_len, is_root, q, k, v, anchor, head, context_output)
    answer = answer.reshape(heads, own_rows, HEAD_SIZE).transpose(1, 0, 2).reshape(own_rows, heads * HEAD_SIZE)
    request_output = jnp.where(mine, answer, jnp.zeros_like(answer))
    return context_output, request_output


def solution(mesh):
    n_z, n_xy = 8, 16
    grid = jax.sharding.Mesh(mesh.devices.reshape(n_z, n_xy, 2), ("z", "xy", "head"))
    ctx = ("z", "xy")
    in_specs = (
        P(ctx, "head"),
        P(ctx, "head"),
        P(ctx, "head"),
        P(ctx),
        P(("z", "xy", "head"), None),
        P(ctx, "head"),
        P(ctx, "head"),
        P(),
    )
    out_specs = (P(ctx, "head"), P(ctx, "head"))
    return jax.shard_map(
        functools.partial(local, n_z, n_xy),
        mesh=grid,
        in_specs=in_specs,
        out_specs=out_specs,
        check_vma=False,
    )
```

time: 1700 us -> 99.2 us (0.06)
  blocking collectives: 1390 us -> 0 us
  waiting for transfers between devices: 190 us -> 15.6 us
  starting transfers between devices: 0.08 us -> 55.6 us
  matrix products: 29.3 us -> 0 us
  loops' own time: 29.1 us -> 0 us
  Pallas kernels: 0 us -> 21 us
    psum x2 -> x0, blocking collectives: 713 us -> none  [the longest x1 682 us: local(): lax.psum((local_total * factor, local_acc * factor[..., None]), 'ctx')]
    pmax x1 -> x0, blocking collectives: 676 us -> none  [local(): global_max = lax.pmax(local_max, 'ctx')]
    psum x2 -> x0, waiting for transfers between devices: 190 us -> none  [the longest x1 190 us: from_root(): return lax.psum(kept, axis)]
    all_to_all x0 -> x6, starting transfers between devices: none -> 35.3 us  [exchange(): return lax.all_to_all(x, axis, split_axis=0, concat_axis=0, tiled=True)]
    dot_general x32 -> x0, matrix products: 29.3 us -> none  [the longest x16 23.3 us: softmax_part(): jnp.einsum('hgrk,khd->hgrd', weights, value_rows, preferred_element_type=...]
    another operation x2 -> x0, loops' own time: 29.1 us -> none  [the longest x1 21 us: local(): per_piece = lax.map(local_piece, jnp.arange(2 * heads_kv, dtype=jnp.int32))]
    pallas_call x0 -> x11, Pallas kernels: none -> 21 us  [the longest x4 12.4 us: context_attention(): pl.pallas_call(functools.partial(context_kernel, count), grid=(1,), out_s...]
    ppermute x0 -> x13, starting transfers between devices: none -> 20.4 us  [move(): return lax.ppermute(x, ('z', 'xy'), pairs)]
  transfers between devices with their start and end apart: 2 -> 19, of which waited for: 1 -> 5; matrix products, arithmetic and copies ran while one was open for 3% -> 1% of each run, Pallas kernels for 0% -> 20%
where the time goes in v1:
time: 99.2 us; the launch traced here: 98.2 us
  starting transfers between devices  55.6 us (56%)
  Pallas kernels  21 us (21%)
  waiting for transfers between devices  15.6 us (16%)
  local copies, waits for them, and re-layouts  2.67 us (3%)
  between operations  2.3 us (2%)
  other arithmetic  1.04 us (1%)
    all_to_all x6, starting transfers between devices, exchange(): return lax.all_to_all(x, axis, split_axis=0, concat_axis=0, tiled=True)  35.3 us
    ppermute x13, starting transfers between devices, move(): return lax.ppermute(x, ('z', 'xy'), pairs)  20.4 us
    all_to_all x6, waiting for transfers between devices, exchange(): return lax.all_to_all(x, axis, split_axis=0, concat_axis=0, tiled=True)  15.5 us
    pallas_call x4, Pallas kernels, context_attention(): pl.pallas_call(functools.partial(context_kernel, count), grid=(1,), out_s...  12.4 us
    pallas_call x1, Pallas kernels, request_partials(): pl.pallas_call(request_kernel, grid=(heads,), out_shape=jax.ShapeDtypeStr...  3.25 us
    pallas_call x2, Pallas kernels, join(): pl.pallas_call(functools.partial(join_kernel, keep_code), out_shape=jax.S...  2.2 us
  transfers between devices with their start and end apart: 19, of which 5 were waited for; matrix products, arithmetic and copies ran while one was open for 1% of the time, Pallas kernels for 20%

profile of v1, /device:TPU:2, one launch (start us, length us, event | category | flops | bytes accessed | tf_op | source)
XLA Modules:
  0.0 98.2 jit_solution(9662228141580971981)
XLA Ops:
  0.7 1.7 %pack.1 = bf16[32,32,128]{2,1,0:T(8,128)(2,1)} custom-call(bf16[16,8192]{1,0:T(8,128)(2,1)} %rq_ref.1), custom_call_target="tpu_custom_call" | custom-call | flops 262144 | bytes 524288 | tf_op jit(solution)/shard_map/pack/pallas_call | solution.py:140
  2.4 7.8 %all-to-all-start = ((bf16[32,32,128]{2,1,0:T(8,128)(2,1)}), bf16[32,32,128]{2,1,0:T(8,128)(2,1)S(1)}, u32[]{:S(2)}, u32[]{:S(2)}) async-start(bf16[32,32,128]{2,1,0:T(8,128)(2,1)} %pack.1), calls=%async_computation | async-start | bytes 524288 | tf_op jit(solution)/shard_map/all_to_all | solution.py:304
  10.8 0.9 copy-done.1
  11.7 0.9 copy-done.3
  12.7 1.3 %collective-permute-start = (bf16[64,1024]{1,0:T(8,128)(2,1)S(1)}, bf16[64,1024]{1,0:T(8,128)(2,1)S(1)}, u32[]{:S(2)}, u32[]{:S(2)}) collective-permute-start(bf16[64,1024]{1,0:T(8,128)(2,1)S(1)} %get-tuple-element.7), channel_id=1, source_target_pairs={{0,8},{1,9}} | collective-permute-start | bytes 393224 | tf_op jit(solution)/shard_map/ppermute | solution.py:325
  16.1 1.8 %all-to-all-done.x_ref = bf16[32,32,128]{2,1,0:T(8,128)(2,1)S(1)} async-done(((bf16[32,32,128]{2,1,0:T(8,128)(2,1)}), bf16[32,32,128]{2,1,0:T(8,128)(2,1)S(1)}, u32[]{:S(2)}, u32[]{:S(2)}) %all-to-all-start) | async-done | bytes 262176 | tf_op jit(solution)/shard_map/all_to_all | solution.py:304
  18.5 8.5 %all-to-all-start.1 = ((bf16[8,64,128]{2,1,0:T(8,128)(2,1)}), bf16[8,64,128]{2,1,0:T(8,128)(2,1)S(1)}, u32[]{:S(2)}, u32[]{:S(2)}) async-start(bf16[8,64,128]{2,1,0:T(8,128)(2,1)} %choose.2), calls=%async_computation.1 | async-start | bytes 262144 | tf_op jit(solution)/shard_map/all_to_all | solution.py:304
  27.1 2.1 %collective-permute-start.3 = (bf16[64,1024]{1,0:T(8,128)(2,1)S(1)}, bf16[64,1024]{1,0:T(8,128)(2,1)S(1)}, u32[]{:S(2)}, u32[]{:S(2)}) collective-permute-start(bf16[64,1024]{1,0:T(8,128)(2,1)S(1)} %add_select_fusion.3), channel_id=1, source_target_pairs={{0,2},{8,10},{16,18},{24,26},{1,3},{9,11},{17,19},{25,27}} | collective-permute-start | bytes 393224 | tf_op jit(solution)/shard_map/ppermute | solution.py:325
  29.2 1.8 %collective-permute-start.4 = (bf16[64,1024]{1,0:T(8,128)(2,1)S(1)}, bf16[64,1024]{1,0:T(8,128)(2,1)S(1)}, u32[]{:S(2)}, u32[]{:S(2)}) collective-permute-start(bf16[64,1024]{1,0:T(8,128)(2,1)S(1)} %add_select_fusion.3), channel_id=1, source_target_pairs={{0,4},{8,12},{16,20},{24,28},{1,5},{9,13},{17,21},{25,29}} | collective-permute-start | bytes 393224 | tf_op jit(solution)/shard_map/ppermute | solution.py:325
  30.9 1.3 %collective-permute-start.5 = (bf16[64,1024]{1,0:T(8,128)(2,1)S(1)}, bf16[64,1024]{1,0:T(8,128)(2,1)S(1)}, u32[]{:S(2)}, u32[]{:S(2)}) collective-permute-start(bf16[64,1024]{1,0:T(8,128)(2,1)S(1)} %add_select_fusion.3), channel_id=1, source_target_pairs={{0,6},{8,14},{16,22},{24,30},{1,7},{9,15},{17,23},{25,31}} | collective-permute-start | bytes 393224 | tf_op jit(solution)/shard_map/ppermute | solution.py:325
  32.3 4.2 %all-to-all-done.1.x_ref = bf16[8,64,128]{2,1,0:T(8,128)(2,1)S(1)} async-done(((bf16[8,64,128]{2,1,0:T(8,128)(2,1)}), bf16[8,64,128]{2,1,0:T(8,128)(2,1)S(1)}, u32[]{:S(2)}, u32[]{:S(2)}) %all-to-all-start.1) | async-done | bytes 131104 | tf_op jit(solution)/shard_map/all_to_all | solution.py:304
  37.3 4.8 %all-to-all-start.2 = ((bf16[16,64,128]{2,1,0:T(8,128)(2,1)}), bf16[16,64,128]{2,1,0:T(8,128)(2,1)S(1)}, u32[]{:S(2)}, u32[]{:S(2)}) async-start(bf16[16,64,128]{2,1,0:T(8,128)(2,1)} %choose.3), calls=%async_computation.2 | async-start | bytes 524288 | tf_op jit(solution)/shard_map/all_to_all | solution.py:304
  42.2 2.3 %collective-permute-start.6 = (bf16[64,1024]{1,0:T(8,128)(2,1)S(1)}, bf16[64,1024]{1,0:T(8,128)(2,1)S(1)}, u32[]{:S(2)}, u32[]{:S(2)}) collective-permute-start(bf16[64,1024]{1,0:T(8,128)(2,1)S(1)} %add_select_fusion.2), channel_id=1, source_target_pairs={{0,96},{2,98},{4,100},{6,102},{8,104},{10,106},{12,108},{14,110},{... | collective-permute-start | bytes 393224 | tf_op jit(solution)/shard_map/ppermute | solution.py:325
  44.5 1.3 %collective-permute-start.7 = (bf16[64,1024]{1,0:T(8,128)(2,1)S(1)}, bf16[64,1024]{1,0:T(8,128)(2,1)S(1)}, u32[]{:S(2)}, u32[]{:S(2)}) collective-permute-start(bf16[64,1024]{1,0:T(8,128)(2,1)S(1)} %add_select_fusion.2), channel_id=1, source_target_pairs={{0,160},{2,162},{4,164},{6,166},{8,168},{10,170},{12,172},{14,174}... | collective-permute-start | bytes 393224 | tf_op jit(solution)/shard_map/ppermute | solution.py:325
  45.8 3.2 %all-to-all-done.2.q_ref = bf16[16,64,128]{2,1,0:T(8,128)(2,1)S(1)} async-done(((bf16[16,64,128]{2,1,0:T(8,128)(2,1)}), bf16[16,64,128]{2,1,0:T(8,128)(2,1)S(1)}, u32[]{:S(2)}, u32[]{:S(2)}) %all-to-all-start.2) | async-done | bytes 262176 | tf_op jit(solution)/shard_map/all_to_all | solution.py:304
  49.0 3.2 %request_partials.1 = bf16[16,80,128]{2,1,0:T(8,128)(2,1)} custom-call(s32[1]{0:T(128)S(6)} %copy.20.len_ref, s32[1]{0:T(128)} %bitcast.2.own_ref, bf16[16,64,128]{2,1,0:T(8,128)(2,1)S(1)} %all-to-all-done.2.q_ref, bf16[256,512]{1,0:T(8,128)(2,1)S(1)} %copy-done.2, bf16[256,512]{1,0:T(8,128)(2,1)S(1)} %copy-done.4, bf16[32,512]{1,0:T(8,128)(2,1)S(1)} %copy-done.5, ...), custom_call_target="tpu_custom_call" | custom-call | flops 150994944 | bytes 3145728 | tf_op jit(solution)/shard_map/request_partials/pallas_call | solution.py:242
  52.2 5.3 %all-to-all-start.3 = ((bf16[16,80,128]{2,1,0:T(8,128)(2,1)}), bf16[16,80,128]{2,1,0:T(8,128)(2,1)S(1)}, u32[]{:S(2)}, u32[]{:S(2)}) async-start(bf16[16,80,128]{2,1,0:T(8,128)(2,1)} %request_partials.1), calls=%async_computation.3 | async-start | bytes 655360 | tf_op jit(solution)/shard_map/all_to_all | solution.py:304
  57.6 2.5 %collective-permute-start.8 = (bf16[64,1024]{1,0:T(8,128)(2,1)S(1)}, bf16[64,1024]{1,0:T(8,128)(2,1)S(1)}, u32[]{:S(2)}, u32[]{:S(2)}) collective-permute-start(bf16[64,1024]{1,0:T(8,128)(2,1)S(1)} %add_select_fusion.1), channel_id=1, source_target_pairs={{0,32},{2,34},{4,36},{6,38},{8,40},{10,42},{12,44},{14,46},{16,48}... | collective-permute-start | bytes 393224 | tf_op jit(solution)/shard_map/ppermute | solution.py:325
  60.1 2.0 %collective-permute-start.9 = (bf16[64,1024]{1,0:T(8,128)(2,1)S(1)}, bf16[64,1024]{1,0:T(8,128)(2,1)}, u32[]{:S(2)}, u32[]{:S(2)}) collective-permute-start(bf16[64,1024]{1,0:T(8,128)(2,1)S(1)} %add_select_fusion.1), channel_id=1, source_target_pairs={{0,224},{2,226},{4,228},{6,230},{8,232},{10,234},{12,236},{14,238}... | collective-permute-start | bytes 393224 | tf_op jit(solution)/shard_map/ppermute | solution.py:325
  62.1 2.5 %all-to-all-done.3.x_ref = bf16[16,80,128]{2,1,0:T(8,128)(2,1)S(1)} async-done(((bf16[16,80,128]{2,1,0:T(8,128)(2,1)}), bf16[16,80,128]{2,1,0:T(8,128)(2,1)S(1)}, u32[]{:S(2)}, u32[]{:S(2)}) %all-to-all-start.3) | async-done | bytes 327712 | tf_op jit(solution)/shard_map/all_to_all | solution.py:304
  64.6 1.1 %join_pieces.2 = bf16[8,80,128]{2,1,0:T(8,128)(2,1)} custom-call(bf16[16,80,128]{2,1,0:T(8,128)(2,1)S(1)} %all-to-all-done.3.x_ref), custom_call_target="tpu_custom_call" | custom-call | flops 1048576 | bytes 524288 | tf_op jit(solution)/shard_map/join_pieces/pallas_call | solution.py:294
  65.7 3.4 %all-to-all-start.4 = ((bf16[8,80,128]{2,1,0:T(8,128)(2,1)}), bf16[8,80,128]{2,1,0:T(8,128)(2,1)S(1)}, u32[]{:S(2)}, u32[]{:S(2)}) async-start(bf16[8,80,128]{2,1,0:T(8,128)(2,1)} %join_pieces.2), calls=%async_computation.4 | async-start | bytes 327680 | tf_op jit(solution)/shard_map/all_to_all | solution.py:304
  69.2 0.9 add_select_fusion.refs_0_.refs_4_
  70.1 1.2 %collective-permute-start.10 = (bf16[64,1024]{1,0:T(8,128)(2,1)S(1)}, bf16[64,1024]{1,0:T(8,128)(2,1)S(1)}, u32[]{:S(2)}, u32[]{:S(2)}) collective-permute-start(bf16[64,1024]{1,0:T(8,128)(2,1)S(1)} %add_select_fusion.refs_0_.refs_4_), channel_id=1, source_target_pairs={{0,8},{2,10},{4,12},{6,14},{8,16},{10,18},{12,20},{14,22},{16,24},... | collective-permute-start | bytes 393224 | tf_op jit(solution)/shard_map/ppermute | solution.py:325
  71.3 2.8 %collective-permute-start.11 = (bf16[64,1024]{1,0:T(8,128)(2,1)S(1)}, bf16[64,1024]{1,0:T(8,128)(2,1)S(1)}, u32[]{:S(2)}, u32[]{:S(2)}) collective-permute-start(bf16[64,1024]{1,0:T(8,128)(2,1)S(1)} %add_select_fusion.refs_0_.refs_4_), channel_id=1, source_target_pairs={{0,16},{2,18},{4,20},{6,22},{8,24},{10,26},{12,28},{14,30},{16,0},... | collective-permute-start | bytes 393224 | tf_op jit(solution)/shard_map/ppermute | solution.py:325
  74.7 3.8 %all-to-all-done.4.x_ref = bf16[8,80,128]{2,1,0:T(8,128)(2,1)S(1)} async-done(((bf16[8,80,128]{2,1,0:T(8,128)(2,1)}), bf16[8,80,128]{2,1,0:T(8,128)(2,1)S(1)}, u32[]{:S(2)}, u32[]{:S(2)}) %all-to-all-start.4) | async-done | bytes 163872 | tf_op jit(solution)/shard_map/all_to_all | solution.py:304
  78.5 1.1 %join_pieces.3 = bf16[16,64,128]{2,1,0:T(8,128)(2,1)} custom-call(bf16[8,80,128]{2,1,0:T(8,128)(2,1)S(1)} %all-to-all-done.4.x_ref), custom_call_target="tpu_custom_call" | custom-call | flops 1048576 | bytes 524288 | tf_op jit(solution)/shard_map/join_pieces/pallas_call | solution.py:294
  79.6 5.5 %all-to-all-start.5 = ((bf16[16,64,128]{2,1,0:T(8,128)(2,1)}), bf16[16,64,128]{2,1,0:T(8,128)(2,1)S(1)}, u32[]{:S(2)}, u32[]{:S(2)}) async-start(bf16[16,64,128]{2,1,0:T(8,128)(2,1)} %join_pieces.3), calls=%async_computation.5 | async-start | bytes 524288 | tf_op jit(solution)/shard_map/all_to_all | solution.py:304
  85.1 3.1 %context_attention.4.refs_8_ = bf16[256,4096]{1,0:T(8,128)(2,1)} custom-call(s32[1]{0:T(128)S(6)} %copy.20.len_ref, s32[1]{0:T(128)} %bitcast.root_ref, bf16[256,4096]{1,0:T(8,128)(2,1)S(1)} %copy-done, bf16[256,512]{1,0:T(8,128)(2,1)S(1)} %copy-done.2, bf16[256,512]{1,0:T(8,128)(2,1)S(1)} %copy-done.4, bf16[64,1024]{1,0:T(8,128)(2,1)S(1)} %add_select_fusion.refs_0_.refs_4_, ...), custom_call_target="tpu_custom_call" | custom-call | flops 536870912 | bytes 1310720 | tf_op jit(solution)/shard_map/context_attention/pallas_call | solution.py:81
  88.2 3.1 %context_attention.5.refs_8_ = bf16[256,4096]{1,0:T(8,128)(2,1)} custom-call(s32[1]{0:T(128)S(6)} %copy.20.len_ref, s32[1]{0:T(128)} %bitcast.root_ref, bf16[256,4096]{1,0:T(8,128)(2,1)S(1)} %copy-done, bf16[256,512]{1,0:T(8,128)(2,1)S(1)} %copy-done.2, bf16[256,512]{1,0:T(8,128)(2,1)S(1)} %copy-done.4, ...), custom_call_target="tpu_custom_call", output_to_operand_aliasing={{}: (13, {})} | custom-call | flops 536870912 | bytes 1310720 | tf_op jit(solution)/shard_map/context_attention/pallas_call | solution.py:81
  91.3 3.1 %context_attention.6.refs_8_ = bf16[256,4096]{1,0:T(8,128)(2,1)} custom-call(s32[1]{0:T(128)S(6)} %copy.20.len_ref, s32[1]{0:T(128)} %bitcast.root_ref, bf16[256,4096]{1,0:T(8,128)(2,1)S(1)} %copy-done, bf16[256,512]{1,0:T(8,128)(2,1)S(1)} %copy-done.2, bf16[256,512]{1,0:T(8,128)(2,1)S(1)} %copy-done.4, ...), custom_call_target="tpu_custom_call", output_to_operand_aliasing={{}: (13, {})} | custom-call | flops 536870912 | bytes 1310720 | tf_op jit(solution)/shard_map/context_attention/pallas_call | solution.py:81
  94.4 3.1 %context_attention.7 = bf16[256,4096]{1,0:T(8,128)(2,1)} custom-call(s32[1]{0:T(128)S(6)} %copy.20.len_ref, s32[1]{0:T(128)} %bitcast.root_ref, bf16[256,4096]{1,0:T(8,128)(2,1)S(1)} %copy-done, bf16[256,512]{1,0:T(8,128)(2,1)S(1)} %copy-done.2, bf16[256,512]{1,0:T(8,128)(2,1)S(1)} %copy-done.4, ...), custom_call_target="tpu_custom_call", output_to_operand_aliasing={{}: (13, {})} | custom-call | flops 536870912 | bytes 1310720 | tf_op jit(solution)/shard_map/context_attention/pallas_call | solution.py:81
  (37 shorter events, 4.2 us)
Async XLA Ops:
  0.6 48.3 %copy-start.5 = (bf16[32,512]{1,0:T(8,128)(2,1)S(1)}, bf16[32,512]{1,0:T(8,128)(2,1)}, u32[]{:S(2)}) copy-start(bf16[32,512]{1,0:T(8,128)(2,1)} %rk_ref.1) | copy-start | bytes 98308
  0.6 48.3 %copy-start.6 = (bf16[32,512]{1,0:T(8,128)(2,1)S(1)}, bf16[32,512]{1,0:T(8,128)(2,1)}, u32[]{:S(2)}) copy-start(bf16[32,512]{1,0:T(8,128)(2,1)} %rv_ref.1) | copy-start | bytes 98308
  2.4 46.6 %copy-start.2 = (bf16[256,512]{1,0:T(8,128)(2,1)S(1)}, bf16[256,512]{1,0:T(8,128)(2,1)}, u32[]{:S(2)}) copy-start(bf16[256,512]{1,0:T(8,128)(2,1)} %k_ref.11) | copy-start | bytes 786436
  2.4 46.6 %copy-start.4 = (bf16[256,512]{1,0:T(8,128)(2,1)S(1)}, bf16[256,512]{1,0:T(8,128)(2,1)}, u32[]{:S(2)}) copy-start(bf16[256,512]{1,0:T(8,128)(2,1)} %v_ref.11) | copy-start | bytes 786436
  2.4 15.5 %all-to-all-start = ((bf16[32,32,128]{2,1,0:T(8,128)(2,1)}), bf16[32,32,128]{2,1,0:T(8,128)(2,1)S(1)}, u32[]{:S(2)}, u32[]{:S(2)}) async-start(bf16[32,32,128]{2,1,0:T(8,128)(2,1)} %pack.1), calls=%async_computation | async-start | bytes 524288 | tf_op jit(solution)/shard_map/all_to_all | solution.py:304
  10.8 1.0 copy-start.1
  11.7 0.9 copy-start.3
  12.7 14.3 %collective-permute-start = (bf16[64,1024]{1,0:T(8,128)(2,1)S(1)}, bf16[64,1024]{1,0:T(8,128)(2,1)S(1)}, u32[]{:S(2)}, u32[]{:S(2)}) collective-permute-start(bf16[64,1024]{1,0:T(8,128)(2,1)S(1)} %get-tuple-element.7), channel_id=1, source_target_pairs={{0,8},{1,9}} | collective-permute-start | bytes 393224 | tf_op jit(solution)/shard_map/ppermute | solution.py:325
  14.0 13.0 %collective-permute-start.1 = (bf16[64,1024]{1,0:T(8,128)(2,1)S(1)}, bf16[64,1024]{1,0:T(8,128)(2,1)S(1)}, u32[]{:S(2)}, u32[]{:S(2)}) collective-permute-start(bf16[64,1024]{1,0:T(8,128)(2,1)S(1)} %get-tuple-element.8), channel_id=1, source_target_pairs={{0,16},{1,17}} | collective-permute-start | bytes 393224 | tf_op jit(solution)/shard_map/ppermute | solution.py:325
  14.7 12.3 %collective-permute-start.2 = (bf16[64,1024]{1,0:T(8,128)(2,1)S(1)}, bf16[64,1024]{1,0:T(8,128)(2,1)S(1)}, u32[]{:S(2)}, u32[]{:S(2)}) collective-permute-start(bf16[64,1024]{1,0:T(8,128)(2,1)S(1)} %get-tuple-element.9), channel_id=1, source_target_pairs={{0,24},{1,25}} | collective-permute-start | bytes 393224 | tf_op jit(solution)/shard_map/ppermute | solution.py:325
  18.5 18.0 %all-to-all-start.1 = ((bf16[8,64,128]{2,1,0:T(8,128)(2,1)}), bf16[8,64,128]{2,1,0:T(8,128)(2,1)S(1)}, u32[]{:S(2)}, u32[]{:S(2)}) async-start(bf16[8,64,128]{2,1,0:T(8,128)(2,1)} %choose.2), calls=%async_computation.1 | async-start | bytes 262144 | tf_op jit(solution)/shard_map/all_to_all | solution.py:304
  27.1 15.0 %collective-permute-start.3 = (bf16[64,1024]{1,0:T(8,128)(2,1)S(1)}, bf16[64,1024]{1,0:T(8,128)(2,1)S(1)}, u32[]{:S(2)}, u32[]{:S(2)}) collective-permute-start(bf16[64,1024]{1,0:T(8,128)(2,1)S(1)} %add_select_fusion.3), channel_id=1, source_target_pairs={{0,2},{8,10},{16,18},{24,26},{1,3},{9,11},{17,19},{25,27}} | collective-permute-start | bytes 393224 | tf_op jit(solution)/shard_map/ppermute | solution.py:325
  29.2 12.9 %collective-permute-start.4 = (bf16[64,1024]{1,0:T(8,128)(2,1)S(1)}, bf16[64,1024]{1,0:T(8,128)(2,1)S(1)}, u32[]{:S(2)}, u32[]{:S(2)}) collective-permute-start(bf16[64,1024]{1,0:T(8,128)(2,1)S(1)} %add_select_fusion.3), channel_id=1, source_target_pairs={{0,4},{8,12},{16,20},{24,28},{1,5},{9,13},{17,21},{25,29}} | collective-permute-start | bytes 393224 | tf_op jit(solution)/shard_map/ppermute | solution.py:325
  30.9 11.2 %collective-permute-start.5 = (bf16[64,1024]{1,0:T(8,128)(2,1)S(1)}, bf16[64,1024]{1,0:T(8,128)(2,1)S(1)}, u32[]{:S(2)}, u32[]{:S(2)}) collective-permute-start(bf16[64,1024]{1,0:T(8,128)(2,1)S(1)} %add_select_fusion.3), channel_id=1, source_target_pairs={{0,6},{8,14},{16,22},{24,30},{1,7},{9,15},{17,23},{25,31}} | collective-permute-start | bytes 393224 | tf_op jit(solution)/shard_map/ppermute | solution.py:325
  37.3 11.7 %all-to-all-start.2 = ((bf16[16,64,128]{2,1,0:T(8,128)(2,1)}), bf16[16,64,128]{2,1,0:T(8,128)(2,1)S(1)}, u32[]{:S(2)}, u32[]{:S(2)}) async-start(bf16[16,64,128]{2,1,0:T(8,128)(2,1)} %choose.3), calls=%async_computation.2 | async-start | bytes 524288 | tf_op jit(solution)/shard_map/all_to_all | solution.py:304
  42.2 15.4 %collective-permute-start.6 = (bf16[64,1024]{1,0:T(8,128)(2,1)S(1)}, bf16[64,1024]{1,0:T(8,128)(2,1)S(1)}, u32[]{:S(2)}, u32[]{:S(2)}) collective-permute-start(bf16[64,1024]{1,0:T(8,128)(2,1)S(1)} %add_select_fusion.2), channel_id=1, source_target_pairs={{0,96},{2,98},{4,100},{6,102},{8,104},{10,106},{12,108},{14,110},{... | collective-permute-start | bytes 393224 | tf_op jit(solution)/shard_map/ppermute | solution.py:325
  44.5 13.1 %collective-permute-start.7 = (bf16[64,1024]{1,0:T(8,128)(2,1)S(1)}, bf16[64,1024]{1,0:T(8,128)(2,1)S(1)}, u32[]{:S(2)}, u32[]{:S(2)}) collective-permute-start(bf16[64,1024]{1,0:T(8,128)(2,1)S(1)} %add_select_fusion.2), channel_id=1, source_target_pairs={{0,160},{2,162},{4,164},{6,166},{8,168},{10,170},{12,172},{14,174}... | collective-permute-start | bytes 393224 | tf_op jit(solution)/shard_map/ppermute | solution.py:325
  49.0 36.1 %copy-start = (bf16[256,4096]{1,0:T(8,128)(2,1)S(1)}, bf16[256,4096]{1,0:T(8,128)(2,1)}, u32[]{:S(2)}) copy-start(bf16[256,4096]{1,0:T(8,128)(2,1)} %q_ref.7) | copy-start | bytes 6291460
  52.2 12.4 %all-to-all-start.3 = ((bf16[16,80,128]{2,1,0:T(8,128)(2,1)}), bf16[16,80,128]{2,1,0:T(8,128)(2,1)S(1)}, u32[]{:S(2)}, u32[]{:S(2)}) async-start(bf16[16,80,128]{2,1,0:T(8,128)(2,1)} %request_partials.1), calls=%async_computation.3 | async-start | bytes 655360 | tf_op jit(solution)/shard_map/all_to_all | solution.py:304
  57.6 11.5 %collective-permute-start.8 = (bf16[64,1024]{1,0:T(8,128)(2,1)S(1)}, bf16[64,1024]{1,0:T(8,128)(2,1)S(1)}, u32[]{:S(2)}, u32[]{:S(2)}) collective-permute-start(bf16[64,1024]{1,0:T(8,128)(2,1)S(1)} %add_select_fusion.1), channel_id=1, source_target_pairs={{0,32},{2,34},{4,36},{6,38},{8,40},{10,42},{12,44},{14,46},{16,48}... | collective-permute-start | bytes 393224 | tf_op jit(solution)/shard_map/ppermute | solution.py:325
  60.1 9.0 %collective-permute-start.9 = (bf16[64,1024]{1,0:T(8,128)(2,1)S(1)}, bf16[64,1024]{1,0:T(8,128)(2,1)}, u32[]{:S(2)}, u32[]{:S(2)}) collective-permute-start(bf16[64,1024]{1,0:T(8,128)(2,1)S(1)} %add_select_fusion.1), channel_id=1, source_target_pairs={{0,224},{2,226},{4,228},{6,230},{8,232},{10,234},{12,236},{14,238}... | collective-permute-start | bytes 393224 | tf_op jit(solution)/shard_map/ppermute | solution.py:325
  65.7 12.7 %all-to-all-start.4 = ((bf16[8,80,128]{2,1,0:T(8,128)(2,1)}), bf16[8,80,128]{2,1,0:T(8,128)(2,1)S(1)}, u32[]{:S(2)}, u32[]{:S(2)}) async-start(bf16[8,80,128]{2,1,0:T(8,128)(2,1)} %join_pieces.2), calls=%async_computation.4 | async-start | bytes 327680 | tf_op jit(solution)/shard_map/all_to_all | solution.py:304
  70.1 14.9 %collective-permute-start.10 = (bf16[64,1024]{1,0:T(8,128)(2,1)S(1)}, bf16[64,1024]{1,0:T(8,128)(2,1)S(1)}, u32[]{:S(2)}, u32[]{:S(2)}) collective-permute-start(bf16[64,1024]{1,0:T(8,128)(2,1)S(1)} %add_select_fusion.refs_0_.refs_4_), channel_id=1, source_target_pairs={{0,8},{2,10},{4,12},{6,14},{8,16},{10,18},{12,20},{14,22},{16,24},... | collective-permute-start | bytes 393224 | tf_op jit(solution)/shard_map/ppermute | solution.py:325
  71.3 13.7 %collective-permute-start.11 = (bf16[64,1024]{1,0:T(8,128)(2,1)S(1)}, bf16[64,1024]{1,0:T(8,128)(2,1)S(1)}, u32[]{:S(2)}, u32[]{:S(2)}) collective-permute-start(bf16[64,1024]{1,0:T(8,128)(2,1)S(1)} %add_select_fusion.refs_0_.refs_4_), channel_id=1, source_target_pairs={{0,16},{2,18},{4,20},{6,22},{8,24},{10,26},{12,28},{14,30},{16,0},... | collective-permute-start | bytes 393224 | tf_op jit(solution)/shard_map/ppermute | solution.py:325
  74.1 10.9 %collective-permute-start.12 = (bf16[64,1024]{1,0:T(8,128)(2,1)S(1)}, bf16[64,1024]{1,0:T(8,128)(2,1)S(1)}, u32[]{:S(2)}, u32[]{:S(2)}) collective-permute-start(bf16[64,1024]{1,0:T(8,128)(2,1)S(1)} %add_select_fusion.refs_0_.refs_4_), channel_id=1, source_target_pairs={{0,24},{2,26},{4,28},{6,30},{8,0},{10,2},{12,4},{14,6},{16,8},{18,... | collective-permute-start | bytes 393224 | tf_op jit(solution)/shard_map/ppermute | solution.py:325
  79.6 17.9 %all-to-all-start.5 = ((bf16[16,64,128]{2,1,0:T(8,128)(2,1)}), bf16[16,64,128]{2,1,0:T(8,128)(2,1)S(1)}, u32[]{:S(2)}, u32[]{:S(2)}) async-start(bf16[16,64,128]{2,1,0:T(8,128)(2,1)} %join_pieces.3), calls=%async_computation.5 | async-start | bytes 524288 | tf_op jit(solution)/shard_map/all_to_all | solution.py:304

commit v2 on v1

v2 whole, which is shorter than its diff:
```python
import functools

import jax
import jax.numpy as jnp
from jax import lax
from jax.experimental import pallas as pl
from jax.experimental.pallas import tpu as pltpu
from jax.sharding import PartitionSpec as P

HEAD_SIZE = 128
GROUP = 8
SCALE = HEAD_SIZE**-0.5
LOG2E = 1.4426950408889634
LN2 = 0.6931471805599453
MARK = 1024.0
VMEM_LIMIT = 32 * 1024 * 1024


def dot_nt(a, b):
    return lax.dot_general(a, b, (((1,), (1,)), ((), ())), preferred_element_type=jnp.float32)


def dot_nn(a, b):
    return lax.dot_general(a, b, (((1,), (0,)), ((), ())), preferred_element_type=jnp.float32)


def context_kernel(count, len_ref, root_ref, q_ref, k_ref, v_ref, *refs):
    ak_refs, av_refs = refs[:count], refs[count : 2 * count]
    o_ref, vs_ref = refs[-2:]
    rows = k_ref.shape[0]
    half = rows // 2
    own_len = len_ref[0]
    root = root_ref[0] > 0
    ak = jnp.concatenate([ref[...] for ref in ak_refs], axis=0)
    ak = jnp.where(root, jnp.broadcast_to(k_ref[0:1, :], ak.shape), ak)
    av = jnp.concatenate([ref[...] for ref in av_refs], axis=0)
    hidden = (av > 100.0) | root
    vs_ref[0:rows, :HEAD_SIZE] = jnp.where(hidden, jnp.zeros_like(av), av)
    vs_ref[0:rows, HEAD_SIZE:] = jnp.where(hidden, jnp.zeros_like(av), jnp.ones_like(av))
    vs_ref[rows:, :HEAD_SIZE] = v_ref[...]
    vs_ref[rows:, HEAD_SIZE:] = jnp.ones((rows, HEAD_SIZE), jnp.bfloat16)
    c = SCALE * LOG2E
    row = lax.broadcasted_iota(jnp.int32, (2 * half, half), 0)
    col = lax.broadcasted_iota(jnp.int32, (2 * half, half), 1)
    causal = jnp.where(col <= lax.rem(row, half), 0.0, -jnp.inf).astype(jnp.float32)

    def lanes(g):
        return slice(g * HEAD_SIZE, (g + 1) * HEAD_SIZE)

    def scores(top, g):
        keys = top + half
        q = jnp.concatenate([q_ref[top:keys, lanes(g)], q_ref[top:keys, lanes(g + 1)]], axis=0)
        sa = dot_nt(q, ak)
        so = dot_nt(q, k_ref[0:keys, :])
        tiles = [sa[:, i : i + half] for i in range(0, rows, half)]
        tiles += [so[:, i : i + half] for i in range(0, top, half)]
        return tiles + [so[:, top:keys] + causal]

    def finish(top, g, tiles):
        keys = top + half
        live = (top + lax.broadcasted_iota(jnp.int32, (half, HEAD_SIZE), 0)) < own_len
        peak = jnp.max(functools.reduce(jnp.maximum, tiles), axis=1, keepdims=True)
        weights = [jnp.exp2((tile - peak) * c).astype(jnp.bfloat16) for tile in tiles]
        acc = dot_nn(jnp.concatenate(weights, axis=1), vs_ref[0 : rows + keys, :])
        total = acc[:, HEAD_SIZE:]
        inverse = pl.reciprocal(total, approx=True)
        inverse = inverse * (2.0 - total * inverse)
        out = acc[:, :HEAD_SIZE] * inverse
        for i in range(2):
            part = jnp.where(live, out[i * half : (i + 1) * half], 0.0)
            o_ref[top:keys, lanes(g + i)] = part.astype(jnp.bfloat16)

    work = [(top, g) for top in (0, half) for g in range(0, GROUP, 2)]
    tiles = scores(*work[0])
    for i, item in enumerate(work):
        later = scores(*work[i + 1]) if i + 1 < len(work) else None
        finish(*item, tiles)
        tiles = later


def context_attention(own_len, is_root, q, k, v, anchor):
    rows, width = q.shape
    heads = k.shape[1] // HEAD_SIZE
    wide = GROUP * HEAD_SIZE
    count = len(anchor)
    slab = anchor[0].shape[0]
    smem = pl.BlockSpec(memory_space=pltpu.SMEM)
    kv_spec = pl.BlockSpec((rows, HEAD_SIZE), lambda h: (0, h))
    wide_spec = pl.BlockSpec((rows, wide), lambda h: (0, h))
    specs = [smem, smem, wide_spec, kv_spec, kv_spec]
    specs += [pl.BlockSpec((slab, HEAD_SIZE), lambda h: (0, h))] * count
    specs += [pl.BlockSpec((slab, HEAD_SIZE), lambda h: (0, heads + h))] * count
    return pl.pallas_call(
        functools.partial(context_kernel, count),
        grid=(heads,),
        out_shape=jax.ShapeDtypeStruct((rows, width), jnp.bfloat16),
        in_specs=specs,
        out_specs=wide_spec,
        scratch_shapes=[pltpu.VMEM((2 * rows, 2 * HEAD_SIZE), jnp.bfloat16)],
        compiler_params=pltpu.CompilerParams(vmem_limit_bytes=VMEM_LIMIT),
        cost_estimate=pl.CostEstimate(
            flops=8 * rows * width * rows, bytes_accessed=5 * 2**20, transcendentals=2 * rows * rows * heads * GROUP
        ),
        name="context_attention",
    )(own_len, is_root, q, k, v, *anchor, *anchor)


def mark_kernel(n_x, len_ref, own_ref, y_ref, k_ref, v_ref, rk_ref, rv_ref, *o_refs):
    rows, width = k_ref.shape
    own = rk_ref.shape[0]
    slab = rows // n_x
    first = jnp.broadcast_to(k_ref[0:1, :], (slab, width))
    for i, o_ref in enumerate(o_refs[:n_x]):
        span = slice(i * slab, (i + 1) * slab)
        valid = (i * slab + lax.broadcasted_iota(jnp.int32, first.shape, 0)) < len_ref[0]
        o_ref[:, :width] = jnp.where(valid, k_ref[span, :], first)
        o_ref[:, width:] = jnp.where(valid, v_ref[span, :], jnp.full_like(first, MARK))
    lines = o_refs[n_x:]
    valid = lax.broadcasted_iota(jnp.int32, (rows, HEAD_SIZE), 0) < len_ref[0]
    is_owner = own_ref[0] > 0
    for i, o_ref in enumerate(lines):
        head = lax.rem(y_ref[0] + i, len(lines))
        lanes = pl.ds(pl.multiple_of(head * HEAD_SIZE, HEAD_SIZE), HEAD_SIZE)
        first = k_ref[0:1, lanes]
        o_ref[0:rows, :] = jnp.where(valid, k_ref[:, lanes], jnp.broadcast_to(first, valid.shape))
        o_ref[rows : rows + own, :] = jnp.where(
            is_owner, rk_ref[:, lanes], jnp.broadcast_to(first, (own, HEAD_SIZE))
        )
        mark = jnp.full((rows, HEAD_SIZE), MARK, jnp.bfloat16)
        o_ref[rows + own : 2 * rows + own, :] = jnp.where(valid, v_ref[:, lanes], mark)
        o_ref[2 * rows + own :, :] = jnp.where(is_owner, rv_ref[:, lanes], mark[0:own])


def mark(own_len, is_owner, y, k, v, rk, rv, n_x, n_y):
    rows, width = k.shape
    vmem = pl.BlockSpec(memory_space=pltpu.VMEM)
    smem = pl.BlockSpec(memory_space=pltpu.SMEM)
    shapes = [jax.ShapeDtypeStruct((rows // n_x, 2 * width), k.dtype)] * n_x
    shapes += [jax.ShapeDtypeStruct((2 * (rows + rk.shape[0]), HEAD_SIZE), k.dtype)] * n_y
    return pl.pallas_call(
        functools.partial(mark_kernel, n_x),
        out_shape=shapes,
        in_specs=[smem] * 3 + [vmem] * 4,
        out_specs=[vmem] * len(shapes),
        compiler_params=pltpu.CompilerParams(vmem_limit_bytes=56 * 1024 * 1024),
        cost_estimate=pl.CostEstimate(flops=2**18, bytes_accessed=2**21, transcendentals=0),
        name="mark",
    )(own_len, is_owner, y, k, v, rk, rv)


def pack_kernel(n_y, rq_ref, o_ref):
    own, width = rq_ref.shape
    targets = o_ref.shape[0] // 2
    some = o_ref.shape[1] // own
    for j in range(targets):
        x, y = j // n_y, j % n_y
        for c in range(2):
            for i in range(some):
                lane = c * (width // 2) + (GROUP * y + some * x + i) * HEAD_SIZE
                o_ref[2 * j + c, i * own : (i + 1) * own, :] = rq_ref[:, lane : lane + HEAD_SIZE]


def pack(rq, targets, n_y):
    vmem = pl.BlockSpec(memory_space=pltpu.VMEM)
    height = rq.size // (2 * targets * HEAD_SIZE)
    return pl.pallas_call(
        functools.partial(pack_kernel, n_y),
        out_shape=jax.ShapeDtypeStruct((2 * targets, height, HEAD_SIZE), jnp.bfloat16),
        in_specs=[vmem],
        out_specs=vmem,
        compiler_params=pltpu.CompilerParams(vmem_limit_bytes=56 * 1024 * 1024),
        cost_estimate=pl.CostEstimate(flops=2**18, bytes_accessed=2**19, transcendentals=0),
        name="pack",
    )(rq)


def plane_kernel(source_ref, x_ref, o_ref):
    own = 16
    source = 2 * source_ref[0]
    parts = []
    for i in range(x_ref.shape[1] // own):
        pick = slice(i * own, (i + 1) * own)
        parts += [x_ref[source, pick, :], x_ref[source + 1, pick, :]]
    part = jnp.concatenate(parts, axis=0)
    for z in range(o_ref.shape[0]):
        o_ref[z] = part


def line_kernel(plane_ref, x_ref, o_ref):
    part = x_ref[plane_ref[0]]
    piece = part.shape[0]
    for j in range(o_ref.shape[0]):
        o_ref[j, 0:piece, :] = part
        o_ref[j, piece : 2 * piece, :] = part


def choose(kernel, index, x, shape):
    vmem = pl.BlockSpec(memory_space=pltpu.VMEM)
    return pl.pallas_call(
        kernel,
        out_shape=jax.ShapeDtypeStruct(shape, x.dtype),
        in_specs=[pl.BlockSpec(memory_space=pltpu.SMEM), vmem],
        out_specs=vmem,
        compiler_params=pltpu.CompilerParams(vmem_limit_bytes=VMEM_LIMIT),
        cost_estimate=pl.CostEstimate(flops=8 * 10**8, bytes_accessed=2**19, transcendentals=0),
        name="choose",
    )(index, x)


def split3(x):
    high = x.astype(jnp.bfloat16).astype(jnp.float32)
    rest = x - high
    mid = rest.astype(jnp.bfloat16).astype(jnp.float32)
    low = (rest - mid).astype(jnp.bfloat16).astype(jnp.float32)
    return high, mid, low


def code_rows(pair, last, height):
    row = lax.broadcasted_iota(jnp.int32, (height, HEAD_SIZE), 0)
    return jnp.where(row == 0, pair, jnp.where(row == 1, last, 0.0)).astype(jnp.bfloat16)


def request_kernel(own, q_ref, *refs):
    lines, o_ref, v_ref = refs[:-2], refs[-2], refs[-1]
    count = q_ref.shape[0]
    height = o_ref.shape[1]
    piece = (height - 16) // 2
    n = count * piece
    both = lines[0].shape[0] // 2
    rows = both - own
    c = SCALE * LOG2E
    q = q_ref[:, 0:piece, :].reshape(n, HEAD_SIZE)
    for i, ref in enumerate(lines):
        for part, (top, at) in (
            (ref[both : both + rows, :], (i * rows, rows)),
            (ref[both + rows :, :], (len(lines) * rows + i * own, own)),
        ):
            hidden = part > 100.0
            v_ref[top : top + at, :HEAD_SIZE] = jnp.where(hidden, jnp.zeros_like(part), part)
            v_ref[top : top + at, HEAD_SIZE:] = jnp.where(hidden, jnp.zeros_like(part), jnp.ones_like(part))
    own_keys = jnp.concatenate([ref[rows:both, :] for ref in lines], axis=0)
    row = lax.rem(lax.broadcasted_iota(jnp.int32, (n, own_keys.shape[0]), 0), own)
    col = lax.rem(lax.broadcasted_iota(jnp.int32, (n, own_keys.shape[0]), 1), own)
    scores = [dot_nt(q, ref[0:rows, :]) for ref in lines]
    scores.append(jnp.where(col <= row, dot_nt(q, own_keys), -jnp.inf))
    tiles = [s[:, i : i + HEAD_SIZE] for s in scores for i in range(0, s.shape[1], HEAD_SIZE)]
    peak = jnp.max(functools.reduce(jnp.maximum, tiles), axis=1, keepdims=True)
    weights = [jnp.exp2((tile - peak) * c).astype(jnp.bfloat16) for tile in tiles]
    acc = dot_nn(jnp.concatenate(weights, axis=1), v_ref[...])
    total = acc[:, HEAD_SIZE:]
    out = acc[:, :HEAD_SIZE] / total
    out_high = out.astype(jnp.bfloat16)
    out_low = (out - out_high.astype(jnp.float32)).astype(jnp.bfloat16)
    lse = peak * SCALE + jnp.log(total)
    high, mid, low = split3(lse)
    row = lax.broadcasted_iota(jnp.int32, (piece, HEAD_SIZE), 0)
    lane = lax.broadcasted_iota(jnp.int32, (piece, HEAD_SIZE), 1)
    for p in range(count):
        part = slice(p * piece, (p + 1) * piece)
        pair = jnp.where(row == lane, high[part], jnp.where(row + piece == lane, mid[part], 0.0))
        last = jnp.where(row == lane, low[part], 0.0)
        o_ref[p, 0:piece, :] = out_high[part]
        o_ref[p, piece : 2 * piece, :] = out_low[part]
        o_ref[p, 2 * piece : height, :] = code_rows(
            jnp.sum(pair, axis=0, keepdims=True), jnp.sum(last, axis=0, keepdims=True), 16
        )


def request_partials(moved, lines, own):
    count, piece = moved.shape[0], moved.shape[1] // 2
    keys = len(lines) * lines[0].shape[0] // 2
    vmem = pl.BlockSpec(memory_space=pltpu.VMEM)
    return pl.pallas_call(
        functools.partial(request_kernel, own),
        out_shape=jax.ShapeDtypeStruct((count, 2 * piece + 16, HEAD_SIZE), jnp.bfloat16),
        in_specs=[vmem] * (1 + len(lines)),
        out_specs=vmem,
        scratch_shapes=[pltpu.VMEM((keys, 2 * HEAD_SIZE), jnp.bfloat16)],
        compiler_params=pltpu.CompilerParams(vmem_limit_bytes=VMEM_LIMIT),
        cost_estimate=pl.CostEstimate(
            flops=2 * 10**9, bytes_accessed=2**20, transcendentals=count * piece * keys
        ),
        name="request_partials",
    )(moved, *lines)


def join_kernel(parts_in, keep_code, *refs):
    x_refs, o_ref = refs[:-1], refs[-1]
    if len(x_refs) == 1:
        x_refs = [x_refs[0].at[i] for i in range(x_refs[0].shape[0])]
    height = x_refs[0].shape[0]
    top = height - 16
    piece = top // parts_in
    count = max(len(x_refs), 8)
    row = lax.broadcasted_iota(jnp.int32, (count, HEAD_SIZE), 0)
    lane = lax.broadcasted_iota(jnp.int32, (count, HEAD_SIZE), 1)
    pair = jnp.zeros((count, HEAD_SIZE), jnp.float32)
    last = jnp.zeros((count, HEAD_SIZE), jnp.float32)
    for i, ref in enumerate(x_refs):
        code = ref[top:height, :].astype(jnp.float32)
        pair = jnp.where(row == i, code[0:1, :], pair)
        last = jnp.where(row == i, code[1:2, :], last)
    lse = jnp.where(lane < piece, pair + pltpu.roll(pair, piece, 1) + last, 0.0)
    lse = jnp.where(row < len(x_refs), lse, -jnp.inf)
    peak = jnp.max(lse, axis=0, keepdims=True)
    weight = jnp.exp(lse - peak)
    total = jnp.sum(weight, axis=0, keepdims=True)
    column = jnp.transpose(weight / total)
    out = jnp.zeros((piece, HEAD_SIZE), jnp.float32)
    for i, ref in enumerate(x_refs):
        part = ref[0:piece, :].astype(jnp.float32)
        if parts_in > 1:
            part = part + ref[piece:top, :].astype(jnp.float32)
        out = out + column[0:piece, i : i + 1] * part
    parts = [out.astype(jnp.bfloat16)]
    if keep_code:
        high, mid, low = split3(peak + jnp.log(total))
        pair = jnp.where(lane[0:1] < piece, high, pltpu.roll(mid, piece, 1))
        parts.append(code_rows(pair, low, 16))
    part = jnp.concatenate(parts, axis=0)
    if len(o_ref.shape) == 2:
        o_ref[...] = part
    else:
        for i in range(o_ref.shape[0]):
            o_ref[i] = part


def join(arrays, copies, parts_in, keep_code):
    height = (arrays[0].shape[-2] - 16) // parts_in + (16 if keep_code else 0)
    shape = (copies, height, HEAD_SIZE) if copies else (height, HEAD_SIZE)
    return pl.pallas_call(
        functools.partial(join_kernel, parts_in, keep_code),
        out_shape=jax.ShapeDtypeStruct(shape, jnp.bfloat16),
        compiler_params=pltpu.CompilerParams(vmem_limit_bytes=VMEM_LIMIT),
        cost_estimate=pl.CostEstimate(flops=2 * 10**9, bytes_accessed=2**19, transcendentals=1024),
        name="join_pieces",
    )(*arrays)


def exchange(x, axis):
    return lax.all_to_all(x, axis, split_axis=0, concat_axis=0, tiled=True)


def local(n_z, n_x, n_y, q, k, v, block_lengths, rq, rk, rv, query_owner):
    n_xy = n_x * n_y
    z, x, y = (lax.axis_index(name) for name in ("z", "x", "y"))
    owner = query_owner[0]
    owner_z, owner_xy = owner // n_xy, owner % n_xy
    own_len = block_lengths
    mine = (z == owner_z) & (x * n_y + y == owner_xy)
    is_owner = mine.astype(jnp.int32).reshape(1)
    is_root = ((z == 0) & (x == 0) & (y == 0)).astype(jnp.int32).reshape(1)
    own_rows = rk.shape[0]

    def move(value, pairs):
        return lax.ppermute(value, ("z", "x", "y"), pairs)

    moved = exchange(pack(rq, n_xy, n_y), ("x", "y", "head"))
    marked = mark(own_len, is_owner, y.reshape(1), k, v, rk, rv, n_x, n_y)
    pieces, lines = marked[:n_x], marked[n_x:]
    got = [move(pieces[i], [(0, i * n_y)]) for i in range(1, n_x)]
    lines = [lines[0]] + [
        lax.ppermute(lines[i], "y", [(a, (a + i) % n_y) for a in range(n_y)]) for i in range(1, n_y)
    ]

    moved = choose(plane_kernel, owner_xy.reshape(1), moved, (n_z, 2 * moved.shape[1], HEAD_SIZE))
    moved, got = lax.optimization_barrier((moved, got))
    anchor = jnp.where(x == 0, pieces[0], got[0] + got[1] + got[2])
    got = [move(anchor, [(i * n_y, i * n_y + j) for i in range(n_x)]) for j in range(1, n_y)]
    moved = exchange(moved, "z")

    moved = choose(line_kernel, owner_z.reshape(1), moved, (n_x, 2 * moved.shape[1], HEAD_SIZE))
    moved, got, lines = lax.optimization_barrier((moved, got, lines))
    anchor = jnp.where(y == 0, anchor, got[0] + got[1] + got[2])
    plane = range(n_xy)
    got = [move(anchor, [(p, to * n_xy + p) for p in plane]) for to in (3, 5)]
    moved = exchange(moved, "x")

    partials = request_partials(moved, lines, own_rows)
    partials, got = lax.optimization_barrier((partials, got))
    anchor = jnp.where(z == 0, anchor, got[0] + got[1])
    steps = (((0, 1), (3, 4), (5, 6)), ((0, 7), (3, 2)))
    got = [move(anchor, [(a * n_xy + p, b * n_xy + p) for a, b in step for p in plane]) for step in steps]
    partials = exchange(partials, "x")

    planes = join([partials], n_z, 2, True)
    planes, got = lax.optimization_barrier((planes, got))
    anchor = jnp.where((z == 0) | (z == 3) | (z == 5), anchor, got[0] + got[1])
    anchors = [anchor]
    for i in range(1, n_x):
        anchors.append(lax.ppermute(anchor, "x", [(a, (a + i) % n_x) for a in range(n_x)]))
    planes = exchange(planes, "z")

    answer = exchange(join([planes], n_xy, 1, False), ("x", "y"))
    context_output = context_attention(own_len, is_root, q, k, v, anchors)
    answer = answer.reshape(n_x, n_y, -1, own_rows, HEAD_SIZE).transpose(3, 1, 0, 2, 4).reshape(own_rows, q.shape[1])
    request_output = jnp.where(mine, answer, jnp.zeros_like(answer))
    return context_output, request_output


def solution(mesh):
    n_z, n_x, n_y = 8, 4, 4
    grid = jax.sharding.Mesh(mesh.devices.reshape(n_z, n_x, n_y, 2), ("z", "x", "y", "head"))
    ctx = ("z", "x", "y")
    in_specs = (
        P(ctx, "head"),
        P(ctx, "head"),
        P(ctx, "head"),
        P(ctx),
        P(ctx + ("head",), None),
        P(ctx, "head"),
        P(ctx, "head"),
        P(),
    )
    out_specs = (P(ctx, "head"), P(ctx, "head"))
    return jax.shard_map(
        functools.partial(local, n_z, n_x, n_y),
        mesh=grid,
        in_specs=in_specs,
        out_specs=out_specs,
        check_vma=False,
    )
```

time: 99.2 us -> 93.8 us (0.946)
  starting transfers between devices: 55.6 us -> 60.5 us
  Pallas kernels: 21 us -> 16.8 us
  waiting for transfers between devices: 15.6 us -> 12.2 us
  local copies, waits for them, and re-layouts: 2.67 us -> 1.12 us
    all_to_all x6, waiting for transfers between devices: 15.5 us -> 10.1 us  [exchange(): return lax.all_to_all(x, axis, split_axis=0, concat_axis=0, tiled=True)]
    pallas_call x9 -> x6, Pallas kernels: 19.6 us -> 15.5 us  [the longest x1 7.94 us: context_attention(): pl.pallas_call(functools.partial(context_kernel, count), grid=(heads,), o...]
    ppermute x13 -> x16, starting transfers between devices: 20.4 us -> 23.8 us  [the longest x10 15.3 us: move(): return lax.ppermute(value, ('z', 'x', 'y'), pairs)]
    ppermute x13 -> x16, waiting for transfers between devices: 0.03 us -> 2.05 us  [the longest x10 2.03 us: move(): return lax.ppermute(value, ('z', 'x', 'y'), pairs)]
    unnamed x14 -> x12, local copies, waits for them, and re-layouts: 1.92 us -> 0.03 us
    all_to_all x6, starting transfers between devices: 35.3 us -> 36.7 us  [exchange(): return lax.all_to_all(x, axis, split_axis=0, concat_axis=0, tiled=True)]
  transfers between devices with their start and end apart: 19 -> 22, of which waited for: 5 -> 6; matrix products, arithmetic and copies ran while one was open for 1% -> 0% of each run, Pallas kernels for 20% -> 16%
where the time goes in v2:
time: 93.8 us; the launch traced here: 92.9 us
  starting transfers between devices  60.5 us (64%)
  Pallas kernels  16.8 us (18%)
  waiting for transfers between devices  12.2 us (13%)
  between operations  2.22 us (2%)
  local copies, waits for them, and re-layouts  1.12 us (1%)
    all_to_all x6, starting transfers between devices, exchange(): return lax.all_to_all(x, axis, split_axis=0, concat_axis=0, tiled=True)  36.7 us
    ppermute x10, starting transfers between devices, move(): return lax.ppermute(value, ('z', 'x', 'y'), pairs)  15.3 us
    all_to_all x6, waiting for transfers between devices, exchange(): return lax.all_to_all(x, axis, split_axis=0, concat_axis=0, tiled=True)  10.1 us
    pallas_call x1, Pallas kernels, context_attention(): pl.pallas_call(functools.partial(context_kernel, count), grid=(heads,), o...  7.94 us
    ppermute x3, starting transfers between devices, local(): lax.ppermute(anchor, 'x', [(a, (a + i) % n_x) for a in range(n_x)])  4.78 us
    ppermute x3, starting transfers between devices, local(): lax.ppermute(lines[i], 'y', [(a, (a + i) % n_y) for a in range(n_y)])  3.76 us
    pallas_call x1, Pallas kernels, mark(): pl.pallas_call(functools.partial(mark_kernel, n_x), out_shape=shapes, in_...  2.08 us
    pallas_call x2, Pallas kernels, join(): pl.pallas_call(functools.partial(join_kernel, parts_in, keep_code), out_s...  2.06 us
  transfers between devices with their start and end apart: 22, of which 6 were waited for; matrix products, arithmetic and copies ran while one was open for 0% of the time, Pallas kernels for 16%

profile of v2, /device:TPU:2, one launch (start us, length us, event | category | flops | bytes accessed | tf_op | source)
XLA Modules:
  0.0 92.9 jit_solution(8781183082412845230)
XLA Ops:
  0.6 1.7 %pack.1 = bf16[32,32,128]{2,1,0:T(8,128)(2,1)} custom-call(bf16[16,8192]{1,0:T(8,128)(2,1)} %rq_ref.1), custom_call_target="tpu_custom_call" | custom-call | flops 262144 | bytes 524288 | tf_op jit(solution)/shard_map/pack/pallas_call | solution.py:166
  2.3 7.6 %all-to-all-start = ((bf16[32,32,128]{2,1,0:T(8,128)(2,1)}), bf16[32,32,128]{2,1,0:T(8,128)(2,1)S(1)}, u32[]{:S(2)}, u32[]{:S(2)}) async-start(bf16[32,32,128]{2,1,0:T(8,128)(2,1)} %pack.1), calls=%async_computation | async-start | bytes 524288 | tf_op jit(solution)/shard_map/all_to_all | solution.py:341
  11.3 2.1 %mark.1 = (bf16[64,1024]{1,0:T(8,128)(2,1)}, bf16[64,1024]{1,0:T(8,128)(2,1)}, bf16[64,1024]{1,0:T(8,128)(2,1)}, bf16[64,1024]{1,0:T(8,128)(2,1)}, bf16[576,128]...) custom-call(s32[1]{0:T(128)S(6)} %copy.11.len_ref, ...), custom_call_target="tpu_custom_call" | custom-call | flops 262144 | bytes 2097152 | tf_op jit(solution)/shard_map/mark/pallas_call | solution.py:140
  13.4 1.4 %collective-permute-start = (bf16[64,1024]{1,0:T(8,128)(2,1)}, bf16[64,1024]{1,0:T(8,128)(2,1)S(1)}, u32[]{:S(2)}, u32[]{:S(2)}) collective-permute-start(bf16[64,1024]{1,0:T(8,128)(2,1)} %get-tuple-element.29), channel_id=1, source_target_pairs={{0,8},{1,9}} | collective-permute-start | bytes 393224 | tf_op jit(solution)/shard_map/ppermute | solution.py:356
  16.2 0.9 collective-permute-start.6
  17.1 2.7 %collective-permute-start.7 = (bf16[576,128]{1,0:T(8,128)(2,1)}, bf16[576,128]{1,0:T(8,128)(2,1)S(1)}, u32[]{:S(2)}, u32[]{:S(2)}) collective-permute-start(bf16[576,128]{1,0:T(8,128)(2,1)} %get-tuple-element.38), channel_id=1, source_target_pairs={{0,4},{2,6},{4,0},{6,2},{1,5},{3,7},{5,1},{7,3},{8,12},{10,14},{12... | collective-permute-start | bytes 442376 | tf_op jit(solution)/shard_map/ppermute | solution.py:363
  20.4 1.3 %collective-permute-done = bf16[64,1024]{1,0:T(8,128)(2,1)S(1)} collective-permute-done((bf16[64,1024]{1,0:T(8,128)(2,1)}, bf16[64,1024]{1,0:T(8,128)(2,1)S(1)}, u32[]{:S(2)}, u32[]{:S(2)}) %collective-permute-start) | collective-permute-done | bytes 131104 | tf_op jit(solution)/shard_map/ppermute | solution.py:356
  21.9 8.5 %all-to-all-start.1 = ((bf16[8,64,128]{2,1,0:T(8,128)(2,1)}), bf16[8,64,128]{2,1,0:T(8,128)(2,1)S(1)}, u32[]{:S(2)}, u32[]{:S(2)}) async-start(bf16[8,64,128]{2,1,0:T(8,128)(2,1)} %choose.2), calls=%async_computation.1 | async-start | bytes 262144 | tf_op jit(solution)/shard_map/all_to_all | solution.py:341
  30.4 2.6 %collective-permute-start.3 = (bf16[64,1024]{1,0:T(8,128)(2,1)S(1)}, bf16[64,1024]{1,0:T(8,128)(2,1)S(1)}, u32[]{:S(2)}, u32[]{:S(2)}) collective-permute-start(bf16[64,1024]{1,0:T(8,128)(2,1)S(1)} %add_select_fusion.3), channel_id=1, source_target_pairs={{0,2},{8,10},{16,18},{24,26},{1,3},{9,11},{17,19},{25,27}} | collective-permute-start | bytes 393224 | tf_op jit(solution)/shard_map/ppermute | solution.py:356
  33.0 1.3 %collective-permute-start.4 = (bf16[64,1024]{1,0:T(8,128)(2,1)S(1)}, bf16[64,1024]{1,0:T(8,128)(2,1)S(1)}, u32[]{:S(2)}, u32[]{:S(2)}) collective-permute-start(bf16[64,1024]{1,0:T(8,128)(2,1)S(1)} %add_select_fusion.3), channel_id=1, source_target_pairs={{0,4},{8,12},{16,20},{24,28},{1,5},{9,13},{17,21},{25,29}} | collective-permute-start | bytes 393224 | tf_op jit(solution)/shard_map/ppermute | solution.py:356
  34.4 1.3 %collective-permute-start.5 = (bf16[64,1024]{1,0:T(8,128)(2,1)S(1)}, bf16[64,1024]{1,0:T(8,128)(2,1)S(1)}, u32[]{:S(2)}, u32[]{:S(2)}) collective-permute-start(bf16[64,1024]{1,0:T(8,128)(2,1)S(1)} %add_select_fusion.3), channel_id=1, source_target_pairs={{0,6},{8,14},{16,22},{24,30},{1,7},{9,15},{17,23},{25,31}} | collective-permute-start | bytes 393224 | tf_op jit(solution)/shard_map/ppermute | solution.py:356
  35.7 3.8 %all-to-all-done.1.x_ref = bf16[8,64,128]{2,1,0:T(8,128)(2,1)S(1)} async-done(((bf16[8,64,128]{2,1,0:T(8,128)(2,1)}), bf16[8,64,128]{2,1,0:T(8,128)(2,1)S(1)}, u32[]{:S(2)}, u32[]{:S(2)}) %all-to-all-start.1) | async-done | bytes 131104 | tf_op jit(solution)/shard_map/all_to_all | solution.py:341
  40.2 4.8 %all-to-all-start.2 = ((bf16[4,128,128]{2,1,0:T(8,128)(2,1)}), bf16[4,128,128]{2,1,0:T(8,128)(2,1)S(1)}, u32[]{:S(2)}, u32[]{:S(2)}) async-start(bf16[4,128,128]{2,1,0:T(8,128)(2,1)} %choose.3), calls=%async_computation.2 | async-start | bytes 262144 | tf_op jit(solution)/shard_map/all_to_all | solution.py:341
  45.0 2.2 %collective-permute-start.10 = (bf16[64,1024]{1,0:T(8,128)(2,1)S(1)}, bf16[64,1024]{1,0:T(8,128)(2,1)S(1)}, u32[]{:S(2)}, u32[]{:S(2)}) collective-permute-start(bf16[64,1024]{1,0:T(8,128)(2,1)S(1)} %add_select_fusion.2), channel_id=1, source_target_pairs={{0,160},{2,162},{4,164},{6,166},{8,168},{10,170},{12,172},{14,174}... | collective-permute-start | bytes 393224 | tf_op jit(solution)/shard_map/ppermute | solution.py:356
  47.3 1.3 %collective-permute-start.9 = (bf16[64,1024]{1,0:T(8,128)(2,1)S(1)}, bf16[64,1024]{1,0:T(8,128)(2,1)S(1)}, u32[]{:S(2)}, u32[]{:S(2)}) collective-permute-start(bf16[64,1024]{1,0:T(8,128)(2,1)S(1)} %add_select_fusion.2), channel_id=1, source_target_pairs={{0,96},{2,98},{4,100},{6,102},{8,104},{10,106},{12,108},{14,110},{... | collective-permute-start | bytes 393224 | tf_op jit(solution)/shard_map/ppermute | solution.py:356
  48.6 0.9 %all-to-all-done.2.q_ref = bf16[4,128,128]{2,1,0:T(8,128)(2,1)S(1)} async-done(((bf16[4,128,128]{2,1,0:T(8,128)(2,1)}), bf16[4,128,128]{2,1,0:T(8,128)(2,1)S(1)}, u32[]{:S(2)}, u32[]{:S(2)}) %all-to-all-start.2) | async-done | bytes 131104 | tf_op jit(solution)/shard_map/all_to_all | solution.py:341
  49.5 1.7 %request_partials.1 = bf16[4,144,128]{2,1,0:T(8,128)(2,1)} custom-call(bf16[4,128,128]{2,1,0:T(8,128)(2,1)S(1)} %all-to-all-done.2.q_ref, bf16[576,128]{1,0:T(8,128)(2,1)S(1)} %copy-done.3, bf16[576,128]{1,0:T(8,128)(2,1)S(1)} %collective-permute-done.6.refs_1_, bf16[576,128]{1,0:T(8,128)(2,1)S(1)} %collective-permute-done.7.refs_2_, ...), custom_call_target="tpu_custom_call" | custom-call | flops 2000000000 | bytes 1048576 | tf_op jit(solution)/shard_map/request_partials/pallas_call | solution.py:273
  51.2 4.8 %all-to-all-start.3 = ((bf16[4,144,128]{2,1,0:T(8,128)(2,1)}), bf16[4,144,128]{2,1,0:T(8,128)(2,1)S(1)}, u32[]{:S(2)}, u32[]{:S(2)}) async-start(bf16[4,144,128]{2,1,0:T(8,128)(2,1)} %request_partials.1), calls=%async_computation.3 | async-start | bytes 294912 | tf_op jit(solution)/shard_map/all_to_all | solution.py:341
  56.0 2.5 %collective-permute-start.11 = (bf16[64,1024]{1,0:T(8,128)(2,1)S(1)}, bf16[64,1024]{1,0:T(8,128)(2,1)S(1)}, u32[]{:S(2)}, u32[]{:S(2)}) collective-permute-start(bf16[64,1024]{1,0:T(8,128)(2,1)S(1)} %add_select_fusion.1), channel_id=1, source_target_pairs={{0,32},{2,34},{4,36},{6,38},{8,40},{10,42},{12,44},{14,46},{16,48}... | collective-permute-start | bytes 393224 | tf_op jit(solution)/shard_map/ppermute | solution.py:356
  58.5 1.3 %collective-permute-start.12 = (bf16[64,1024]{1,0:T(8,128)(2,1)S(1)}, bf16[64,1024]{1,0:T(8,128)(2,1)S(1)}, u32[]{:S(2)}, u32[]{:S(2)}) collective-permute-start(bf16[64,1024]{1,0:T(8,128)(2,1)S(1)} %add_select_fusion.1), channel_id=1, source_target_pairs={{0,224},{2,226},{4,228},{6,230},{8,232},{10,234},{12,236},{14,238}... | collective-permute-start | bytes 393224 | tf_op jit(solution)/shard_map/ppermute | solution.py:356
  59.8 0.8 all-to-all-done.3.refs_0_
  60.6 1.0 %join_pieces.2 = bf16[8,80,128]{2,1,0:T(8,128)(2,1)} custom-call(bf16[4,144,128]{2,1,0:T(8,128)(2,1)S(1)} %all-to-all-done.3.refs_0_), custom_call_target="tpu_custom_call" | custom-call | flops 2000000000 | bytes 524288 | tf_op jit(solution)/shard_map/join_pieces/pallas_call | solution.py:331
  61.6 0.7 collective-permute-done.12
  62.3 6.0 %all-to-all-start.4 = ((bf16[8,80,128]{2,1,0:T(8,128)(2,1)}), bf16[8,80,128]{2,1,0:T(8,128)(2,1)S(1)}, u32[]{:S(2)}, u32[]{:S(2)}) async-start(bf16[8,80,128]{2,1,0:T(8,128)(2,1)} %join_pieces.2), calls=%async_computation.4 | async-start | bytes 327680 | tf_op jit(solution)/shard_map/all_to_all | solution.py:341
  68.4 1.5 %collective-permute-start.13 = (bf16[64,1024]{1,0:T(8,128)(2,1)S(1)}, bf16[64,1024]{1,0:T(8,128)(2,1)S(1)}, u32[]{:S(2)}, u32[]{:S(2)}) collective-permute-start(bf16[64,1024]{1,0:T(8,128)(2,1)S(1)} %add_select_fusion.refs_0_.refs_4_), channel_id=1, source_target_pairs={{0,8},{8,16},{16,24},{24,0},{1,9},{9,17},{17,25},{25,1},{2,10},{10... | collective-permute-start | bytes 393224 | tf_op jit(solution)/shard_map/ppermute | solution.py:391
  69.9 0.7 collective-permute-start.14
  70.7 2.5 %collective-permute-start.15 = (bf16[64,1024]{1,0:T(8,128)(2,1)S(1)}, bf16[64,1024]{1,0:T(8,128)(2,1)S(1)}, u32[]{:S(2)}, u32[]{:S(2)}) collective-permute-start(bf16[64,1024]{1,0:T(8,128)(2,1)S(1)} %add_select_fusion.refs_0_.refs_4_), channel_id=1, source_target_pairs={{0,24},{8,0},{16,8},{24,16},{1,25},{9,1},{17,9},{25,17},{2,26},{10... | collective-permute-start | bytes 393224 | tf_op jit(solution)/shard_map/ppermute | solution.py:391
  73.2 4.6 %all-to-all-done.4.refs_0_ = bf16[8,80,128]{2,1,0:T(8,128)(2,1)S(1)} async-done(((bf16[8,80,128]{2,1,0:T(8,128)(2,1)}), bf16[8,80,128]{2,1,0:T(8,128)(2,1)S(1)}, u32[]{:S(2)}, u32[]{:S(2)}) %all-to-all-start.4) | async-done | bytes 163872 | tf_op jit(solution)/shard_map/all_to_all | solution.py:341
  77.7 1.1 %join_pieces.3 = bf16[16,64,128]{2,1,0:T(8,128)(2,1)} custom-call(bf16[8,80,128]{2,1,0:T(8,128)(2,1)S(1)} %all-to-all-done.4.refs_0_), custom_call_target="tpu_custom_call" | custom-call | flops 2000000000 | bytes 524288 | tf_op jit(solution)/shard_map/join_pieces/pallas_call | solution.py:331
  78.8 5.0 %all-to-all-start.5 = ((bf16[16,64,128]{2,1,0:T(8,128)(2,1)}), bf16[16,64,128]{2,1,0:T(8,128)(2,1)}, u32[]{:S(2)}, u32[]{:S(2)}) async-start(bf16[16,64,128]{2,1,0:T(8,128)(2,1)} %join_pieces.3), calls=%async_computation.5 | async-start | bytes 524288 | tf_op jit(solution)/shard_map/all_to_all | solution.py:341
  83.8 7.9 %context_attention.1 = bf16[256,4096]{1,0:T(8,128)(2,1)} custom-call(s32[1]{0:T(128)S(6)} %copy.11.len_ref, s32[1]{0:T(128)} %bitcast.root_ref, bf16[256,4096]{1,0:T(8,128)(2,1)S(1)} %copy-done.2, bf16[256,512]{1,0:T(8,128)(2,1)S(1)} %copy-done, bf16[256,512]{1,0:T(8,128)(2,1)S(1)} %copy-done.1, bf16[64,1024]{1,0:T(8,128)(2,1)S(1)} %add_select_fusion.refs_0_.refs_4_, ...), custom_call_target="tpu_custom_call" | custom-call | flops 2147483648 | bytes 5242880 | tf_op jit(solution)/shard_map/context_attention/pallas_call | solution.py:93
  92.0 0.9 select_n.68
  (39 shorter events, 3.2 us)
Async XLA Ops:
  2.3 17.4 %all-to-all-start = ((bf16[32,32,128]{2,1,0:T(8,128)(2,1)}), bf16[32,32,128]{2,1,0:T(8,128)(2,1)S(1)}, u32[]{:S(2)}, u32[]{:S(2)}) async-start(bf16[32,32,128]{2,1,0:T(8,128)(2,1)} %pack.1), calls=%async_computation | async-start | bytes 524288 | tf_op jit(solution)/shard_map/all_to_all | solution.py:341
  13.4 8.4 %copy-start.5 = (bf16[576,128]{1,0:T(8,128)(2,1)S(1)}, bf16[576,128]{1,0:T(8,128)(2,1)}, u32[]{:S(2)}) copy-start(bf16[576,128]{1,0:T(8,128)(2,1)} %get-tuple-element.39) | copy-start | bytes 442372
  13.4 17.0 %copy-start.4 = (bf16[64,1024]{1,0:T(8,128)(2,1)S(1)}, bf16[64,1024]{1,0:T(8,128)(2,1)}, u32[]{:S(2)}) copy-start(bf16[64,1024]{1,0:T(8,128)(2,1)} %get-tuple-element.28) | copy-start | bytes 393220
  13.4 8.4 %collective-permute-start = (bf16[64,1024]{1,0:T(8,128)(2,1)}, bf16[64,1024]{1,0:T(8,128)(2,1)S(1)}, u32[]{:S(2)}, u32[]{:S(2)}) collective-permute-start(bf16[64,1024]{1,0:T(8,128)(2,1)} %get-tuple-element.29), channel_id=1, source_target_pairs={{0,8},{1,9}} | collective-permute-start | bytes 393224 | tf_op jit(solution)/shard_map/ppermute | solution.py:356
  14.8 7.1 %collective-permute-start.1 = (bf16[64,1024]{1,0:T(8,128)(2,1)}, bf16[64,1024]{1,0:T(8,128)(2,1)S(1)}, u32[]{:S(2)}, u32[]{:S(2)}) collective-permute-start(bf16[64,1024]{1,0:T(8,128)(2,1)} %get-tuple-element.30), channel_id=1, source_target_pairs={{0,16},{1,17}} | collective-permute-start | bytes 393224 | tf_op jit(solution)/shard_map/ppermute | solution.py:356
  15.5 6.4 %collective-permute-start.2 = (bf16[64,1024]{1,0:T(8,128)(2,1)}, bf16[64,1024]{1,0:T(8,128)(2,1)S(1)}, u32[]{:S(2)}, u32[]{:S(2)}) collective-permute-start(bf16[64,1024]{1,0:T(8,128)(2,1)} %get-tuple-element.31), channel_id=1, source_target_pairs={{0,24},{1,25}} | collective-permute-start | bytes 393224 | tf_op jit(solution)/shard_map/ppermute | solution.py:356
  16.2 18.2 %collective-permute-start.6 = (bf16[576,128]{1,0:T(8,128)(2,1)}, bf16[576,128]{1,0:T(8,128)(2,1)S(1)}, u32[]{:S(2)}, u32[]{:S(2)}) collective-permute-start(bf16[576,128]{1,0:T(8,128)(2,1)} %get-tuple-element.37), channel_id=1, source_target_pairs={{0,2},{2,4},{4,6},{6,0},{1,3},{3,5},{5,7},{7,1},{8,10},{10,12},{12... | collective-permute-start | bytes 442376 | tf_op jit(solution)/shard_map/ppermute | solution.py:363
  17.1 23.1 %collective-permute-start.7 = (bf16[576,128]{1,0:T(8,128)(2,1)}, bf16[576,128]{1,0:T(8,128)(2,1)S(1)}, u32[]{:S(2)}, u32[]{:S(2)}) collective-permute-start(bf16[576,128]{1,0:T(8,128)(2,1)} %get-tuple-element.38), channel_id=1, source_target_pairs={{0,4},{2,6},{4,0},{6,2},{1,5},{3,7},{5,1},{7,3},{8,12},{10,14},{12... | collective-permute-start | bytes 442376 | tf_op jit(solution)/shard_map/ppermute | solution.py:363
  21.7 18.4 %collective-permute-start.8 = (bf16[576,128]{1,0:T(8,128)(2,1)S(1)}, bf16[576,128]{1,0:T(8,128)(2,1)S(1)}, u32[]{:S(2)}, u32[]{:S(2)}) collective-permute-start(bf16[576,128]{1,0:T(8,128)(2,1)S(1)} %copy-done.5), channel_id=1, source_target_pairs={{0,6},{2,0},{4,2},{6,4},{1,7},{3,1},{5,3},{7,5},{8,14},{10,8},{12,... | collective-permute-start | bytes 442376 | tf_op jit(solution)/shard_map/ppermute | solution.py:363
  21.9 17.5 %all-to-all-start.1 = ((bf16[8,64,128]{2,1,0:T(8,128)(2,1)}), bf16[8,64,128]{2,1,0:T(8,128)(2,1)S(1)}, u32[]{:S(2)}, u32[]{:S(2)}) async-start(bf16[8,64,128]{2,1,0:T(8,128)(2,1)} %choose.2), calls=%async_computation.1 | async-start | bytes 262144 | tf_op jit(solution)/shard_map/all_to_all | solution.py:341
  30.4 19.1 %copy-start.3 = (bf16[576,128]{1,0:T(8,128)(2,1)S(1)}, bf16[576,128]{1,0:T(8,128)(2,1)}, u32[]{:S(2)}) copy-start(bf16[576,128]{1,0:T(8,128)(2,1)} %get-tuple-element.44.refs_0_) | copy-start | bytes 442372
  30.4 9.7 %collective-permute-start.3 = (bf16[64,1024]{1,0:T(8,128)(2,1)S(1)}, bf16[64,1024]{1,0:T(8,128)(2,1)S(1)}, u32[]{:S(2)}, u32[]{:S(2)}) collective-permute-start(bf16[64,1024]{1,0:T(8,128)(2,1)S(1)} %add_select_fusion.3), channel_id=1, source_target_pairs={{0,2},{8,10},{16,18},{24,26},{1,3},{9,11},{17,19},{25,27}} | collective-permute-start | bytes 393224 | tf_op jit(solution)/shard_map/ppermute | solution.py:356
  33.0 7.1 %collective-permute-start.4 = (bf16[64,1024]{1,0:T(8,128)(2,1)S(1)}, bf16[64,1024]{1,0:T(8,128)(2,1)S(1)}, u32[]{:S(2)}, u32[]{:S(2)}) collective-permute-start(bf16[64,1024]{1,0:T(8,128)(2,1)S(1)} %add_select_fusion.3), channel_id=1, source_target_pairs={{0,4},{8,12},{16,20},{24,28},{1,5},{9,13},{17,21},{25,29}} | collective-permute-start | bytes 393224 | tf_op jit(solution)/shard_map/ppermute | solution.py:356
  34.4 5.8 %collective-permute-start.5 = (bf16[64,1024]{1,0:T(8,128)(2,1)S(1)}, bf16[64,1024]{1,0:T(8,128)(2,1)S(1)}, u32[]{:S(2)}, u32[]{:S(2)}) collective-permute-start(bf16[64,1024]{1,0:T(8,128)(2,1)S(1)} %add_select_fusion.3), channel_id=1, source_target_pairs={{0,6},{8,14},{16,22},{24,30},{1,7},{9,15},{17,23},{25,31}} | collective-permute-start | bytes 393224 | tf_op jit(solution)/shard_map/ppermute | solution.py:356
  40.2 9.3 %all-to-all-start.2 = ((bf16[4,128,128]{2,1,0:T(8,128)(2,1)}), bf16[4,128,128]{2,1,0:T(8,128)(2,1)S(1)}, u32[]{:S(2)}, u32[]{:S(2)}) async-start(bf16[4,128,128]{2,1,0:T(8,128)(2,1)} %choose.3), calls=%async_computation.2 | async-start | bytes 262144 | tf_op jit(solution)/shard_map/all_to_all | solution.py:341
  45.0 6.2 %collective-permute-start.10 = (bf16[64,1024]{1,0:T(8,128)(2,1)S(1)}, bf16[64,1024]{1,0:T(8,128)(2,1)S(1)}, u32[]{:S(2)}, u32[]{:S(2)}) collective-permute-start(bf16[64,1024]{1,0:T(8,128)(2,1)S(1)} %add_select_fusion.2), channel_id=1, source_target_pairs={{0,160},{2,162},{4,164},{6,166},{8,168},{10,170},{12,172},{14,174}... | collective-permute-start | bytes 393224 | tf_op jit(solution)/shard_map/ppermute | solution.py:356
  47.3 4.0 %collective-permute-start.9 = (bf16[64,1024]{1,0:T(8,128)(2,1)S(1)}, bf16[64,1024]{1,0:T(8,128)(2,1)S(1)}, u32[]{:S(2)}, u32[]{:S(2)}) collective-permute-start(bf16[64,1024]{1,0:T(8,128)(2,1)S(1)} %add_select_fusion.2), channel_id=1, source_target_pairs={{0,96},{2,98},{4,100},{6,102},{8,104},{10,106},{12,108},{14,110},{... | collective-permute-start | bytes 393224 | tf_op jit(solution)/shard_map/ppermute | solution.py:356
  51.2 9.4 %all-to-all-start.3 = ((bf16[4,144,128]{2,1,0:T(8,128)(2,1)}), bf16[4,144,128]{2,1,0:T(8,128)(2,1)S(1)}, u32[]{:S(2)}, u32[]{:S(2)}) async-start(bf16[4,144,128]{2,1,0:T(8,128)(2,1)} %request_partials.1), calls=%async_computation.3 | async-start | bytes 294912 | tf_op jit(solution)/shard_map/all_to_all | solution.py:341
  56.0 5.6 %collective-permute-start.11 = (bf16[64,1024]{1,0:T(8,128)(2,1)S(1)}, bf16[64,1024]{1,0:T(8,128)(2,1)S(1)}, u32[]{:S(2)}, u32[]{:S(2)}) collective-permute-start(bf16[64,1024]{1,0:T(8,128)(2,1)S(1)} %add_select_fusion.1), channel_id=1, source_target_pairs={{0,32},{2,34},{4,36},{6,38},{8,40},{10,42},{12,44},{14,46},{16,48}... | collective-permute-start | bytes 393224 | tf_op jit(solution)/shard_map/ppermute | solution.py:356
  58.5 3.8 %collective-permute-start.12 = (bf16[64,1024]{1,0:T(8,128)(2,1)S(1)}, bf16[64,1024]{1,0:T(8,128)(2,1)S(1)}, u32[]{:S(2)}, u32[]{:S(2)}) collective-permute-start(bf16[64,1024]{1,0:T(8,128)(2,1)S(1)} %add_select_fusion.1), channel_id=1, source_target_pairs={{0,224},{2,226},{4,228},{6,230},{8,232},{10,234},{12,236},{14,238}... | collective-permute-start | bytes 393224 | tf_op jit(solution)/shard_map/ppermute | solution.py:356
  62.3 15.4 %all-to-all-start.4 = ((bf16[8,80,128]{2,1,0:T(8,128)(2,1)}), bf16[8,80,128]{2,1,0:T(8,128)(2,1)S(1)}, u32[]{:S(2)}, u32[]{:S(2)}) async-start(bf16[8,80,128]{2,1,0:T(8,128)(2,1)} %join_pieces.2), calls=%async_computation.4 | async-start | bytes 327680 | tf_op jit(solution)/shard_map/all_to_all | solution.py:341
  68.3 15.5 %copy-start = (bf16[256,512]{1,0:T(8,128)(2,1)S(1)}, bf16[256,512]{1,0:T(8,128)(2,1)}, u32[]{:S(2)}) copy-start(bf16[256,512]{1,0:T(8,128)(2,1)} %k_ref.3) | copy-start | bytes 786436
  68.3 15.5 %copy-start.1 = (bf16[256,512]{1,0:T(8,128)(2,1)S(1)}, bf16[256,512]{1,0:T(8,128)(2,1)}, u32[]{:S(2)}) copy-start(bf16[256,512]{1,0:T(8,128)(2,1)} %v_ref.3) | copy-start | bytes 786436
  68.4 15.5 %copy-start.2 = (bf16[256,4096]{1,0:T(8,128)(2,1)S(1)}, bf16[256,4096]{1,0:T(8,128)(2,1)}, u32[]{:S(2)}) copy-start(bf16[256,4096]{1,0:T(8,128)(2,1)} %q_ref.1) | copy-start | bytes 6291460
  68.4 15.4 %collective-permute-start.13 = (bf16[64,1024]{1,0:T(8,128)(2,1)S(1)}, bf16[64,1024]{1,0:T(8,128)(2,1)S(1)}, u32[]{:S(2)}, u32[]{:S(2)}) collective-permute-start(bf16[64,1024]{1,0:T(8,128)(2,1)S(1)} %add_select_fusion.refs_0_.refs_4_), channel_id=1, source_target_pairs={{0,8},{8,16},{16,24},{24,0},{1,9},{9,17},{17,25},{25,1},{2,10},{10... | collective-permute-start | bytes 393224 | tf_op jit(solution)/shard_map/ppermute | solution.py:391
  69.9 13.9 %collective-permute-start.14 = (bf16[64,1024]{1,0:T(8,128)(2,1)S(1)}, bf16[64,1024]{1,0:T(8,128)(2,1)S(1)}, u32[]{:S(2)}, u32[]{:S(2)}) collective-permute-start(bf16[64,1024]{1,0:T(8,128)(2,1)S(1)} %add_select_fusion.refs_0_.refs_4_), channel_id=1, source_target_pairs={{0,16},{8,24},{16,0},{24,8},{1,17},{9,25},{17,1},{25,9},{2,18},{10... | collective-permute-start | bytes 393224 | tf_op jit(solution)/shard_map/ppermute | solution.py:391
  70.7 13.2 %collective-permute-start.15 = (bf16[64,1024]{1,0:T(8,128)(2,1)S(1)}, bf16[64,1024]{1,0:T(8,128)(2,1)S(1)}, u32[]{:S(2)}, u32[]{:S(2)}) collective-permute-start(bf16[64,1024]{1,0:T(8,128)(2,1)S(1)} %add_select_fusion.refs_0_.refs_4_), channel_id=1, source_target_pairs={{0,24},{8,0},{16,8},{24,16},{1,25},{9,1},{17,9},{25,17},{2,26},{10... | collective-permute-start | bytes 393224 | tf_op jit(solution)/shard_map/ppermute | solution.py:391
  78.8 13.0 %all-to-all-start.5 = ((bf16[16,64,128]{2,1,0:T(8,128)(2,1)}), bf16[16,64,128]{2,1,0:T(8,128)(2,1)}, u32[]{:S(2)}, u32[]{:S(2)}) async-start(bf16[16,64,128]{2,1,0:T(8,128)(2,1)} %join_pieces.3), calls=%async_computation.5 | async-start | bytes 524288 | tf_op jit(solution)/shard_map/all_to_all | solution.py:341

commit v3 on v2

--- a/solution.py
+++ b/solution.py
@@ -187,14 +187,10 @@
 
 
 def line_kernel(plane_ref, x_ref, o_ref):
-    part = x_ref[plane_ref[0]]
-    piece = part.shape[0]
-    for j in range(o_ref.shape[0]):
-        o_ref[j, 0:piece, :] = part
-        o_ref[j, piece : 2 * piece, :] = part
-
-
-def choose(kernel, index, x, shape):
+    o_ref[...] = x_ref[plane_ref[0]]
+
+
+def choose(kernel, index, x, shape, flops):
     vmem = pl.BlockSpec(memory_space=pltpu.VMEM)
     return pl.pallas_call(
         kernel,
@@ -202,7 +198,7 @@
         in_specs=[pl.BlockSpec(memory_space=pltpu.SMEM), vmem],
         out_specs=vmem,
         compiler_params=pltpu.CompilerParams(vmem_limit_bytes=VMEM_LIMIT),
-        cost_estimate=pl.CostEstimate(flops=8 * 10**8, bytes_accessed=2**19, transcendentals=0),
+        cost_estimate=pl.CostEstimate(flops=flops, bytes_accessed=2**19, transcendentals=0),
         name="choose",
     )(index, x)
 
@@ -220,16 +216,15 @@
     return jnp.where(row == 0, pair, jnp.where(row == 1, last, 0.0)).astype(jnp.bfloat16)
 
 
-def request_kernel(own, q_ref, *refs):
-    lines, o_ref, v_ref = refs[:-2], refs[-2], refs[-1]
-    count = q_ref.shape[0]
-    height = o_ref.shape[1]
-    piece = (height - 16) // 2
+def request_kernel(own, count, *refs):
+    q_refs, lines = refs[:count], refs[count : -count - 1]
+    o_refs, v_ref = refs[-count - 1 : -1], refs[-1]
+    piece = q_refs[0].shape[0]
     n = count * piece
     both = lines[0].shape[0] // 2
     rows = both - own
     c = SCALE * LOG2E
-    q = q_ref[:, 0:piece, :].reshape(n, HEAD_SIZE)
+    q = jnp.concatenate([ref[...] for ref in q_refs], axis=0)
     for i, ref in enumerate(lines):
         for part, (top, at) in (
             (ref[both : both + rows, :], (i * rows, rows)),
@@ -255,33 +250,33 @@
     high, mid, low = split3(lse)
     row = lax.broadcasted_iota(jnp.int32, (piece, HEAD_SIZE), 0)
     lane = lax.broadcasted_iota(jnp.int32, (piece, HEAD_SIZE), 1)
-    for p in range(count):
+    for p, o_ref in enumerate(o_refs):
         part = slice(p * piece, (p + 1) * piece)
         pair = jnp.where(row == lane, high[part], jnp.where(row + piece == lane, mid[part], 0.0))
         last = jnp.where(row == lane, low[part], 0.0)
-        o_ref[p, 0:piece, :] = out_high[part]
-        o_ref[p, piece : 2 * piece, :] = out_low[part]
-        o_ref[p, 2 * piece : height, :] = code_rows(
+        o_ref[0:piece, :] = out_high[part]
+        o_ref[piece : 2 * piece, :] = out_low[part]
+        o_ref[2 * piece :, :] = code_rows(
             jnp.sum(pair, axis=0, keepdims=True), jnp.sum(last, axis=0, keepdims=True), 16
         )
 
 
-def request_partials(moved, lines, own):
-    count, piece = moved.shape[0], moved.shape[1] // 2
+def request_partials(queries, lines, own):
+    count, piece = len(queries), queries[0].shape[0]
     keys = len(lines) * lines[0].shape[0] // 2
     vmem = pl.BlockSpec(memory_space=pltpu.VMEM)
     return pl.pallas_call(
-        functools.partial(request_kernel, own),
-        out_shape=jax.ShapeDtypeStruct((count, 2 * piece + 16, HEAD_SIZE), jnp.bfloat16),
-        in_specs=[vmem] * (1 + len(lines)),
-        out_specs=vmem,
+        functools.partial(request_kernel, own, count),
+        out_shape=[jax.ShapeDtypeStruct((2 * piece + 16, HEAD_SIZE), jnp.bfloat16)] * count,
+        in_specs=[vmem] * (count + len(lines)),
+        out_specs=[vmem] * count,
         scratch_shapes=[pltpu.VMEM((keys, 2 * HEAD_SIZE), jnp.bfloat16)],
         compiler_params=pltpu.CompilerParams(vmem_limit_bytes=VMEM_LIMIT),
         cost_estimate=pl.CostEstimate(
-            flops=2 * 10**9, bytes_accessed=2**20, transcendentals=count * piece * keys
+            flops=3 * 10**9, bytes_accessed=2**20, transcendentals=count * piece * keys
         ),
         name="request_partials",
-    )(moved, *lines)
+    )(*queries, *lines)
 
 
 def join_kernel(parts_in, keep_code, *refs):
@@ -332,7 +327,7 @@
         functools.partial(join_kernel, parts_in, keep_code),
         out_shape=jax.ShapeDtypeStruct(shape, jnp.bfloat16),
         compiler_params=pltpu.CompilerParams(vmem_limit_bytes=VMEM_LIMIT),
-        cost_estimate=pl.CostEstimate(flops=2 * 10**9, bytes_accessed=2**19, transcendentals=1024),
+        cost_estimate=pl.CostEstimate(flops=3 * 10**9, bytes_accessed=2**19, transcendentals=1024),
         name="join_pieces",
     )(*arrays)
 
@@ -355,6 +350,9 @@
     def move(value, pairs):
         return lax.ppermute(value, ("z", "x", "y"), pairs)
 
+    def shift_x(value, count):
+        return lax.ppermute(value, "x", [(a, (a + count) % n_x) for a in range(n_x)])
+
     moved = exchange(pack(rq, n_xy, n_y), ("x", "y", "head"))
     marked = mark(own_len, is_owner, y.reshape(1), k, v, rk, rv, n_x, n_y)
     pieces, lines = marked[:n_x], marked[n_x:]
@@ -363,32 +361,30 @@
         lax.ppermute(lines[i], "y", [(a, (a + i) % n_y) for a in range(n_y)]) for i in range(1, n_y)
     ]
 
-    moved = choose(plane_kernel, owner_xy.reshape(1), moved, (n_z, 2 * moved.shape[1], HEAD_SIZE))
+    moved = choose(plane_kernel, owner_xy.reshape(1), moved, (n_z, 2 * moved.shape[1], HEAD_SIZE), 8 * 10**8)
     moved, got = lax.optimization_barrier((moved, got))
     anchor = jnp.where(x == 0, pieces[0], got[0] + got[1] + got[2])
     got = [move(anchor, [(i * n_y, i * n_y + j) for i in range(n_x)]) for j in range(1, n_y)]
     moved = exchange(moved, "z")
 
-    moved = choose(line_kernel, owner_z.reshape(1), moved, (n_x, 2 * moved.shape[1], HEAD_SIZE))
+    moved = choose(line_kernel, owner_z.reshape(1), moved, moved.shape[1:], 3 * 10**9)
     moved, got, lines = lax.optimization_barrier((moved, got, lines))
     anchor = jnp.where(y == 0, anchor, got[0] + got[1] + got[2])
     plane = range(n_xy)
     got = [move(anchor, [(p, to * n_xy + p) for p in plane]) for to in (3, 5)]
-    moved = exchange(moved, "x")
-
-    partials = request_partials(moved, lines, own_rows)
-    partials, got = lax.optimization_barrier((partials, got))
+    queries = [moved] + [shift_x(moved, i) for i in range(1, n_x)]
+
+    partials = request_partials(queries, lines, own_rows)
     anchor = jnp.where(z == 0, anchor, got[0] + got[1])
     steps = (((0, 1), (3, 4), (5, 6)), ((0, 7), (3, 2)))
     got = [move(anchor, [(a * n_xy + p, b * n_xy + p) for a, b in step for p in plane]) for step in steps]
-    partials = exchange(partials, "x")
-
-    planes = join([partials], n_z, 2, True)
-    planes, got = lax.optimization_barrier((planes, got))
+    partials = [partials[0]] + [shift_x(partials[i], n_x - i) for i in range(1, n_x)]
+
+    planes = join(partials, n_z, 2, True)
     anchor = jnp.where((z == 0) | (z == 3) | (z == 5), anchor, got[0] + got[1])
     anchors = [anchor]
     for i in range(1, n_x):
-        anchors.append(lax.ppermute(anchor, "x", [(a, (a + i) % n_x) for a in range(n_x)]))
+        anchors.append(shift_x(anchor, i))
     planes = exchange(planes, "z")
 
     answer = exchange(join([planes], n_xy, 1, False), ("x", "y"))

time: 93.8 us -> 87.4 us (0.932)
  starting transfers between devices: 60.5 us -> 56.9 us
  waiting for transfers between devices: 12.2 us -> 10.2 us
  Pallas kernels: 16.8 us -> 15.5 us
    all_to_all x6 -> x4, starting transfers between devices: 36.7 us -> 26 us  [exchange(): return lax.all_to_all(x, axis, split_axis=0, concat_axis=0, tiled=True)]
    ppermute x3 -> x9, starting transfers between devices: 4.78 us -> 13.8 us  [shift_x(): lax.ppermute(value, 'x', [(a, (a + count) % n_x) for a in range(n_x)])]
    ppermute x10, starting transfers between devices: 15.3 us -> 13.4 us  [move(): return lax.ppermute(value, ('z', 'x', 'y'), pairs)]
    all_to_all x6 -> x4, waiting for transfers between devices: 10.1 us -> 8.88 us  [exchange(): return lax.all_to_all(x, axis, split_axis=0, concat_axis=0, tiled=True)]
  transfers between devices with their start and end apart: 22 -> 26, of which waited for: 6 -> 3; matrix products, arithmetic and copies ran while one was open for 0% -> 0% of each run, Pallas kernels for 16% -> 16%
where the time goes in v3:
time: 87.4 us; the launch traced here: 86.2 us
  starting transfers between devices  56.9 us (65%)
  Pallas kernels  15.5 us (18%)
  waiting for transfers between devices  10.2 us (12%)
  between operations  2.32 us (3%)
  local copies, waits for them, and re-layouts  1.12 us (1%)
    all_to_all x4, starting transfers between devices, exchange(): return lax.all_to_all(x, axis, split_axis=0, concat_axis=0, tiled=True)  26 us
    ppermute x9, starting transfers between devices, shift_x(): lax.ppermute(value, 'x', [(a, (a + count) % n_x) for a in range(n_x)])  13.8 us
    ppermute x10, starting transfers between devices, move(): return lax.ppermute(value, ('z', 'x', 'y'), pairs)  13.4 us
    all_to_all x4, waiting for transfers between devices, exchange(): return lax.all_to_all(x, axis, split_axis=0, concat_axis=0, tiled=True)  8.88 us
    pallas_call x1, Pallas kernels, context_attention(): pl.pallas_call(functools.partial(context_kernel, count), grid=(heads,), o...  7.94 us
    ppermute x3, starting transfers between devices, local(): lax.ppermute(lines[i], 'y', [(a, (a + i) % n_y) for a in range(n_y)])  3.76 us
    pallas_call x1, Pallas kernels, mark(): pl.pallas_call(functools.partial(mark_kernel, n_x), out_shape=shapes, in_...  2.09 us
    pallas_call x2, Pallas kernels, join(): pl.pallas_call(functools.partial(join_kernel, parts_in, keep_code), out_s...  2.06 us
  transfers between devices with their start and end apart: 26, of which 3 were waited for; matrix products, arithmetic and copies ran while one was open for 0% of the time, Pallas kernels for 16%

profile of v3, /device:TPU:2, one launch (start us, length us, event | category | flops | bytes accessed | tf_op | source)
XLA Modules:
  0.0 86.2 jit_solution(1707160532093858960)
XLA Ops:
  0.6 1.7 %pack.1 = bf16[32,32,128]{2,1,0:T(8,128)(2,1)} custom-call(bf16[16,8192]{1,0:T(8,128)(2,1)} %rq_ref.1), custom_call_target="tpu_custom_call" | custom-call | flops 262144 | bytes 524288 | tf_op jit(solution)/shard_map/pack/pallas_call | solution.py:166
  2.3 7.6 %all-to-all-start = ((bf16[32,32,128]{2,1,0:T(8,128)(2,1)}), bf16[32,32,128]{2,1,0:T(8,128)(2,1)S(1)}, u32[]{:S(2)}, u32[]{:S(2)}) async-start(bf16[32,32,128]{2,1,0:T(8,128)(2,1)} %pack.1), calls=%async_computation | async-start | bytes 524288 | tf_op jit(solution)/shard_map/all_to_all | solution.py:336
  11.3 2.1 %mark.1 = (bf16[64,1024]{1,0:T(8,128)(2,1)}, bf16[64,1024]{1,0:T(8,128)(2,1)}, bf16[64,1024]{1,0:T(8,128)(2,1)}, bf16[64,1024]{1,0:T(8,128)(2,1)}, bf16[576,128]...) custom-call(s32[1]{0:T(128)S(6)} %copy.11.len_ref, ...), custom_call_target="tpu_custom_call" | custom-call | flops 262144 | bytes 2097152 | tf_op jit(solution)/shard_map/mark/pallas_call | solution.py:140
  13.4 1.4 %collective-permute-start = (bf16[64,1024]{1,0:T(8,128)(2,1)}, bf16[64,1024]{1,0:T(8,128)(2,1)S(1)}, u32[]{:S(2)}, u32[]{:S(2)}) collective-permute-start(bf16[64,1024]{1,0:T(8,128)(2,1)} %get-tuple-element.27), channel_id=1, source_target_pairs={{0,8},{1,9}} | collective-permute-start | bytes 393224 | tf_op jit(solution)/shard_map/ppermute | solution.py:351
  16.2 0.9 %collective-permute-start.6 = (bf16[576,128]{1,0:T(8,128)(2,1)}, bf16[576,128]{1,0:T(8,128)(2,1)S(1)}, u32[]{:S(2)}, u32[]{:S(2)}) collective-permute-start(bf16[576,128]{1,0:T(8,128)(2,1)} %get-tuple-element.35), channel_id=1, source_target_pairs={{0,2},{2,4},{4,6},{6,0},{1,3},{3,5},{5,7},{7,1},{8,10},{10,12},{12... | collective-permute-start | bytes 442376 | tf_op jit(solution)/shard_map/ppermute | solution.py:361
  17.1 2.7 %collective-permute-start.7 = (bf16[576,128]{1,0:T(8,128)(2,1)}, bf16[576,128]{1,0:T(8,128)(2,1)S(1)}, u32[]{:S(2)}, u32[]{:S(2)}) collective-permute-start(bf16[576,128]{1,0:T(8,128)(2,1)} %get-tuple-element.36), channel_id=1, source_target_pairs={{0,4},{2,6},{4,0},{6,2},{1,5},{3,7},{5,1},{7,3},{8,12},{10,14},{12... | collective-permute-start | bytes 442376 | tf_op jit(solution)/shard_map/ppermute | solution.py:361
  19.8 0.7 choose.2
  20.4 1.3 %collective-permute-done = bf16[64,1024]{1,0:T(8,128)(2,1)S(1)} collective-permute-done((bf16[64,1024]{1,0:T(8,128)(2,1)}, bf16[64,1024]{1,0:T(8,128)(2,1)S(1)}, u32[]{:S(2)}, u32[]{:S(2)}) %collective-permute-start) | collective-permute-done | bytes 131104 | tf_op jit(solution)/shard_map/ppermute | solution.py:351
  21.9 8.5 %all-to-all-start.1 = ((bf16[8,64,128]{2,1,0:T(8,128)(2,1)}), bf16[8,64,128]{2,1,0:T(8,128)(2,1)S(1)}, u32[]{:S(2)}, u32[]{:S(2)}) async-start(bf16[8,64,128]{2,1,0:T(8,128)(2,1)} %choose.2), calls=%async_computation.1 | async-start | bytes 262144 | tf_op jit(solution)/shard_map/all_to_all | solution.py:336
  30.4 1.9 %collective-permute-start.5 = (bf16[64,1024]{1,0:T(8,128)(2,1)S(1)}, bf16[64,1024]{1,0:T(8,128)(2,1)S(1)}, u32[]{:S(2)}, u32[]{:S(2)}) collective-permute-start(bf16[64,1024]{1,0:T(8,128)(2,1)S(1)} %add_select_fusion.3), channel_id=1, source_target_pairs={{0,6},{8,14},{16,22},{24,30},{1,7},{9,15},{17,23},{25,31}} | collective-permute-start | bytes 393224 | tf_op jit(solution)/shard_map/ppermute | solution.py:351
  32.4 1.3 %collective-permute-start.4 = (bf16[64,1024]{1,0:T(8,128)(2,1)S(1)}, bf16[64,1024]{1,0:T(8,128)(2,1)S(1)}, u32[]{:S(2)}, u32[]{:S(2)}) collective-permute-start(bf16[64,1024]{1,0:T(8,128)(2,1)S(1)} %add_select_fusion.3), channel_id=1, source_target_pairs={{0,4},{8,12},{16,20},{24,28},{1,5},{9,13},{17,21},{25,29}} | collective-permute-start | bytes 393224 | tf_op jit(solution)/shard_map/ppermute | solution.py:351
  33.7 1.3 %collective-permute-start.3 = (bf16[64,1024]{1,0:T(8,128)(2,1)S(1)}, bf16[64,1024]{1,0:T(8,128)(2,1)S(1)}, u32[]{:S(2)}, u32[]{:S(2)}) collective-permute-start(bf16[64,1024]{1,0:T(8,128)(2,1)S(1)} %add_select_fusion.3), channel_id=1, source_target_pairs={{0,2},{8,10},{16,18},{24,26},{1,3},{9,11},{17,19},{25,27}} | collective-permute-start | bytes 393224 | tf_op jit(solution)/shard_map/ppermute | solution.py:351
  35.0 4.5 %all-to-all-done.1.x_ref = bf16[8,64,128]{2,1,0:T(8,128)(2,1)S(1)} async-done(((bf16[8,64,128]{2,1,0:T(8,128)(2,1)}), bf16[8,64,128]{2,1,0:T(8,128)(2,1)S(1)}, u32[]{:S(2)}, u32[]{:S(2)}) %all-to-all-start.1) | async-done | bytes 131104 | tf_op jit(solution)/shard_map/all_to_all | solution.py:336
  40.2 2.4 %collective-permute-start.17 = (bf16[64,128]{1,0:T(8,128)(2,1)S(1)}, bf16[64,128]{1,0:T(8,128)(2,1)S(1)}, u32[]{:S(2)}, u32[]{:S(2)}) collective-permute-start(bf16[64,128]{1,0:T(8,128)(2,1)S(1)} %choose.3.refs_0_), channel_id=1, source_target_pairs={{0,16},{8,24},{16,0},{24,8},{1,17},{9,25},{17,1},{25,9},{2,18},{10... | collective-permute-start | bytes 49160 | tf_op jit(solution)/shard_map/ppermute | solution.py:354
  42.5 1.8 %collective-permute-start.16 = (bf16[64,128]{1,0:T(8,128)(2,1)S(1)}, bf16[64,128]{1,0:T(8,128)(2,1)S(1)}, u32[]{:S(2)}, u32[]{:S(2)}) collective-permute-start(bf16[64,128]{1,0:T(8,128)(2,1)S(1)} %choose.3.refs_0_), channel_id=1, source_target_pairs={{0,8},{8,16},{16,24},{24,0},{1,9},{9,17},{17,25},{25,1},{2,10},{10... | collective-permute-start | bytes 49160 | tf_op jit(solution)/shard_map/ppermute | solution.py:354
  44.4 2.2 %collective-permute-start.10 = (bf16[64,1024]{1,0:T(8,128)(2,1)S(1)}, bf16[64,1024]{1,0:T(8,128)(2,1)S(1)}, u32[]{:S(2)}, u32[]{:S(2)}) collective-permute-start(bf16[64,1024]{1,0:T(8,128)(2,1)S(1)} %add_select_fusion.2), channel_id=1, source_target_pairs={{0,160},{2,162},{4,164},{6,166},{8,168},{10,170},{12,172},{14,174}... | collective-permute-start | bytes 393224 | tf_op jit(solution)/shard_map/ppermute | solution.py:351
  46.6 1.3 %collective-permute-start.9 = (bf16[64,1024]{1,0:T(8,128)(2,1)S(1)}, bf16[64,1024]{1,0:T(8,128)(2,1)S(1)}, u32[]{:S(2)}, u32[]{:S(2)}) collective-permute-start(bf16[64,1024]{1,0:T(8,128)(2,1)S(1)} %add_select_fusion.2), channel_id=1, source_target_pairs={{0,96},{2,98},{4,100},{6,102},{8,104},{10,106},{12,108},{14,110},{... | collective-permute-start | bytes 393224 | tf_op jit(solution)/shard_map/ppermute | solution.py:351
  48.0 1.0 %request_partials.1 = (bf16[144,128]{1,0:T(8,128)(2,1)S(1)}, bf16[144,128]{1,0:T(8,128)(2,1)S(1)}, bf16[144,128]{1,0:T(8,128)(2,1)S(1)}, bf16[144,128]{1,0:T(8,128)(2,1)S(1)}) custom-call(bf16[64,128]{1,0:T(8,128)(2,1)S(1)} %choose.3.refs_0_, bf16[64,128]{1,0:T(8,128)(2,1)S(1)} %collective-permute-done.16.refs_1_, ...), custom_call_target="tpu_custom_call" | custom-call | flops 3000000000 | bytes 1048576 | tf_op jit(solution)/shard_map/request_partials/pallas_call | solution.py:268
  49.0 0.7 collective-permute-start.19
  49.8 0.9 %collective-permute-start.20 = (bf16[144,128]{1,0:T(8,128)(2,1)S(1)}, bf16[144,128]{1,0:T(8,128)(2,1)S(1)}, u32[]{:S(2)}, u32[]{:S(2)}) collective-permute-start(bf16[144,128]{1,0:T(8,128)(2,1)S(1)} %get-tuple-element.48), channel_id=1, source_target_pairs={{0,16},{8,24},{16,0},{24,8},{1,17},{9,25},{17,1},{25,9},{2,18},{10... | collective-permute-start | bytes 110600 | tf_op jit(solution)/shard_map/ppermute | solution.py:354
  50.7 2.5 %collective-permute-start.21 = (bf16[144,128]{1,0:T(8,128)(2,1)S(1)}, bf16[144,128]{1,0:T(8,128)(2,1)S(1)}, u32[]{:S(2)}, u32[]{:S(2)}) collective-permute-start(bf16[144,128]{1,0:T(8,128)(2,1)S(1)} %get-tuple-element.49), channel_id=1, source_target_pairs={{0,8},{8,16},{16,24},{24,0},{1,9},{9,17},{17,25},{25,1},{2,10},{10... | collective-permute-start | bytes 110600 | tf_op jit(solution)/shard_map/ppermute | solution.py:354
  53.2 1.3 %collective-permute-start.12 = (bf16[64,1024]{1,0:T(8,128)(2,1)S(1)}, bf16[64,1024]{1,0:T(8,128)(2,1)S(1)}, u32[]{:S(2)}, u32[]{:S(2)}) collective-permute-start(bf16[64,1024]{1,0:T(8,128)(2,1)S(1)} %add_select_fusion.1), channel_id=1, source_target_pairs={{0,224},{2,226},{4,228},{6,230},{8,232},{10,234},{12,236},{14,238}... | collective-permute-start | bytes 393224 | tf_op jit(solution)/shard_map/ppermute | solution.py:351
  54.5 1.3 %collective-permute-start.11 = (bf16[64,1024]{1,0:T(8,128)(2,1)S(1)}, bf16[64,1024]{1,0:T(8,128)(2,1)S(1)}, u32[]{:S(2)}, u32[]{:S(2)}) collective-permute-start(bf16[64,1024]{1,0:T(8,128)(2,1)S(1)} %add_select_fusion.1), channel_id=1, source_target_pairs={{0,32},{2,34},{4,36},{6,38},{8,40},{10,42},{12,44},{14,46},{16,48}... | collective-permute-start | bytes 393224 | tf_op jit(solution)/shard_map/ppermute | solution.py:351
  55.8 1.0 %join_pieces.2 = bf16[8,80,128]{2,1,0:T(8,128)(2,1)} custom-call(bf16[144,128]{1,0:T(8,128)(2,1)S(1)} %get-tuple-element.46.refs_0_, bf16[144,128]{1,0:T(8,128)(2,1)S(1)} %collective-permute-done.19.refs_1_, bf16[144,128]{1,0:T(8,128)(2,1)S(1)} %collective-permute-done.20.refs_2_, bf16[144,128]{1,0:T(8,128)(2,1)S(1)} %collective-permute-done.21.refs_3_), custom_call_target="tpu_custom_call" | custom-call | flops 3000000000 | bytes 524288 | tf_op jit(solution)/shard_map/join_pieces/pallas_call | solution.py:326
  56.8 3.4 %all-to-all-start.2 = ((bf16[8,80,128]{2,1,0:T(8,128)(2,1)}), bf16[8,80,128]{2,1,0:T(8,128)(2,1)S(1)}, u32[]{:S(2)}, u32[]{:S(2)}) async-start(bf16[8,80,128]{2,1,0:T(8,128)(2,1)} %join_pieces.2), calls=%async_computation.2 | async-start | bytes 327680 | tf_op jit(solution)/shard_map/all_to_all | solution.py:336
  60.3 2.6 %collective-permute-start.15 = (bf16[64,1024]{1,0:T(8,128)(2,1)S(1)}, bf16[64,1024]{1,0:T(8,128)(2,1)S(1)}, u32[]{:S(2)}, u32[]{:S(2)}) collective-permute-start(bf16[64,1024]{1,0:T(8,128)(2,1)S(1)} %add_select_fusion.refs_0_.refs_4_), channel_id=1, source_target_pairs={{0,24},{8,0},{16,8},{24,16},{1,25},{9,1},{17,9},{25,17},{2,26},{10... | collective-permute-start | bytes 393224 | tf_op jit(solution)/shard_map/ppermute | solution.py:354
  63.6 1.6 %collective-permute-start.13 = (bf16[64,1024]{1,0:T(8,128)(2,1)S(1)}, bf16[64,1024]{1,0:T(8,128)(2,1)S(1)}, u32[]{:S(2)}, u32[]{:S(2)}) collective-permute-start(bf16[64,1024]{1,0:T(8,128)(2,1)S(1)} %add_select_fusion.refs_0_.refs_4_), channel_id=1, source_target_pairs={{0,8},{8,16},{16,24},{24,0},{1,9},{9,17},{17,25},{25,1},{2,10},{10... | collective-permute-start | bytes 393224 | tf_op jit(solution)/shard_map/ppermute | solution.py:354
  65.1 4.4 %all-to-all-done.2.refs_0_ = bf16[8,80,128]{2,1,0:T(8,128)(2,1)S(1)} async-done(((bf16[8,80,128]{2,1,0:T(8,128)(2,1)}), bf16[8,80,128]{2,1,0:T(8,128)(2,1)S(1)}, u32[]{:S(2)}, u32[]{:S(2)}) %all-to-all-start.2) | async-done | bytes 163872 | tf_op jit(solution)/shard_map/all_to_all | solution.py:336
  69.5 1.1 %join_pieces.3 = bf16[16,64,128]{2,1,0:T(8,128)(2,1)} custom-call(bf16[8,80,128]{2,1,0:T(8,128)(2,1)S(1)} %all-to-all-done.2.refs_0_), custom_call_target="tpu_custom_call" | custom-call | flops 3000000000 | bytes 524288 | tf_op jit(solution)/shard_map/join_pieces/pallas_call | solution.py:326
  70.6 6.5 %all-to-all-start.3 = ((bf16[16,64,128]{2,1,0:T(8,128)(2,1)}), bf16[16,64,128]{2,1,0:T(8,128)(2,1)}, u32[]{:S(2)}, u32[]{:S(2)}) async-start(bf16[16,64,128]{2,1,0:T(8,128)(2,1)} %join_pieces.3), calls=%async_computation.3 | async-start | bytes 524288 | tf_op jit(solution)/shard_map/all_to_all | solution.py:336
  77.2 7.9 %context_attention.1 = bf16[256,4096]{1,0:T(8,128)(2,1)} custom-call(s32[1]{0:T(128)S(6)} %copy.11.len_ref, s32[1]{0:T(128)} %bitcast.root_ref, bf16[256,4096]{1,0:T(8,128)(2,1)S(1)} %copy-done.2, bf16[256,512]{1,0:T(8,128)(2,1)S(1)} %copy-done, bf16[256,512]{1,0:T(8,128)(2,1)S(1)} %copy-done.1, bf16[64,1024]{1,0:T(8,128)(2,1)S(1)} %add_select_fusion.refs_0_.refs_4_, ...), custom_call_target="tpu_custom_call" | custom-call | flops 2147483648 | bytes 5242880 | tf_op jit(solution)/shard_map/context_attention/pallas_call | solution.py:93
  85.4 0.9 %select_n.68 = bf16[32,4096]{1,0:T(8,128)(2,1)} reshape(bf16[32,4,4,2,128]{4,3,2,1,0:T(2,128)(2,1)S(1)} %copy.10) | data formatting | bytes 524288 | tf_op jit(solution)/shard_map/jit(_where)/select_n | solution.py:393
  (47 shorter events, 3.2 us)
Async XLA Ops:
  2.3 17.4 %all-to-all-start = ((bf16[32,32,128]{2,1,0:T(8,128)(2,1)}), bf16[32,32,128]{2,1,0:T(8,128)(2,1)S(1)}, u32[]{:S(2)}, u32[]{:S(2)}) async-start(bf16[32,32,128]{2,1,0:T(8,128)(2,1)} %pack.1), calls=%async_computation | async-start | bytes 524288 | tf_op jit(solution)/shard_map/all_to_all | solution.py:336
  13.4 8.4 %copy-start.5 = (bf16[576,128]{1,0:T(8,128)(2,1)S(1)}, bf16[576,128]{1,0:T(8,128)(2,1)}, u32[]{:S(2)}) copy-start(bf16[576,128]{1,0:T(8,128)(2,1)} %get-tuple-element.37) | copy-start | bytes 442372
  13.4 17.0 %copy-start.4 = (bf16[64,1024]{1,0:T(8,128)(2,1)S(1)}, bf16[64,1024]{1,0:T(8,128)(2,1)}, u32[]{:S(2)}) copy-start(bf16[64,1024]{1,0:T(8,128)(2,1)} %get-tuple-element.26) | copy-start | bytes 393220
  13.4 8.4 %collective-permute-start = (bf16[64,1024]{1,0:T(8,128)(2,1)}, bf16[64,1024]{1,0:T(8,128)(2,1)S(1)}, u32[]{:S(2)}, u32[]{:S(2)}) collective-permute-start(bf16[64,1024]{1,0:T(8,128)(2,1)} %get-tuple-element.27), channel_id=1, source_target_pairs={{0,8},{1,9}} | collective-permute-start | bytes 393224 | tf_op jit(solution)/shard_map/ppermute | solution.py:351
  14.8 7.1 %collective-permute-start.1 = (bf16[64,1024]{1,0:T(8,128)(2,1)}, bf16[64,1024]{1,0:T(8,128)(2,1)S(1)}, u32[]{:S(2)}, u32[]{:S(2)}) collective-permute-start(bf16[64,1024]{1,0:T(8,128)(2,1)} %get-tuple-element.28), channel_id=1, source_target_pairs={{0,16},{1,17}} | collective-permute-start | bytes 393224 | tf_op jit(solution)/shard_map/ppermute | solution.py:351
  15.5 6.4 %collective-permute-start.2 = (bf16[64,1024]{1,0:T(8,128)(2,1)}, bf16[64,1024]{1,0:T(8,128)(2,1)S(1)}, u32[]{:S(2)}, u32[]{:S(2)}) collective-permute-start(bf16[64,1024]{1,0:T(8,128)(2,1)} %get-tuple-element.29), channel_id=1, source_target_pairs={{0,24},{1,25}} | collective-permute-start | bytes 393224 | tf_op jit(solution)/shard_map/ppermute | solution.py:351
  16.2 17.5 %collective-permute-start.6 = (bf16[576,128]{1,0:T(8,128)(2,1)}, bf16[576,128]{1,0:T(8,128)(2,1)S(1)}, u32[]{:S(2)}, u32[]{:S(2)}) collective-permute-start(bf16[576,128]{1,0:T(8,128)(2,1)} %get-tuple-element.35), channel_id=1, source_target_pairs={{0,2},{2,4},{4,6},{6,0},{1,3},{3,5},{5,7},{7,1},{8,10},{10,12},{12... | collective-permute-start | bytes 442376 | tf_op jit(solution)/shard_map/ppermute | solution.py:361
  17.1 22.4 %collective-permute-start.7 = (bf16[576,128]{1,0:T(8,128)(2,1)}, bf16[576,128]{1,0:T(8,128)(2,1)S(1)}, u32[]{:S(2)}, u32[]{:S(2)}) collective-permute-start(bf16[576,128]{1,0:T(8,128)(2,1)} %get-tuple-element.36), channel_id=1, source_target_pairs={{0,4},{2,6},{4,0},{6,2},{1,5},{3,7},{5,1},{7,3},{8,12},{10,14},{12... | collective-permute-start | bytes 442376 | tf_op jit(solution)/shard_map/ppermute | solution.py:361
  21.7 17.7 %collective-permute-start.8 = (bf16[576,128]{1,0:T(8,128)(2,1)S(1)}, bf16[576,128]{1,0:T(8,128)(2,1)S(1)}, u32[]{:S(2)}, u32[]{:S(2)}) collective-permute-start(bf16[576,128]{1,0:T(8,128)(2,1)S(1)} %copy-done.5), channel_id=1, source_target_pairs={{0,6},{2,0},{4,2},{6,4},{1,7},{3,1},{5,3},{7,5},{8,14},{10,8},{12,... | collective-permute-start | bytes 442376 | tf_op jit(solution)/shard_map/ppermute | solution.py:361
  21.9 17.5 %all-to-all-start.1 = ((bf16[8,64,128]{2,1,0:T(8,128)(2,1)}), bf16[8,64,128]{2,1,0:T(8,128)(2,1)S(1)}, u32[]{:S(2)}, u32[]{:S(2)}) async-start(bf16[8,64,128]{2,1,0:T(8,128)(2,1)} %choose.2), calls=%async_computation.1 | async-start | bytes 262144 | tf_op jit(solution)/shard_map/all_to_all | solution.py:336
  30.4 9.1 %collective-permute-start.5 = (bf16[64,1024]{1,0:T(8,128)(2,1)S(1)}, bf16[64,1024]{1,0:T(8,128)(2,1)S(1)}, u32[]{:S(2)}, u32[]{:S(2)}) collective-permute-start(bf16[64,1024]{1,0:T(8,128)(2,1)S(1)} %add_select_fusion.3), channel_id=1, source_target_pairs={{0,6},{8,14},{16,22},{24,30},{1,7},{9,15},{17,23},{25,31}} | collective-permute-start | bytes 393224 | tf_op jit(solution)/shard_map/ppermute | solution.py:351
  32.4 7.1 %collective-permute-start.4 = (bf16[64,1024]{1,0:T(8,128)(2,1)S(1)}, bf16[64,1024]{1,0:T(8,128)(2,1)S(1)}, u32[]{:S(2)}, u32[]{:S(2)}) collective-permute-start(bf16[64,1024]{1,0:T(8,128)(2,1)S(1)} %add_select_fusion.3), channel_id=1, source_target_pairs={{0,4},{8,12},{16,20},{24,28},{1,5},{9,13},{17,21},{25,29}} | collective-permute-start | bytes 393224 | tf_op jit(solution)/shard_map/ppermute | solution.py:351
  33.7 5.8 %collective-permute-start.3 = (bf16[64,1024]{1,0:T(8,128)(2,1)S(1)}, bf16[64,1024]{1,0:T(8,128)(2,1)S(1)}, u32[]{:S(2)}, u32[]{:S(2)}) collective-permute-start(bf16[64,1024]{1,0:T(8,128)(2,1)S(1)} %add_select_fusion.3), channel_id=1, source_target_pairs={{0,2},{8,10},{16,18},{24,26},{1,3},{9,11},{17,19},{25,27}} | collective-permute-start | bytes 393224 | tf_op jit(solution)/shard_map/ppermute | solution.py:351
  39.5 8.5 %copy-start.3 = (bf16[576,128]{1,0:T(8,128)(2,1)S(1)}, bf16[576,128]{1,0:T(8,128)(2,1)}, u32[]{:S(2)}) copy-start(bf16[576,128]{1,0:T(8,128)(2,1)} %get-tuple-element.42.refs_4_) | copy-start | bytes 442372
  39.5 8.4 %collective-permute-start.18 = (bf16[64,128]{1,0:T(8,128)(2,1)S(1)}, bf16[64,128]{1,0:T(8,128)(2,1)S(1)}, u32[]{:S(2)}, u32[]{:S(2)}) collective-permute-start(bf16[64,128]{1,0:T(8,128)(2,1)S(1)} %choose.3.refs_0_), channel_id=1, source_target_pairs={{0,24},{8,0},{16,8},{24,16},{1,25},{9,1},{17,9},{25,17},{2,26},{10... | collective-permute-start | bytes 49160 | tf_op jit(solution)/shard_map/ppermute | solution.py:354
  40.2 7.8 %collective-permute-start.17 = (bf16[64,128]{1,0:T(8,128)(2,1)S(1)}, bf16[64,128]{1,0:T(8,128)(2,1)S(1)}, u32[]{:S(2)}, u32[]{:S(2)}) collective-permute-start(bf16[64,128]{1,0:T(8,128)(2,1)S(1)} %choose.3.refs_0_), channel_id=1, source_target_pairs={{0,16},{8,24},{16,0},{24,8},{1,17},{9,25},{17,1},{25,9},{2,18},{10... | collective-permute-start | bytes 49160 | tf_op jit(solution)/shard_map/ppermute | solution.py:354
  42.5 5.4 %collective-permute-start.16 = (bf16[64,128]{1,0:T(8,128)(2,1)S(1)}, bf16[64,128]{1,0:T(8,128)(2,1)S(1)}, u32[]{:S(2)}, u32[]{:S(2)}) collective-permute-start(bf16[64,128]{1,0:T(8,128)(2,1)S(1)} %choose.3.refs_0_), channel_id=1, source_target_pairs={{0,8},{8,16},{16,24},{24,0},{1,9},{9,17},{17,25},{25,1},{2,10},{10... | collective-permute-start | bytes 49160 | tf_op jit(solution)/shard_map/ppermute | solution.py:354
  44.4 8.8 %collective-permute-start.10 = (bf16[64,1024]{1,0:T(8,128)(2,1)S(1)}, bf16[64,1024]{1,0:T(8,128)(2,1)S(1)}, u32[]{:S(2)}, u32[]{:S(2)}) collective-permute-start(bf16[64,1024]{1,0:T(8,128)(2,1)S(1)} %add_select_fusion.2), channel_id=1, source_target_pairs={{0,160},{2,162},{4,164},{6,166},{8,168},{10,170},{12,172},{14,174}... | collective-permute-start | bytes 393224 | tf_op jit(solution)/shard_map/ppermute | solution.py:351
  46.6 6.5 %collective-permute-start.9 = (bf16[64,1024]{1,0:T(8,128)(2,1)S(1)}, bf16[64,1024]{1,0:T(8,128)(2,1)S(1)}, u32[]{:S(2)}, u32[]{:S(2)}) collective-permute-start(bf16[64,1024]{1,0:T(8,128)(2,1)S(1)} %add_select_fusion.2), channel_id=1, source_target_pairs={{0,96},{2,98},{4,100},{6,102},{8,104},{10,106},{12,108},{14,110},{... | collective-permute-start | bytes 393224 | tf_op jit(solution)/shard_map/ppermute | solution.py:351
  49.0 6.8 %collective-permute-start.19 = (bf16[144,128]{1,0:T(8,128)(2,1)S(1)}, bf16[144,128]{1,0:T(8,128)(2,1)S(1)}, u32[]{:S(2)}, u32[]{:S(2)}) collective-permute-start(bf16[144,128]{1,0:T(8,128)(2,1)S(1)} %get-tuple-element.47), channel_id=1, source_target_pairs={{0,24},{8,0},{16,8},{24,16},{1,25},{9,1},{17,9},{25,17},{2,26},{10... | collective-permute-start | bytes 110600 | tf_op jit(solution)/shard_map/ppermute | solution.py:354
  49.8 6.0 %collective-permute-start.20 = (bf16[144,128]{1,0:T(8,128)(2,1)S(1)}, bf16[144,128]{1,0:T(8,128)(2,1)S(1)}, u32[]{:S(2)}, u32[]{:S(2)}) collective-permute-start(bf16[144,128]{1,0:T(8,128)(2,1)S(1)} %get-tuple-element.48), channel_id=1, source_target_pairs={{0,16},{8,24},{16,0},{24,8},{1,17},{9,25},{17,1},{25,9},{2,18},{10... | collective-permute-start | bytes 110600 | tf_op jit(solution)/shard_map/ppermute | solution.py:354
  50.7 5.1 %collective-permute-start.21 = (bf16[144,128]{1,0:T(8,128)(2,1)S(1)}, bf16[144,128]{1,0:T(8,128)(2,1)S(1)}, u32[]{:S(2)}, u32[]{:S(2)}) collective-permute-start(bf16[144,128]{1,0:T(8,128)(2,1)S(1)} %get-tuple-element.49), channel_id=1, source_target_pairs={{0,8},{8,16},{16,24},{24,0},{1,9},{9,17},{17,25},{25,1},{2,10},{10... | collective-permute-start | bytes 110600 | tf_op jit(solution)/shard_map/ppermute | solution.py:354
  53.2 7.0 %collective-permute-start.12 = (bf16[64,1024]{1,0:T(8,128)(2,1)S(1)}, bf16[64,1024]{1,0:T(8,128)(2,1)S(1)}, u32[]{:S(2)}, u32[]{:S(2)}) collective-permute-start(bf16[64,1024]{1,0:T(8,128)(2,1)S(1)} %add_select_fusion.1), channel_id=1, source_target_pairs={{0,224},{2,226},{4,228},{6,230},{8,232},{10,234},{12,236},{14,238}... | collective-permute-start | bytes 393224 | tf_op jit(solution)/shard_map/ppermute | solution.py:351
  54.5 5.7 %collective-permute-start.11 = (bf16[64,1024]{1,0:T(8,128)(2,1)S(1)}, bf16[64,1024]{1,0:T(8,128)(2,1)S(1)}, u32[]{:S(2)}, u32[]{:S(2)}) collective-permute-start(bf16[64,1024]{1,0:T(8,128)(2,1)S(1)} %add_select_fusion.1), channel_id=1, source_target_pairs={{0,32},{2,34},{4,36},{6,38},{8,40},{10,42},{12,44},{14,46},{16,48}... | collective-permute-start | bytes 393224 | tf_op jit(solution)/shard_map/ppermute | solution.py:351
  56.8 12.7 %all-to-all-start.2 = ((bf16[8,80,128]{2,1,0:T(8,128)(2,1)}), bf16[8,80,128]{2,1,0:T(8,128)(2,1)S(1)}, u32[]{:S(2)}, u32[]{:S(2)}) async-start(bf16[8,80,128]{2,1,0:T(8,128)(2,1)} %join_pieces.2), calls=%async_computation.2 | async-start | bytes 327680 | tf_op jit(solution)/shard_map/all_to_all | solution.py:336
  60.3 16.9 %copy-start = (bf16[256,512]{1,0:T(8,128)(2,1)S(1)}, bf16[256,512]{1,0:T(8,128)(2,1)}, u32[]{:S(2)}) copy-start(bf16[256,512]{1,0:T(8,128)(2,1)} %k_ref.3) | copy-start | bytes 786436
  60.3 16.9 %copy-start.1 = (bf16[256,512]{1,0:T(8,128)(2,1)S(1)}, bf16[256,512]{1,0:T(8,128)(2,1)}, u32[]{:S(2)}) copy-start(bf16[256,512]{1,0:T(8,128)(2,1)} %v_ref.3) | copy-start | bytes 786436
  60.3 16.9 %copy-start.2 = (bf16[256,4096]{1,0:T(8,128)(2,1)S(1)}, bf16[256,4096]{1,0:T(8,128)(2,1)}, u32[]{:S(2)}) copy-start(bf16[256,4096]{1,0:T(8,128)(2,1)} %q_ref.1) | copy-start | bytes 6291460
  60.3 16.8 %collective-permute-start.15 = (bf16[64,1024]{1,0:T(8,128)(2,1)S(1)}, bf16[64,1024]{1,0:T(8,128)(2,1)S(1)}, u32[]{:S(2)}, u32[]{:S(2)}) collective-permute-start(bf16[64,1024]{1,0:T(8,128)(2,1)S(1)} %add_select_fusion.refs_0_.refs_4_), channel_id=1, source_target_pairs={{0,24},{8,0},{16,8},{24,16},{1,25},{9,1},{17,9},{25,17},{2,26},{10... | collective-permute-start | bytes 393224 | tf_op jit(solution)/shard_map/ppermute | solution.py:354
  62.9 14.2 %collective-permute-start.14 = (bf16[64,1024]{1,0:T(8,128)(2,1)S(1)}, bf16[64,1024]{1,0:T(8,128)(2,1)S(1)}, u32[]{:S(2)}, u32[]{:S(2)}) collective-permute-start(bf16[64,1024]{1,0:T(8,128)(2,1)S(1)} %add_select_fusion.refs_0_.refs_4_), channel_id=1, source_target_pairs={{0,16},{8,24},{16,0},{24,8},{1,17},{9,25},{17,1},{25,9},{2,18},{10... | collective-permute-start | bytes 393224 | tf_op jit(solution)/shard_map/ppermute | solution.py:354
  63.6 13.6 %collective-permute-start.13 = (bf16[64,1024]{1,0:T(8,128)(2,1)S(1)}, bf16[64,1024]{1,0:T(8,128)(2,1)S(1)}, u32[]{:S(2)}, u32[]{:S(2)}) collective-permute-start(bf16[64,1024]{1,0:T(8,128)(2,1)S(1)} %add_select_fusion.refs_0_.refs_4_), channel_id=1, source_target_pairs={{0,8},{8,16},{16,24},{24,0},{1,9},{9,17},{17,25},{25,1},{2,10},{10... | collective-permute-start | bytes 393224 | tf_op jit(solution)/shard_map/ppermute | solution.py:354
  70.6 14.5 %all-to-all-start.3 = ((bf16[16,64,128]{2,1,0:T(8,128)(2,1)}), bf16[16,64,128]{2,1,0:T(8,128)(2,1)}, u32[]{:S(2)}, u32[]{:S(2)}) async-start(bf16[16,64,128]{2,1,0:T(8,128)(2,1)} %join_pieces.3), calls=%async_computation.3 | async-start | bytes 524288 | tf_op jit(solution)/shard_map/all_to_all | solution.py:336

commit v4 on v3

--- a/solution.py
+++ b/solution.py
@@ -131,23 +131,6 @@
         o_ref[2 * rows + own :, :] = jnp.where(is_owner, rv_ref[:, lanes], mark[0:own])
 
 
-def mark(own_len, is_owner, y, k, v, rk, rv, n_x, n_y):
-    rows, width = k.shape
-    vmem = pl.BlockSpec(memory_space=pltpu.VMEM)
-    smem = pl.BlockSpec(memory_space=pltpu.SMEM)
-    shapes = [jax.ShapeDtypeStruct((rows // n_x, 2 * width), k.dtype)] * n_x
-    shapes += [jax.ShapeDtypeStruct((2 * (rows + rk.shape[0]), HEAD_SIZE), k.dtype)] * n_y
-    return pl.pallas_call(
-        functools.partial(mark_kernel, n_x),
-        out_shape=shapes,
-        in_specs=[smem] * 3 + [vmem] * 4,
-        out_specs=[vmem] * len(shapes),
-        compiler_params=pltpu.CompilerParams(vmem_limit_bytes=56 * 1024 * 1024),
-        cost_estimate=pl.CostEstimate(flops=2**18, bytes_accessed=2**21, transcendentals=0),
-        name="mark",
-    )(own_len, is_owner, y, k, v, rk, rv)
-
-
 def pack_kernel(n_y, rq_ref, o_ref):
     own, width = rq_ref.shape
     targets = o_ref.shape[0] // 2
@@ -160,18 +143,29 @@
                 o_ref[2 * j + c, i * own : (i + 1) * own, :] = rq_ref[:, lane : lane + HEAD_SIZE]
 
 
-def pack(rq, targets, n_y):
+def prepare_kernel(n_x, n_y, len_ref, own_ref, y_ref, rq_ref, k_ref, v_ref, rk_ref, rv_ref, sent_ref, *o_refs):
+    pack_kernel(n_y, rq_ref, sent_ref)
+    mark_kernel(n_x, len_ref, own_ref, y_ref, k_ref, v_ref, rk_ref, rv_ref, *o_refs)
+
+
+def prepare(own_len, is_owner, y, rq, k, v, rk, rv, n_x, n_y):
+    rows, width = k.shape
     vmem = pl.BlockSpec(memory_space=pltpu.VMEM)
-    height = rq.size // (2 * targets * HEAD_SIZE)
-    return pl.pallas_call(
-        functools.partial(pack_kernel, n_y),
-        out_shape=jax.ShapeDtypeStruct((2 * targets, height, HEAD_SIZE), jnp.bfloat16),
-        in_specs=[vmem],
-        out_specs=vmem,
+    smem = pl.BlockSpec(memory_space=pltpu.SMEM)
+    targets = 2 * n_x * n_y
+    shapes = [jax.ShapeDtypeStruct((targets, rq.size // (targets * HEAD_SIZE), HEAD_SIZE), k.dtype)]
+    shapes += [jax.ShapeDtypeStruct((rows // n_x, 2 * width), k.dtype)] * n_x
+    shapes += [jax.ShapeDtypeStruct((2 * (rows + rk.shape[0]), HEAD_SIZE), k.dtype)] * n_y
+    out = pl.pallas_call(
+        functools.partial(prepare_kernel, n_x, n_y),
+        out_shape=shapes,
+        in_specs=[smem] * 3 + [vmem] * 5,
+        out_specs=[vmem] * len(shapes),
         compiler_params=pltpu.CompilerParams(vmem_limit_bytes=56 * 1024 * 1024),
-        cost_estimate=pl.CostEstimate(flops=2**18, bytes_accessed=2**19, transcendentals=0),
-        name="pack",
-    )(rq)
+        cost_estimate=pl.CostEstimate(flops=2**18, bytes_accessed=5 * 2**19, transcendentals=0),
+        name="prepare",
+    )(own_len, is_owner, y, rq, k, v, rk, rv)
+    return out[0], out[1 : 1 + n_x], out[1 + n_x :]
 
 
 def plane_kernel(source_ref, x_ref, o_ref):
@@ -187,7 +181,7 @@
 
 
 def line_kernel(plane_ref, x_ref, o_ref):
-    o_ref[...] = x_ref[plane_ref[0]]
+    o_ref[...] = x_ref[plane_ref[0], 0 : o_ref.shape[0], :]
 
 
 def choose(kernel, index, x, shape, flops):
@@ -332,8 +326,8 @@
     )(*arrays)
 
 
-def exchange(x, axis):
-    return lax.all_to_all(x, axis, split_axis=0, concat_axis=0, tiled=True)
+def exchange(x, axis, groups=None):
+    return lax.all_to_all(x, axis, split_axis=0, concat_axis=0, axis_index_groups=groups, tiled=True)
 
 
 def local(n_z, n_x, n_y, q, k, v, block_lengths, rq, rk, rv, query_owner):
@@ -346,6 +340,7 @@
     is_owner = mine.astype(jnp.int32).reshape(1)
     is_root = ((z == 0) & (x == 0) & (y == 0)).astype(jnp.int32).reshape(1)
     own_rows = rk.shape[0]
+    down = [list(range(n_z))[::-1]]
 
     def move(value, pairs):
         return lax.ppermute(value, ("z", "x", "y"), pairs)
@@ -353,21 +348,21 @@
     def shift_x(value, count):
         return lax.ppermute(value, "x", [(a, (a + count) % n_x) for a in range(n_x)])
 
-    moved = exchange(pack(rq, n_xy, n_y), ("x", "y", "head"))
-    marked = mark(own_len, is_owner, y.reshape(1), k, v, rk, rv, n_x, n_y)
-    pieces, lines = marked[:n_x], marked[n_x:]
+    sent, pieces, lines = prepare(own_len, is_owner, y.reshape(1), rq, k, v, rk, rv, n_x, n_y)
+    moved = exchange(sent, ("x", "y", "head"))
     got = [move(pieces[i], [(0, i * n_y)]) for i in range(1, n_x)]
     lines = [lines[0]] + [
         lax.ppermute(lines[i], "y", [(a, (a + i) % n_y) for a in range(n_y)]) for i in range(1, n_y)
     ]
 
-    moved = choose(plane_kernel, owner_xy.reshape(1), moved, (n_z, 2 * moved.shape[1], HEAD_SIZE), 8 * 10**8)
+    piece = (2 * moved.shape[1], HEAD_SIZE)
+    moved = choose(plane_kernel, owner_xy.reshape(1), moved, (n_z,) + piece, 8 * 10**8)
     moved, got = lax.optimization_barrier((moved, got))
     anchor = jnp.where(x == 0, pieces[0], got[0] + got[1] + got[2])
     got = [move(anchor, [(i * n_y, i * n_y + j) for i in range(n_x)]) for j in range(1, n_y)]
-    moved = exchange(moved, "z")
-
-    moved = choose(line_kernel, owner_z.reshape(1), moved, moved.shape[1:], 3 * 10**9)
+    moved = exchange(moved, "z", down)
+
+    moved = choose(line_kernel, (n_z - 1 - owner_z).reshape(1), moved, piece, 3 * 10**9)
     moved, got, lines = lax.optimization_barrier((moved, got, lines))
     anchor = jnp.where(y == 0, anchor, got[0] + got[1] + got[2])
     plane = range(n_xy)
@@ -385,7 +380,7 @@
     anchors = [anchor]
     for i in range(1, n_x):
         anchors.append(shift_x(anchor, i))
-    planes = exchange(planes, "z")
+    planes = exchange(planes, "z", down)
 
     answer = exchange(join([planes], n_xy, 1, False), ("x", "y"))
     context_output = context_attention(own_len, is_root, q, k, v, anchors)

time: 87.4 us -> 85 us (0.973)
  waiting for transfers between devices: 10.2 us -> 6.9 us
  starting transfers between devices: 56.9 us -> 59.9 us
  Pallas kernels: 15.5 us -> 14.1 us
    all_to_all x4, waiting for transfers between devices: 8.88 us -> 2.9 us  [exchange(): lax.all_to_all(x, axis, split_axis=0, concat_axis=0, axis_index_groups=gr...]
    ppermute x10, waiting for transfers between devices: 1.32 us -> 3.97 us  [move(): return lax.ppermute(value, ('z', 'x', 'y'), pairs)]
    all_to_all x4, starting transfers between devices: 26 us -> 27.9 us  [exchange(): lax.all_to_all(x, axis, split_axis=0, concat_axis=0, axis_index_groups=gr...]
    pallas_call x2 -> x1, Pallas kernels: 3.78 us -> 2.35 us  [prepare(): pl.pallas_call(functools.partial(prepare_kernel, n_x, n_y), out_shape=sha...]
    ppermute x3, starting transfers between devices: 3.76 us -> 4.71 us  [local(): lax.ppermute(lines[i], 'y', [(a, (a + i) % n_y) for a in range(n_y)])]
  transfers between devices with their start and end apart: 26 -> 26, of which waited for: 3 -> 5; matrix products, arithmetic and copies ran while one was open for 0% -> 0% of each run, Pallas kernels for 16% -> 14%
where the time goes in v4:
time: 85 us; the launch traced here: 84.3 us
  starting transfers between devices  59.9 us (70%)
  Pallas kernels  14.1 us (17%)
  waiting for transfers between devices  6.9 us (8%)
  between operations  2.26 us (3%)
  local copies, waits for them, and re-layouts  1.12 us (1%)
    all_to_all x4, starting transfers between devices, exchange(): lax.all_to_all(x, axis, split_axis=0, concat_axis=0, axis_index_groups=gr...  27.9 us
    ppermute x10, starting transfers between devices, move(): return lax.ppermute(value, ('z', 'x', 'y'), pairs)  13.7 us
    ppermute x9, starting transfers between devices, shift_x(): lax.ppermute(value, 'x', [(a, (a + count) % n_x) for a in range(n_x)])  13.6 us
    pallas_call x1, Pallas kernels, context_attention(): pl.pallas_call(functools.partial(context_kernel, count), grid=(heads,), o...  7.93 us
    ppermute x3, starting transfers between devices, local(): lax.ppermute(lines[i], 'y', [(a, (a + i) % n_y) for a in range(n_y)])  4.71 us
    ppermute x10, waiting for transfers between devices, move(): return lax.ppermute(value, ('z', 'x', 'y'), pairs)  3.97 us
    all_to_all x4, waiting for transfers between devices, exchange(): lax.all_to_all(x, axis, split_axis=0, concat_axis=0, axis_index_groups=gr...  2.9 us
    pallas_call x1, Pallas kernels, prepare(): pl.pallas_call(functools.partial(prepare_kernel, n_x, n_y), out_shape=sha...  2.35 us
  transfers between devices with their start and end apart: 26, of which 5 were waited for; matrix products, arithmetic and copies ran while one was open for 0% of the time, Pallas kernels for 14%

profile of v4, /device:TPU:2, one launch (start us, length us, event | category | flops | bytes accessed | tf_op | source)
XLA Modules:
  0.0 84.3 jit_solution(16245724623001425375)
XLA Ops:
  2.0 2.3 %prepare.1 = (bf16[32,32,128]{2,1,0:T(8,128)(2,1)}, bf16[64,1024]{1,0:T(8,128)(2,1)}, bf16[64,1024]{1,0:T(8,128)(2,1)}, bf16[64,1024]{1,0:T(8,128)(2,1)}, bf16[6...) custom-call(s32[1]{0:T(128)S(6)} %copy.11.len_ref, ...), custom_call_target="tpu_custom_call" | custom-call | flops 262144 | bytes 2621440 | tf_op jit(solution)/shard_map/prepare/pallas_call | solution.py:159
  4.3 7.8 %all-to-all-start = ((bf16[32,32,128]{2,1,0:T(8,128)(2,1)}), bf16[32,32,128]{2,1,0:T(8,128)(2,1)S(1)}, u32[]{:S(2)}, u32[]{:S(2)}) async-start(bf16[32,32,128]{2,1,0:T(8,128)(2,1)} %get-tuple-element.28), calls=%async_computation | async-start | bytes 524288 | tf_op jit(solution)/shard_map/all_to_all | solution.py:330
  12.1 1.3 %collective-permute-start = (bf16[64,1024]{1,0:T(8,128)(2,1)}, bf16[64,1024]{1,0:T(8,128)(2,1)S(1)}, u32[]{:S(2)}, u32[]{:S(2)}) collective-permute-start(bf16[64,1024]{1,0:T(8,128)(2,1)} %get-tuple-element.29), channel_id=1, source_target_pairs={{0,8},{1,9}} | collective-permute-start | bytes 393224 | tf_op jit(solution)/shard_map/ppermute | solution.py:346
  14.7 0.9 %collective-permute-start.6 = (bf16[576,128]{1,0:T(8,128)(2,1)}, bf16[576,128]{1,0:T(8,128)(2,1)S(1)}, u32[]{:S(2)}, u32[]{:S(2)}) collective-permute-start(bf16[576,128]{1,0:T(8,128)(2,1)} %get-tuple-element.37), channel_id=1, source_target_pairs={{0,2},{2,4},{4,6},{6,0},{1,3},{3,5},{5,7},{7,1},{8,10},{10,12},{12... | collective-permute-start | bytes 442376 | tf_op jit(solution)/shard_map/ppermute | solution.py:355
  15.7 2.7 %collective-permute-start.7 = (bf16[576,128]{1,0:T(8,128)(2,1)}, bf16[576,128]{1,0:T(8,128)(2,1)S(1)}, u32[]{:S(2)}, u32[]{:S(2)}) collective-permute-start(bf16[576,128]{1,0:T(8,128)(2,1)} %get-tuple-element.38), channel_id=1, source_target_pairs={{0,4},{2,6},{4,0},{6,2},{1,5},{3,7},{5,1},{7,3},{8,12},{10,14},{12... | collective-permute-start | bytes 442376 | tf_op jit(solution)/shard_map/ppermute | solution.py:355
  18.3 1.5 %all-to-all-done.x_ref = bf16[32,32,128]{2,1,0:T(8,128)(2,1)S(1)} async-done(((bf16[32,32,128]{2,1,0:T(8,128)(2,1)}), bf16[32,32,128]{2,1,0:T(8,128)(2,1)S(1)}, u32[]{:S(2)}, u32[]{:S(2)}) %all-to-all-start) | async-done | bytes 262176 | tf_op jit(solution)/shard_map/all_to_all | solution.py:330
  20.5 1.1 %collective-permute-start.8 = (bf16[576,128]{1,0:T(8,128)(2,1)S(1)}, bf16[576,128]{1,0:T(8,128)(2,1)S(1)}, u32[]{:S(2)}, u32[]{:S(2)}) collective-permute-start(bf16[576,128]{1,0:T(8,128)(2,1)S(1)} %copy-done.5), channel_id=1, source_target_pairs={{0,6},{2,0},{4,2},{6,4},{1,7},{3,1},{5,3},{7,5},{8,14},{10,8},{12,... | collective-permute-start | bytes 442376 | tf_op jit(solution)/shard_map/ppermute | solution.py:355
  21.6 9.2 %all-to-all-start.1 = ((bf16[8,64,128]{2,1,0:T(8,128)(2,1)}), bf16[8,64,128]{2,1,0:T(8,128)(2,1)S(1)}, u32[]{:S(2)}, u32[]{:S(2)}) async-start(bf16[8,64,128]{2,1,0:T(8,128)(2,1)} %choose.2), calls=%async_computation.1 | async-start | bytes 262144 | tf_op jit(solution)/shard_map/all_to_all | solution.py:330
  30.8 2.6 %collective-permute-start.5 = (bf16[64,1024]{1,0:T(8,128)(2,1)S(1)}, bf16[64,1024]{1,0:T(8,128)(2,1)S(1)}, u32[]{:S(2)}, u32[]{:S(2)}) collective-permute-start(bf16[64,1024]{1,0:T(8,128)(2,1)S(1)} %add_select_fusion.3), channel_id=1, source_target_pairs={{0,6},{8,14},{16,22},{24,30},{1,7},{9,15},{17,23},{25,31}} | collective-permute-start | bytes 393224 | tf_op jit(solution)/shard_map/ppermute | solution.py:346
  33.5 1.3 %collective-permute-start.4 = (bf16[64,1024]{1,0:T(8,128)(2,1)S(1)}, bf16[64,1024]{1,0:T(8,128)(2,1)S(1)}, u32[]{:S(2)}, u32[]{:S(2)}) collective-permute-start(bf16[64,1024]{1,0:T(8,128)(2,1)S(1)} %add_select_fusion.3), channel_id=1, source_target_pairs={{0,4},{8,12},{16,20},{24,28},{1,5},{9,13},{17,21},{25,29}} | collective-permute-start | bytes 393224 | tf_op jit(solution)/shard_map/ppermute | solution.py:346
  34.8 1.3 %collective-permute-start.3 = (bf16[64,1024]{1,0:T(8,128)(2,1)S(1)}, bf16[64,1024]{1,0:T(8,128)(2,1)S(1)}, u32[]{:S(2)}, u32[]{:S(2)}) collective-permute-start(bf16[64,1024]{1,0:T(8,128)(2,1)S(1)} %add_select_fusion.3), channel_id=1, source_target_pairs={{0,2},{8,10},{16,18},{24,26},{1,3},{9,11},{17,19},{25,27}} | collective-permute-start | bytes 393224 | tf_op jit(solution)/shard_map/ppermute | solution.py:346
  36.5 2.1 %collective-permute-done.4 = bf16[64,1024]{1,0:T(8,128)(2,1)S(1)} collective-permute-done((bf16[64,1024]{1,0:T(8,128)(2,1)S(1)}, bf16[64,1024]{1,0:T(8,128)(2,1)S(1)}, u32[]{:S(2)}, u32[]{:S(2)}) %collective-permute-start.4) | collective-permute-done | bytes 131104 | tf_op jit(solution)/shard_map/ppermute | solution.py:346
  38.6 1.8 %collective-permute-done.3 = bf16[64,1024]{1,0:T(8,128)(2,1)S(1)} collective-permute-done((bf16[64,1024]{1,0:T(8,128)(2,1)S(1)}, bf16[64,1024]{1,0:T(8,128)(2,1)S(1)}, u32[]{:S(2)}, u32[]{:S(2)}) %collective-permute-start.3) | collective-permute-done | bytes 131104 | tf_op jit(solution)/shard_map/ppermute | solution.py:346
  40.5 1.4 %collective-permute-start.18 = (bf16[64,128]{1,0:T(8,128)(2,1)S(1)}, bf16[64,128]{1,0:T(8,128)(2,1)S(1)}, u32[]{:S(2)}, u32[]{:S(2)}) collective-permute-start(bf16[64,128]{1,0:T(8,128)(2,1)S(1)} %choose.3.refs_0_), channel_id=1, source_target_pairs={{0,24},{8,0},{16,8},{24,16},{1,25},{9,1},{17,9},{25,17},{2,26},{10... | collective-permute-start | bytes 49160 | tf_op jit(solution)/shard_map/ppermute | solution.py:349
  42.6 1.9 %collective-permute-start.16 = (bf16[64,128]{1,0:T(8,128)(2,1)S(1)}, bf16[64,128]{1,0:T(8,128)(2,1)S(1)}, u32[]{:S(2)}, u32[]{:S(2)}) collective-permute-start(bf16[64,128]{1,0:T(8,128)(2,1)S(1)} %choose.3.refs_0_), channel_id=1, source_target_pairs={{0,8},{8,16},{16,24},{24,0},{1,9},{9,17},{17,25},{25,1},{2,10},{10... | collective-permute-start | bytes 49160 | tf_op jit(solution)/shard_map/ppermute | solution.py:349
  44.5 1.6 %collective-permute-start.10 = (bf16[64,1024]{1,0:T(8,128)(2,1)S(1)}, bf16[64,1024]{1,0:T(8,128)(2,1)S(1)}, u32[]{:S(2)}, u32[]{:S(2)}) collective-permute-start(bf16[64,1024]{1,0:T(8,128)(2,1)S(1)} %add_select_fusion.2), channel_id=1, source_target_pairs={{0,160},{2,162},{4,164},{6,166},{8,168},{10,170},{12,172},{14,174}... | collective-permute-start | bytes 393224 | tf_op jit(solution)/shard_map/ppermute | solution.py:346
  46.2 1.3 %collective-permute-start.9 = (bf16[64,1024]{1,0:T(8,128)(2,1)S(1)}, bf16[64,1024]{1,0:T(8,128)(2,1)S(1)}, u32[]{:S(2)}, u32[]{:S(2)}) collective-permute-start(bf16[64,1024]{1,0:T(8,128)(2,1)S(1)} %add_select_fusion.2), channel_id=1, source_target_pairs={{0,96},{2,98},{4,100},{6,102},{8,104},{10,106},{12,108},{14,110},{... | collective-permute-start | bytes 393224 | tf_op jit(solution)/shard_map/ppermute | solution.py:346
  47.5 1.0 %request_partials.1 = (bf16[144,128]{1,0:T(8,128)(2,1)S(1)}, bf16[144,128]{1,0:T(8,128)(2,1)S(1)}, bf16[144,128]{1,0:T(8,128)(2,1)S(1)}, bf16[144,128]{1,0:T(8,128)(2,1)S(1)}) custom-call(bf16[64,128]{1,0:T(8,128)(2,1)S(1)} %choose.3.refs_0_, bf16[64,128]{1,0:T(8,128)(2,1)S(1)} %collective-permute-done.16.refs_1_, ...), custom_call_target="tpu_custom_call" | custom-call | flops 3000000000 | bytes 1048576 | tf_op jit(solution)/shard_map/request_partials/pallas_call | solution.py:262
  48.6 2.1 %collective-permute-start.19 = (bf16[144,128]{1,0:T(8,128)(2,1)S(1)}, bf16[144,128]{1,0:T(8,128)(2,1)S(1)}, u32[]{:S(2)}, u32[]{:S(2)}) collective-permute-start(bf16[144,128]{1,0:T(8,128)(2,1)S(1)} %get-tuple-element.49), channel_id=1, source_target_pairs={{0,24},{8,0},{16,8},{24,16},{1,25},{9,1},{17,9},{25,17},{2,26},{10... | collective-permute-start | bytes 110600 | tf_op jit(solution)/shard_map/ppermute | solution.py:349
  50.6 1.0 %collective-permute-start.20 = (bf16[144,128]{1,0:T(8,128)(2,1)S(1)}, bf16[144,128]{1,0:T(8,128)(2,1)S(1)}, u32[]{:S(2)}, u32[]{:S(2)}) collective-permute-start(bf16[144,128]{1,0:T(8,128)(2,1)S(1)} %get-tuple-element.50), channel_id=1, source_target_pairs={{0,16},{8,24},{16,0},{24,8},{1,17},{9,25},{17,1},{25,9},{2,18},{10... | collective-permute-start | bytes 110600 | tf_op jit(solution)/shard_map/ppermute | solution.py:349
  51.6 1.8 %collective-permute-start.21 = (bf16[144,128]{1,0:T(8,128)(2,1)S(1)}, bf16[144,128]{1,0:T(8,128)(2,1)S(1)}, u32[]{:S(2)}, u32[]{:S(2)}) collective-permute-start(bf16[144,128]{1,0:T(8,128)(2,1)S(1)} %get-tuple-element.51), channel_id=1, source_target_pairs={{0,8},{8,16},{16,24},{24,0},{1,9},{9,17},{17,25},{25,1},{2,10},{10... | collective-permute-start | bytes 110600 | tf_op jit(solution)/shard_map/ppermute | solution.py:349
  53.4 1.6 %collective-permute-start.12 = (bf16[64,1024]{1,0:T(8,128)(2,1)S(1)}, bf16[64,1024]{1,0:T(8,128)(2,1)S(1)}, u32[]{:S(2)}, u32[]{:S(2)}) collective-permute-start(bf16[64,1024]{1,0:T(8,128)(2,1)S(1)} %add_select_fusion.1), channel_id=1, source_target_pairs={{0,224},{2,226},{4,228},{6,230},{8,232},{10,234},{12,236},{14,238}... | collective-permute-start | bytes 393224 | tf_op jit(solution)/shard_map/ppermute | solution.py:346
  55.0 1.3 %collective-permute-start.11 = (bf16[64,1024]{1,0:T(8,128)(2,1)S(1)}, bf16[64,1024]{1,0:T(8,128)(2,1)S(1)}, u32[]{:S(2)}, u32[]{:S(2)}) collective-permute-start(bf16[64,1024]{1,0:T(8,128)(2,1)S(1)} %add_select_fusion.1), channel_id=1, source_target_pairs={{0,32},{2,34},{4,36},{6,38},{8,40},{10,42},{12,44},{14,46},{16,48}... | collective-permute-start | bytes 393224 | tf_op jit(solution)/shard_map/ppermute | solution.py:346
  56.4 1.0 %join_pieces.2 = bf16[8,80,128]{2,1,0:T(8,128)(2,1)} custom-call(bf16[144,128]{1,0:T(8,128)(2,1)S(1)} %get-tuple-element.48.refs_0_, bf16[144,128]{1,0:T(8,128)(2,1)S(1)} %collective-permute-done.19.refs_1_, bf16[144,128]{1,0:T(8,128)(2,1)S(1)} %collective-permute-done.20.refs_2_, bf16[144,128]{1,0:T(8,128)(2,1)S(1)} %collective-permute-done.21.refs_3_), custom_call_target="tpu_custom_call" | custom-call | flops 3000000000 | bytes 524288 | tf_op jit(solution)/shard_map/join_pieces/pallas_call | solution.py:320
  57.4 4.5 %all-to-all-start.2 = ((bf16[8,80,128]{2,1,0:T(8,128)(2,1)}), bf16[8,80,128]{2,1,0:T(8,128)(2,1)S(1)}, u32[]{:S(2)}, u32[]{:S(2)}) async-start(bf16[8,80,128]{2,1,0:T(8,128)(2,1)} %join_pieces.2), calls=%async_computation.2 | async-start | bytes 327680 | tf_op jit(solution)/shard_map/all_to_all | solution.py:330
  61.9 1.6 %collective-permute-start.15 = (bf16[64,1024]{1,0:T(8,128)(2,1)S(1)}, bf16[64,1024]{1,0:T(8,128)(2,1)S(1)}, u32[]{:S(2)}, u32[]{:S(2)}) collective-permute-start(bf16[64,1024]{1,0:T(8,128)(2,1)S(1)} %add_select_fusion.refs_0_.refs_4_), channel_id=1, source_target_pairs={{0,24},{8,0},{16,8},{24,16},{1,25},{9,1},{17,9},{25,17},{2,26},{10... | collective-permute-start | bytes 393224 | tf_op jit(solution)/shard_map/ppermute | solution.py:349
  63.5 1.7 %collective-permute-start.14 = (bf16[64,1024]{1,0:T(8,128)(2,1)S(1)}, bf16[64,1024]{1,0:T(8,128)(2,1)S(1)}, u32[]{:S(2)}, u32[]{:S(2)}) collective-permute-start(bf16[64,1024]{1,0:T(8,128)(2,1)S(1)} %add_select_fusion.refs_0_.refs_4_), channel_id=1, source_target_pairs={{0,16},{8,24},{16,0},{24,8},{1,17},{9,25},{17,1},{25,9},{2,18},{10... | collective-permute-start | bytes 393224 | tf_op jit(solution)/shard_map/ppermute | solution.py:349
  65.3 1.4 %collective-permute-start.13 = (bf16[64,1024]{1,0:T(8,128)(2,1)S(1)}, bf16[64,1024]{1,0:T(8,128)(2,1)S(1)}, u32[]{:S(2)}, u32[]{:S(2)}) collective-permute-start(bf16[64,1024]{1,0:T(8,128)(2,1)S(1)} %add_select_fusion.refs_0_.refs_4_), channel_id=1, source_target_pairs={{0,8},{8,16},{16,24},{24,0},{1,9},{9,17},{17,25},{25,1},{2,10},{10... | collective-permute-start | bytes 393224 | tf_op jit(solution)/shard_map/ppermute | solution.py:349
  66.7 1.0 %all-to-all-done.2.refs_0_ = bf16[8,80,128]{2,1,0:T(8,128)(2,1)S(1)} async-done(((bf16[8,80,128]{2,1,0:T(8,128)(2,1)}), bf16[8,80,128]{2,1,0:T(8,128)(2,1)S(1)}, u32[]{:S(2)}, u32[]{:S(2)}) %all-to-all-start.2) | async-done | bytes 163872 | tf_op jit(solution)/shard_map/all_to_all | solution.py:330
  67.8 1.1 %join_pieces.3 = bf16[16,64,128]{2,1,0:T(8,128)(2,1)} custom-call(bf16[8,80,128]{2,1,0:T(8,128)(2,1)S(1)} %all-to-all-done.2.refs_0_), custom_call_target="tpu_custom_call" | custom-call | flops 3000000000 | bytes 524288 | tf_op jit(solution)/shard_map/join_pieces/pallas_call | solution.py:320
  68.8 6.4 %all-to-all-start.3 = ((bf16[16,64,128]{2,1,0:T(8,128)(2,1)}), bf16[16,64,128]{2,1,0:T(8,128)(2,1)}, u32[]{:S(2)}, u32[]{:S(2)}) async-start(bf16[16,64,128]{2,1,0:T(8,128)(2,1)} %join_pieces.3), calls=%async_computation.3 | async-start | bytes 524288 | tf_op jit(solution)/shard_map/all_to_all | solution.py:330
  75.3 7.9 %context_attention.1 = bf16[256,4096]{1,0:T(8,128)(2,1)} custom-call(s32[1]{0:T(128)S(6)} %copy.11.len_ref, s32[1]{0:T(128)} %bitcast.root_ref, bf16[256,4096]{1,0:T(8,128)(2,1)S(1)} %copy-done.2, bf16[256,512]{1,0:T(8,128)(2,1)S(1)} %copy-done, bf16[256,512]{1,0:T(8,128)(2,1)S(1)} %copy-done.1, bf16[64,1024]{1,0:T(8,128)(2,1)S(1)} %add_select_fusion.refs_0_.refs_4_, ...), custom_call_target="tpu_custom_call" | custom-call | flops 2147483648 | bytes 5242880 | tf_op jit(solution)/shard_map/context_attention/pallas_call | solution.py:93
  (46 shorter events, 4.4 us)
Async XLA Ops:
  4.3 16.2 %copy-start.5 = (bf16[576,128]{1,0:T(8,128)(2,1)S(1)}, bf16[576,128]{1,0:T(8,128)(2,1)}, u32[]{:S(2)}) copy-start(bf16[576,128]{1,0:T(8,128)(2,1)} %get-tuple-element.39) | copy-start | bytes 442372
  4.3 26.5 %copy-start.4 = (bf16[64,1024]{1,0:T(8,128)(2,1)S(1)}, bf16[64,1024]{1,0:T(8,128)(2,1)}, u32[]{:S(2)}) copy-start(bf16[64,1024]{1,0:T(8,128)(2,1)} %get-tuple-element.27) | copy-start | bytes 393220
  4.3 15.5 %all-to-all-start = ((bf16[32,32,128]{2,1,0:T(8,128)(2,1)}), bf16[32,32,128]{2,1,0:T(8,128)(2,1)S(1)}, u32[]{:S(2)}, u32[]{:S(2)}) async-start(bf16[32,32,128]{2,1,0:T(8,128)(2,1)} %get-tuple-element.28), calls=%async_computation | async-start | bytes 524288 | tf_op jit(solution)/shard_map/all_to_all | solution.py:330
  12.1 8.4 %collective-permute-start = (bf16[64,1024]{1,0:T(8,128)(2,1)}, bf16[64,1024]{1,0:T(8,128)(2,1)S(1)}, u32[]{:S(2)}, u32[]{:S(2)}) collective-permute-start(bf16[64,1024]{1,0:T(8,128)(2,1)} %get-tuple-element.29), channel_id=1, source_target_pairs={{0,8},{1,9}} | collective-permute-start | bytes 393224 | tf_op jit(solution)/shard_map/ppermute | solution.py:346
  13.4 8.2 %collective-permute-start.1 = (bf16[64,1024]{1,0:T(8,128)(2,1)}, bf16[64,1024]{1,0:T(8,128)(2,1)S(1)}, u32[]{:S(2)}, u32[]{:S(2)}) collective-permute-start(bf16[64,1024]{1,0:T(8,128)(2,1)} %get-tuple-element.30), channel_id=1, source_target_pairs={{0,16},{1,17}} | collective-permute-start | bytes 393224 | tf_op jit(solution)/shard_map/ppermute | solution.py:346
  14.1 7.5 %collective-permute-start.2 = (bf16[64,1024]{1,0:T(8,128)(2,1)}, bf16[64,1024]{1,0:T(8,128)(2,1)S(1)}, u32[]{:S(2)}, u32[]{:S(2)}) collective-permute-start(bf16[64,1024]{1,0:T(8,128)(2,1)} %get-tuple-element.31), channel_id=1, source_target_pairs={{0,24},{1,25}} | collective-permute-start | bytes 393224 | tf_op jit(solution)/shard_map/ppermute | solution.py:346
  14.7 20.0 %collective-permute-start.6 = (bf16[576,128]{1,0:T(8,128)(2,1)}, bf16[576,128]{1,0:T(8,128)(2,1)S(1)}, u32[]{:S(2)}, u32[]{:S(2)}) collective-permute-start(bf16[576,128]{1,0:T(8,128)(2,1)} %get-tuple-element.37), channel_id=1, source_target_pairs={{0,2},{2,4},{4,6},{6,0},{1,3},{3,5},{5,7},{7,1},{8,10},{10,12},{12... | collective-permute-start | bytes 442376 | tf_op jit(solution)/shard_map/ppermute | solution.py:355
  15.7 20.8 %collective-permute-start.7 = (bf16[576,128]{1,0:T(8,128)(2,1)}, bf16[576,128]{1,0:T(8,128)(2,1)S(1)}, u32[]{:S(2)}, u32[]{:S(2)}) collective-permute-start(bf16[576,128]{1,0:T(8,128)(2,1)} %get-tuple-element.38), channel_id=1, source_target_pairs={{0,4},{2,6},{4,0},{6,2},{1,5},{3,7},{5,1},{7,3},{8,12},{10,14},{12... | collective-permute-start | bytes 442376 | tf_op jit(solution)/shard_map/ppermute | solution.py:355
  20.5 16.0 %collective-permute-start.8 = (bf16[576,128]{1,0:T(8,128)(2,1)S(1)}, bf16[576,128]{1,0:T(8,128)(2,1)S(1)}, u32[]{:S(2)}, u32[]{:S(2)}) collective-permute-start(bf16[576,128]{1,0:T(8,128)(2,1)S(1)} %copy-done.5), channel_id=1, source_target_pairs={{0,6},{2,0},{4,2},{6,4},{1,7},{3,1},{5,3},{7,5},{8,14},{10,8},{12,... | collective-permute-start | bytes 442376 | tf_op jit(solution)/shard_map/ppermute | solution.py:355
  21.6 14.9 %all-to-all-start.1 = ((bf16[8,64,128]{2,1,0:T(8,128)(2,1)}), bf16[8,64,128]{2,1,0:T(8,128)(2,1)S(1)}, u32[]{:S(2)}, u32[]{:S(2)}) async-start(bf16[8,64,128]{2,1,0:T(8,128)(2,1)} %choose.2), calls=%async_computation.1 | async-start | bytes 262144 | tf_op jit(solution)/shard_map/all_to_all | solution.py:330
  30.8 5.7 %collective-permute-start.5 = (bf16[64,1024]{1,0:T(8,128)(2,1)S(1)}, bf16[64,1024]{1,0:T(8,128)(2,1)S(1)}, u32[]{:S(2)}, u32[]{:S(2)}) collective-permute-start(bf16[64,1024]{1,0:T(8,128)(2,1)S(1)} %add_select_fusion.3), channel_id=1, source_target_pairs={{0,6},{8,14},{16,22},{24,30},{1,7},{9,15},{17,23},{25,31}} | collective-permute-start | bytes 393224 | tf_op jit(solution)/shard_map/ppermute | solution.py:346
  33.5 5.2 %collective-permute-start.4 = (bf16[64,1024]{1,0:T(8,128)(2,1)S(1)}, bf16[64,1024]{1,0:T(8,128)(2,1)S(1)}, u32[]{:S(2)}, u32[]{:S(2)}) collective-permute-start(bf16[64,1024]{1,0:T(8,128)(2,1)S(1)} %add_select_fusion.3), channel_id=1, source_target_pairs={{0,4},{8,12},{16,20},{24,28},{1,5},{9,13},{17,21},{25,29}} | collective-permute-start | bytes 393224 | tf_op jit(solution)/shard_map/ppermute | solution.py:346
  34.8 5.7 %collective-permute-start.3 = (bf16[64,1024]{1,0:T(8,128)(2,1)S(1)}, bf16[64,1024]{1,0:T(8,128)(2,1)S(1)}, u32[]{:S(2)}, u32[]{:S(2)}) collective-permute-start(bf16[64,1024]{1,0:T(8,128)(2,1)S(1)} %add_select_fusion.3), channel_id=1, source_target_pairs={{0,2},{8,10},{16,18},{24,26},{1,3},{9,11},{17,19},{25,27}} | collective-permute-start | bytes 393224 | tf_op jit(solution)/shard_map/ppermute | solution.py:346
  36.5 11.0 %copy-start.3 = (bf16[576,128]{1,0:T(8,128)(2,1)S(1)}, bf16[576,128]{1,0:T(8,128)(2,1)}, u32[]{:S(2)}) copy-start(bf16[576,128]{1,0:T(8,128)(2,1)} %get-tuple-element.44.refs_4_) | copy-start | bytes 442372
  40.5 7.0 %collective-permute-start.18 = (bf16[64,128]{1,0:T(8,128)(2,1)S(1)}, bf16[64,128]{1,0:T(8,128)(2,1)S(1)}, u32[]{:S(2)}, u32[]{:S(2)}) collective-permute-start(bf16[64,128]{1,0:T(8,128)(2,1)S(1)} %choose.3.refs_0_), channel_id=1, source_target_pairs={{0,24},{8,0},{16,8},{24,16},{1,25},{9,1},{17,9},{25,17},{2,26},{10... | collective-permute-start | bytes 49160 | tf_op jit(solution)/shard_map/ppermute | solution.py:349
  41.9 5.6 %collective-permute-start.17 = (bf16[64,128]{1,0:T(8,128)(2,1)S(1)}, bf16[64,128]{1,0:T(8,128)(2,1)S(1)}, u32[]{:S(2)}, u32[]{:S(2)}) collective-permute-start(bf16[64,128]{1,0:T(8,128)(2,1)S(1)} %choose.3.refs_0_), channel_id=1, source_target_pairs={{0,16},{8,24},{16,0},{24,8},{1,17},{9,25},{17,1},{25,9},{2,18},{10... | collective-permute-start | bytes 49160 | tf_op jit(solution)/shard_map/ppermute | solution.py:349
  42.6 4.9 %collective-permute-start.16 = (bf16[64,128]{1,0:T(8,128)(2,1)S(1)}, bf16[64,128]{1,0:T(8,128)(2,1)S(1)}, u32[]{:S(2)}, u32[]{:S(2)}) collective-permute-start(bf16[64,128]{1,0:T(8,128)(2,1)S(1)} %choose.3.refs_0_), channel_id=1, source_target_pairs={{0,8},{8,16},{16,24},{24,0},{1,9},{9,17},{17,25},{25,1},{2,10},{10... | collective-permute-start | bytes 49160 | tf_op jit(solution)/shard_map/ppermute | solution.py:349
  44.5 8.9 %collective-permute-start.10 = (bf16[64,1024]{1,0:T(8,128)(2,1)S(1)}, bf16[64,1024]{1,0:T(8,128)(2,1)S(1)}, u32[]{:S(2)}, u32[]{:S(2)}) collective-permute-start(bf16[64,1024]{1,0:T(8,128)(2,1)S(1)} %add_select_fusion.2), channel_id=1, source_target_pairs={{0,160},{2,162},{4,164},{6,166},{8,168},{10,170},{12,172},{14,174}... | collective-permute-start | bytes 393224 | tf_op jit(solution)/shard_map/ppermute | solution.py:346
  46.2 7.2 %collective-permute-start.9 = (bf16[64,1024]{1,0:T(8,128)(2,1)S(1)}, bf16[64,1024]{1,0:T(8,128)(2,1)S(1)}, u32[]{:S(2)}, u32[]{:S(2)}) collective-permute-start(bf16[64,1024]{1,0:T(8,128)(2,1)S(1)} %add_select_fusion.2), channel_id=1, source_target_pairs={{0,96},{2,98},{4,100},{6,102},{8,104},{10,106},{12,108},{14,110},{... | collective-permute-start | bytes 393224 | tf_op jit(solution)/shard_map/ppermute | solution.py:346
  48.6 7.8 %collective-permute-start.19 = (bf16[144,128]{1,0:T(8,128)(2,1)S(1)}, bf16[144,128]{1,0:T(8,128)(2,1)S(1)}, u32[]{:S(2)}, u32[]{:S(2)}) collective-permute-start(bf16[144,128]{1,0:T(8,128)(2,1)S(1)} %get-tuple-element.49), channel_id=1, source_target_pairs={{0,24},{8,0},{16,8},{24,16},{1,25},{9,1},{17,9},{25,17},{2,26},{10... | collective-permute-start | bytes 110600 | tf_op jit(solution)/shard_map/ppermute | solution.py:349
  50.6 5.7 %collective-permute-start.20 = (bf16[144,128]{1,0:T(8,128)(2,1)S(1)}, bf16[144,128]{1,0:T(8,128)(2,1)S(1)}, u32[]{:S(2)}, u32[]{:S(2)}) collective-permute-start(bf16[144,128]{1,0:T(8,128)(2,1)S(1)} %get-tuple-element.50), channel_id=1, source_target_pairs={{0,16},{8,24},{16,0},{24,8},{1,17},{9,25},{17,1},{25,9},{2,18},{10... | collective-permute-start | bytes 110600 | tf_op jit(solution)/shard_map/ppermute | solution.py:349
  51.6 4.8 %collective-permute-start.21 = (bf16[144,128]{1,0:T(8,128)(2,1)S(1)}, bf16[144,128]{1,0:T(8,128)(2,1)S(1)}, u32[]{:S(2)}, u32[]{:S(2)}) collective-permute-start(bf16[144,128]{1,0:T(8,128)(2,1)S(1)} %get-tuple-element.51), channel_id=1, source_target_pairs={{0,8},{8,16},{16,24},{24,0},{1,9},{9,17},{17,25},{25,1},{2,10},{10... | collective-permute-start | bytes 110600 | tf_op jit(solution)/shard_map/ppermute | solution.py:349
  53.4 8.4 %collective-permute-start.12 = (bf16[64,1024]{1,0:T(8,128)(2,1)S(1)}, bf16[64,1024]{1,0:T(8,128)(2,1)S(1)}, u32[]{:S(2)}, u32[]{:S(2)}) collective-permute-start(bf16[64,1024]{1,0:T(8,128)(2,1)S(1)} %add_select_fusion.1), channel_id=1, source_target_pairs={{0,224},{2,226},{4,228},{6,230},{8,232},{10,234},{12,236},{14,238}... | collective-permute-start | bytes 393224 | tf_op jit(solution)/shard_map/ppermute | solution.py:346
  55.0 6.8 %collective-permute-start.11 = (bf16[64,1024]{1,0:T(8,128)(2,1)S(1)}, bf16[64,1024]{1,0:T(8,128)(2,1)S(1)}, u32[]{:S(2)}, u32[]{:S(2)}) collective-permute-start(bf16[64,1024]{1,0:T(8,128)(2,1)S(1)} %add_select_fusion.1), channel_id=1, source_target_pairs={{0,32},{2,34},{4,36},{6,38},{8,40},{10,42},{12,44},{14,46},{16,48}... | collective-permute-start | bytes 393224 | tf_op jit(solution)/shard_map/ppermute | solution.py:346
  57.4 10.4 %all-to-all-start.2 = ((bf16[8,80,128]{2,1,0:T(8,128)(2,1)}), bf16[8,80,128]{2,1,0:T(8,128)(2,1)S(1)}, u32[]{:S(2)}, u32[]{:S(2)}) async-start(bf16[8,80,128]{2,1,0:T(8,128)(2,1)} %join_pieces.2), calls=%async_computation.2 | async-start | bytes 327680 | tf_op jit(solution)/shard_map/all_to_all | solution.py:330
  61.9 13.4 %copy-start = (bf16[256,512]{1,0:T(8,128)(2,1)S(1)}, bf16[256,512]{1,0:T(8,128)(2,1)}, u32[]{:S(2)}) copy-start(bf16[256,512]{1,0:T(8,128)(2,1)} %k_ref.3) | copy-start | bytes 786436
  61.9 13.4 %copy-start.1 = (bf16[256,512]{1,0:T(8,128)(2,1)S(1)}, bf16[256,512]{1,0:T(8,128)(2,1)}, u32[]{:S(2)}) copy-start(bf16[256,512]{1,0:T(8,128)(2,1)} %v_ref.3) | copy-start | bytes 786436
  61.9 13.3 %copy-start.2 = (bf16[256,4096]{1,0:T(8,128)(2,1)S(1)}, bf16[256,4096]{1,0:T(8,128)(2,1)}, u32[]{:S(2)}) copy-start(bf16[256,4096]{1,0:T(8,128)(2,1)} %q_ref.1) | copy-start | bytes 6291460
  61.9 13.3 %collective-permute-start.15 = (bf16[64,1024]{1,0:T(8,128)(2,1)S(1)}, bf16[64,1024]{1,0:T(8,128)(2,1)S(1)}, u32[]{:S(2)}, u32[]{:S(2)}) collective-permute-start(bf16[64,1024]{1,0:T(8,128)(2,1)S(1)} %add_select_fusion.refs_0_.refs_4_), channel_id=1, source_target_pairs={{0,24},{8,0},{16,8},{24,16},{1,25},{9,1},{17,9},{25,17},{2,26},{10... | collective-permute-start | bytes 393224 | tf_op jit(solution)/shard_map/ppermute | solution.py:349
  63.5 11.7 %collective-permute-start.14 = (bf16[64,1024]{1,0:T(8,128)(2,1)S(1)}, bf16[64,1024]{1,0:T(8,128)(2,1)S(1)}, u32[]{:S(2)}, u32[]{:S(2)}) collective-permute-start(bf16[64,1024]{1,0:T(8,128)(2,1)S(1)} %add_select_fusion.refs_0_.refs_4_), channel_id=1, source_target_pairs={{0,16},{8,24},{16,0},{24,8},{1,17},{9,25},{17,1},{25,9},{2,18},{10... | collective-permute-start | bytes 393224 | tf_op jit(solution)/shard_map/ppermute | solution.py:349
  65.3 10.0 %collective-permute-start.13 = (bf16[64,1024]{1,0:T(8,128)(2,1)S(1)}, bf16[64,1024]{1,0:T(8,128)(2,1)S(1)}, u32[]{:S(2)}, u32[]{:S(2)}) collective-permute-start(bf16[64,1024]{1,0:T(8,128)(2,1)S(1)} %add_select_fusion.refs_0_.refs_4_), channel_id=1, source_target_pairs={{0,8},{8,16},{16,24},{24,0},{1,9},{9,17},{17,25},{25,1},{2,10},{10... | collective-permute-start | bytes 393224 | tf_op jit(solution)/shard_map/ppermute | solution.py:349
  68.8 14.4 %all-to-all-start.3 = ((bf16[16,64,128]{2,1,0:T(8,128)(2,1)}), bf16[16,64,128]{2,1,0:T(8,128)(2,1)}, u32[]{:S(2)}, u32[]{:S(2)}) async-start(bf16[16,64,128]{2,1,0:T(8,128)(2,1)} %join_pieces.3), calls=%async_computation.3 | async-start | bytes 524288 | tf_op jit(solution)/shard_map/all_to_all | solution.py:330

commit v5 on v4

--- a/solution.py
+++ b/solution.py
@@ -14,6 +14,12 @@
 LN2 = 0.6931471805599453
 MARK = 1024.0
 VMEM_LIMIT = 32 * 1024 * 1024
+STACK = 8
+N_X, N_Y = 4, 4
+
+
+def place():
+    return (lax.axis_index("z") * N_X + lax.axis_index("x")) * N_Y + lax.axis_index("y")
 
 
 def dot_nt(a, b):
@@ -24,13 +30,14 @@
     return lax.dot_general(a, b, (((1,), (0,)), ((), ())), preferred_element_type=jnp.float32)
 
 
-def context_kernel(count, len_ref, root_ref, q_ref, k_ref, v_ref, *refs):
+def context_kernel(count, len_ref, q_ref, k_ref, v_ref, *refs):
     ak_refs, av_refs = refs[:count], refs[count : 2 * count]
-    o_ref, vs_ref = refs[-2:]
+    o_ref, zero_ref, vs_ref = refs[-3:]
+    zero_ref[...] = jnp.zeros_like(zero_ref)
     rows = k_ref.shape[0]
     half = rows // 2
     own_len = len_ref[0]
-    root = root_ref[0] > 0
+    root = place() == 0
     ak = jnp.concatenate([ref[...] for ref in ak_refs], axis=0)
     ak = jnp.where(root, jnp.broadcast_to(k_ref[0:1, :], ak.shape), ak)
     av = jnp.concatenate([ref[...] for ref in av_refs], axis=0)
@@ -40,8 +47,8 @@
     vs_ref[rows:, :HEAD_SIZE] = v_ref[...]
     vs_ref[rows:, HEAD_SIZE:] = jnp.ones((rows, HEAD_SIZE), jnp.bfloat16)
     c = SCALE * LOG2E
-    row = lax.broadcasted_iota(jnp.int32, (2 * half, half), 0)
-    col = lax.broadcasted_iota(jnp.int32, (2 * half, half), 1)
+    row = lax.broadcasted_iota(jnp.int32, (STACK * half, half), 0)
+    col = lax.broadcasted_iota(jnp.int32, (STACK * half, half), 1)
     causal = jnp.where(col <= lax.rem(row, half), 0.0, -jnp.inf).astype(jnp.float32)
 
     def lanes(g):
@@ -49,7 +56,7 @@
 
     def scores(top, g):
         keys = top + half
-        q = jnp.concatenate([q_ref[top:keys, lanes(g)], q_ref[top:keys, lanes(g + 1)]], axis=0)
+        q = jnp.concatenate([q_ref[top:keys, lanes(g + i)] for i in range(STACK)], axis=0)
         sa = dot_nt(q, ak)
         so = dot_nt(q, k_ref[0:keys, :])
         tiles = [sa[:, i : i + half] for i in range(0, rows, half)]
@@ -66,11 +73,11 @@
         inverse = pl.reciprocal(total, approx=True)
         inverse = inverse * (2.0 - total * inverse)
         out = acc[:, :HEAD_SIZE] * inverse
-        for i in range(2):
+        for i in range(STACK):
             part = jnp.where(live, out[i * half : (i + 1) * half], 0.0)
             o_ref[top:keys, lanes(g + i)] = part.astype(jnp.bfloat16)
 
-    work = [(top, g) for top in (0, half) for g in range(0, GROUP, 2)]
+    work = [(top, g) for top in (0, half) for g in range(0, GROUP, STACK)]
     tiles = scores(*work[0])
     for i, item in enumerate(work):
         later = scores(*work[i + 1]) if i + 1 < len(work) else None
@@ -78,7 +85,7 @@
         tiles = later
 
 
-def context_attention(own_len, is_root, q, k, v, anchor):
+def context_attention(own_len, q, k, v, anchor, own_rows):
     rows, width = q.shape
     heads = k.shape[1] // HEAD_SIZE
     wide = GROUP * HEAD_SIZE
@@ -87,25 +94,28 @@
     smem = pl.BlockSpec(memory_space=pltpu.SMEM)
     kv_spec = pl.BlockSpec((rows, HEAD_SIZE), lambda h: (0, h))
     wide_spec = pl.BlockSpec((rows, wide), lambda h: (0, h))
-    specs = [smem, smem, wide_spec, kv_spec, kv_spec]
+    specs = [smem, wide_spec, kv_spec, kv_spec]
     specs += [pl.BlockSpec((slab, HEAD_SIZE), lambda h: (0, h))] * count
     specs += [pl.BlockSpec((slab, HEAD_SIZE), lambda h: (0, heads + h))] * count
     return pl.pallas_call(
         functools.partial(context_kernel, count),
         grid=(heads,),
-        out_shape=jax.ShapeDtypeStruct((rows, width), jnp.bfloat16),
+        out_shape=[
+            jax.ShapeDtypeStruct((rows, width), jnp.bfloat16),
+            jax.ShapeDtypeStruct((own_rows, width), jnp.bfloat16),
+        ],
         in_specs=specs,
-        out_specs=wide_spec,
+        out_specs=[wide_spec, pl.BlockSpec((own_rows, wide), lambda h: (0, h))],
         scratch_shapes=[pltpu.VMEM((2 * rows, 2 * HEAD_SIZE), jnp.bfloat16)],
         compiler_params=pltpu.CompilerParams(vmem_limit_bytes=VMEM_LIMIT),
         cost_estimate=pl.CostEstimate(
             flops=8 * rows * width * rows, bytes_accessed=5 * 2**20, transcendentals=2 * rows * rows * heads * GROUP
         ),
         name="context_attention",
-    )(own_len, is_root, q, k, v, *anchor, *anchor)
-
-
-def mark_kernel(n_x, len_ref, own_ref, y_ref, k_ref, v_ref, rk_ref, rv_ref, *o_refs):
+    )(own_len, q, k, v, *anchor, *anchor)
+
+
+def mark_kernel(n_x, len_ref, k_ref, v_ref, rk_ref, rv_ref, *o_refs):
     rows, width = k_ref.shape
     own = rk_ref.shape[0]
     slab = rows // n_x
@@ -117,18 +127,16 @@
         o_ref[:, width:] = jnp.where(valid, v_ref[span, :], jnp.full_like(first, MARK))
     lines = o_refs[n_x:]
     valid = lax.broadcasted_iota(jnp.int32, (rows, HEAD_SIZE), 0) < len_ref[0]
-    is_owner = own_ref[0] > 0
+    y = lax.axis_index("y")
     for i, o_ref in enumerate(lines):
-        head = lax.rem(y_ref[0] + i, len(lines))
+        head = lax.rem(y + i, len(lines))
         lanes = pl.ds(pl.multiple_of(head * HEAD_SIZE, HEAD_SIZE), HEAD_SIZE)
         first = k_ref[0:1, lanes]
         o_ref[0:rows, :] = jnp.where(valid, k_ref[:, lanes], jnp.broadcast_to(first, valid.shape))
-        o_ref[rows : rows + own, :] = jnp.where(
-            is_owner, rk_ref[:, lanes], jnp.broadcast_to(first, (own, HEAD_SIZE))
-        )
+        o_ref[rows : rows + own, :] = rk_ref[:, lanes]
         mark = jnp.full((rows, HEAD_SIZE), MARK, jnp.bfloat16)
         o_ref[rows + own : 2 * rows + own, :] = jnp.where(valid, v_ref[:, lanes], mark)
-        o_ref[2 * rows + own :, :] = jnp.where(is_owner, rv_ref[:, lanes], mark[0:own])
+        o_ref[2 * rows + own :, :] = rv_ref[:, lanes]
 
 
 def pack_kernel(n_y, rq_ref, o_ref):
@@ -143,15 +151,14 @@
                 o_ref[2 * j + c, i * own : (i + 1) * own, :] = rq_ref[:, lane : lane + HEAD_SIZE]
 
 
-def prepare_kernel(n_x, n_y, len_ref, own_ref, y_ref, rq_ref, k_ref, v_ref, rk_ref, rv_ref, sent_ref, *o_refs):
+def prepare_kernel(n_x, n_y, len_ref, rq_ref, k_ref, v_ref, rk_ref, rv_ref, sent_ref, *o_refs):
     pack_kernel(n_y, rq_ref, sent_ref)
-    mark_kernel(n_x, len_ref, own_ref, y_ref, k_ref, v_ref, rk_ref, rv_ref, *o_refs)
-
-
-def prepare(own_len, is_owner, y, rq, k, v, rk, rv, n_x, n_y):
+    mark_kernel(n_x, len_ref, k_ref, v_ref, rk_ref, rv_ref, *o_refs)
+
+
+def prepare(own_len, rq, k, v, rk, rv, n_x, n_y):
     rows, width = k.shape
     vmem = pl.BlockSpec(memory_space=pltpu.VMEM)
-    smem = pl.BlockSpec(memory_space=pltpu.SMEM)
     targets = 2 * n_x * n_y
     shapes = [jax.ShapeDtypeStruct((targets, rq.size // (targets * HEAD_SIZE), HEAD_SIZE), k.dtype)]
     shapes += [jax.ShapeDtypeStruct((rows // n_x, 2 * width), k.dtype)] * n_x
@@ -159,18 +166,18 @@
     out = pl.pallas_call(
         functools.partial(prepare_kernel, n_x, n_y),
         out_shape=shapes,
-        in_specs=[smem] * 3 + [vmem] * 5,
+        in_specs=[pl.BlockSpec(memory_space=pltpu.SMEM)] + [vmem] * 5,
         out_specs=[vmem] * len(shapes),
         compiler_params=pltpu.CompilerParams(vmem_limit_bytes=56 * 1024 * 1024),
         cost_estimate=pl.CostEstimate(flops=2**18, bytes_accessed=5 * 2**19, transcendentals=0),
         name="prepare",
-    )(own_len, is_owner, y, rq, k, v, rk, rv)
+    )(own_len, rq, k, v, rk, rv)
     return out[0], out[1 : 1 + n_x], out[1 + n_x :]
 
 
-def plane_kernel(source_ref, x_ref, o_ref):
+def plane_kernel(owner_ref, x_ref, o_ref):
     own = 16
-    source = 2 * source_ref[0]
+    source = 2 * lax.rem(owner_ref[0], N_X * N_Y)
     parts = []
     for i in range(x_ref.shape[1] // own):
         pick = slice(i * own, (i + 1) * own)
@@ -180,11 +187,11 @@
         o_ref[z] = part
 
 
-def line_kernel(plane_ref, x_ref, o_ref):
-    o_ref[...] = x_ref[plane_ref[0], 0 : o_ref.shape[0], :]
-
-
-def choose(kernel, index, x, shape, flops):
+def line_kernel(owner_ref, x_ref, o_ref):
+    o_ref[...] = x_ref[x_ref.shape[0] - 1 - lax.div(owner_ref[0], N_X * N_Y)]
+
+
+def choose(kernel, owner, x, shape, flops):
     vmem = pl.BlockSpec(memory_space=pltpu.VMEM)
     return pl.pallas_call(
         kernel,
@@ -194,7 +201,7 @@
         compiler_params=pltpu.CompilerParams(vmem_limit_bytes=VMEM_LIMIT),
         cost_estimate=pl.CostEstimate(flops=flops, bytes_accessed=2**19, transcendentals=0),
         name="choose",
-    )(index, x)
+    )(owner, x)
 
 
 def split3(x):
@@ -210,7 +217,7 @@
     return jnp.where(row == 0, pair, jnp.where(row == 1, last, 0.0)).astype(jnp.bfloat16)
 
 
-def request_kernel(own, count, *refs):
+def request_kernel(own, count, owner_ref, *refs):
     q_refs, lines = refs[:count], refs[count : -count - 1]
     o_refs, v_ref = refs[-count - 1 : -1], refs[-1]
     piece = q_refs[0].shape[0]
@@ -220,18 +227,22 @@
     c = SCALE * LOG2E
     q = jnp.concatenate([ref[...] for ref in q_refs], axis=0)
     for i, ref in enumerate(lines):
-        for part, (top, at) in (
-            (ref[both : both + rows, :], (i * rows, rows)),
-            (ref[both + rows :, :], (len(lines) * rows + i * own, own)),
-        ):
-            hidden = part > 100.0
-            v_ref[top : top + at, :HEAD_SIZE] = jnp.where(hidden, jnp.zeros_like(part), part)
-            v_ref[top : top + at, HEAD_SIZE:] = jnp.where(hidden, jnp.zeros_like(part), jnp.ones_like(part))
+        part = ref[both : both + rows, :]
+        hidden = part > 100.0
+        top = i * rows
+        v_ref[top : top + rows, :HEAD_SIZE] = jnp.where(hidden, jnp.zeros_like(part), part)
+        v_ref[top : top + rows, HEAD_SIZE:] = jnp.where(hidden, jnp.zeros_like(part), jnp.ones_like(part))
+        top = len(lines) * rows + i * own
+        v_ref[top : top + own, :HEAD_SIZE] = ref[both + rows :, :]
+        v_ref[top : top + own, HEAD_SIZE:] = jnp.ones((own, HEAD_SIZE), jnp.bfloat16)
+    owner = owner_ref[0]
+    same = lax.div(owner, N_Y) == lax.div(place(), N_Y)
+    asked = jnp.where(same, lax.rem(lax.axis_index("y") - lax.rem(owner, N_Y) + N_Y, N_Y), -1)
     own_keys = jnp.concatenate([ref[rows:both, :] for ref in lines], axis=0)
     row = lax.rem(lax.broadcasted_iota(jnp.int32, (n, own_keys.shape[0]), 0), own)
-    col = lax.rem(lax.broadcasted_iota(jnp.int32, (n, own_keys.shape[0]), 1), own)
+    col = lax.broadcasted_iota(jnp.int32, (n, own_keys.shape[0]), 1) - asked * own
     scores = [dot_nt(q, ref[0:rows, :]) for ref in lines]
-    scores.append(jnp.where(col <= row, dot_nt(q, own_keys), -jnp.inf))
+    scores.append(jnp.where((asked >= 0) & (col >= 0) & (col <= row), dot_nt(q, own_keys), -jnp.inf))
     tiles = [s[:, i : i + HEAD_SIZE] for s in scores for i in range(0, s.shape[1], HEAD_SIZE)]
     peak = jnp.max(functools.reduce(jnp.maximum, tiles), axis=1, keepdims=True)
     weights = [jnp.exp2((tile - peak) * c).astype(jnp.bfloat16) for tile in tiles]
@@ -255,14 +266,14 @@
         )
 
 
-def request_partials(queries, lines, own):
+def request_partials(owner, queries, lines, own):
     count, piece = len(queries), queries[0].shape[0]
     keys = len(lines) * lines[0].shape[0] // 2
     vmem = pl.BlockSpec(memory_space=pltpu.VMEM)
     return pl.pallas_call(
         functools.partial(request_kernel, own, count),
         out_shape=[jax.ShapeDtypeStruct((2 * piece + 16, HEAD_SIZE), jnp.bfloat16)] * count,
-        in_specs=[vmem] * (count + len(lines)),
+        in_specs=[pl.BlockSpec(memory_space=pltpu.SMEM)] + [vmem] * (count + len(lines)),
         out_specs=[vmem] * count,
         scratch_shapes=[pltpu.VMEM((keys, 2 * HEAD_SIZE), jnp.bfloat16)],
         compiler_params=pltpu.CompilerParams(vmem_limit_bytes=VMEM_LIMIT),
@@ -270,7 +281,7 @@
             flops=3 * 10**9, bytes_accessed=2**20, transcendentals=count * piece * keys
         ),
         name="request_partials",
-    )(*queries, *lines)
+    )(owner, *queries, *lines)
 
 
 def join_kernel(parts_in, keep_code, *refs):
@@ -326,6 +337,37 @@
     )(*arrays)
 
 
+def answer_kernel(owner_ref, x_ref, _, o_ref, rows_ref, sem):
+    own = rows_ref.shape[0]
+    some = x_ref.shape[1] // own
+
+    @pl.when(place() == owner_ref[0])
+    def _():
+        for j in range(x_ref.shape[0]):
+            x, y = j // N_Y, j % N_Y
+            for i in range(some):
+                lane = (GROUP * y + some * x + i) * HEAD_SIZE
+                rows_ref[:, lane : lane + HEAD_SIZE] = x_ref[j, i * own : (i + 1) * own, :]
+        copy = pltpu.make_async_copy(rows_ref, o_ref, sem)
+        copy.start()
+        copy.wait()
+
+
+def answer_rows(owner, x, zeros):
+    any_spec = pl.BlockSpec(memory_space=pl.ANY)
+    return pl.pallas_call(
+        answer_kernel,
+        out_shape=jax.ShapeDtypeStruct(zeros.shape, zeros.dtype),
+        in_specs=[pl.BlockSpec(memory_space=pltpu.SMEM), pl.BlockSpec(memory_space=pltpu.VMEM), any_spec],
+        out_specs=any_spec,
+        input_output_aliases={2: 0},
+        scratch_shapes=[pltpu.VMEM(zeros.shape, zeros.dtype), pltpu.SemaphoreType.DMA],
+        compiler_params=pltpu.CompilerParams(vmem_limit_bytes=VMEM_LIMIT),
+        cost_estimate=pl.CostEstimate(flops=2**18, bytes_accessed=2**19, transcendentals=0),
+        name="answer_rows",
+    )(owner, x, zeros)
+
+
 def exchange(x, axis, groups=None):
     return lax.all_to_all(x, axis, split_axis=0, concat_axis=0, axis_index_groups=groups, tiled=True)
 
@@ -333,12 +375,7 @@
 def local(n_z, n_x, n_y, q, k, v, block_lengths, rq, rk, rv, query_owner):
     n_xy = n_x * n_y
     z, x, y = (lax.axis_index(name) for name in ("z", "x", "y"))
-    owner = query_owner[0]
-    owner_z, owner_xy = owner // n_xy, owner % n_xy
     own_len = block_lengths
-    mine = (z == owner_z) & (x * n_y + y == owner_xy)
-    is_owner = mine.astype(jnp.int32).reshape(1)
-    is_root = ((z == 0) & (x == 0) & (y == 0)).astype(jnp.int32).reshape(1)
     own_rows = rk.shape[0]
     down = [list(range(n_z))[::-1]]
 
@@ -348,7 +385,7 @@
     def shift_x(value, count):
         return lax.ppermute(value, "x", [(a, (a + count) % n_x) for a in range(n_x)])
 
-    sent, pieces, lines = prepare(own_len, is_owner, y.reshape(1), rq, k, v, rk, rv, n_x, n_y)
+    sent, pieces, lines = prepare(own_len, rq, k, v, rk, rv, n_x, n_y)
     moved = exchange(sent, ("x", "y", "head"))
     got = [move(pieces[i], [(0, i * n_y)]) for i in range(1, n_x)]
     lines = [lines[0]] + [
@@ -356,41 +393,40 @@
     ]
 
     piece = (2 * moved.shape[1], HEAD_SIZE)
-    moved = choose(plane_kernel, owner_xy.reshape(1), moved, (n_z,) + piece, 8 * 10**8)
     moved, got = lax.optimization_barrier((moved, got))
+    moved = choose(plane_kernel, query_owner, moved, (n_z,) + piece, 8 * 10**8)
     anchor = jnp.where(x == 0, pieces[0], got[0] + got[1] + got[2])
     got = [move(anchor, [(i * n_y, i * n_y + j) for i in range(n_x)]) for j in range(1, n_y)]
     moved = exchange(moved, "z", down)
 
-    moved = choose(line_kernel, (n_z - 1 - owner_z).reshape(1), moved, piece, 3 * 10**9)
-    moved, got, lines = lax.optimization_barrier((moved, got, lines))
+    moved = choose(line_kernel, query_owner, moved, piece, 3 * 10**9)
+    moved, lines = lax.optimization_barrier((moved, lines))
     anchor = jnp.where(y == 0, anchor, got[0] + got[1] + got[2])
     plane = range(n_xy)
-    got = [move(anchor, [(p, to * n_xy + p) for p in plane]) for to in (3, 5)]
+    got = [move(anchor, [(p, to * n_xy + p) for p in plane]) for to in (2, 6)]
     queries = [moved] + [shift_x(moved, i) for i in range(1, n_x)]
 
-    partials = request_partials(queries, lines, own_rows)
+    partials = request_partials(query_owner, queries, lines, own_rows)
     anchor = jnp.where(z == 0, anchor, got[0] + got[1])
-    steps = (((0, 1), (3, 4), (5, 6)), ((0, 7), (3, 2)))
+    steps = (((0, 1), (2, 3), (6, 5)), ((0, 7), (2, 4)))
     got = [move(anchor, [(a * n_xy + p, b * n_xy + p) for a, b in step for p in plane]) for step in steps]
     partials = [partials[0]] + [shift_x(partials[i], n_x - i) for i in range(1, n_x)]
 
     planes = join(partials, n_z, 2, True)
-    anchor = jnp.where((z == 0) | (z == 3) | (z == 5), anchor, got[0] + got[1])
+    anchor = jnp.where((z == 0) | (z == 2) | (z == 6), anchor, got[0] + got[1])
     anchors = [anchor]
     for i in range(1, n_x):
         anchors.append(shift_x(anchor, i))
     planes = exchange(planes, "z", down)
 
     answer = exchange(join([planes], n_xy, 1, False), ("x", "y"))
-    context_output = context_attention(own_len, is_root, q, k, v, anchors)
-    answer = answer.reshape(n_x, n_y, -1, own_rows, HEAD_SIZE).transpose(3, 1, 0, 2, 4).reshape(own_rows, q.shape[1])
-    request_output = jnp.where(mine, answer, jnp.zeros_like(answer))
+    context_output, zeros = context_attention(own_len, q, k, v, anchors, own_rows)
+    request_output = answer_rows(query_owner, answer, zeros)
     return context_output, request_output
 
 
 def solution(mesh):
-    n_z, n_x, n_y = 8, 4, 4
+    n_z, n_x, n_y = 8, N_X, N_Y
     grid = jax.sharding.Mesh(mesh.devices.reshape(n_z, n_x, n_y, 2), ("z", "x", "y", "head"))
     ctx = ("z", "x", "y")
     in_specs = (

time: 85 us -> 81.3 us (0.956)
  waiting for transfers between devices: 6.9 us -> 3.01 us
  starting transfers between devices: 59.9 us -> 61.7 us
  local copies, waits for them, and re-layouts: 1.12 us -> 0.03 us
    ppermute x10, starting transfers between devices: 13.7 us -> 16.8 us  [move(): return lax.ppermute(value, ('z', 'x', 'y'), pairs)]
    ppermute x10, waiting for transfers between devices: 3.97 us -> 1.35 us  [move(): return lax.ppermute(value, ('z', 'x', 'y'), pairs)]
    all_to_all x4, waiting for transfers between devices: 2.9 us -> 1.63 us  [exchange(): lax.all_to_all(x, axis, split_axis=0, concat_axis=0, axis_index_groups=gr...]
    select_n x2 -> x0, local copies, waits for them, and re-layouts: 1.09 us -> none  [local(): request_output = jnp.where(mine, answer, jnp.zeros_like(answer))]
    ppermute x3, starting transfers between devices: 4.71 us -> 3.82 us  [local(): lax.ppermute(lines[i], 'y', [(a, (a + i) % n_y) for a in range(n_y)])]
  transfers between devices with their start and end apart: 26 -> 26, of which waited for: 5 -> 3; matrix products, arithmetic and copies ran while one was open for 0% -> 0% of each run, Pallas kernels for 14% -> 14%
where the time goes in v5:
time: 81.3 us; the launch traced here: 80.7 us
  starting transfers between devices  61.7 us (76%)
  Pallas kernels  13.6 us (17%)
  waiting for transfers between devices  3.01 us (4%)
  between operations  2.21 us (3%)
    all_to_all x4, starting transfers between devices, exchange(): lax.all_to_all(x, axis, split_axis=0, concat_axis=0, axis_index_groups=gr...  27.3 us
    ppermute x10, starting transfers between devices, move(): return lax.ppermute(value, ('z', 'x', 'y'), pairs)  16.8 us
    ppermute x9, starting transfers between devices, shift_x(): lax.ppermute(value, 'x', [(a, (a + count) % n_x) for a in range(n_x)])  13.8 us
    pallas_call x1, Pallas kernels, context_attention(): pl.pallas_call(functools.partial(context_kernel, count), grid=(heads,), o...  7.47 us
    ppermute x3, starting transfers between devices, local(): lax.ppermute(lines[i], 'y', [(a, (a + i) % n_y) for a in range(n_y)])  3.82 us
    pallas_call x1, Pallas kernels, prepare(): pl.pallas_call(functools.partial(prepare_kernel, n_x, n_y), out_shape=sha...  2.36 us
    pallas_call x2, Pallas kernels, join(): pl.pallas_call(functools.partial(join_kernel, parts_in, keep_code), out_s...  2.05 us
    all_to_all x4, waiting for transfers between devices, exchange(): lax.all_to_all(x, axis, split_axis=0, concat_axis=0, axis_index_groups=gr...  1.63 us
  transfers between devices with their start and end apart: 26, of which 3 were waited for; matrix products, arithmetic and copies ran while one was open for 0% of the time, Pallas kernels for 14%

profile of v5, /device:TPU:2, one launch (start us, length us, event | category | flops | bytes accessed | tf_op | source)
XLA Modules:
  0.0 80.7 jit_solution(11211055983689776491)
XLA Ops:
  1.3 2.4 %prepare.1 = (bf16[32,32,128]{2,1,0:T(8,128)(2,1)}, bf16[64,1024]{1,0:T(8,128)(2,1)}, bf16[64,1024]{1,0:T(8,128)(2,1)}, bf16[64,1024]{1,0:T(8,128)(2,1)}, bf16[6...) custom-call(s32[1]{0:T(128)S(6)} %copy.12.len_ref, ...), custom_call_target="tpu_custom_call" | custom-call | flops 262144 | bytes 2621440 | tf_op jit(solution)/shard_map/prepare/pallas_call | solution.py:166
  3.6 7.8 %all-to-all-start = ((bf16[32,32,128]{2,1,0:T(8,128)(2,1)}), bf16[32,32,128]{2,1,0:T(8,128)(2,1)S(1)}, u32[]{:S(2)}, u32[]{:S(2)}) async-start(bf16[32,32,128]{2,1,0:T(8,128)(2,1)} %get-tuple-element.27), calls=%async_computation | async-start | bytes 524288 | tf_op jit(solution)/shard_map/all_to_all | solution.py:372
  11.4 1.3 %collective-permute-start = (bf16[64,1024]{1,0:T(8,128)(2,1)}, bf16[64,1024]{1,0:T(8,128)(2,1)S(1)}, u32[]{:S(2)}, u32[]{:S(2)}) collective-permute-start(bf16[64,1024]{1,0:T(8,128)(2,1)} %get-tuple-element.28), channel_id=1, source_target_pairs={{0,8},{1,9}} | collective-permute-start | bytes 393224 | tf_op jit(solution)/shard_map/ppermute | solution.py:383
  12.7 0.7 collective-permute-start.1
  13.4 0.7 collective-permute-start.2
  14.1 0.9 %collective-permute-start.13 = (bf16[576,128]{1,0:T(8,128)(2,1)}, bf16[576,128]{1,0:T(8,128)(2,1)S(1)}, u32[]{:S(2)}, u32[]{:S(2)}) collective-permute-start(bf16[576,128]{1,0:T(8,128)(2,1)} %get-tuple-element.37), channel_id=1, source_target_pairs={{0,2},{2,4},{4,6},{6,0},{1,3},{3,5},{5,7},{7,1},{8,10},{10,12},{12... | collective-permute-start | bytes 442376 | tf_op jit(solution)/shard_map/ppermute | solution.py:392
  15.0 2.7 %collective-permute-start.14 = (bf16[576,128]{1,0:T(8,128)(2,1)}, bf16[576,128]{1,0:T(8,128)(2,1)S(1)}, u32[]{:S(2)}, u32[]{:S(2)}) collective-permute-start(bf16[576,128]{1,0:T(8,128)(2,1)} %get-tuple-element.38), channel_id=1, source_target_pairs={{0,4},{2,6},{4,0},{6,2},{1,5},{3,7},{5,1},{7,3},{8,12},{10,14},{12... | collective-permute-start | bytes 442376 | tf_op jit(solution)/shard_map/ppermute | solution.py:392
  18.3 1.3 %collective-permute-done = bf16[64,1024]{1,0:T(8,128)(2,1)S(1)} collective-permute-done((bf16[64,1024]{1,0:T(8,128)(2,1)}, bf16[64,1024]{1,0:T(8,128)(2,1)S(1)}, u32[]{:S(2)}, u32[]{:S(2)}) %collective-permute-start) | collective-permute-done | bytes 131104 | tf_op jit(solution)/shard_map/ppermute | solution.py:383
  19.9 0.7 choose.2
  20.5 9.2 %all-to-all-start.1 = ((bf16[8,64,128]{2,1,0:T(8,128)(2,1)}), bf16[8,64,128]{2,1,0:T(8,128)(2,1)S(1)}, u32[]{:S(2)}, u32[]{:S(2)}) async-start(bf16[8,64,128]{2,1,0:T(8,128)(2,1)} %choose.2), calls=%async_computation.1 | async-start | bytes 262144 | tf_op jit(solution)/shard_map/all_to_all | solution.py:372
  29.8 2.4 %collective-permute-start.5 = (bf16[64,1024]{1,0:T(8,128)(2,1)S(1)}, bf16[64,1024]{1,0:T(8,128)(2,1)S(1)}, u32[]{:S(2)}, u32[]{:S(2)}) collective-permute-start(bf16[64,1024]{1,0:T(8,128)(2,1)S(1)} %add_select_fusion.3), channel_id=1, source_target_pairs={{0,6},{8,14},{16,22},{24,30},{1,7},{9,15},{17,23},{25,31}} | collective-permute-start | bytes 393224 | tf_op jit(solution)/shard_map/ppermute | solution.py:383
  32.2 1.3 %collective-permute-start.4 = (bf16[64,1024]{1,0:T(8,128)(2,1)S(1)}, bf16[64,1024]{1,0:T(8,128)(2,1)S(1)}, u32[]{:S(2)}, u32[]{:S(2)}) collective-permute-start(bf16[64,1024]{1,0:T(8,128)(2,1)S(1)} %add_select_fusion.3), channel_id=1, source_target_pairs={{0,4},{8,12},{16,20},{24,28},{1,5},{9,13},{17,21},{25,29}} | collective-permute-start | bytes 393224 | tf_op jit(solution)/shard_map/ppermute | solution.py:383
  33.5 1.3 %collective-permute-start.3 = (bf16[64,1024]{1,0:T(8,128)(2,1)S(1)}, bf16[64,1024]{1,0:T(8,128)(2,1)S(1)}, u32[]{:S(2)}, u32[]{:S(2)}) collective-permute-start(bf16[64,1024]{1,0:T(8,128)(2,1)S(1)} %add_select_fusion.3), channel_id=1, source_target_pairs={{0,2},{8,10},{16,18},{24,26},{1,3},{9,11},{17,19},{25,27}} | collective-permute-start | bytes 393224 | tf_op jit(solution)/shard_map/ppermute | solution.py:383
  35.4 1.0 %collective-permute-start.18 = (bf16[64,128]{1,0:T(8,128)(2,1)S(1)}, bf16[64,128]{1,0:T(8,128)(2,1)S(1)}, u32[]{:S(2)}, u32[]{:S(2)}) collective-permute-start(bf16[64,128]{1,0:T(8,128)(2,1)S(1)} %choose.3.refs_0_), channel_id=1, source_target_pairs={{0,24},{8,0},{16,8},{24,16},{1,25},{9,1},{17,9},{25,17},{2,26},{10... | collective-permute-start | bytes 49160 | tf_op jit(solution)/shard_map/ppermute | solution.py:386
  36.4 2.0 %collective-permute-start.17 = (bf16[64,128]{1,0:T(8,128)(2,1)S(1)}, bf16[64,128]{1,0:T(8,128)(2,1)S(1)}, u32[]{:S(2)}, u32[]{:S(2)}) collective-permute-start(bf16[64,128]{1,0:T(8,128)(2,1)S(1)} %choose.3.refs_0_), channel_id=1, source_target_pairs={{0,16},{8,24},{16,0},{24,8},{1,17},{9,25},{17,1},{25,9},{2,18},{10... | collective-permute-start | bytes 49160 | tf_op jit(solution)/shard_map/ppermute | solution.py:386
  38.4 1.8 %collective-permute-start.16 = (bf16[64,128]{1,0:T(8,128)(2,1)S(1)}, bf16[64,128]{1,0:T(8,128)(2,1)S(1)}, u32[]{:S(2)}, u32[]{:S(2)}) collective-permute-start(bf16[64,128]{1,0:T(8,128)(2,1)S(1)} %choose.3.refs_0_), channel_id=1, source_target_pairs={{0,8},{8,16},{16,24},{24,0},{1,9},{9,17},{17,25},{25,1},{2,10},{10... | collective-permute-start | bytes 49160 | tf_op jit(solution)/shard_map/ppermute | solution.py:386
  40.3 5.3 %collective-permute-start.7 = (bf16[64,1024]{1,0:T(8,128)(2,1)S(1)}, bf16[64,1024]{1,0:T(8,128)(2,1)S(1)}, u32[]{:S(2)}, u32[]{:S(2)}) collective-permute-start(bf16[64,1024]{1,0:T(8,128)(2,1)S(1)} %add_select_fusion.2), channel_id=1, source_target_pairs={{0,192},{2,194},{4,196},{6,198},{8,200},{10,202},{12,204},{14,206}... | collective-permute-start | bytes 393224 | tf_op jit(solution)/shard_map/ppermute | solution.py:383
  45.6 1.3 %collective-permute-start.6 = (bf16[64,1024]{1,0:T(8,128)(2,1)S(1)}, bf16[64,1024]{1,0:T(8,128)(2,1)S(1)}, u32[]{:S(2)}, u32[]{:S(2)}) collective-permute-start(bf16[64,1024]{1,0:T(8,128)(2,1)S(1)} %add_select_fusion.2), channel_id=1, source_target_pairs={{0,64},{2,66},{4,68},{6,70},{8,72},{10,74},{12,76},{14,78},{16,80}... | collective-permute-start | bytes 393224 | tf_op jit(solution)/shard_map/ppermute | solution.py:383
  46.9 1.1 %request_partials.1 = (bf16[144,128]{1,0:T(8,128)(2,1)S(1)}, bf16[144,128]{1,0:T(8,128)(2,1)S(1)}, bf16[144,128]{1,0:T(8,128)(2,1)S(1)}, bf16[144,128]{1,0:T(8,128)(2,1)S(1)}) custom-call(s32[1]{0:T(128)S(6)} %copy.13.owner_ref, bf16[64,128]{1,0:T(8,128)(2,1)S(1)} %choose.3.refs_0_, bf16[64,128]{1,0:T(8,128)(2,1)S(1)} %collective-permute-done.16.refs_1_, ...), custom_call_target="tpu_custom_call" | custom-call | flops 3000000000 | bytes 1048576 | tf_op jit(solution)/shard_map/request_partials/pallas_call | solution.py:273
  48.3 2.1 %collective-permute-start.20 = (bf16[144,128]{1,0:T(8,128)(2,1)S(1)}, bf16[144,128]{1,0:T(8,128)(2,1)S(1)}, u32[]{:S(2)}, u32[]{:S(2)}) collective-permute-start(bf16[144,128]{1,0:T(8,128)(2,1)S(1)} %get-tuple-element.47), channel_id=1, source_target_pairs={{0,16},{8,24},{16,0},{24,8},{1,17},{9,25},{17,1},{25,9},{2,18},{10... | collective-permute-start | bytes 110600 | tf_op jit(solution)/shard_map/ppermute | solution.py:386
  50.4 1.8 %collective-permute-start.21 = (bf16[144,128]{1,0:T(8,128)(2,1)S(1)}, bf16[144,128]{1,0:T(8,128)(2,1)S(1)}, u32[]{:S(2)}, u32[]{:S(2)}) collective-permute-start(bf16[144,128]{1,0:T(8,128)(2,1)S(1)} %get-tuple-element.48), channel_id=1, source_target_pairs={{0,8},{8,16},{16,24},{24,0},{1,9},{9,17},{17,25},{25,1},{2,10},{10... | collective-permute-start | bytes 110600 | tf_op jit(solution)/shard_map/ppermute | solution.py:386
  52.2 1.3 %collective-permute-start.9 = (bf16[64,1024]{1,0:T(8,128)(2,1)S(1)}, bf16[64,1024]{1,0:T(8,128)(2,1)S(1)}, u32[]{:S(2)}, u32[]{:S(2)}) collective-permute-start(bf16[64,1024]{1,0:T(8,128)(2,1)S(1)} %add_select_fusion.1), channel_id=1, source_target_pairs={{0,224},{2,226},{4,228},{6,230},{8,232},{10,234},{12,236},{14,238}... | collective-permute-start | bytes 393224 | tf_op jit(solution)/shard_map/ppermute | solution.py:383
  53.5 1.3 %collective-permute-start.8 = (bf16[64,1024]{1,0:T(8,128)(2,1)S(1)}, bf16[64,1024]{1,0:T(8,128)(2,1)S(1)}, u32[]{:S(2)}, u32[]{:S(2)}) collective-permute-start(bf16[64,1024]{1,0:T(8,128)(2,1)S(1)} %add_select_fusion.1), channel_id=1, source_target_pairs={{0,32},{2,34},{4,36},{6,38},{8,40},{10,42},{12,44},{14,46},{16,48}... | collective-permute-start | bytes 393224 | tf_op jit(solution)/shard_map/ppermute | solution.py:383
  54.9 1.0 %join_pieces.2 = bf16[8,80,128]{2,1,0:T(8,128)(2,1)} custom-call(bf16[144,128]{1,0:T(8,128)(2,1)S(1)} %get-tuple-element.45.refs_0_, bf16[144,128]{1,0:T(8,128)(2,1)S(1)} %collective-permute-done.19.refs_1_, bf16[144,128]{1,0:T(8,128)(2,1)S(1)} %collective-permute-done.20.refs_2_, bf16[144,128]{1,0:T(8,128)(2,1)S(1)} %collective-permute-done.21.refs_3_), custom_call_target="tpu_custom_call" | custom-call | flops 3000000000 | bytes 524288 | tf_op jit(solution)/shard_map/join_pieces/pallas_call | solution.py:331
  55.8 4.5 %all-to-all-start.2 = ((bf16[8,80,128]{2,1,0:T(8,128)(2,1)}), bf16[8,80,128]{2,1,0:T(8,128)(2,1)S(1)}, u32[]{:S(2)}, u32[]{:S(2)}) async-start(bf16[8,80,128]{2,1,0:T(8,128)(2,1)} %join_pieces.2), calls=%async_computation.2 | async-start | bytes 327680 | tf_op jit(solution)/shard_map/all_to_all | solution.py:372
  60.4 2.6 %collective-permute-start.12 = (bf16[64,1024]{1,0:T(8,128)(2,1)S(1)}, bf16[64,1024]{1,0:T(8,128)(2,1)S(1)}, u32[]{:S(2)}, u32[]{:S(2)}) collective-permute-start(bf16[64,1024]{1,0:T(8,128)(2,1)S(1)} %add_select_fusion.refs_0_.refs_4_), channel_id=1, source_target_pairs={{0,24},{8,0},{16,8},{24,16},{1,25},{9,1},{17,9},{25,17},{2,26},{10... | collective-permute-start | bytes 393224 | tf_op jit(solution)/shard_map/ppermute | solution.py:386
  63.0 0.6 collective-permute-start.11
  63.6 1.6 %collective-permute-start.10 = (bf16[64,1024]{1,0:T(8,128)(2,1)S(1)}, bf16[64,1024]{1,0:T(8,128)(2,1)S(1)}, u32[]{:S(2)}, u32[]{:S(2)}) collective-permute-start(bf16[64,1024]{1,0:T(8,128)(2,1)S(1)} %add_select_fusion.refs_0_.refs_4_), channel_id=1, source_target_pairs={{0,8},{8,16},{16,24},{24,0},{1,9},{9,17},{17,25},{25,1},{2,10},{10... | collective-permute-start | bytes 393224 | tf_op jit(solution)/shard_map/ppermute | solution.py:386
  65.2 1.0 %all-to-all-done.2.refs_0_ = bf16[8,80,128]{2,1,0:T(8,128)(2,1)S(1)} async-done(((bf16[8,80,128]{2,1,0:T(8,128)(2,1)}), bf16[8,80,128]{2,1,0:T(8,128)(2,1)S(1)}, u32[]{:S(2)}, u32[]{:S(2)}) %all-to-all-start.2) | async-done | bytes 163872 | tf_op jit(solution)/shard_map/all_to_all | solution.py:372
  66.2 1.1 %join_pieces.3 = bf16[16,64,128]{2,1,0:T(8,128)(2,1)} custom-call(bf16[8,80,128]{2,1,0:T(8,128)(2,1)S(1)} %all-to-all-done.2.refs_0_), custom_call_target="tpu_custom_call" | custom-call | flops 3000000000 | bytes 524288 | tf_op jit(solution)/shard_map/join_pieces/pallas_call | solution.py:331
  67.3 5.8 %all-to-all-start.3 = ((bf16[16,64,128]{2,1,0:T(8,128)(2,1)}), bf16[16,64,128]{2,1,0:T(8,128)(2,1)S(1)}, u32[]{:S(2)}, u32[]{:S(2)}) async-start(bf16[16,64,128]{2,1,0:T(8,128)(2,1)} %join_pieces.3), calls=%async_computation.3 | async-start | bytes 524288 | tf_op jit(solution)/shard_map/all_to_all | solution.py:372
  73.2 7.5 %context_attention.1 = (bf16[256,4096]{1,0:T(8,128)(2,1)}, bf16[32,4096]{1,0:T(8,128)(2,1)}) custom-call(s32[1]{0:T(128)S(6)} %copy.12.len_ref, bf16[256,4096]{1,0:T(8,128)(2,1)S(1)} %copy-done.2, bf16[256,512]{1,0:T(8,128)(2,1)S(1)} %copy-done, bf16[256,512]{1,0:T(8,128)(2,1)S(1)} %copy-done.1, bf16[64,1024]{1,0:T(8,128)(2,1)S(1)} %add_select_fusion.refs_0_.refs_4_, ...), custom_call_target="tpu_custom_call" | custom-call | flops 2147483648 | bytes 5242880 | tf_op jit(solution)/shard_map/context_attention/pallas_call | solution.py:100
  (42 shorter events, 1.3 us)
Async XLA Ops:
  3.6 26.1 %copy-start.4 = (bf16[64,1024]{1,0:T(8,128)(2,1)S(1)}, bf16[64,1024]{1,0:T(8,128)(2,1)}, u32[]{:S(2)}) copy-start(bf16[64,1024]{1,0:T(8,128)(2,1)} %get-tuple-element.26) | copy-start | bytes 393220
  3.6 16.2 %all-to-all-start = ((bf16[32,32,128]{2,1,0:T(8,128)(2,1)}), bf16[32,32,128]{2,1,0:T(8,128)(2,1)S(1)}, u32[]{:S(2)}, u32[]{:S(2)}) async-start(bf16[32,32,128]{2,1,0:T(8,128)(2,1)} %get-tuple-element.27), calls=%async_computation | async-start | bytes 524288 | tf_op jit(solution)/shard_map/all_to_all | solution.py:372
  11.4 8.2 %collective-permute-start = (bf16[64,1024]{1,0:T(8,128)(2,1)}, bf16[64,1024]{1,0:T(8,128)(2,1)S(1)}, u32[]{:S(2)}, u32[]{:S(2)}) collective-permute-start(bf16[64,1024]{1,0:T(8,128)(2,1)} %get-tuple-element.28), channel_id=1, source_target_pairs={{0,8},{1,9}} | collective-permute-start | bytes 393224 | tf_op jit(solution)/shard_map/ppermute | solution.py:383
  12.7 7.2 %collective-permute-start.1 = (bf16[64,1024]{1,0:T(8,128)(2,1)}, bf16[64,1024]{1,0:T(8,128)(2,1)S(1)}, u32[]{:S(2)}, u32[]{:S(2)}) collective-permute-start(bf16[64,1024]{1,0:T(8,128)(2,1)} %get-tuple-element.29), channel_id=1, source_target_pairs={{0,16},{1,17}} | collective-permute-start | bytes 393224 | tf_op jit(solution)/shard_map/ppermute | solution.py:383
  13.4 6.5 %collective-permute-start.2 = (bf16[64,1024]{1,0:T(8,128)(2,1)}, bf16[64,1024]{1,0:T(8,128)(2,1)S(1)}, u32[]{:S(2)}, u32[]{:S(2)}) collective-permute-start(bf16[64,1024]{1,0:T(8,128)(2,1)} %get-tuple-element.30), channel_id=1, source_target_pairs={{0,24},{1,25}} | collective-permute-start | bytes 393224 | tf_op jit(solution)/shard_map/ppermute | solution.py:383
  14.1 19.4 %collective-permute-start.13 = (bf16[576,128]{1,0:T(8,128)(2,1)}, bf16[576,128]{1,0:T(8,128)(2,1)S(1)}, u32[]{:S(2)}, u32[]{:S(2)}) collective-permute-start(bf16[576,128]{1,0:T(8,128)(2,1)} %get-tuple-element.37), channel_id=1, source_target_pairs={{0,2},{2,4},{4,6},{6,0},{1,3},{3,5},{5,7},{7,1},{8,10},{10,12},{12... | collective-permute-start | bytes 442376 | tf_op jit(solution)/shard_map/ppermute | solution.py:392
  15.0 20.4 %collective-permute-start.14 = (bf16[576,128]{1,0:T(8,128)(2,1)}, bf16[576,128]{1,0:T(8,128)(2,1)S(1)}, u32[]{:S(2)}, u32[]{:S(2)}) collective-permute-start(bf16[576,128]{1,0:T(8,128)(2,1)} %get-tuple-element.38), channel_id=1, source_target_pairs={{0,4},{2,6},{4,0},{6,2},{1,5},{3,7},{5,1},{7,3},{8,12},{10,14},{12... | collective-permute-start | bytes 442376 | tf_op jit(solution)/shard_map/ppermute | solution.py:392
  19.6 15.8 %collective-permute-start.15 = (bf16[576,128]{1,0:T(8,128)(2,1)}, bf16[576,128]{1,0:T(8,128)(2,1)S(1)}, u32[]{:S(2)}, u32[]{:S(2)}) collective-permute-start(bf16[576,128]{1,0:T(8,128)(2,1)} %get-tuple-element.39), channel_id=1, source_target_pairs={{0,6},{2,0},{4,2},{6,4},{1,7},{3,1},{5,3},{7,5},{8,14},{10,8},{12,... | collective-permute-start | bytes 442376 | tf_op jit(solution)/shard_map/ppermute | solution.py:392
  20.5 14.8 %all-to-all-start.1 = ((bf16[8,64,128]{2,1,0:T(8,128)(2,1)}), bf16[8,64,128]{2,1,0:T(8,128)(2,1)S(1)}, u32[]{:S(2)}, u32[]{:S(2)}) async-start(bf16[8,64,128]{2,1,0:T(8,128)(2,1)} %choose.2), calls=%async_computation.1 | async-start | bytes 262144 | tf_op jit(solution)/shard_map/all_to_all | solution.py:372
  29.7 17.2 %copy-start.3 = (bf16[576,128]{1,0:T(8,128)(2,1)S(1)}, bf16[576,128]{1,0:T(8,128)(2,1)}, u32[]{:S(2)}) copy-start(bf16[576,128]{1,0:T(8,128)(2,1)} %get-tuple-element.41.refs_4_) | copy-start | bytes 442372
  29.8 8.7 %collective-permute-start.5 = (bf16[64,1024]{1,0:T(8,128)(2,1)S(1)}, bf16[64,1024]{1,0:T(8,128)(2,1)S(1)}, u32[]{:S(2)}, u32[]{:S(2)}) collective-permute-start(bf16[64,1024]{1,0:T(8,128)(2,1)S(1)} %add_select_fusion.3), channel_id=1, source_target_pairs={{0,6},{8,14},{16,22},{24,30},{1,7},{9,15},{17,23},{25,31}} | collective-permute-start | bytes 393224 | tf_op jit(solution)/shard_map/ppermute | solution.py:383
  32.2 8.1 %collective-permute-start.4 = (bf16[64,1024]{1,0:T(8,128)(2,1)S(1)}, bf16[64,1024]{1,0:T(8,128)(2,1)S(1)}, u32[]{:S(2)}, u32[]{:S(2)}) collective-permute-start(bf16[64,1024]{1,0:T(8,128)(2,1)S(1)} %add_select_fusion.3), channel_id=1, source_target_pairs={{0,4},{8,12},{16,20},{24,28},{1,5},{9,13},{17,21},{25,29}} | collective-permute-start | bytes 393224 | tf_op jit(solution)/shard_map/ppermute | solution.py:383
  33.5 6.8 %collective-permute-start.3 = (bf16[64,1024]{1,0:T(8,128)(2,1)S(1)}, bf16[64,1024]{1,0:T(8,128)(2,1)S(1)}, u32[]{:S(2)}, u32[]{:S(2)}) collective-permute-start(bf16[64,1024]{1,0:T(8,128)(2,1)S(1)} %add_select_fusion.3), channel_id=1, source_target_pairs={{0,2},{8,10},{16,18},{24,26},{1,3},{9,11},{17,19},{25,27}} | collective-permute-start | bytes 393224 | tf_op jit(solution)/shard_map/ppermute | solution.py:383
  35.4 11.5 %collective-permute-start.18 = (bf16[64,128]{1,0:T(8,128)(2,1)S(1)}, bf16[64,128]{1,0:T(8,128)(2,1)S(1)}, u32[]{:S(2)}, u32[]{:S(2)}) collective-permute-start(bf16[64,128]{1,0:T(8,128)(2,1)S(1)} %choose.3.refs_0_), channel_id=1, source_target_pairs={{0,24},{8,0},{16,8},{24,16},{1,25},{9,1},{17,9},{25,17},{2,26},{10... | collective-permute-start | bytes 49160 | tf_op jit(solution)/shard_map/ppermute | solution.py:386
  36.4 10.5 %collective-permute-start.17 = (bf16[64,128]{1,0:T(8,128)(2,1)S(1)}, bf16[64,128]{1,0:T(8,128)(2,1)S(1)}, u32[]{:S(2)}, u32[]{:S(2)}) collective-permute-start(bf16[64,128]{1,0:T(8,128)(2,1)S(1)} %choose.3.refs_0_), channel_id=1, source_target_pairs={{0,16},{8,24},{16,0},{24,8},{1,17},{9,25},{17,1},{25,9},{2,18},{10... | collective-permute-start | bytes 49160 | tf_op jit(solution)/shard_map/ppermute | solution.py:386
  38.4 8.5 %collective-permute-start.16 = (bf16[64,128]{1,0:T(8,128)(2,1)S(1)}, bf16[64,128]{1,0:T(8,128)(2,1)S(1)}, u32[]{:S(2)}, u32[]{:S(2)}) collective-permute-start(bf16[64,128]{1,0:T(8,128)(2,1)S(1)} %choose.3.refs_0_), channel_id=1, source_target_pairs={{0,8},{8,16},{16,24},{24,0},{1,9},{9,17},{17,25},{25,1},{2,10},{10... | collective-permute-start | bytes 49160 | tf_op jit(solution)/shard_map/ppermute | solution.py:386
  40.3 11.9 %collective-permute-start.7 = (bf16[64,1024]{1,0:T(8,128)(2,1)S(1)}, bf16[64,1024]{1,0:T(8,128)(2,1)S(1)}, u32[]{:S(2)}, u32[]{:S(2)}) collective-permute-start(bf16[64,1024]{1,0:T(8,128)(2,1)S(1)} %add_select_fusion.2), channel_id=1, source_target_pairs={{0,192},{2,194},{4,196},{6,198},{8,200},{10,202},{12,204},{14,206}... | collective-permute-start | bytes 393224 | tf_op jit(solution)/shard_map/ppermute | solution.py:383
  45.6 6.6 %collective-permute-start.6 = (bf16[64,1024]{1,0:T(8,128)(2,1)S(1)}, bf16[64,1024]{1,0:T(8,128)(2,1)S(1)}, u32[]{:S(2)}, u32[]{:S(2)}) collective-permute-start(bf16[64,1024]{1,0:T(8,128)(2,1)S(1)} %add_select_fusion.2), channel_id=1, source_target_pairs={{0,64},{2,66},{4,68},{6,70},{8,72},{10,74},{12,76},{14,78},{16,80}... | collective-permute-start | bytes 393224 | tf_op jit(solution)/shard_map/ppermute | solution.py:383
  48.0 6.8 %collective-permute-start.19 = (bf16[144,128]{1,0:T(8,128)(2,1)S(1)}, bf16[144,128]{1,0:T(8,128)(2,1)S(1)}, u32[]{:S(2)}, u32[]{:S(2)}) collective-permute-start(bf16[144,128]{1,0:T(8,128)(2,1)S(1)} %get-tuple-element.46), channel_id=1, source_target_pairs={{0,24},{8,0},{16,8},{24,16},{1,25},{9,1},{17,9},{25,17},{2,26},{10... | collective-permute-start | bytes 110600 | tf_op jit(solution)/shard_map/ppermute | solution.py:386
  48.3 6.6 %collective-permute-start.20 = (bf16[144,128]{1,0:T(8,128)(2,1)S(1)}, bf16[144,128]{1,0:T(8,128)(2,1)S(1)}, u32[]{:S(2)}, u32[]{:S(2)}) collective-permute-start(bf16[144,128]{1,0:T(8,128)(2,1)S(1)} %get-tuple-element.47), channel_id=1, source_target_pairs={{0,16},{8,24},{16,0},{24,8},{1,17},{9,25},{17,1},{25,9},{2,18},{10... | collective-permute-start | bytes 110600 | tf_op jit(solution)/shard_map/ppermute | solution.py:386
  50.4 4.5 %collective-permute-start.21 = (bf16[144,128]{1,0:T(8,128)(2,1)S(1)}, bf16[144,128]{1,0:T(8,128)(2,1)S(1)}, u32[]{:S(2)}, u32[]{:S(2)}) collective-permute-start(bf16[144,128]{1,0:T(8,128)(2,1)S(1)} %get-tuple-element.48), channel_id=1, source_target_pairs={{0,8},{8,16},{16,24},{24,0},{1,9},{9,17},{17,25},{25,1},{2,10},{10... | collective-permute-start | bytes 110600 | tf_op jit(solution)/shard_map/ppermute | solution.py:386
  52.2 8.1 %collective-permute-start.9 = (bf16[64,1024]{1,0:T(8,128)(2,1)S(1)}, bf16[64,1024]{1,0:T(8,128)(2,1)S(1)}, u32[]{:S(2)}, u32[]{:S(2)}) collective-permute-start(bf16[64,1024]{1,0:T(8,128)(2,1)S(1)} %add_select_fusion.1), channel_id=1, source_target_pairs={{0,224},{2,226},{4,228},{6,230},{8,232},{10,234},{12,236},{14,238}... | collective-permute-start | bytes 393224 | tf_op jit(solution)/shard_map/ppermute | solution.py:383
  53.5 6.8 %collective-permute-start.8 = (bf16[64,1024]{1,0:T(8,128)(2,1)S(1)}, bf16[64,1024]{1,0:T(8,128)(2,1)S(1)}, u32[]{:S(2)}, u32[]{:S(2)}) collective-permute-start(bf16[64,1024]{1,0:T(8,128)(2,1)S(1)} %add_select_fusion.1), channel_id=1, source_target_pairs={{0,32},{2,34},{4,36},{6,38},{8,40},{10,42},{12,44},{14,46},{16,48}... | collective-permute-start | bytes 393224 | tf_op jit(solution)/shard_map/ppermute | solution.py:383
  55.8 10.4 %all-to-all-start.2 = ((bf16[8,80,128]{2,1,0:T(8,128)(2,1)}), bf16[8,80,128]{2,1,0:T(8,128)(2,1)S(1)}, u32[]{:S(2)}, u32[]{:S(2)}) async-start(bf16[8,80,128]{2,1,0:T(8,128)(2,1)} %join_pieces.2), calls=%async_computation.2 | async-start | bytes 327680 | tf_op jit(solution)/shard_map/all_to_all | solution.py:372
  60.4 12.8 %copy-start = (bf16[256,512]{1,0:T(8,128)(2,1)S(1)}, bf16[256,512]{1,0:T(8,128)(2,1)}, u32[]{:S(2)}) copy-start(bf16[256,512]{1,0:T(8,128)(2,1)} %k_ref.3) | copy-start | bytes 786436
  60.4 12.8 %copy-start.1 = (bf16[256,512]{1,0:T(8,128)(2,1)S(1)}, bf16[256,512]{1,0:T(8,128)(2,1)}, u32[]{:S(2)}) copy-start(bf16[256,512]{1,0:T(8,128)(2,1)} %v_ref.3) | copy-start | bytes 786436
  60.4 12.8 %copy-start.2 = (bf16[256,4096]{1,0:T(8,128)(2,1)S(1)}, bf16[256,4096]{1,0:T(8,128)(2,1)}, u32[]{:S(2)}) copy-start(bf16[256,4096]{1,0:T(8,128)(2,1)} %q_ref.1) | copy-start | bytes 6291460
  60.4 12.7 %collective-permute-start.12 = (bf16[64,1024]{1,0:T(8,128)(2,1)S(1)}, bf16[64,1024]{1,0:T(8,128)(2,1)S(1)}, u32[]{:S(2)}, u32[]{:S(2)}) collective-permute-start(bf16[64,1024]{1,0:T(8,128)(2,1)S(1)} %add_select_fusion.refs_0_.refs_4_), channel_id=1, source_target_pairs={{0,24},{8,0},{16,8},{24,16},{1,25},{9,1},{17,9},{25,17},{2,26},{10... | collective-permute-start | bytes 393224 | tf_op jit(solution)/shard_map/ppermute | solution.py:386
  63.0 10.1 %collective-permute-start.11 = (bf16[64,1024]{1,0:T(8,128)(2,1)S(1)}, bf16[64,1024]{1,0:T(8,128)(2,1)S(1)}, u32[]{:S(2)}, u32[]{:S(2)}) collective-permute-start(bf16[64,1024]{1,0:T(8,128)(2,1)S(1)} %add_select_fusion.refs_0_.refs_4_), channel_id=1, source_target_pairs={{0,16},{8,24},{16,0},{24,8},{1,17},{9,25},{17,1},{25,9},{2,18},{10... | collective-permute-start | bytes 393224 | tf_op jit(solution)/shard_map/ppermute | solution.py:386
  63.6 9.5 %collective-permute-start.10 = (bf16[64,1024]{1,0:T(8,128)(2,1)S(1)}, bf16[64,1024]{1,0:T(8,128)(2,1)S(1)}, u32[]{:S(2)}, u32[]{:S(2)}) collective-permute-start(bf16[64,1024]{1,0:T(8,128)(2,1)S(1)} %add_select_fusion.refs_0_.refs_4_), channel_id=1, source_target_pairs={{0,8},{8,16},{16,24},{24,0},{1,9},{9,17},{17,25},{25,1},{2,10},{10... | collective-permute-start | bytes 393224 | tf_op jit(solution)/shard_map/ppermute | solution.py:386
  67.3 13.4 %all-to-all-start.3 = ((bf16[16,64,128]{2,1,0:T(8,128)(2,1)}), bf16[16,64,128]{2,1,0:T(8,128)(2,1)S(1)}, u32[]{:S(2)}, u32[]{:S(2)}) async-start(bf16[16,64,128]{2,1,0:T(8,128)(2,1)} %join_pieces.3), calls=%async_computation.3 | async-start | bytes 524288 | tf_op jit(solution)/shard_map/all_to_all | solution.py:372

commit v6 on v5

--- a/solution.py
+++ b/solution.py
@@ -14,7 +14,7 @@
 LN2 = 0.6931471805599453
 MARK = 1024.0
 VMEM_LIMIT = 32 * 1024 * 1024
-STACK = 8
+STACK = 4
 N_X, N_Y = 4, 4
 
 
@@ -396,18 +396,19 @@
     moved, got = lax.optimization_barrier((moved, got))
     moved = choose(plane_kernel, query_owner, moved, (n_z,) + piece, 8 * 10**8)
     anchor = jnp.where(x == 0, pieces[0], got[0] + got[1] + got[2])
-    got = [move(anchor, [(i * n_y, i * n_y + j) for i in range(n_x)]) for j in range(1, n_y)]
+    got = [move(anchor, [(i * n_y, (to * n_x + i) * n_y) for i in range(n_x)]) for to in (2, 6)]
     moved = exchange(moved, "z", down)
 
     moved = choose(line_kernel, query_owner, moved, piece, 3 * 10**9)
     moved, lines = lax.optimization_barrier((moved, lines))
+    anchor = jnp.where(z == 0, anchor, got[0] + got[1])
+    rows = [(to * n_x + i) * n_y for to in (0, 2, 6) for i in range(n_x)]
+    got = [move(anchor, [(p, p + j) for p in rows]) for j in range(1, n_y)]
+    queries = [moved] + [shift_x(moved, i) for i in range(1, n_x)]
+
+    partials = request_partials(query_owner, queries, lines, own_rows)
     anchor = jnp.where(y == 0, anchor, got[0] + got[1] + got[2])
     plane = range(n_xy)
-    got = [move(anchor, [(p, to * n_xy + p) for p in plane]) for to in (2, 6)]
-    queries = [moved] + [shift_x(moved, i) for i in range(1, n_x)]
-
-    partials = request_partials(query_owner, queries, lines, own_rows)
-    anchor = jnp.where(z == 0, anchor, got[0] + got[1])
     steps = (((0, 1), (2, 3), (6, 5)), ((0, 7), (2, 4)))
     got = [move(anchor, [(a * n_xy + p, b * n_xy + p) for a, b in step for p in plane]) for step in steps]
     partials = [partials[0]] + [shift_x(partials[i], n_x - i) for i in range(1, n_x)]

time: 81.3 us -> 81 us (level)
  no operation moved by 1% of the time
where the time goes in v6:
time: 81 us; the launch traced here: 80.2 us
  starting transfers between devices  61.3 us (76%)
  Pallas kernels  13.3 us (16%)
  waiting for transfers between devices  3.28 us (4%)
  between operations  2.21 us (3%)
    all_to_all x4, starting transfers between devices, exchange(): lax.all_to_all(x, axis, split_axis=0, concat_axis=0, axis_index_groups=gr...  27.3 us
    ppermute x10, starting transfers between devices, move(): return lax.ppermute(value, ('z', 'x', 'y'), pairs)  16.2 us
    ppermute x9, starting transfers between devices, shift_x(): lax.ppermute(value, 'x', [(a, (a + count) % n_x) for a in range(n_x)])  14 us
    pallas_call x1, Pallas kernels, context_attention(): pl.pallas_call(functools.partial(context_kernel, count), grid=(heads,), o...  7.12 us
    ppermute x3, starting transfers between devices, local(): lax.ppermute(lines[i], 'y', [(a, (a + i) % n_y) for a in range(n_y)])  3.82 us
    pallas_call x1, Pallas kernels, prepare(): pl.pallas_call(functools.partial(prepare_kernel, n_x, n_y), out_shape=sha...  2.36 us
    pallas_call x2, Pallas kernels, join(): pl.pallas_call(functools.partial(join_kernel, parts_in, keep_code), out_s...  2.05 us
    all_to_all x4, waiting for transfers between devices, exchange(): lax.all_to_all(x, axis, split_axis=0, concat_axis=0, axis_index_groups=gr...  1.9 us
  transfers between devices with their start and end apart: 26, of which 3 were waited for; matrix products, arithmetic and copies ran while one was open for 0% of the time, Pallas kernels for 14%

profile of v6, /device:TPU:2, one launch (start us, length us, event | category | flops | bytes accessed | tf_op | source)
XLA Modules:
  0.0 80.2 jit_solution(2320160338526204925)
XLA Ops:
  1.3 2.4 %prepare.1 = (bf16[32,32,128]{2,1,0:T(8,128)(2,1)}, bf16[64,1024]{1,0:T(8,128)(2,1)}, bf16[64,1024]{1,0:T(8,128)(2,1)}, bf16[64,1024]{1,0:T(8,128)(2,1)}, bf16[6...) custom-call(s32[1]{0:T(128)S(6)} %copy.12.len_ref, ...), custom_call_target="tpu_custom_call" | custom-call | flops 262144 | bytes 2621440 | tf_op jit(solution)/shard_map/prepare/pallas_call | solution.py:166
  3.6 7.8 %all-to-all-start = ((bf16[32,32,128]{2,1,0:T(8,128)(2,1)}), bf16[32,32,128]{2,1,0:T(8,128)(2,1)S(1)}, u32[]{:S(2)}, u32[]{:S(2)}) async-start(bf16[32,32,128]{2,1,0:T(8,128)(2,1)} %get-tuple-element.27), calls=%async_computation | async-start | bytes 524288 | tf_op jit(solution)/shard_map/all_to_all | solution.py:372
  11.4 1.3 %collective-permute-start = (bf16[64,1024]{1,0:T(8,128)(2,1)}, bf16[64,1024]{1,0:T(8,128)(2,1)S(1)}, u32[]{:S(2)}, u32[]{:S(2)}) collective-permute-start(bf16[64,1024]{1,0:T(8,128)(2,1)} %get-tuple-element.28), channel_id=1, source_target_pairs={{0,8},{1,9}} | collective-permute-start | bytes 393224 | tf_op jit(solution)/shard_map/ppermute | solution.py:383
  12.7 0.7 collective-permute-start.1
  13.4 0.7 collective-permute-start.2
  14.1 0.9 %collective-permute-start.13 = (bf16[576,128]{1,0:T(8,128)(2,1)}, bf16[576,128]{1,0:T(8,128)(2,1)S(1)}, u32[]{:S(2)}, u32[]{:S(2)}) collective-permute-start(bf16[576,128]{1,0:T(8,128)(2,1)} %get-tuple-element.37), channel_id=1, source_target_pairs={{0,2},{2,4},{4,6},{6,0},{1,3},{3,5},{5,7},{7,1},{8,10},{10,12},{12... | collective-permute-start | bytes 442376 | tf_op jit(solution)/shard_map/ppermute | solution.py:392
  15.0 2.7 %collective-permute-start.14 = (bf16[576,128]{1,0:T(8,128)(2,1)}, bf16[576,128]{1,0:T(8,128)(2,1)S(1)}, u32[]{:S(2)}, u32[]{:S(2)}) collective-permute-start(bf16[576,128]{1,0:T(8,128)(2,1)} %get-tuple-element.38), channel_id=1, source_target_pairs={{0,4},{2,6},{4,0},{6,2},{1,5},{3,7},{5,1},{7,3},{8,12},{10,14},{12... | collective-permute-start | bytes 442376 | tf_op jit(solution)/shard_map/ppermute | solution.py:392
  18.3 1.3 %collective-permute-done = bf16[64,1024]{1,0:T(8,128)(2,1)S(1)} collective-permute-done((bf16[64,1024]{1,0:T(8,128)(2,1)}, bf16[64,1024]{1,0:T(8,128)(2,1)S(1)}, u32[]{:S(2)}, u32[]{:S(2)}) %collective-permute-start) | collective-permute-done | bytes 131104 | tf_op jit(solution)/shard_map/ppermute | solution.py:383
  19.9 0.7 choose.2
  20.5 9.2 %all-to-all-start.1 = ((bf16[8,64,128]{2,1,0:T(8,128)(2,1)}), bf16[8,64,128]{2,1,0:T(8,128)(2,1)S(1)}, u32[]{:S(2)}, u32[]{:S(2)}) async-start(bf16[8,64,128]{2,1,0:T(8,128)(2,1)} %choose.2), calls=%async_computation.1 | async-start | bytes 262144 | tf_op jit(solution)/shard_map/all_to_all | solution.py:372
  29.8 3.5 %collective-permute-start.4 = (bf16[64,1024]{1,0:T(8,128)(2,1)S(1)}, bf16[64,1024]{1,0:T(8,128)(2,1)S(1)}, u32[]{:S(2)}, u32[]{:S(2)}) collective-permute-start(bf16[64,1024]{1,0:T(8,128)(2,1)S(1)} %add_select_fusion.3), channel_id=1, source_target_pairs={{0,192},{8,200},{16,208},{24,216},{1,193},{9,201},{17,209},{25,217}} | collective-permute-start | bytes 393224 | tf_op jit(solution)/shard_map/ppermute | solution.py:383
  33.2 1.6 %collective-permute-start.3 = (bf16[64,1024]{1,0:T(8,128)(2,1)S(1)}, bf16[64,1024]{1,0:T(8,128)(2,1)S(1)}, u32[]{:S(2)}, u32[]{:S(2)}) collective-permute-start(bf16[64,1024]{1,0:T(8,128)(2,1)S(1)} %add_select_fusion.3), channel_id=1, source_target_pairs={{0,64},{8,72},{16,80},{24,88},{1,65},{9,73},{17,81},{25,89}} | collective-permute-start | bytes 393224 | tf_op jit(solution)/shard_map/ppermute | solution.py:383
  35.4 0.9 %collective-permute-start.18 = (bf16[64,128]{1,0:T(8,128)(2,1)S(1)}, bf16[64,128]{1,0:T(8,128)(2,1)S(1)}, u32[]{:S(2)}, u32[]{:S(2)}) collective-permute-start(bf16[64,128]{1,0:T(8,128)(2,1)S(1)} %choose.3.refs_0_), channel_id=1, source_target_pairs={{0,24},{8,0},{16,8},{24,16},{1,25},{9,1},{17,9},{25,17},{2,26},{10... | collective-permute-start | bytes 49160 | tf_op jit(solution)/shard_map/ppermute | solution.py:386
  36.3 2.2 %collective-permute-start.17 = (bf16[64,128]{1,0:T(8,128)(2,1)S(1)}, bf16[64,128]{1,0:T(8,128)(2,1)S(1)}, u32[]{:S(2)}, u32[]{:S(2)}) collective-permute-start(bf16[64,128]{1,0:T(8,128)(2,1)S(1)} %choose.3.refs_0_), channel_id=1, source_target_pairs={{0,16},{8,24},{16,0},{24,8},{1,17},{9,25},{17,1},{25,9},{2,18},{10... | collective-permute-start | bytes 49160 | tf_op jit(solution)/shard_map/ppermute | solution.py:386
  38.4 1.8 %collective-permute-start.16 = (bf16[64,128]{1,0:T(8,128)(2,1)S(1)}, bf16[64,128]{1,0:T(8,128)(2,1)S(1)}, u32[]{:S(2)}, u32[]{:S(2)}) collective-permute-start(bf16[64,128]{1,0:T(8,128)(2,1)S(1)} %choose.3.refs_0_), channel_id=1, source_target_pairs={{0,8},{8,16},{16,24},{24,0},{1,9},{9,17},{17,25},{25,1},{2,10},{10... | collective-permute-start | bytes 49160 | tf_op jit(solution)/shard_map/ppermute | solution.py:386
  40.3 1.9 %collective-permute-start.7 = (bf16[64,1024]{1,0:T(8,128)(2,1)S(1)}, bf16[64,1024]{1,0:T(8,128)(2,1)S(1)}, u32[]{:S(2)}, u32[]{:S(2)}) collective-permute-start(bf16[64,1024]{1,0:T(8,128)(2,1)S(1)} %add_select_fusion.2), channel_id=1, source_target_pairs={{0,6},{8,14},{16,22},{24,30},{64,70},{72,78},{80,86},{88,94},{192,... | collective-permute-start | bytes 393224 | tf_op jit(solution)/shard_map/ppermute | solution.py:383
  42.2 1.3 %collective-permute-start.6 = (bf16[64,1024]{1,0:T(8,128)(2,1)S(1)}, bf16[64,1024]{1,0:T(8,128)(2,1)S(1)}, u32[]{:S(2)}, u32[]{:S(2)}) collective-permute-start(bf16[64,1024]{1,0:T(8,128)(2,1)S(1)} %add_select_fusion.2), channel_id=1, source_target_pairs={{0,4},{8,12},{16,20},{24,28},{64,68},{72,76},{80,84},{88,92},{192,... | collective-permute-start | bytes 393224 | tf_op jit(solution)/shard_map/ppermute | solution.py:383
  43.6 1.3 %collective-permute-start.5 = (bf16[64,1024]{1,0:T(8,128)(2,1)S(1)}, bf16[64,1024]{1,0:T(8,128)(2,1)S(1)}, u32[]{:S(2)}, u32[]{:S(2)}) collective-permute-start(bf16[64,1024]{1,0:T(8,128)(2,1)S(1)} %add_select_fusion.2), channel_id=1, source_target_pairs={{0,2},{8,10},{16,18},{24,26},{64,66},{72,74},{80,82},{88,90},{192,... | collective-permute-start | bytes 393224 | tf_op jit(solution)/shard_map/ppermute | solution.py:383
  44.9 1.1 %request_partials.1 = (bf16[144,128]{1,0:T(8,128)(2,1)S(1)}, bf16[144,128]{1,0:T(8,128)(2,1)S(1)}, bf16[144,128]{1,0:T(8,128)(2,1)S(1)}, bf16[144,128]{1,0:T(8,128)(2,1)S(1)}) custom-call(s32[1]{0:T(128)S(6)} %copy.13.owner_ref, bf16[64,128]{1,0:T(8,128)(2,1)S(1)} %choose.3.refs_0_, bf16[64,128]{1,0:T(8,128)(2,1)S(1)} %collective-permute-done.16.refs_1_, ...), custom_call_target="tpu_custom_call" | custom-call | flops 3000000000 | bytes 1048576 | tf_op jit(solution)/shard_map/request_partials/pallas_call | solution.py:273
  46.2 2.6 %collective-permute-start.20 = (bf16[144,128]{1,0:T(8,128)(2,1)S(1)}, bf16[144,128]{1,0:T(8,128)(2,1)S(1)}, u32[]{:S(2)}, u32[]{:S(2)}) collective-permute-start(bf16[144,128]{1,0:T(8,128)(2,1)S(1)} %get-tuple-element.47), channel_id=1, source_target_pairs={{0,16},{8,24},{16,0},{24,8},{1,17},{9,25},{17,1},{25,9},{2,18},{10... | collective-permute-start | bytes 110600 | tf_op jit(solution)/shard_map/ppermute | solution.py:386
  48.8 1.8 %collective-permute-start.21 = (bf16[144,128]{1,0:T(8,128)(2,1)S(1)}, bf16[144,128]{1,0:T(8,128)(2,1)S(1)}, u32[]{:S(2)}, u32[]{:S(2)}) collective-permute-start(bf16[144,128]{1,0:T(8,128)(2,1)S(1)} %get-tuple-element.48), channel_id=1, source_target_pairs={{0,8},{8,16},{16,24},{24,0},{1,9},{9,17},{17,25},{25,1},{2,10},{10... | collective-permute-start | bytes 110600 | tf_op jit(solution)/shard_map/ppermute | solution.py:386
  50.7 2.7 %collective-permute-start.9 = (bf16[64,1024]{1,0:T(8,128)(2,1)S(1)}, bf16[64,1024]{1,0:T(8,128)(2,1)S(1)}, u32[]{:S(2)}, u32[]{:S(2)}) collective-permute-start(bf16[64,1024]{1,0:T(8,128)(2,1)S(1)} %add_select_fusion.1), channel_id=1, source_target_pairs={{0,224},{2,226},{4,228},{6,230},{8,232},{10,234},{12,236},{14,238}... | collective-permute-start | bytes 393224 | tf_op jit(solution)/shard_map/ppermute | solution.py:383
  53.3 1.3 %collective-permute-start.8 = (bf16[64,1024]{1,0:T(8,128)(2,1)S(1)}, bf16[64,1024]{1,0:T(8,128)(2,1)S(1)}, u32[]{:S(2)}, u32[]{:S(2)}) collective-permute-start(bf16[64,1024]{1,0:T(8,128)(2,1)S(1)} %add_select_fusion.1), channel_id=1, source_target_pairs={{0,32},{2,34},{4,36},{6,38},{8,40},{10,42},{12,44},{14,46},{16,48}... | collective-permute-start | bytes 393224 | tf_op jit(solution)/shard_map/ppermute | solution.py:383
  54.7 1.0 %join_pieces.2 = bf16[8,80,128]{2,1,0:T(8,128)(2,1)} custom-call(bf16[144,128]{1,0:T(8,128)(2,1)S(1)} %get-tuple-element.45.refs_0_, bf16[144,128]{1,0:T(8,128)(2,1)S(1)} %collective-permute-done.19.refs_1_, bf16[144,128]{1,0:T(8,128)(2,1)S(1)} %collective-permute-done.20.refs_2_, bf16[144,128]{1,0:T(8,128)(2,1)S(1)} %collective-permute-done.21.refs_3_), custom_call_target="tpu_custom_call" | custom-call | flops 3000000000 | bytes 524288 | tf_op jit(solution)/shard_map/join_pieces/pallas_call | solution.py:331
  55.7 4.5 %all-to-all-start.2 = ((bf16[8,80,128]{2,1,0:T(8,128)(2,1)}), bf16[8,80,128]{2,1,0:T(8,128)(2,1)S(1)}, u32[]{:S(2)}, u32[]{:S(2)}) async-start(bf16[8,80,128]{2,1,0:T(8,128)(2,1)} %join_pieces.2), calls=%async_computation.2 | async-start | bytes 327680 | tf_op jit(solution)/shard_map/all_to_all | solution.py:372
  60.3 1.9 %collective-permute-start.12 = (bf16[64,1024]{1,0:T(8,128)(2,1)S(1)}, bf16[64,1024]{1,0:T(8,128)(2,1)S(1)}, u32[]{:S(2)}, u32[]{:S(2)}) collective-permute-start(bf16[64,1024]{1,0:T(8,128)(2,1)S(1)} %add_select_fusion.refs_0_.refs_4_), channel_id=1, source_target_pairs={{0,24},{8,0},{16,8},{24,16},{1,25},{9,1},{17,9},{25,17},{2,26},{10... | collective-permute-start | bytes 393224 | tf_op jit(solution)/shard_map/ppermute | solution.py:386
  62.2 1.6 %collective-permute-start.11 = (bf16[64,1024]{1,0:T(8,128)(2,1)S(1)}, bf16[64,1024]{1,0:T(8,128)(2,1)S(1)}, u32[]{:S(2)}, u32[]{:S(2)}) collective-permute-start(bf16[64,1024]{1,0:T(8,128)(2,1)S(1)} %add_select_fusion.refs_0_.refs_4_), channel_id=1, source_target_pairs={{0,16},{8,24},{16,0},{24,8},{1,17},{9,25},{17,1},{25,9},{2,18},{10... | collective-permute-start | bytes 393224 | tf_op jit(solution)/shard_map/ppermute | solution.py:386
  63.7 1.0 %collective-permute-start.10 = (bf16[64,1024]{1,0:T(8,128)(2,1)S(1)}, bf16[64,1024]{1,0:T(8,128)(2,1)S(1)}, u32[]{:S(2)}, u32[]{:S(2)}) collective-permute-start(bf16[64,1024]{1,0:T(8,128)(2,1)S(1)} %add_select_fusion.refs_0_.refs_4_), channel_id=1, source_target_pairs={{0,8},{8,16},{16,24},{24,0},{1,9},{9,17},{17,25},{25,1},{2,10},{10... | collective-permute-start | bytes 393224 | tf_op jit(solution)/shard_map/ppermute | solution.py:386
  64.7 1.3 %all-to-all-done.2.refs_0_ = bf16[8,80,128]{2,1,0:T(8,128)(2,1)S(1)} async-done(((bf16[8,80,128]{2,1,0:T(8,128)(2,1)}), bf16[8,80,128]{2,1,0:T(8,128)(2,1)S(1)}, u32[]{:S(2)}, u32[]{:S(2)}) %all-to-all-start.2) | async-done | bytes 163872 | tf_op jit(solution)/shard_map/all_to_all | solution.py:372
  66.1 1.1 %join_pieces.3 = bf16[16,64,128]{2,1,0:T(8,128)(2,1)} custom-call(bf16[8,80,128]{2,1,0:T(8,128)(2,1)S(1)} %all-to-all-done.2.refs_0_), custom_call_target="tpu_custom_call" | custom-call | flops 3000000000 | bytes 524288 | tf_op jit(solution)/shard_map/join_pieces/pallas_call | solution.py:331
  67.1 5.9 %all-to-all-start.3 = ((bf16[16,64,128]{2,1,0:T(8,128)(2,1)}), bf16[16,64,128]{2,1,0:T(8,128)(2,1)S(1)}, u32[]{:S(2)}, u32[]{:S(2)}) async-start(bf16[16,64,128]{2,1,0:T(8,128)(2,1)} %join_pieces.3), calls=%async_computation.3 | async-start | bytes 524288 | tf_op jit(solution)/shard_map/all_to_all | solution.py:372
  73.1 7.1 %context_attention.1 = (bf16[256,4096]{1,0:T(8,128)(2,1)}, bf16[32,4096]{1,0:T(8,128)(2,1)}) custom-call(s32[1]{0:T(128)S(6)} %copy.12.len_ref, bf16[256,4096]{1,0:T(8,128)(2,1)S(1)} %copy-done.2, bf16[256,512]{1,0:T(8,128)(2,1)S(1)} %copy-done, bf16[256,512]{1,0:T(8,128)(2,1)S(1)} %copy-done.1, bf16[64,1024]{1,0:T(8,128)(2,1)S(1)} %add_select_fusion.refs_0_.refs_4_, ...), custom_call_target="tpu_custom_call" | custom-call | flops 2147483648 | bytes 5242880 | tf_op jit(solution)/shard_map/context_attention/pallas_call | solution.py:100
  (42 shorter events, 1.3 us)
Async XLA Ops:
  3.6 26.1 %copy-start.4 = (bf16[64,1024]{1,0:T(8,128)(2,1)S(1)}, bf16[64,1024]{1,0:T(8,128)(2,1)}, u32[]{:S(2)}) copy-start(bf16[64,1024]{1,0:T(8,128)(2,1)} %get-tuple-element.26) | copy-start | bytes 393220
  3.6 16.2 %all-to-all-start = ((bf16[32,32,128]{2,1,0:T(8,128)(2,1)}), bf16[32,32,128]{2,1,0:T(8,128)(2,1)S(1)}, u32[]{:S(2)}, u32[]{:S(2)}) async-start(bf16[32,32,128]{2,1,0:T(8,128)(2,1)} %get-tuple-element.27), calls=%async_computation | async-start | bytes 524288 | tf_op jit(solution)/shard_map/all_to_all | solution.py:372
  11.4 8.2 %collective-permute-start = (bf16[64,1024]{1,0:T(8,128)(2,1)}, bf16[64,1024]{1,0:T(8,128)(2,1)S(1)}, u32[]{:S(2)}, u32[]{:S(2)}) collective-permute-start(bf16[64,1024]{1,0:T(8,128)(2,1)} %get-tuple-element.28), channel_id=1, source_target_pairs={{0,8},{1,9}} | collective-permute-start | bytes 393224 | tf_op jit(solution)/shard_map/ppermute | solution.py:383
  12.7 7.2 %collective-permute-start.1 = (bf16[64,1024]{1,0:T(8,128)(2,1)}, bf16[64,1024]{1,0:T(8,128)(2,1)S(1)}, u32[]{:S(2)}, u32[]{:S(2)}) collective-permute-start(bf16[64,1024]{1,0:T(8,128)(2,1)} %get-tuple-element.29), channel_id=1, source_target_pairs={{0,16},{1,17}} | collective-permute-start | bytes 393224 | tf_op jit(solution)/shard_map/ppermute | solution.py:383
  13.4 6.5 %collective-permute-start.2 = (bf16[64,1024]{1,0:T(8,128)(2,1)}, bf16[64,1024]{1,0:T(8,128)(2,1)S(1)}, u32[]{:S(2)}, u32[]{:S(2)}) collective-permute-start(bf16[64,1024]{1,0:T(8,128)(2,1)} %get-tuple-element.30), channel_id=1, source_target_pairs={{0,24},{1,25}} | collective-permute-start | bytes 393224 | tf_op jit(solution)/shard_map/ppermute | solution.py:383
  14.1 21.3 %collective-permute-start.13 = (bf16[576,128]{1,0:T(8,128)(2,1)}, bf16[576,128]{1,0:T(8,128)(2,1)S(1)}, u32[]{:S(2)}, u32[]{:S(2)}) collective-permute-start(bf16[576,128]{1,0:T(8,128)(2,1)} %get-tuple-element.37), channel_id=1, source_target_pairs={{0,2},{2,4},{4,6},{6,0},{1,3},{3,5},{5,7},{7,1},{8,10},{10,12},{12... | collective-permute-start | bytes 442376 | tf_op jit(solution)/shard_map/ppermute | solution.py:392
  15.0 20.4 %collective-permute-start.14 = (bf16[576,128]{1,0:T(8,128)(2,1)}, bf16[576,128]{1,0:T(8,128)(2,1)S(1)}, u32[]{:S(2)}, u32[]{:S(2)}) collective-permute-start(bf16[576,128]{1,0:T(8,128)(2,1)} %get-tuple-element.38), channel_id=1, source_target_pairs={{0,4},{2,6},{4,0},{6,2},{1,5},{3,7},{5,1},{7,3},{8,12},{10,14},{12... | collective-permute-start | bytes 442376 | tf_op jit(solution)/shard_map/ppermute | solution.py:392
  19.6 15.8 %collective-permute-start.15 = (bf16[576,128]{1,0:T(8,128)(2,1)}, bf16[576,128]{1,0:T(8,128)(2,1)S(1)}, u32[]{:S(2)}, u32[]{:S(2)}) collective-permute-start(bf16[576,128]{1,0:T(8,128)(2,1)} %get-tuple-element.39), channel_id=1, source_target_pairs={{0,6},{2,0},{4,2},{6,4},{1,7},{3,1},{5,3},{7,5},{8,14},{10,8},{12,... | collective-permute-start | bytes 442376 | tf_op jit(solution)/shard_map/ppermute | solution.py:392
  20.5 14.8 %all-to-all-start.1 = ((bf16[8,64,128]{2,1,0:T(8,128)(2,1)}), bf16[8,64,128]{2,1,0:T(8,128)(2,1)S(1)}, u32[]{:S(2)}, u32[]{:S(2)}) async-start(bf16[8,64,128]{2,1,0:T(8,128)(2,1)} %choose.2), calls=%async_computation.1 | async-start | bytes 262144 | tf_op jit(solution)/shard_map/all_to_all | solution.py:372
  29.7 15.1 %copy-start.3 = (bf16[576,128]{1,0:T(8,128)(2,1)S(1)}, bf16[576,128]{1,0:T(8,128)(2,1)}, u32[]{:S(2)}) copy-start(bf16[576,128]{1,0:T(8,128)(2,1)} %get-tuple-element.41.refs_4_) | copy-start | bytes 442372
  29.8 10.5 %collective-permute-start.4 = (bf16[64,1024]{1,0:T(8,128)(2,1)S(1)}, bf16[64,1024]{1,0:T(8,128)(2,1)S(1)}, u32[]{:S(2)}, u32[]{:S(2)}) collective-permute-start(bf16[64,1024]{1,0:T(8,128)(2,1)S(1)} %add_select_fusion.3), channel_id=1, source_target_pairs={{0,192},{8,200},{16,208},{24,216},{1,193},{9,201},{17,209},{25,217}} | collective-permute-start | bytes 393224 | tf_op jit(solution)/shard_map/ppermute | solution.py:383
  33.2 7.0 %collective-permute-start.3 = (bf16[64,1024]{1,0:T(8,128)(2,1)S(1)}, bf16[64,1024]{1,0:T(8,128)(2,1)S(1)}, u32[]{:S(2)}, u32[]{:S(2)}) collective-permute-start(bf16[64,1024]{1,0:T(8,128)(2,1)S(1)} %add_select_fusion.3), channel_id=1, source_target_pairs={{0,64},{8,72},{16,80},{24,88},{1,65},{9,73},{17,81},{25,89}} | collective-permute-start | bytes 393224 | tf_op jit(solution)/shard_map/ppermute | solution.py:383
  35.4 8.1 %collective-permute-start.18 = (bf16[64,128]{1,0:T(8,128)(2,1)S(1)}, bf16[64,128]{1,0:T(8,128)(2,1)S(1)}, u32[]{:S(2)}, u32[]{:S(2)}) collective-permute-start(bf16[64,128]{1,0:T(8,128)(2,1)S(1)} %choose.3.refs_0_), channel_id=1, source_target_pairs={{0,24},{8,0},{16,8},{24,16},{1,25},{9,1},{17,9},{25,17},{2,26},{10... | collective-permute-start | bytes 49160 | tf_op jit(solution)/shard_map/ppermute | solution.py:386
  36.3 8.6 %collective-permute-start.17 = (bf16[64,128]{1,0:T(8,128)(2,1)S(1)}, bf16[64,128]{1,0:T(8,128)(2,1)S(1)}, u32[]{:S(2)}, u32[]{:S(2)}) collective-permute-start(bf16[64,128]{1,0:T(8,128)(2,1)S(1)} %choose.3.refs_0_), channel_id=1, source_target_pairs={{0,16},{8,24},{16,0},{24,8},{1,17},{9,25},{17,1},{25,9},{2,18},{10... | collective-permute-start | bytes 49160 | tf_op jit(solution)/shard_map/ppermute | solution.py:386
  38.4 6.4 %collective-permute-start.16 = (bf16[64,128]{1,0:T(8,128)(2,1)S(1)}, bf16[64,128]{1,0:T(8,128)(2,1)S(1)}, u32[]{:S(2)}, u32[]{:S(2)}) collective-permute-start(bf16[64,128]{1,0:T(8,128)(2,1)S(1)} %choose.3.refs_0_), channel_id=1, source_target_pairs={{0,8},{8,16},{16,24},{24,0},{1,9},{9,17},{17,25},{25,1},{2,10},{10... | collective-permute-start | bytes 49160 | tf_op jit(solution)/shard_map/ppermute | solution.py:386
  40.3 8.5 %collective-permute-start.7 = (bf16[64,1024]{1,0:T(8,128)(2,1)S(1)}, bf16[64,1024]{1,0:T(8,128)(2,1)S(1)}, u32[]{:S(2)}, u32[]{:S(2)}) collective-permute-start(bf16[64,1024]{1,0:T(8,128)(2,1)S(1)} %add_select_fusion.2), channel_id=1, source_target_pairs={{0,6},{8,14},{16,22},{24,30},{64,70},{72,78},{80,86},{88,94},{192,... | collective-permute-start | bytes 393224 | tf_op jit(solution)/shard_map/ppermute | solution.py:383
  42.2 8.4 %collective-permute-start.6 = (bf16[64,1024]{1,0:T(8,128)(2,1)S(1)}, bf16[64,1024]{1,0:T(8,128)(2,1)S(1)}, u32[]{:S(2)}, u32[]{:S(2)}) collective-permute-start(bf16[64,1024]{1,0:T(8,128)(2,1)S(1)} %add_select_fusion.2), channel_id=1, source_target_pairs={{0,4},{8,12},{16,20},{24,28},{64,68},{72,76},{80,84},{88,92},{192,... | collective-permute-start | bytes 393224 | tf_op jit(solution)/shard_map/ppermute | solution.py:383
  43.6 7.1 %collective-permute-start.5 = (bf16[64,1024]{1,0:T(8,128)(2,1)S(1)}, bf16[64,1024]{1,0:T(8,128)(2,1)S(1)}, u32[]{:S(2)}, u32[]{:S(2)}) collective-permute-start(bf16[64,1024]{1,0:T(8,128)(2,1)S(1)} %add_select_fusion.2), channel_id=1, source_target_pairs={{0,2},{8,10},{16,18},{24,26},{64,66},{72,74},{80,82},{88,90},{192,... | collective-permute-start | bytes 393224 | tf_op jit(solution)/shard_map/ppermute | solution.py:383
  46.0 8.7 %collective-permute-start.19 = (bf16[144,128]{1,0:T(8,128)(2,1)S(1)}, bf16[144,128]{1,0:T(8,128)(2,1)S(1)}, u32[]{:S(2)}, u32[]{:S(2)}) collective-permute-start(bf16[144,128]{1,0:T(8,128)(2,1)S(1)} %get-tuple-element.46), channel_id=1, source_target_pairs={{0,24},{8,0},{16,8},{24,16},{1,25},{9,1},{17,9},{25,17},{2,26},{10... | collective-permute-start | bytes 110600 | tf_op jit(solution)/shard_map/ppermute | solution.py:386
  46.2 8.4 %collective-permute-start.20 = (bf16[144,128]{1,0:T(8,128)(2,1)S(1)}, bf16[144,128]{1,0:T(8,128)(2,1)S(1)}, u32[]{:S(2)}, u32[]{:S(2)}) collective-permute-start(bf16[144,128]{1,0:T(8,128)(2,1)S(1)} %get-tuple-element.47), channel_id=1, source_target_pairs={{0,16},{8,24},{16,0},{24,8},{1,17},{9,25},{17,1},{25,9},{2,18},{10... | collective-permute-start | bytes 110600 | tf_op jit(solution)/shard_map/ppermute | solution.py:386
  48.8 5.9 %collective-permute-start.21 = (bf16[144,128]{1,0:T(8,128)(2,1)S(1)}, bf16[144,128]{1,0:T(8,128)(2,1)S(1)}, u32[]{:S(2)}, u32[]{:S(2)}) collective-permute-start(bf16[144,128]{1,0:T(8,128)(2,1)S(1)} %get-tuple-element.48), channel_id=1, source_target_pairs={{0,8},{8,16},{16,24},{24,0},{1,9},{9,17},{17,25},{25,1},{2,10},{10... | collective-permute-start | bytes 110600 | tf_op jit(solution)/shard_map/ppermute | solution.py:386
  50.7 9.5 %collective-permute-start.9 = (bf16[64,1024]{1,0:T(8,128)(2,1)S(1)}, bf16[64,1024]{1,0:T(8,128)(2,1)S(1)}, u32[]{:S(2)}, u32[]{:S(2)}) collective-permute-start(bf16[64,1024]{1,0:T(8,128)(2,1)S(1)} %add_select_fusion.1), channel_id=1, source_target_pairs={{0,224},{2,226},{4,228},{6,230},{8,232},{10,234},{12,236},{14,238}... | collective-permute-start | bytes 393224 | tf_op jit(solution)/shard_map/ppermute | solution.py:383
  53.3 6.8 %collective-permute-start.8 = (bf16[64,1024]{1,0:T(8,128)(2,1)S(1)}, bf16[64,1024]{1,0:T(8,128)(2,1)S(1)}, u32[]{:S(2)}, u32[]{:S(2)}) collective-permute-start(bf16[64,1024]{1,0:T(8,128)(2,1)S(1)} %add_select_fusion.1), channel_id=1, source_target_pairs={{0,32},{2,34},{4,36},{6,38},{8,40},{10,42},{12,44},{14,46},{16,48}... | collective-permute-start | bytes 393224 | tf_op jit(solution)/shard_map/ppermute | solution.py:383
  55.7 10.4 %all-to-all-start.2 = ((bf16[8,80,128]{2,1,0:T(8,128)(2,1)}), bf16[8,80,128]{2,1,0:T(8,128)(2,1)S(1)}, u32[]{:S(2)}, u32[]{:S(2)}) async-start(bf16[8,80,128]{2,1,0:T(8,128)(2,1)} %join_pieces.2), calls=%async_computation.2 | async-start | bytes 327680 | tf_op jit(solution)/shard_map/all_to_all | solution.py:372
  60.2 12.8 %copy-start = (bf16[256,512]{1,0:T(8,128)(2,1)S(1)}, bf16[256,512]{1,0:T(8,128)(2,1)}, u32[]{:S(2)}) copy-start(bf16[256,512]{1,0:T(8,128)(2,1)} %k_ref.3) | copy-start | bytes 786436
  60.2 12.8 %copy-start.1 = (bf16[256,512]{1,0:T(8,128)(2,1)S(1)}, bf16[256,512]{1,0:T(8,128)(2,1)}, u32[]{:S(2)}) copy-start(bf16[256,512]{1,0:T(8,128)(2,1)} %v_ref.3) | copy-start | bytes 786436
  60.2 12.8 %copy-start.2 = (bf16[256,4096]{1,0:T(8,128)(2,1)S(1)}, bf16[256,4096]{1,0:T(8,128)(2,1)}, u32[]{:S(2)}) copy-start(bf16[256,4096]{1,0:T(8,128)(2,1)} %q_ref.1) | copy-start | bytes 6291460
  60.3 12.8 %collective-permute-start.12 = (bf16[64,1024]{1,0:T(8,128)(2,1)S(1)}, bf16[64,1024]{1,0:T(8,128)(2,1)S(1)}, u32[]{:S(2)}, u32[]{:S(2)}) collective-permute-start(bf16[64,1024]{1,0:T(8,128)(2,1)S(1)} %add_select_fusion.refs_0_.refs_4_), channel_id=1, source_target_pairs={{0,24},{8,0},{16,8},{24,16},{1,25},{9,1},{17,9},{25,17},{2,26},{10... | collective-permute-start | bytes 393224 | tf_op jit(solution)/shard_map/ppermute | solution.py:386
  62.2 10.8 %collective-permute-start.11 = (bf16[64,1024]{1,0:T(8,128)(2,1)S(1)}, bf16[64,1024]{1,0:T(8,128)(2,1)S(1)}, u32[]{:S(2)}, u32[]{:S(2)}) collective-permute-start(bf16[64,1024]{1,0:T(8,128)(2,1)S(1)} %add_select_fusion.refs_0_.refs_4_), channel_id=1, source_target_pairs={{0,16},{8,24},{16,0},{24,8},{1,17},{9,25},{17,1},{25,9},{2,18},{10... | collective-permute-start | bytes 393224 | tf_op jit(solution)/shard_map/ppermute | solution.py:386
  63.7 9.3 %collective-permute-start.10 = (bf16[64,1024]{1,0:T(8,128)(2,1)S(1)}, bf16[64,1024]{1,0:T(8,128)(2,1)S(1)}, u32[]{:S(2)}, u32[]{:S(2)}) collective-permute-start(bf16[64,1024]{1,0:T(8,128)(2,1)S(1)} %add_select_fusion.refs_0_.refs_4_), channel_id=1, source_target_pairs={{0,8},{8,16},{16,24},{24,0},{1,9},{9,17},{17,25},{25,1},{2,10},{10... | collective-permute-start | bytes 393224 | tf_op jit(solution)/shard_map/ppermute | solution.py:386
  67.1 13.1 %all-to-all-start.3 = ((bf16[16,64,128]{2,1,0:T(8,128)(2,1)}), bf16[16,64,128]{2,1,0:T(8,128)(2,1)S(1)}, u32[]{:S(2)}, u32[]{:S(2)}) async-start(bf16[16,64,128]{2,1,0:T(8,128)(2,1)} %join_pieces.3), calls=%async_computation.3 | async-start | bytes 524288 | tf_op jit(solution)/shard_map/all_to_all | solution.py:372

commit v7 on v6

--- a/solution.py
+++ b/solution.py
@@ -31,21 +31,14 @@
 
 
 def context_kernel(count, len_ref, q_ref, k_ref, v_ref, *refs):
-    ak_refs, av_refs = refs[:count], refs[count : 2 * count]
-    o_ref, zero_ref, vs_ref = refs[-3:]
+    anchor_refs = refs[:count]
+    o_ref, zero_ref, vs_ref, out_ref, sems = refs[-5:]
     zero_ref[...] = jnp.zeros_like(zero_ref)
-    rows = k_ref.shape[0]
+    rows, width = k_ref.shape
     half = rows // 2
+    heads = width // HEAD_SIZE
     own_len = len_ref[0]
     root = place() == 0
-    ak = jnp.concatenate([ref[...] for ref in ak_refs], axis=0)
-    ak = jnp.where(root, jnp.broadcast_to(k_ref[0:1, :], ak.shape), ak)
-    av = jnp.concatenate([ref[...] for ref in av_refs], axis=0)
-    hidden = (av > 100.0) | root
-    vs_ref[0:rows, :HEAD_SIZE] = jnp.where(hidden, jnp.zeros_like(av), av)
-    vs_ref[0:rows, HEAD_SIZE:] = jnp.where(hidden, jnp.zeros_like(av), jnp.ones_like(av))
-    vs_ref[rows:, :HEAD_SIZE] = v_ref[...]
-    vs_ref[rows:, HEAD_SIZE:] = jnp.ones((rows, HEAD_SIZE), jnp.bfloat16)
     c = SCALE * LOG2E
     row = lax.broadcasted_iota(jnp.int32, (STACK * half, half), 0)
     col = lax.broadcasted_iota(jnp.int32, (STACK * half, half), 1)
@@ -54,65 +47,86 @@
     def lanes(g):
         return slice(g * HEAD_SIZE, (g + 1) * HEAD_SIZE)
 
-    def scores(top, g):
+    def load(h):
+        ak = jnp.concatenate([ref[:, lanes(h)] for ref in anchor_refs], axis=0)
+        ak = jnp.where(root, jnp.broadcast_to(k_ref[0:1, lanes(h)], ak.shape), ak)
+        av = jnp.concatenate([ref[:, lanes(heads + h)] for ref in anchor_refs], axis=0)
+        hidden = (av > 100.0) | root
+        vs_ref[h, 0:rows, :HEAD_SIZE] = jnp.where(hidden, jnp.zeros_like(av), av)
+        vs_ref[h, 0:rows, HEAD_SIZE:] = jnp.where(hidden, jnp.zeros_like(av), jnp.ones_like(av))
+        vs_ref[h, rows:, :HEAD_SIZE] = v_ref[:, lanes(h)]
+        vs_ref[h, rows:, HEAD_SIZE:] = jnp.ones((rows, HEAD_SIZE), jnp.bfloat16)
+        return ak
+
+    def scores(h, top, g, ak):
         keys = top + half
         q = jnp.concatenate([q_ref[top:keys, lanes(g + i)] for i in range(STACK)], axis=0)
         sa = dot_nt(q, ak)
-        so = dot_nt(q, k_ref[0:keys, :])
+        so = dot_nt(q, k_ref[0:keys, lanes(h)])
         tiles = [sa[:, i : i + half] for i in range(0, rows, half)]
         tiles += [so[:, i : i + half] for i in range(0, top, half)]
         return tiles + [so[:, top:keys] + causal]
 
-    def finish(top, g, tiles):
+    def finish(index, h, top, g, tiles):
         keys = top + half
         live = (top + lax.broadcasted_iota(jnp.int32, (half, HEAD_SIZE), 0)) < own_len
         peak = jnp.max(functools.reduce(jnp.maximum, tiles), axis=1, keepdims=True)
         weights = [jnp.exp2((tile - peak) * c).astype(jnp.bfloat16) for tile in tiles]
-        acc = dot_nn(jnp.concatenate(weights, axis=1), vs_ref[0 : rows + keys, :])
+        acc = dot_nn(jnp.concatenate(weights, axis=1), vs_ref[h, 0 : rows + keys, :])
         total = acc[:, HEAD_SIZE:]
         inverse = pl.reciprocal(total, approx=True)
         inverse = inverse * (2.0 - total * inverse)
         out = acc[:, :HEAD_SIZE] * inverse
         for i in range(STACK):
             part = jnp.where(live, out[i * half : (i + 1) * half], 0.0)
-            o_ref[top:keys, lanes(g + i)] = part.astype(jnp.bfloat16)
-
-    work = [(top, g) for top in (0, half) for g in range(0, GROUP, STACK)]
-    tiles = scores(*work[0])
+            out_ref[top:keys, lanes(g + i)] = part.astype(jnp.bfloat16)
+        where = (slice(top, keys), slice(g * HEAD_SIZE, (g + STACK) * HEAD_SIZE))
+        copy = pltpu.make_async_copy(out_ref.at[where], o_ref.at[where], sems.at[index])
+        copy.start()
+        return copy
+
+    work = [
+        (h, top, h * GROUP + g) for h in range(heads) for top in (half, 0) for g in range(0, GROUP, STACK)
+    ]
+    ak = load(0)
+    tiles = scores(*work[0], ak)
+    copies = []
     for i, item in enumerate(work):
-        later = scores(*work[i + 1]) if i + 1 < len(work) else None
-        finish(*item, tiles)
+        later = None
+        if i + 1 < len(work):
+            if work[i + 1][0] != item[0]:
+                ak = load(work[i + 1][0])
+            later = scores(*work[i + 1], ak)
+        copies.append(finish(i, *item, tiles))
         tiles = later
+    for copy in copies:
+        copy.wait()
 
 
 def context_attention(own_len, q, k, v, anchor, own_rows):
     rows, width = q.shape
     heads = k.shape[1] // HEAD_SIZE
-    wide = GROUP * HEAD_SIZE
-    count = len(anchor)
-    slab = anchor[0].shape[0]
-    smem = pl.BlockSpec(memory_space=pltpu.SMEM)
-    kv_spec = pl.BlockSpec((rows, HEAD_SIZE), lambda h: (0, h))
-    wide_spec = pl.BlockSpec((rows, wide), lambda h: (0, h))
-    specs = [smem, wide_spec, kv_spec, kv_spec]
-    specs += [pl.BlockSpec((slab, HEAD_SIZE), lambda h: (0, h))] * count
-    specs += [pl.BlockSpec((slab, HEAD_SIZE), lambda h: (0, heads + h))] * count
+    vmem = pl.BlockSpec(memory_space=pltpu.VMEM)
+    tiles = 2 * heads * GROUP // STACK
     return pl.pallas_call(
-        functools.partial(context_kernel, count),
-        grid=(heads,),
+        functools.partial(context_kernel, len(anchor)),
         out_shape=[
             jax.ShapeDtypeStruct((rows, width), jnp.bfloat16),
             jax.ShapeDtypeStruct((own_rows, width), jnp.bfloat16),
         ],
-        in_specs=specs,
-        out_specs=[wide_spec, pl.BlockSpec((own_rows, wide), lambda h: (0, h))],
-        scratch_shapes=[pltpu.VMEM((2 * rows, 2 * HEAD_SIZE), jnp.bfloat16)],
+        in_specs=[pl.BlockSpec(memory_space=pltpu.SMEM)] + [vmem] * (3 + len(anchor)),
+        out_specs=[pl.BlockSpec(memory_space=pl.ANY), vmem],
+        scratch_shapes=[
+            pltpu.VMEM((heads, 2 * rows, 2 * HEAD_SIZE), jnp.bfloat16),
+            pltpu.VMEM((rows, width), jnp.bfloat16),
+            pltpu.SemaphoreType.DMA((tiles,)),
+        ],
         compiler_params=pltpu.CompilerParams(vmem_limit_bytes=VMEM_LIMIT),
         cost_estimate=pl.CostEstimate(
             flops=8 * rows * width * rows, bytes_accessed=5 * 2**20, transcendentals=2 * rows * rows * heads * GROUP
         ),
         name="context_attention",
-    )(own_len, q, k, v, *anchor, *anchor)
+    )(own_len, q, k, v, *anchor)
 
 
 def mark_kernel(n_x, len_ref, k_ref, v_ref, rk_ref, rv_ref, *o_refs):
@@ -396,25 +410,25 @@
     moved, got = lax.optimization_barrier((moved, got))
     moved = choose(plane_kernel, query_owner, moved, (n_z,) + piece, 8 * 10**8)
     anchor = jnp.where(x == 0, pieces[0], got[0] + got[1] + got[2])
-    got = [move(anchor, [(i * n_y, (to * n_x + i) * n_y) for i in range(n_x)]) for to in (2, 6)]
+    got = [move(anchor, [(i * n_y, (to * n_x + i) * n_y) for i in range(n_x)]) for to in (3, 5)]
     moved = exchange(moved, "z", down)
 
     moved = choose(line_kernel, query_owner, moved, piece, 3 * 10**9)
     moved, lines = lax.optimization_barrier((moved, lines))
     anchor = jnp.where(z == 0, anchor, got[0] + got[1])
-    rows = [(to * n_x + i) * n_y for to in (0, 2, 6) for i in range(n_x)]
+    rows = [(to * n_x + i) * n_y for to in (0, 3, 5) for i in range(n_x)]
     got = [move(anchor, [(p, p + j) for p in rows]) for j in range(1, n_y)]
     queries = [moved] + [shift_x(moved, i) for i in range(1, n_x)]
 
     partials = request_partials(query_owner, queries, lines, own_rows)
     anchor = jnp.where(y == 0, anchor, got[0] + got[1] + got[2])
     plane = range(n_xy)
-    steps = (((0, 1), (2, 3), (6, 5)), ((0, 7), (2, 4)))
+    steps = (((0, 1), (3, 4), (5, 6)), ((3, 2), (5, 7)))
     got = [move(anchor, [(a * n_xy + p, b * n_xy + p) for a, b in step for p in plane]) for step in steps]
     partials = [partials[0]] + [shift_x(partials[i], n_x - i) for i in range(1, n_x)]
 
     planes = join(partials, n_z, 2, True)
-    anchor = jnp.where((z == 0) | (z == 2) | (z == 6), anchor, got[0] + got[1])
+    anchor = jnp.where((z == 0) | (z == 3) | (z == 5), anchor, got[0] + got[1])
     anchors = [anchor]
     for i in range(1, n_x):
         anchors.append(shift_x(anchor, i))

time: 81 us -> 80.8 us (level)
    ppermute x10, starting transfers between devices: 16.2 us -> 14.7 us  [move(): return lax.ppermute(value, ('z', 'x', 'y'), pairs)]
    all_to_all x4, starting transfers between devices: 27.3 us -> 28.6 us  [exchange(): lax.all_to_all(x, axis, split_axis=0, concat_axis=0, axis_index_groups=gr...]
  transfers between devices with their start and end apart: 26 -> 26, of which waited for: 3 -> 3; matrix products, arithmetic and copies ran while one was open for 0% -> 0% of each run, Pallas kernels for 14% -> 13%
where the time goes in v7:
time: 80.8 us; the launch traced here: 79.7 us
  starting transfers between devices  60.8 us (75%)
  Pallas kernels  13 us (16%)
  waiting for transfers between devices  3.46 us (4%)
  between operations  2.4 us (3%)
    all_to_all x4, starting transfers between devices, exchange(): lax.all_to_all(x, axis, split_axis=0, concat_axis=0, axis_index_groups=gr...  28.6 us
    ppermute x10, starting transfers between devices, move(): return lax.ppermute(value, ('z', 'x', 'y'), pairs)  14.7 us
    ppermute x9, starting transfers between devices, shift_x(): lax.ppermute(value, 'x', [(a, (a + count) % n_x) for a in range(n_x)])  13.6 us
    pallas_call x1, Pallas kernels, context_attention(): pl.pallas_call(functools.partial(context_kernel, len(anchor)), out_shape=...  6.78 us
    ppermute x3, starting transfers between devices, local(): lax.ppermute(lines[i], 'y', [(a, (a + i) % n_y) for a in range(n_y)])  3.82 us
    pallas_call x1, Pallas kernels, prepare(): pl.pallas_call(functools.partial(prepare_kernel, n_x, n_y), out_shape=sha...  2.36 us
    pallas_call x2, Pallas kernels, join(): pl.pallas_call(functools.partial(join_kernel, parts_in, keep_code), out_s...  2.04 us
    all_to_all x4, waiting for transfers between devices, exchange(): lax.all_to_all(x, axis, split_axis=0, concat_axis=0, axis_index_groups=gr...  1.97 us
  transfers between devices with their start and end apart: 26, of which 3 were waited for; matrix products, arithmetic and copies ran while one was open for 0% of the time, Pallas kernels for 13%

profile of v7, /device:TPU:2, one launch (start us, length us, event | category | flops | bytes accessed | tf_op | source)
XLA Modules:
  0.0 79.7 jit_solution(10868565031322989226)
XLA Ops:
  1.3 2.4 %prepare.1 = (bf16[32,32,128]{2,1,0:T(8,128)(2,1)}, bf16[64,1024]{1,0:T(8,128)(2,1)}, bf16[64,1024]{1,0:T(8,128)(2,1)}, bf16[64,1024]{1,0:T(8,128)(2,1)}, bf16[6...) custom-call(s32[1]{0:T(128)S(6)} %copy.12.len_ref, ...), custom_call_target="tpu_custom_call" | custom-call | flops 262144 | bytes 2621440 | tf_op jit(solution)/shard_map/prepare/pallas_call | solution.py:180
  3.6 7.8 %all-to-all-start = ((bf16[32,32,128]{2,1,0:T(8,128)(2,1)}), bf16[32,32,128]{2,1,0:T(8,128)(2,1)S(1)}, u32[]{:S(2)}, u32[]{:S(2)}) async-start(bf16[32,32,128]{2,1,0:T(8,128)(2,1)} %get-tuple-element.27), calls=%async_computation | async-start | bytes 524288 | tf_op jit(solution)/shard_map/all_to_all | solution.py:386
  11.4 1.3 %collective-permute-start = (bf16[64,1024]{1,0:T(8,128)(2,1)}, bf16[64,1024]{1,0:T(8,128)(2,1)S(1)}, u32[]{:S(2)}, u32[]{:S(2)}) collective-permute-start(bf16[64,1024]{1,0:T(8,128)(2,1)} %get-tuple-element.28), channel_id=1, source_target_pairs={{0,8},{1,9}} | collective-permute-start | bytes 393224 | tf_op jit(solution)/shard_map/ppermute | solution.py:397
  12.7 0.7 collective-permute-start.1
  13.4 0.7 collective-permute-start.2
  14.1 0.9 %collective-permute-start.13 = (bf16[576,128]{1,0:T(8,128)(2,1)}, bf16[576,128]{1,0:T(8,128)(2,1)S(1)}, u32[]{:S(2)}, u32[]{:S(2)}) collective-permute-start(bf16[576,128]{1,0:T(8,128)(2,1)} %get-tuple-element.37), channel_id=1, source_target_pairs={{0,2},{2,4},{4,6},{6,0},{1,3},{3,5},{5,7},{7,1},{8,10},{10,12},{12... | collective-permute-start | bytes 442376 | tf_op jit(solution)/shard_map/ppermute | solution.py:406
  15.0 2.7 %collective-permute-start.14 = (bf16[576,128]{1,0:T(8,128)(2,1)}, bf16[576,128]{1,0:T(8,128)(2,1)S(1)}, u32[]{:S(2)}, u32[]{:S(2)}) collective-permute-start(bf16[576,128]{1,0:T(8,128)(2,1)} %get-tuple-element.38), channel_id=1, source_target_pairs={{0,4},{2,6},{4,0},{6,2},{1,5},{3,7},{5,1},{7,3},{8,12},{10,14},{12... | collective-permute-start | bytes 442376 | tf_op jit(solution)/shard_map/ppermute | solution.py:406
  18.3 1.3 %collective-permute-done = bf16[64,1024]{1,0:T(8,128)(2,1)S(1)} collective-permute-done((bf16[64,1024]{1,0:T(8,128)(2,1)}, bf16[64,1024]{1,0:T(8,128)(2,1)S(1)}, u32[]{:S(2)}, u32[]{:S(2)}) %collective-permute-start) | collective-permute-done | bytes 131104 | tf_op jit(solution)/shard_map/ppermute | solution.py:397
  19.9 0.7 choose.2
  20.5 9.2 %all-to-all-start.1 = ((bf16[8,64,128]{2,1,0:T(8,128)(2,1)}), bf16[8,64,128]{2,1,0:T(8,128)(2,1)S(1)}, u32[]{:S(2)}, u32[]{:S(2)}) async-start(bf16[8,64,128]{2,1,0:T(8,128)(2,1)} %choose.2), calls=%async_computation.1 | async-start | bytes 262144 | tf_op jit(solution)/shard_map/all_to_all | solution.py:386
  29.8 4.4 %collective-permute-start.4 = (bf16[64,1024]{1,0:T(8,128)(2,1)S(1)}, bf16[64,1024]{1,0:T(8,128)(2,1)S(1)}, u32[]{:S(2)}, u32[]{:S(2)}) collective-permute-start(bf16[64,1024]{1,0:T(8,128)(2,1)S(1)} %add_select_fusion.3), channel_id=1, source_target_pairs={{0,160},{8,168},{16,176},{24,184},{1,161},{9,169},{17,177},{25,185}} | collective-permute-start | bytes 393224 | tf_op jit(solution)/shard_map/ppermute | solution.py:397
  34.1 1.6 %collective-permute-start.3 = (bf16[64,1024]{1,0:T(8,128)(2,1)S(1)}, bf16[64,1024]{1,0:T(8,128)(2,1)S(1)}, u32[]{:S(2)}, u32[]{:S(2)}) collective-permute-start(bf16[64,1024]{1,0:T(8,128)(2,1)S(1)} %add_select_fusion.3), channel_id=1, source_target_pairs={{0,96},{8,104},{16,112},{24,120},{1,97},{9,105},{17,113},{25,121}} | collective-permute-start | bytes 393224 | tf_op jit(solution)/shard_map/ppermute | solution.py:397
  35.8 0.8 %collective-permute-start.18 = (bf16[64,128]{1,0:T(8,128)(2,1)S(1)}, bf16[64,128]{1,0:T(8,128)(2,1)S(1)}, u32[]{:S(2)}, u32[]{:S(2)}) collective-permute-start(bf16[64,128]{1,0:T(8,128)(2,1)S(1)} %choose.3.refs_0_), channel_id=1, source_target_pairs={{0,24},{8,0},{16,8},{24,16},{1,25},{9,1},{17,9},{25,17},{2,26},{10... | collective-permute-start | bytes 49160 | tf_op jit(solution)/shard_map/ppermute | solution.py:400
  36.6 2.2 %collective-permute-start.17 = (bf16[64,128]{1,0:T(8,128)(2,1)S(1)}, bf16[64,128]{1,0:T(8,128)(2,1)S(1)}, u32[]{:S(2)}, u32[]{:S(2)}) collective-permute-start(bf16[64,128]{1,0:T(8,128)(2,1)S(1)} %choose.3.refs_0_), channel_id=1, source_target_pairs={{0,16},{8,24},{16,0},{24,8},{1,17},{9,25},{17,1},{25,9},{2,18},{10... | collective-permute-start | bytes 49160 | tf_op jit(solution)/shard_map/ppermute | solution.py:400
  38.8 1.8 %collective-permute-start.16 = (bf16[64,128]{1,0:T(8,128)(2,1)S(1)}, bf16[64,128]{1,0:T(8,128)(2,1)S(1)}, u32[]{:S(2)}, u32[]{:S(2)}) collective-permute-start(bf16[64,128]{1,0:T(8,128)(2,1)S(1)} %choose.3.refs_0_), channel_id=1, source_target_pairs={{0,8},{8,16},{16,24},{24,0},{1,9},{9,17},{17,25},{25,1},{2,10},{10... | collective-permute-start | bytes 49160 | tf_op jit(solution)/shard_map/ppermute | solution.py:400
  40.7 1.6 %collective-permute-start.7 = (bf16[64,1024]{1,0:T(8,128)(2,1)S(1)}, bf16[64,1024]{1,0:T(8,128)(2,1)S(1)}, u32[]{:S(2)}, u32[]{:S(2)}) collective-permute-start(bf16[64,1024]{1,0:T(8,128)(2,1)S(1)} %add_select_fusion.2), channel_id=1, source_target_pairs={{0,6},{8,14},{16,22},{24,30},{96,102},{104,110},{112,118},{120,126... | collective-permute-start | bytes 393224 | tf_op jit(solution)/shard_map/ppermute | solution.py:397
  42.2 1.3 %collective-permute-start.6 = (bf16[64,1024]{1,0:T(8,128)(2,1)S(1)}, bf16[64,1024]{1,0:T(8,128)(2,1)S(1)}, u32[]{:S(2)}, u32[]{:S(2)}) collective-permute-start(bf16[64,1024]{1,0:T(8,128)(2,1)S(1)} %add_select_fusion.2), channel_id=1, source_target_pairs={{0,4},{8,12},{16,20},{24,28},{96,100},{104,108},{112,116},{120,124... | collective-permute-start | bytes 393224 | tf_op jit(solution)/shard_map/ppermute | solution.py:397
  43.6 1.3 %collective-permute-start.5 = (bf16[64,1024]{1,0:T(8,128)(2,1)S(1)}, bf16[64,1024]{1,0:T(8,128)(2,1)S(1)}, u32[]{:S(2)}, u32[]{:S(2)}) collective-permute-start(bf16[64,1024]{1,0:T(8,128)(2,1)S(1)} %add_select_fusion.2), channel_id=1, source_target_pairs={{0,2},{8,10},{16,18},{24,26},{96,98},{104,106},{112,114},{120,122}... | collective-permute-start | bytes 393224 | tf_op jit(solution)/shard_map/ppermute | solution.py:397
  44.9 1.1 %request_partials.1 = (bf16[144,128]{1,0:T(8,128)(2,1)S(1)}, bf16[144,128]{1,0:T(8,128)(2,1)S(1)}, bf16[144,128]{1,0:T(8,128)(2,1)S(1)}, bf16[144,128]{1,0:T(8,128)(2,1)S(1)}) custom-call(s32[1]{0:T(128)S(6)} %copy.13.owner_ref, bf16[64,128]{1,0:T(8,128)(2,1)S(1)} %choose.3.refs_0_, bf16[64,128]{1,0:T(8,128)(2,1)S(1)} %collective-permute-done.16.refs_1_, ...), custom_call_target="tpu_custom_call" | custom-call | flops 3000000000 | bytes 1048576 | tf_op jit(solution)/shard_map/request_partials/pallas_call | solution.py:287
  46.2 2.6 %collective-permute-start.20 = (bf16[144,128]{1,0:T(8,128)(2,1)S(1)}, bf16[144,128]{1,0:T(8,128)(2,1)S(1)}, u32[]{:S(2)}, u32[]{:S(2)}) collective-permute-start(bf16[144,128]{1,0:T(8,128)(2,1)S(1)} %get-tuple-element.47), channel_id=1, source_target_pairs={{0,16},{8,24},{16,0},{24,8},{1,17},{9,25},{17,1},{25,9},{2,18},{10... | collective-permute-start | bytes 110600 | tf_op jit(solution)/shard_map/ppermute | solution.py:400
  48.8 1.8 %collective-permute-start.21 = (bf16[144,128]{1,0:T(8,128)(2,1)S(1)}, bf16[144,128]{1,0:T(8,128)(2,1)S(1)}, u32[]{:S(2)}, u32[]{:S(2)}) collective-permute-start(bf16[144,128]{1,0:T(8,128)(2,1)S(1)} %get-tuple-element.48), channel_id=1, source_target_pairs={{0,8},{8,16},{16,24},{24,0},{1,9},{9,17},{17,25},{25,1},{2,10},{10... | collective-permute-start | bytes 110600 | tf_op jit(solution)/shard_map/ppermute | solution.py:400
  50.7 0.7 collective-permute-start.9
  51.3 1.3 %collective-permute-start.8 = (bf16[64,1024]{1,0:T(8,128)(2,1)S(1)}, bf16[64,1024]{1,0:T(8,128)(2,1)S(1)}, u32[]{:S(2)}, u32[]{:S(2)}) collective-permute-start(bf16[64,1024]{1,0:T(8,128)(2,1)S(1)} %add_select_fusion.1), channel_id=1, source_target_pairs={{0,32},{2,34},{4,36},{6,38},{8,40},{10,42},{12,44},{14,46},{16,48}... | collective-permute-start | bytes 393224 | tf_op jit(solution)/shard_map/ppermute | solution.py:397
  52.8 1.0 %join_pieces.2 = bf16[8,80,128]{2,1,0:T(8,128)(2,1)} custom-call(bf16[144,128]{1,0:T(8,128)(2,1)S(1)} %get-tuple-element.45.refs_0_, bf16[144,128]{1,0:T(8,128)(2,1)S(1)} %collective-permute-done.19.refs_1_, bf16[144,128]{1,0:T(8,128)(2,1)S(1)} %collective-permute-done.20.refs_2_, bf16[144,128]{1,0:T(8,128)(2,1)S(1)} %collective-permute-done.21.refs_3_), custom_call_target="tpu_custom_call" | custom-call | flops 3000000000 | bytes 524288 | tf_op jit(solution)/shard_map/join_pieces/pallas_call | solution.py:345
  53.8 6.4 %all-to-all-start.2 = ((bf16[8,80,128]{2,1,0:T(8,128)(2,1)}), bf16[8,80,128]{2,1,0:T(8,128)(2,1)S(1)}, u32[]{:S(2)}, u32[]{:S(2)}) async-start(bf16[8,80,128]{2,1,0:T(8,128)(2,1)} %join_pieces.2), calls=%async_computation.2 | async-start | bytes 327680 | tf_op jit(solution)/shard_map/all_to_all | solution.py:386
  60.3 1.9 %collective-permute-start.12 = (bf16[64,1024]{1,0:T(8,128)(2,1)S(1)}, bf16[64,1024]{1,0:T(8,128)(2,1)S(1)}, u32[]{:S(2)}, u32[]{:S(2)}) collective-permute-start(bf16[64,1024]{1,0:T(8,128)(2,1)S(1)} %add_select_fusion.refs_0_), channel_id=1, source_target_pairs={{0,24},{8,0},{16,8},{24,16},{1,25},{9,1},{17,9},{25,17},{2,26},{10... | collective-permute-start | bytes 393224 | tf_op jit(solution)/shard_map/ppermute | solution.py:400
  62.2 1.1 %collective-permute-start.11 = (bf16[64,1024]{1,0:T(8,128)(2,1)S(1)}, bf16[64,1024]{1,0:T(8,128)(2,1)S(1)}, u32[]{:S(2)}, u32[]{:S(2)}) collective-permute-start(bf16[64,1024]{1,0:T(8,128)(2,1)S(1)} %add_select_fusion.refs_0_), channel_id=1, source_target_pairs={{0,16},{8,24},{16,0},{24,8},{1,17},{9,25},{17,1},{25,9},{2,18},{10... | collective-permute-start | bytes 393224 | tf_op jit(solution)/shard_map/ppermute | solution.py:400
  63.3 1.1 %collective-permute-start.10 = (bf16[64,1024]{1,0:T(8,128)(2,1)S(1)}, bf16[64,1024]{1,0:T(8,128)(2,1)S(1)}, u32[]{:S(2)}, u32[]{:S(2)}) collective-permute-start(bf16[64,1024]{1,0:T(8,128)(2,1)S(1)} %add_select_fusion.refs_0_), channel_id=1, source_target_pairs={{0,8},{8,16},{16,24},{24,0},{1,9},{9,17},{17,25},{25,1},{2,10},{10... | collective-permute-start | bytes 393224 | tf_op jit(solution)/shard_map/ppermute | solution.py:400
  64.4 2.0 %all-to-all-done.2.refs_0_ = bf16[8,80,128]{2,1,0:T(8,128)(2,1)S(1)} async-done(((bf16[8,80,128]{2,1,0:T(8,128)(2,1)}), bf16[8,80,128]{2,1,0:T(8,128)(2,1)S(1)}, u32[]{:S(2)}, u32[]{:S(2)}) %all-to-all-start.2) | async-done | bytes 163872 | tf_op jit(solution)/shard_map/all_to_all | solution.py:386
  66.4 1.1 %join_pieces.3 = bf16[16,64,128]{2,1,0:T(8,128)(2,1)} custom-call(bf16[8,80,128]{2,1,0:T(8,128)(2,1)S(1)} %all-to-all-done.2.refs_0_), custom_call_target="tpu_custom_call" | custom-call | flops 3000000000 | bytes 524288 | tf_op jit(solution)/shard_map/join_pieces/pallas_call | solution.py:345
  67.4 5.3 %all-to-all-start.3 = ((bf16[16,64,128]{2,1,0:T(8,128)(2,1)}), bf16[16,64,128]{2,1,0:T(8,128)(2,1)S(1)}, u32[]{:S(2)}, u32[]{:S(2)}) async-start(bf16[16,64,128]{2,1,0:T(8,128)(2,1)} %join_pieces.3), calls=%async_computation.3 | async-start | bytes 524288 | tf_op jit(solution)/shard_map/all_to_all | solution.py:386
  72.8 6.8 %context_attention.1 = (bf16[256,4096]{1,0:T(8,128)(2,1)}, bf16[32,4096]{1,0:T(8,128)(2,1)}) custom-call(s32[1]{0:T(128)S(6)} %copy.12.len_ref, bf16[256,4096]{1,0:T(8,128)(2,1)S(1)} %copy-done.2, bf16[256,512]{1,0:T(8,128)(2,1)S(1)} %copy-done, bf16[256,512]{1,0:T(8,128)(2,1)S(1)} %copy-done.1, bf16[64,1024]{1,0:T(8,128)(2,1)S(1)} %add_select_fusion.refs_0_, ...), custom_call_target="tpu_custom_call" | custom-call | flops 2147483648 | bytes 5242880 | tf_op jit(solution)/shard_map/context_attention/pallas_call | solution.py:111
  (42 shorter events, 0.8 us)
Async XLA Ops:
  3.6 26.1 %copy-start.4 = (bf16[64,1024]{1,0:T(8,128)(2,1)S(1)}, bf16[64,1024]{1,0:T(8,128)(2,1)}, u32[]{:S(2)}) copy-start(bf16[64,1024]{1,0:T(8,128)(2,1)} %get-tuple-element.26) | copy-start | bytes 393220
  3.6 16.2 %all-to-all-start = ((bf16[32,32,128]{2,1,0:T(8,128)(2,1)}), bf16[32,32,128]{2,1,0:T(8,128)(2,1)S(1)}, u32[]{:S(2)}, u32[]{:S(2)}) async-start(bf16[32,32,128]{2,1,0:T(8,128)(2,1)} %get-tuple-element.27), calls=%async_computation | async-start | bytes 524288 | tf_op jit(solution)/shard_map/all_to_all | solution.py:386
  11.4 8.2 %collective-permute-start = (bf16[64,1024]{1,0:T(8,128)(2,1)}, bf16[64,1024]{1,0:T(8,128)(2,1)S(1)}, u32[]{:S(2)}, u32[]{:S(2)}) collective-permute-start(bf16[64,1024]{1,0:T(8,128)(2,1)} %get-tuple-element.28), channel_id=1, source_target_pairs={{0,8},{1,9}} | collective-permute-start | bytes 393224 | tf_op jit(solution)/shard_map/ppermute | solution.py:397
  12.7 7.2 %collective-permute-start.1 = (bf16[64,1024]{1,0:T(8,128)(2,1)}, bf16[64,1024]{1,0:T(8,128)(2,1)S(1)}, u32[]{:S(2)}, u32[]{:S(2)}) collective-permute-start(bf16[64,1024]{1,0:T(8,128)(2,1)} %get-tuple-element.29), channel_id=1, source_target_pairs={{0,16},{1,17}} | collective-permute-start | bytes 393224 | tf_op jit(solution)/shard_map/ppermute | solution.py:397
  13.4 6.5 %collective-permute-start.2 = (bf16[64,1024]{1,0:T(8,128)(2,1)}, bf16[64,1024]{1,0:T(8,128)(2,1)S(1)}, u32[]{:S(2)}, u32[]{:S(2)}) collective-permute-start(bf16[64,1024]{1,0:T(8,128)(2,1)} %get-tuple-element.30), channel_id=1, source_target_pairs={{0,24},{1,25}} | collective-permute-start | bytes 393224 | tf_op jit(solution)/shard_map/ppermute | solution.py:397
  14.1 21.7 %collective-permute-start.13 = (bf16[576,128]{1,0:T(8,128)(2,1)}, bf16[576,128]{1,0:T(8,128)(2,1)S(1)}, u32[]{:S(2)}, u32[]{:S(2)}) collective-permute-start(bf16[576,128]{1,0:T(8,128)(2,1)} %get-tuple-element.37), channel_id=1, source_target_pairs={{0,2},{2,4},{4,6},{6,0},{1,3},{3,5},{5,7},{7,1},{8,10},{10,12},{12... | collective-permute-start | bytes 442376 | tf_op jit(solution)/shard_map/ppermute | solution.py:406
  15.0 20.8 %collective-permute-start.14 = (bf16[576,128]{1,0:T(8,128)(2,1)}, bf16[576,128]{1,0:T(8,128)(2,1)S(1)}, u32[]{:S(2)}, u32[]{:S(2)}) collective-permute-start(bf16[576,128]{1,0:T(8,128)(2,1)} %get-tuple-element.38), channel_id=1, source_target_pairs={{0,4},{2,6},{4,0},{6,2},{1,5},{3,7},{5,1},{7,3},{8,12},{10,14},{12... | collective-permute-start | bytes 442376 | tf_op jit(solution)/shard_map/ppermute | solution.py:406
  19.6 16.1 %collective-permute-start.15 = (bf16[576,128]{1,0:T(8,128)(2,1)}, bf16[576,128]{1,0:T(8,128)(2,1)S(1)}, u32[]{:S(2)}, u32[]{:S(2)}) collective-permute-start(bf16[576,128]{1,0:T(8,128)(2,1)} %get-tuple-element.39), channel_id=1, source_target_pairs={{0,6},{2,0},{4,2},{6,4},{1,7},{3,1},{5,3},{7,5},{8,14},{10,8},{12,... | collective-permute-start | bytes 442376 | tf_op jit(solution)/shard_map/ppermute | solution.py:406
  20.5 15.2 %all-to-all-start.1 = ((bf16[8,64,128]{2,1,0:T(8,128)(2,1)}), bf16[8,64,128]{2,1,0:T(8,128)(2,1)S(1)}, u32[]{:S(2)}, u32[]{:S(2)}) async-start(bf16[8,64,128]{2,1,0:T(8,128)(2,1)} %choose.2), calls=%async_computation.1 | async-start | bytes 262144 | tf_op jit(solution)/shard_map/all_to_all | solution.py:386
  29.7 15.1 %copy-start.3 = (bf16[576,128]{1,0:T(8,128)(2,1)S(1)}, bf16[576,128]{1,0:T(8,128)(2,1)}, u32[]{:S(2)}) copy-start(bf16[576,128]{1,0:T(8,128)(2,1)} %get-tuple-element.41.refs_4_) | copy-start | bytes 442372
  29.8 10.9 %collective-permute-start.4 = (bf16[64,1024]{1,0:T(8,128)(2,1)S(1)}, bf16[64,1024]{1,0:T(8,128)(2,1)S(1)}, u32[]{:S(2)}, u32[]{:S(2)}) collective-permute-start(bf16[64,1024]{1,0:T(8,128)(2,1)S(1)} %add_select_fusion.3), channel_id=1, source_target_pairs={{0,160},{8,168},{16,176},{24,184},{1,161},{9,169},{17,177},{25,185}} | collective-permute-start | bytes 393224 | tf_op jit(solution)/shard_map/ppermute | solution.py:397
  34.1 6.5 %collective-permute-start.3 = (bf16[64,1024]{1,0:T(8,128)(2,1)S(1)}, bf16[64,1024]{1,0:T(8,128)(2,1)S(1)}, u32[]{:S(2)}, u32[]{:S(2)}) collective-permute-start(bf16[64,1024]{1,0:T(8,128)(2,1)S(1)} %add_select_fusion.3), channel_id=1, source_target_pairs={{0,96},{8,104},{16,112},{24,120},{1,97},{9,105},{17,113},{25,121}} | collective-permute-start | bytes 393224 | tf_op jit(solution)/shard_map/ppermute | solution.py:397
  35.8 7.8 %collective-permute-start.18 = (bf16[64,128]{1,0:T(8,128)(2,1)S(1)}, bf16[64,128]{1,0:T(8,128)(2,1)S(1)}, u32[]{:S(2)}, u32[]{:S(2)}) collective-permute-start(bf16[64,128]{1,0:T(8,128)(2,1)S(1)} %choose.3.refs_0_), channel_id=1, source_target_pairs={{0,24},{8,0},{16,8},{24,16},{1,25},{9,1},{17,9},{25,17},{2,26},{10... | collective-permute-start | bytes 49160 | tf_op jit(solution)/shard_map/ppermute | solution.py:400
  36.6 8.3 %collective-permute-start.17 = (bf16[64,128]{1,0:T(8,128)(2,1)S(1)}, bf16[64,128]{1,0:T(8,128)(2,1)S(1)}, u32[]{:S(2)}, u32[]{:S(2)}) collective-permute-start(bf16[64,128]{1,0:T(8,128)(2,1)S(1)} %choose.3.refs_0_), channel_id=1, source_target_pairs={{0,16},{8,24},{16,0},{24,8},{1,17},{9,25},{17,1},{25,9},{2,18},{10... | collective-permute-start | bytes 49160 | tf_op jit(solution)/shard_map/ppermute | solution.py:400
  38.8 6.1 %collective-permute-start.16 = (bf16[64,128]{1,0:T(8,128)(2,1)S(1)}, bf16[64,128]{1,0:T(8,128)(2,1)S(1)}, u32[]{:S(2)}, u32[]{:S(2)}) collective-permute-start(bf16[64,128]{1,0:T(8,128)(2,1)S(1)} %choose.3.refs_0_), channel_id=1, source_target_pairs={{0,8},{8,16},{16,24},{24,0},{1,9},{9,17},{17,25},{25,1},{2,10},{10... | collective-permute-start | bytes 49160 | tf_op jit(solution)/shard_map/ppermute | solution.py:400
  40.7 8.2 %collective-permute-start.7 = (bf16[64,1024]{1,0:T(8,128)(2,1)S(1)}, bf16[64,1024]{1,0:T(8,128)(2,1)S(1)}, u32[]{:S(2)}, u32[]{:S(2)}) collective-permute-start(bf16[64,1024]{1,0:T(8,128)(2,1)S(1)} %add_select_fusion.2), channel_id=1, source_target_pairs={{0,6},{8,14},{16,22},{24,30},{96,102},{104,110},{112,118},{120,126... | collective-permute-start | bytes 393224 | tf_op jit(solution)/shard_map/ppermute | solution.py:397
  42.2 8.4 %collective-permute-start.6 = (bf16[64,1024]{1,0:T(8,128)(2,1)S(1)}, bf16[64,1024]{1,0:T(8,128)(2,1)S(1)}, u32[]{:S(2)}, u32[]{:S(2)}) collective-permute-start(bf16[64,1024]{1,0:T(8,128)(2,1)S(1)} %add_select_fusion.2), channel_id=1, source_target_pairs={{0,4},{8,12},{16,20},{24,28},{96,100},{104,108},{112,116},{120,124... | collective-permute-start | bytes 393224 | tf_op jit(solution)/shard_map/ppermute | solution.py:397
  43.6 7.1 %collective-permute-start.5 = (bf16[64,1024]{1,0:T(8,128)(2,1)S(1)}, bf16[64,1024]{1,0:T(8,128)(2,1)S(1)}, u32[]{:S(2)}, u32[]{:S(2)}) collective-permute-start(bf16[64,1024]{1,0:T(8,128)(2,1)S(1)} %add_select_fusion.2), channel_id=1, source_target_pairs={{0,2},{8,10},{16,18},{24,26},{96,98},{104,106},{112,114},{120,122}... | collective-permute-start | bytes 393224 | tf_op jit(solution)/shard_map/ppermute | solution.py:397
  46.0 6.7 %collective-permute-start.19 = (bf16[144,128]{1,0:T(8,128)(2,1)S(1)}, bf16[144,128]{1,0:T(8,128)(2,1)S(1)}, u32[]{:S(2)}, u32[]{:S(2)}) collective-permute-start(bf16[144,128]{1,0:T(8,128)(2,1)S(1)} %get-tuple-element.46), channel_id=1, source_target_pairs={{0,24},{8,0},{16,8},{24,16},{1,25},{9,1},{17,9},{25,17},{2,26},{10... | collective-permute-start | bytes 110600 | tf_op jit(solution)/shard_map/ppermute | solution.py:400
  46.2 6.4 %collective-permute-start.20 = (bf16[144,128]{1,0:T(8,128)(2,1)S(1)}, bf16[144,128]{1,0:T(8,128)(2,1)S(1)}, u32[]{:S(2)}, u32[]{:S(2)}) collective-permute-start(bf16[144,128]{1,0:T(8,128)(2,1)S(1)} %get-tuple-element.47), channel_id=1, source_target_pairs={{0,16},{8,24},{16,0},{24,8},{1,17},{9,25},{17,1},{25,9},{2,18},{10... | collective-permute-start | bytes 110600 | tf_op jit(solution)/shard_map/ppermute | solution.py:400
  48.8 4.0 %collective-permute-start.21 = (bf16[144,128]{1,0:T(8,128)(2,1)S(1)}, bf16[144,128]{1,0:T(8,128)(2,1)S(1)}, u32[]{:S(2)}, u32[]{:S(2)}) collective-permute-start(bf16[144,128]{1,0:T(8,128)(2,1)S(1)} %get-tuple-element.48), channel_id=1, source_target_pairs={{0,8},{8,16},{16,24},{24,0},{1,9},{9,17},{17,25},{25,1},{2,10},{10... | collective-permute-start | bytes 110600 | tf_op jit(solution)/shard_map/ppermute | solution.py:400
  50.7 9.5 %collective-permute-start.9 = (bf16[64,1024]{1,0:T(8,128)(2,1)S(1)}, bf16[64,1024]{1,0:T(8,128)(2,1)S(1)}, u32[]{:S(2)}, u32[]{:S(2)}) collective-permute-start(bf16[64,1024]{1,0:T(8,128)(2,1)S(1)} %add_select_fusion.1), channel_id=1, source_target_pairs={{96,64},{98,66},{100,68},{102,70},{104,72},{106,74},{108,76},{110,... | collective-permute-start | bytes 393224 | tf_op jit(solution)/shard_map/ppermute | solution.py:397
  51.3 8.9 %collective-permute-start.8 = (bf16[64,1024]{1,0:T(8,128)(2,1)S(1)}, bf16[64,1024]{1,0:T(8,128)(2,1)S(1)}, u32[]{:S(2)}, u32[]{:S(2)}) collective-permute-start(bf16[64,1024]{1,0:T(8,128)(2,1)S(1)} %add_select_fusion.1), channel_id=1, source_target_pairs={{0,32},{2,34},{4,36},{6,38},{8,40},{10,42},{12,44},{14,46},{16,48}... | collective-permute-start | bytes 393224 | tf_op jit(solution)/shard_map/ppermute | solution.py:397
  53.8 12.6 %all-to-all-start.2 = ((bf16[8,80,128]{2,1,0:T(8,128)(2,1)}), bf16[8,80,128]{2,1,0:T(8,128)(2,1)S(1)}, u32[]{:S(2)}, u32[]{:S(2)}) async-start(bf16[8,80,128]{2,1,0:T(8,128)(2,1)} %join_pieces.2), calls=%async_computation.2 | async-start | bytes 327680 | tf_op jit(solution)/shard_map/all_to_all | solution.py:386
  60.2 12.5 %copy-start = (bf16[256,512]{1,0:T(8,128)(2,1)S(1)}, bf16[256,512]{1,0:T(8,128)(2,1)}, u32[]{:S(2)}) copy-start(bf16[256,512]{1,0:T(8,128)(2,1)} %k_ref.3) | copy-start | bytes 786436
  60.3 12.5 %copy-start.1 = (bf16[256,512]{1,0:T(8,128)(2,1)S(1)}, bf16[256,512]{1,0:T(8,128)(2,1)}, u32[]{:S(2)}) copy-start(bf16[256,512]{1,0:T(8,128)(2,1)} %v_ref.3) | copy-start | bytes 786436
  60.3 12.5 %copy-start.2 = (bf16[256,4096]{1,0:T(8,128)(2,1)S(1)}, bf16[256,4096]{1,0:T(8,128)(2,1)}, u32[]{:S(2)}) copy-start(bf16[256,4096]{1,0:T(8,128)(2,1)} %q_ref.1) | copy-start | bytes 6291460
  60.3 12.4 %collective-permute-start.12 = (bf16[64,1024]{1,0:T(8,128)(2,1)S(1)}, bf16[64,1024]{1,0:T(8,128)(2,1)S(1)}, u32[]{:S(2)}, u32[]{:S(2)}) collective-permute-start(bf16[64,1024]{1,0:T(8,128)(2,1)S(1)} %add_select_fusion.refs_0_), channel_id=1, source_target_pairs={{0,24},{8,0},{16,8},{24,16},{1,25},{9,1},{17,9},{25,17},{2,26},{10... | collective-permute-start | bytes 393224 | tf_op jit(solution)/shard_map/ppermute | solution.py:400
  62.2 10.5 %collective-permute-start.11 = (bf16[64,1024]{1,0:T(8,128)(2,1)S(1)}, bf16[64,1024]{1,0:T(8,128)(2,1)S(1)}, u32[]{:S(2)}, u32[]{:S(2)}) collective-permute-start(bf16[64,1024]{1,0:T(8,128)(2,1)S(1)} %add_select_fusion.refs_0_), channel_id=1, source_target_pairs={{0,16},{8,24},{16,0},{24,8},{1,17},{9,25},{17,1},{25,9},{2,18},{10... | collective-permute-start | bytes 393224 | tf_op jit(solution)/shard_map/ppermute | solution.py:400
  63.3 9.4 %collective-permute-start.10 = (bf16[64,1024]{1,0:T(8,128)(2,1)S(1)}, bf16[64,1024]{1,0:T(8,128)(2,1)S(1)}, u32[]{:S(2)}, u32[]{:S(2)}) collective-permute-start(bf16[64,1024]{1,0:T(8,128)(2,1)S(1)} %add_select_fusion.refs_0_), channel_id=1, source_target_pairs={{0,8},{8,16},{16,24},{24,0},{1,9},{9,17},{17,25},{25,1},{2,10},{10... | collective-permute-start | bytes 393224 | tf_op jit(solution)/shard_map/ppermute | solution.py:400
  67.4 12.1 %all-to-all-start.3 = ((bf16[16,64,128]{2,1,0:T(8,128)(2,1)}), bf16[16,64,128]{2,1,0:T(8,128)(2,1)S(1)}, u32[]{:S(2)}, u32[]{:S(2)}) async-start(bf16[16,64,128]{2,1,0:T(8,128)(2,1)} %join_pieces.3), calls=%async_computation.3 | async-start | bytes 524288 | tf_op jit(solution)/shard_map/all_to_all | solution.py:386

commit v8 on v7

--- a/solution.py
+++ b/solution.py
@@ -16,6 +16,8 @@
 VMEM_LIMIT = 32 * 1024 * 1024
 STACK = 4
 N_X, N_Y = 4, 4
+PLANES = (4, 2, 1, 7, 6, 5, 3, 0)
+SWAPS = (0, 3, 2, 1)
 
 
 def place():
@@ -143,7 +145,7 @@
     valid = lax.broadcasted_iota(jnp.int32, (rows, HEAD_SIZE), 0) < len_ref[0]
     y = lax.axis_index("y")
     for i, o_ref in enumerate(lines):
-        head = lax.rem(y + i, len(lines))
+        head = y ^ SWAPS[i]
         lanes = pl.ds(pl.multiple_of(head * HEAD_SIZE, HEAD_SIZE), HEAD_SIZE)
         first = k_ref[0:1, lanes]
         o_ref[0:rows, :] = jnp.where(valid, k_ref[:, lanes], jnp.broadcast_to(first, valid.shape))
@@ -202,7 +204,11 @@
 
 
 def line_kernel(owner_ref, x_ref, o_ref):
-    o_ref[...] = x_ref[x_ref.shape[0] - 1 - lax.div(owner_ref[0], N_X * N_Y)]
+    owner_z = lax.div(owner_ref[0], N_X * N_Y)
+    spot = 0
+    for i, z in enumerate(PLANES):
+        spot = jnp.where(owner_z == z, i, spot)
+    o_ref[...] = x_ref[spot]
 
 
 def choose(kernel, owner, x, shape, flops):
@@ -251,7 +257,8 @@
         v_ref[top : top + own, HEAD_SIZE:] = jnp.ones((own, HEAD_SIZE), jnp.bfloat16)
     owner = owner_ref[0]
     same = lax.div(owner, N_Y) == lax.div(place(), N_Y)
-    asked = jnp.where(same, lax.rem(lax.axis_index("y") - lax.rem(owner, N_Y) + N_Y, N_Y), -1)
+    apart = lax.axis_index("y") ^ lax.rem(owner, N_Y)
+    asked = jnp.where(same, jnp.where(apart == 0, 0, N_Y - apart), -1)
     own_keys = jnp.concatenate([ref[rows:both, :] for ref in lines], axis=0)
     row = lax.rem(lax.broadcasted_iota(jnp.int32, (n, own_keys.shape[0]), 0), own)
     col = lax.broadcasted_iota(jnp.int32, (n, own_keys.shape[0]), 1) - asked * own
@@ -396,42 +403,40 @@
     def move(value, pairs):
         return lax.ppermute(value, ("z", "x", "y"), pairs)
 
-    def shift_x(value, count):
-        return lax.ppermute(value, "x", [(a, (a + count) % n_x) for a in range(n_x)])
+    def swap(value, axis, apart):
+        return lax.ppermute(value, axis, [(a, a ^ apart) for a in range(4)])
 
     sent, pieces, lines = prepare(own_len, rq, k, v, rk, rv, n_x, n_y)
     moved = exchange(sent, ("x", "y", "head"))
     got = [move(pieces[i], [(0, i * n_y)]) for i in range(1, n_x)]
-    lines = [lines[0]] + [
-        lax.ppermute(lines[i], "y", [(a, (a + i) % n_y) for a in range(n_y)]) for i in range(1, n_y)
-    ]
+    lines = [lines[0]] + [swap(lines[i], "y", SWAPS[i]) for i in range(1, n_y)]
 
     piece = (2 * moved.shape[1], HEAD_SIZE)
     moved, got = lax.optimization_barrier((moved, got))
     moved = choose(plane_kernel, query_owner, moved, (n_z,) + piece, 8 * 10**8)
     anchor = jnp.where(x == 0, pieces[0], got[0] + got[1] + got[2])
     got = [move(anchor, [(i * n_y, (to * n_x + i) * n_y) for i in range(n_x)]) for to in (3, 5)]
-    moved = exchange(moved, "z", down)
+    moved = exchange(moved, "z", [list(PLANES)])
 
     moved = choose(line_kernel, query_owner, moved, piece, 3 * 10**9)
     moved, lines = lax.optimization_barrier((moved, lines))
     anchor = jnp.where(z == 0, anchor, got[0] + got[1])
     rows = [(to * n_x + i) * n_y for to in (0, 3, 5) for i in range(n_x)]
     got = [move(anchor, [(p, p + j) for p in rows]) for j in range(1, n_y)]
-    queries = [moved] + [shift_x(moved, i) for i in range(1, n_x)]
+    queries = [moved] + [swap(moved, "x", i) for i in range(1, n_x)]
 
     partials = request_partials(query_owner, queries, lines, own_rows)
     anchor = jnp.where(y == 0, anchor, got[0] + got[1] + got[2])
     plane = range(n_xy)
     steps = (((0, 1), (3, 4), (5, 6)), ((3, 2), (5, 7)))
     got = [move(anchor, [(a * n_xy + p, b * n_xy + p) for a, b in step for p in plane]) for step in steps]
-    partials = [partials[0]] + [shift_x(partials[i], n_x - i) for i in range(1, n_x)]
+    partials = [partials[0]] + [swap(partials[i], "x", i) for i in SWAPS[1:]]
 
     planes = join(partials, n_z, 2, True)
     anchor = jnp.where((z == 0) | (z == 3) | (z == 5), anchor, got[0] + got[1])
     anchors = [anchor]
     for i in range(1, n_x):
-        anchors.append(shift_x(anchor, i))
+        anchors.append(swap(anchor, "x", i))
     planes = exchange(planes, "z", down)
 
     answer = exchange(join([planes], n_xy, 1, False), ("x", "y"))

time: 80.8 us -> 81.5 us (level)
  waiting for transfers between devices: 3.46 us -> 5.12 us
  starting transfers between devices: 60.8 us -> 59.8 us
    ppermute x12, starting transfers between devices: 17.4 us -> 15.5 us  [swap(): return lax.ppermute(value, axis, [(a, a ^ apart) for a in range(4)])]
    all_to_all x4, starting transfers between devices: 28.6 us -> 29.8 us  [exchange(): lax.all_to_all(x, axis, split_axis=0, concat_axis=0, axis_index_groups=gr...]
    ppermute x12, waiting for transfers between devices: 0.15 us -> 1.27 us  [swap(): return lax.ppermute(value, axis, [(a, a ^ apart) for a in range(4)])]
  transfers between devices with their start and end apart: 26 -> 26, of which waited for: 3 -> 5; matrix products, arithmetic and copies ran while one was open for 0% -> 0% of each run, Pallas kernels for 13% -> 13%
where the time goes in v8:
time: 81.5 us; the launch traced here: 80.4 us
  starting transfers between devices  59.8 us (73%)
  Pallas kernels  12.9 us (16%)
  waiting for transfers between devices  5.12 us (6%)
  between operations  2.38 us (3%)
    all_to_all x4, starting transfers between devices, exchange(): lax.all_to_all(x, axis, split_axis=0, concat_axis=0, axis_index_groups=gr...  29.8 us
    ppermute x12, starting transfers between devices, swap(): return lax.ppermute(value, axis, [(a, a ^ apart) for a in range(4)])  15.5 us
    ppermute x10, starting transfers between devices, move(): return lax.ppermute(value, ('z', 'x', 'y'), pairs)  14.4 us
    pallas_call x1, Pallas kernels, context_attention(): pl.pallas_call(functools.partial(context_kernel, len(anchor)), out_shape=...  6.79 us
    pallas_call x1, Pallas kernels, prepare(): pl.pallas_call(functools.partial(prepare_kernel, n_x, n_y), out_shape=sha...  2.33 us
    pallas_call x2, Pallas kernels, join(): pl.pallas_call(functools.partial(join_kernel, parts_in, keep_code), out_s...  2.04 us
    ppermute x10, waiting for transfers between devices, move(): return lax.ppermute(value, ('z', 'x', 'y'), pairs)  1.95 us
    all_to_all x4, waiting for transfers between devices, exchange(): lax.all_to_all(x, axis, split_axis=0, concat_axis=0, axis_index_groups=gr...  1.9 us
  transfers between devices with their start and end apart: 26, of which 5 were waited for; matrix products, arithmetic and copies ran while one was open for 0% of the time, Pallas kernels for 13%

profile of v8, /device:TPU:2, one launch (start us, length us, event | category | flops | bytes accessed | tf_op | source)
XLA Modules:
  0.0 80.4 jit_solution(14926584364333473252)
XLA Ops:
  1.3 2.3 %prepare.1 = (bf16[32,32,128]{2,1,0:T(8,128)(2,1)}, bf16[64,1024]{1,0:T(8,128)(2,1)}, bf16[64,1024]{1,0:T(8,128)(2,1)}, bf16[64,1024]{1,0:T(8,128)(2,1)}, bf16[6...) custom-call(s32[1]{0:T(128)S(6)} %copy.12.len_ref, ...), custom_call_target="tpu_custom_call" | custom-call | flops 262144 | bytes 2621440 | tf_op jit(solution)/shard_map/prepare/pallas_call | solution.py:182
  3.6 7.8 %all-to-all-start = ((bf16[32,32,128]{2,1,0:T(8,128)(2,1)}), bf16[32,32,128]{2,1,0:T(8,128)(2,1)S(1)}, u32[]{:S(2)}, u32[]{:S(2)}) async-start(bf16[32,32,128]{2,1,0:T(8,128)(2,1)} %get-tuple-element.27), calls=%async_computation | async-start | bytes 524288 | tf_op jit(solution)/shard_map/all_to_all | solution.py:393
  11.4 1.3 %collective-permute-start = (bf16[64,1024]{1,0:T(8,128)(2,1)}, bf16[64,1024]{1,0:T(8,128)(2,1)S(1)}, u32[]{:S(2)}, u32[]{:S(2)}) collective-permute-start(bf16[64,1024]{1,0:T(8,128)(2,1)} %get-tuple-element.28), channel_id=1, source_target_pairs={{0,8},{1,9}} | collective-permute-start | bytes 393224 | tf_op jit(solution)/shard_map/ppermute | solution.py:404
  12.7 0.7 collective-permute-start.1
  13.4 0.7 collective-permute-start.2
  14.0 2.1 %collective-permute-start.13 = (bf16[576,128]{1,0:T(8,128)(2,1)}, bf16[576,128]{1,0:T(8,128)(2,1)S(1)}, u32[]{:S(2)}, u32[]{:S(2)}) collective-permute-start(bf16[576,128]{1,0:T(8,128)(2,1)} %get-tuple-element.37), channel_id=1, source_target_pairs={{0,6},{2,4},{4,2},{6,0},{1,7},{3,5},{5,3},{7,1},{8,14},{10,12},{12... | collective-permute-start | bytes 442376 | tf_op jit(solution)/shard_map/ppermute | solution.py:407
  16.2 0.9 %collective-permute-start.14 = (bf16[576,128]{1,0:T(8,128)(2,1)}, bf16[576,128]{1,0:T(8,128)(2,1)S(1)}, u32[]{:S(2)}, u32[]{:S(2)}) collective-permute-start(bf16[576,128]{1,0:T(8,128)(2,1)} %get-tuple-element.38), channel_id=1, source_target_pairs={{0,4},{2,6},{4,0},{6,2},{1,5},{3,7},{5,1},{7,3},{8,12},{10,14},{12... | collective-permute-start | bytes 442376 | tf_op jit(solution)/shard_map/ppermute | solution.py:407
  17.7 1.9 %collective-permute-done = bf16[64,1024]{1,0:T(8,128)(2,1)S(1)} collective-permute-done((bf16[64,1024]{1,0:T(8,128)(2,1)}, bf16[64,1024]{1,0:T(8,128)(2,1)S(1)}, u32[]{:S(2)}, u32[]{:S(2)}) %collective-permute-start) | collective-permute-done | bytes 131104 | tf_op jit(solution)/shard_map/ppermute | solution.py:404
  19.6 0.7 choose.2
  20.3 10.0 %all-to-all-start.1 = ((bf16[8,64,128]{2,1,0:T(8,128)(2,1)}), bf16[8,64,128]{2,1,0:T(8,128)(2,1)S(1)}, u32[]{:S(2)}, u32[]{:S(2)}) async-start(bf16[8,64,128]{2,1,0:T(8,128)(2,1)} %choose.2), calls=%async_computation.1 | async-start | bytes 262144 | tf_op jit(solution)/shard_map/all_to_all | solution.py:393
  30.3 2.6 %collective-permute-start.4 = (bf16[64,1024]{1,0:T(8,128)(2,1)S(1)}, bf16[64,1024]{1,0:T(8,128)(2,1)S(1)}, u32[]{:S(2)}, u32[]{:S(2)}) collective-permute-start(bf16[64,1024]{1,0:T(8,128)(2,1)S(1)} %add_select_fusion.3), channel_id=1, source_target_pairs={{0,160},{8,168},{16,176},{24,184},{1,161},{9,169},{17,177},{25,185}} | collective-permute-start | bytes 393224 | tf_op jit(solution)/shard_map/ppermute | solution.py:404
  32.9 1.3 %collective-permute-start.3 = (bf16[64,1024]{1,0:T(8,128)(2,1)S(1)}, bf16[64,1024]{1,0:T(8,128)(2,1)S(1)}, u32[]{:S(2)}, u32[]{:S(2)}) collective-permute-start(bf16[64,1024]{1,0:T(8,128)(2,1)S(1)} %add_select_fusion.3), channel_id=1, source_target_pairs={{0,96},{8,104},{16,112},{24,120},{1,97},{9,105},{17,113},{25,121}} | collective-permute-start | bytes 393224 | tf_op jit(solution)/shard_map/ppermute | solution.py:404
  34.5 0.8 %collective-permute-start.18 = (bf16[64,128]{1,0:T(8,128)(2,1)S(1)}, bf16[64,128]{1,0:T(8,128)(2,1)S(1)}, u32[]{:S(2)}, u32[]{:S(2)}) collective-permute-start(bf16[64,128]{1,0:T(8,128)(2,1)S(1)} %choose.3.refs_0_), channel_id=1, source_target_pairs={{0,24},{8,16},{16,8},{24,0},{1,25},{9,17},{17,9},{25,1},{2,26},{10... | collective-permute-start | bytes 49160 | tf_op jit(solution)/shard_map/ppermute | solution.py:407
  35.4 2.8 %collective-permute-start.17 = (bf16[64,128]{1,0:T(8,128)(2,1)S(1)}, bf16[64,128]{1,0:T(8,128)(2,1)S(1)}, u32[]{:S(2)}, u32[]{:S(2)}) collective-permute-start(bf16[64,128]{1,0:T(8,128)(2,1)S(1)} %choose.3.refs_0_), channel_id=1, source_target_pairs={{0,16},{8,24},{16,0},{24,8},{1,17},{9,25},{17,1},{25,9},{2,18},{10... | collective-permute-start | bytes 49160 | tf_op jit(solution)/shard_map/ppermute | solution.py:407
  38.7 3.4 %collective-permute-start.7 = (bf16[64,1024]{1,0:T(8,128)(2,1)S(1)}, bf16[64,1024]{1,0:T(8,128)(2,1)S(1)}, u32[]{:S(2)}, u32[]{:S(2)}) collective-permute-start(bf16[64,1024]{1,0:T(8,128)(2,1)S(1)} %add_select_fusion.2), channel_id=1, source_target_pairs={{0,6},{8,14},{16,22},{24,30},{96,102},{104,110},{112,118},{120,126... | collective-permute-start | bytes 393224 | tf_op jit(solution)/shard_map/ppermute | solution.py:404
  42.1 1.3 %collective-permute-start.6 = (bf16[64,1024]{1,0:T(8,128)(2,1)S(1)}, bf16[64,1024]{1,0:T(8,128)(2,1)S(1)}, u32[]{:S(2)}, u32[]{:S(2)}) collective-permute-start(bf16[64,1024]{1,0:T(8,128)(2,1)S(1)} %add_select_fusion.2), channel_id=1, source_target_pairs={{0,4},{8,12},{16,20},{24,28},{96,100},{104,108},{112,116},{120,124... | collective-permute-start | bytes 393224 | tf_op jit(solution)/shard_map/ppermute | solution.py:404
  43.4 1.3 %collective-permute-start.5 = (bf16[64,1024]{1,0:T(8,128)(2,1)S(1)}, bf16[64,1024]{1,0:T(8,128)(2,1)S(1)}, u32[]{:S(2)}, u32[]{:S(2)}) collective-permute-start(bf16[64,1024]{1,0:T(8,128)(2,1)S(1)} %add_select_fusion.2), channel_id=1, source_target_pairs={{0,2},{8,10},{16,18},{24,26},{96,98},{104,106},{112,114},{120,122}... | collective-permute-start | bytes 393224 | tf_op jit(solution)/shard_map/ppermute | solution.py:404
  44.8 1.1 %request_partials.1 = (bf16[144,128]{1,0:T(8,128)(2,1)S(1)}, bf16[144,128]{1,0:T(8,128)(2,1)S(1)}, bf16[144,128]{1,0:T(8,128)(2,1)S(1)}, bf16[144,128]{1,0:T(8,128)(2,1)S(1)}) custom-call(s32[1]{0:T(128)S(6)} %copy.13.owner_ref, bf16[64,128]{1,0:T(8,128)(2,1)S(1)} %choose.3.refs_0_, bf16[64,128]{1,0:T(8,128)(2,1)S(1)} %collective-permute-done.16.refs_1_, ...), custom_call_target="tpu_custom_call" | custom-call | flops 3000000000 | bytes 1048576 | tf_op jit(solution)/shard_map/request_partials/pallas_call | solution.py:294
  45.8 1.4 %collective-permute-start.19 = (bf16[144,128]{1,0:T(8,128)(2,1)S(1)}, bf16[144,128]{1,0:T(8,128)(2,1)S(1)}, u32[]{:S(2)}, u32[]{:S(2)}) collective-permute-start(bf16[144,128]{1,0:T(8,128)(2,1)S(1)} %get-tuple-element.46), channel_id=1, source_target_pairs={{0,24},{8,16},{16,8},{24,0},{1,25},{9,17},{17,9},{25,1},{2,26},{10... | collective-permute-start | bytes 110600 | tf_op jit(solution)/shard_map/ppermute | solution.py:407
  47.2 2.2 %collective-permute-start.20 = (bf16[144,128]{1,0:T(8,128)(2,1)S(1)}, bf16[144,128]{1,0:T(8,128)(2,1)S(1)}, u32[]{:S(2)}, u32[]{:S(2)}) collective-permute-start(bf16[144,128]{1,0:T(8,128)(2,1)S(1)} %get-tuple-element.47), channel_id=1, source_target_pairs={{0,16},{8,24},{16,0},{24,8},{1,17},{9,25},{17,1},{25,9},{2,18},{10... | collective-permute-start | bytes 110600 | tf_op jit(solution)/shard_map/ppermute | solution.py:407
  49.3 0.7 collective-permute-start.21
  50.0 0.7 collective-permute-start.9
  50.7 1.3 %collective-permute-start.8 = (bf16[64,1024]{1,0:T(8,128)(2,1)S(1)}, bf16[64,1024]{1,0:T(8,128)(2,1)S(1)}, u32[]{:S(2)}, u32[]{:S(2)}) collective-permute-start(bf16[64,1024]{1,0:T(8,128)(2,1)S(1)} %add_select_fusion.1), channel_id=1, source_target_pairs={{0,32},{2,34},{4,36},{6,38},{8,40},{10,42},{12,44},{14,46},{16,48}... | collective-permute-start | bytes 393224 | tf_op jit(solution)/shard_map/ppermute | solution.py:404
  53.3 1.0 %join_pieces.2 = bf16[8,80,128]{2,1,0:T(8,128)(2,1)} custom-call(bf16[144,128]{1,0:T(8,128)(2,1)S(1)} %get-tuple-element.45.refs_0_, bf16[144,128]{1,0:T(8,128)(2,1)S(1)} %collective-permute-done.19.refs_1_, bf16[144,128]{1,0:T(8,128)(2,1)S(1)} %collective-permute-done.20.refs_2_, bf16[144,128]{1,0:T(8,128)(2,1)S(1)} %collective-permute-done.21.refs_3_), custom_call_target="tpu_custom_call" | custom-call | flops 3000000000 | bytes 524288 | tf_op jit(solution)/shard_map/join_pieces/pallas_call | solution.py:352
  54.3 6.6 %all-to-all-start.2 = ((bf16[8,80,128]{2,1,0:T(8,128)(2,1)}), bf16[8,80,128]{2,1,0:T(8,128)(2,1)S(1)}, u32[]{:S(2)}, u32[]{:S(2)}) async-start(bf16[8,80,128]{2,1,0:T(8,128)(2,1)} %join_pieces.2), calls=%async_computation.2 | async-start | bytes 327680 | tf_op jit(solution)/shard_map/all_to_all | solution.py:393
  61.0 0.9 %collective-permute-start.12 = (bf16[64,1024]{1,0:T(8,128)(2,1)S(1)}, bf16[64,1024]{1,0:T(8,128)(2,1)S(1)}, u32[]{:S(2)}, u32[]{:S(2)}) collective-permute-start(bf16[64,1024]{1,0:T(8,128)(2,1)S(1)} %add_select_fusion.refs_0_), channel_id=1, source_target_pairs={{0,24},{8,16},{16,8},{24,0},{1,25},{9,17},{17,9},{25,1},{2,26},{10... | collective-permute-start | bytes 393224 | tf_op jit(solution)/shard_map/ppermute | solution.py:407
  61.9 2.1 %collective-permute-start.11 = (bf16[64,1024]{1,0:T(8,128)(2,1)S(1)}, bf16[64,1024]{1,0:T(8,128)(2,1)S(1)}, u32[]{:S(2)}, u32[]{:S(2)}) collective-permute-start(bf16[64,1024]{1,0:T(8,128)(2,1)S(1)} %add_select_fusion.refs_0_), channel_id=1, source_target_pairs={{0,16},{8,24},{16,0},{24,8},{1,17},{9,25},{17,1},{25,9},{2,18},{10... | collective-permute-start | bytes 393224 | tf_op jit(solution)/shard_map/ppermute | solution.py:407
  64.0 1.1 %collective-permute-start.10 = (bf16[64,1024]{1,0:T(8,128)(2,1)S(1)}, bf16[64,1024]{1,0:T(8,128)(2,1)S(1)}, u32[]{:S(2)}, u32[]{:S(2)}) collective-permute-start(bf16[64,1024]{1,0:T(8,128)(2,1)S(1)} %add_select_fusion.refs_0_), channel_id=1, source_target_pairs={{0,8},{8,0},{16,24},{24,16},{1,9},{9,1},{17,25},{25,17},{2,10},{10... | collective-permute-start | bytes 393224 | tf_op jit(solution)/shard_map/ppermute | solution.py:407
  65.1 1.6 %all-to-all-done.2.refs_0_ = bf16[8,80,128]{2,1,0:T(8,128)(2,1)S(1)} async-done(((bf16[8,80,128]{2,1,0:T(8,128)(2,1)}), bf16[8,80,128]{2,1,0:T(8,128)(2,1)S(1)}, u32[]{:S(2)}, u32[]{:S(2)}) %all-to-all-start.2) | async-done | bytes 163872 | tf_op jit(solution)/shard_map/all_to_all | solution.py:393
  66.8 1.1 %join_pieces.3 = bf16[16,64,128]{2,1,0:T(8,128)(2,1)} custom-call(bf16[8,80,128]{2,1,0:T(8,128)(2,1)S(1)} %all-to-all-done.2.refs_0_), custom_call_target="tpu_custom_call" | custom-call | flops 3000000000 | bytes 524288 | tf_op jit(solution)/shard_map/join_pieces/pallas_call | solution.py:352
  67.8 5.5 %all-to-all-start.3 = ((bf16[16,64,128]{2,1,0:T(8,128)(2,1)}), bf16[16,64,128]{2,1,0:T(8,128)(2,1)S(1)}, u32[]{:S(2)}, u32[]{:S(2)}) async-start(bf16[16,64,128]{2,1,0:T(8,128)(2,1)} %join_pieces.3), calls=%async_computation.3 | async-start | bytes 524288 | tf_op jit(solution)/shard_map/all_to_all | solution.py:393
  73.4 6.8 %context_attention.1 = (bf16[256,4096]{1,0:T(8,128)(2,1)}, bf16[32,4096]{1,0:T(8,128)(2,1)}) custom-call(s32[1]{0:T(128)S(6)} %copy.12.len_ref, bf16[256,4096]{1,0:T(8,128)(2,1)S(1)} %copy-done.2, bf16[256,512]{1,0:T(8,128)(2,1)S(1)} %copy-done, bf16[256,512]{1,0:T(8,128)(2,1)S(1)} %copy-done.1, bf16[64,1024]{1,0:T(8,128)(2,1)S(1)} %add_select_fusion.refs_0_, ...), custom_call_target="tpu_custom_call" | custom-call | flops 2147483648 | bytes 5242880 | tf_op jit(solution)/shard_map/context_attention/pallas_call | solution.py:113
  (42 shorter events, 2.3 us)
Async XLA Ops:
  3.6 26.7 %copy-start.4 = (bf16[64,1024]{1,0:T(8,128)(2,1)S(1)}, bf16[64,1024]{1,0:T(8,128)(2,1)}, u32[]{:S(2)}) copy-start(bf16[64,1024]{1,0:T(8,128)(2,1)} %get-tuple-element.26) | copy-start | bytes 393220
  3.6 16.0 %all-to-all-start = ((bf16[32,32,128]{2,1,0:T(8,128)(2,1)}), bf16[32,32,128]{2,1,0:T(8,128)(2,1)S(1)}, u32[]{:S(2)}, u32[]{:S(2)}) async-start(bf16[32,32,128]{2,1,0:T(8,128)(2,1)} %get-tuple-element.27), calls=%async_computation | async-start | bytes 524288 | tf_op jit(solution)/shard_map/all_to_all | solution.py:393
  11.4 8.2 %collective-permute-start = (bf16[64,1024]{1,0:T(8,128)(2,1)}, bf16[64,1024]{1,0:T(8,128)(2,1)S(1)}, u32[]{:S(2)}, u32[]{:S(2)}) collective-permute-start(bf16[64,1024]{1,0:T(8,128)(2,1)} %get-tuple-element.28), channel_id=1, source_target_pairs={{0,8},{1,9}} | collective-permute-start | bytes 393224 | tf_op jit(solution)/shard_map/ppermute | solution.py:404
  12.7 6.9 %collective-permute-start.1 = (bf16[64,1024]{1,0:T(8,128)(2,1)}, bf16[64,1024]{1,0:T(8,128)(2,1)S(1)}, u32[]{:S(2)}, u32[]{:S(2)}) collective-permute-start(bf16[64,1024]{1,0:T(8,128)(2,1)} %get-tuple-element.29), channel_id=1, source_target_pairs={{0,16},{1,17}} | collective-permute-start | bytes 393224 | tf_op jit(solution)/shard_map/ppermute | solution.py:404
  13.4 6.3 %collective-permute-start.2 = (bf16[64,1024]{1,0:T(8,128)(2,1)}, bf16[64,1024]{1,0:T(8,128)(2,1)S(1)}, u32[]{:S(2)}, u32[]{:S(2)}) collective-permute-start(bf16[64,1024]{1,0:T(8,128)(2,1)} %get-tuple-element.30), channel_id=1, source_target_pairs={{0,24},{1,25}} | collective-permute-start | bytes 393224 | tf_op jit(solution)/shard_map/ppermute | solution.py:404
  14.0 20.5 %collective-permute-start.13 = (bf16[576,128]{1,0:T(8,128)(2,1)}, bf16[576,128]{1,0:T(8,128)(2,1)S(1)}, u32[]{:S(2)}, u32[]{:S(2)}) collective-permute-start(bf16[576,128]{1,0:T(8,128)(2,1)} %get-tuple-element.37), channel_id=1, source_target_pairs={{0,6},{2,4},{4,2},{6,0},{1,7},{3,5},{5,3},{7,1},{8,14},{10,12},{12... | collective-permute-start | bytes 442376 | tf_op jit(solution)/shard_map/ppermute | solution.py:407
  16.2 18.3 %collective-permute-start.14 = (bf16[576,128]{1,0:T(8,128)(2,1)}, bf16[576,128]{1,0:T(8,128)(2,1)S(1)}, u32[]{:S(2)}, u32[]{:S(2)}) collective-permute-start(bf16[576,128]{1,0:T(8,128)(2,1)} %get-tuple-element.38), channel_id=1, source_target_pairs={{0,4},{2,6},{4,0},{6,2},{1,5},{3,7},{5,1},{7,3},{8,12},{10,14},{12... | collective-permute-start | bytes 442376 | tf_op jit(solution)/shard_map/ppermute | solution.py:407
  19.6 14.9 %collective-permute-start.15 = (bf16[576,128]{1,0:T(8,128)(2,1)}, bf16[576,128]{1,0:T(8,128)(2,1)S(1)}, u32[]{:S(2)}, u32[]{:S(2)}) collective-permute-start(bf16[576,128]{1,0:T(8,128)(2,1)} %get-tuple-element.39), channel_id=1, source_target_pairs={{0,2},{2,0},{4,6},{6,4},{1,3},{3,1},{5,7},{7,5},{8,10},{10,8},{12,... | collective-permute-start | bytes 442376 | tf_op jit(solution)/shard_map/ppermute | solution.py:407
  20.3 14.2 %all-to-all-start.1 = ((bf16[8,64,128]{2,1,0:T(8,128)(2,1)}), bf16[8,64,128]{2,1,0:T(8,128)(2,1)S(1)}, u32[]{:S(2)}, u32[]{:S(2)}) async-start(bf16[8,64,128]{2,1,0:T(8,128)(2,1)} %choose.2), calls=%async_computation.1 | async-start | bytes 262144 | tf_op jit(solution)/shard_map/all_to_all | solution.py:393
  30.3 14.4 %copy-start.3 = (bf16[576,128]{1,0:T(8,128)(2,1)S(1)}, bf16[576,128]{1,0:T(8,128)(2,1)}, u32[]{:S(2)}) copy-start(bf16[576,128]{1,0:T(8,128)(2,1)} %get-tuple-element.41.refs_4_) | copy-start | bytes 442372
  30.3 8.4 %collective-permute-start.4 = (bf16[64,1024]{1,0:T(8,128)(2,1)S(1)}, bf16[64,1024]{1,0:T(8,128)(2,1)S(1)}, u32[]{:S(2)}, u32[]{:S(2)}) collective-permute-start(bf16[64,1024]{1,0:T(8,128)(2,1)S(1)} %add_select_fusion.3), channel_id=1, source_target_pairs={{0,160},{8,168},{16,176},{24,184},{1,161},{9,169},{17,177},{25,185}} | collective-permute-start | bytes 393224 | tf_op jit(solution)/shard_map/ppermute | solution.py:404
  32.9 5.8 %collective-permute-start.3 = (bf16[64,1024]{1,0:T(8,128)(2,1)S(1)}, bf16[64,1024]{1,0:T(8,128)(2,1)S(1)}, u32[]{:S(2)}, u32[]{:S(2)}) collective-permute-start(bf16[64,1024]{1,0:T(8,128)(2,1)S(1)} %add_select_fusion.3), channel_id=1, source_target_pairs={{0,96},{8,104},{16,112},{24,120},{1,97},{9,105},{17,113},{25,121}} | collective-permute-start | bytes 393224 | tf_op jit(solution)/shard_map/ppermute | solution.py:404
  34.5 8.9 %collective-permute-start.18 = (bf16[64,128]{1,0:T(8,128)(2,1)S(1)}, bf16[64,128]{1,0:T(8,128)(2,1)S(1)}, u32[]{:S(2)}, u32[]{:S(2)}) collective-permute-start(bf16[64,128]{1,0:T(8,128)(2,1)S(1)} %choose.3.refs_0_), channel_id=1, source_target_pairs={{0,24},{8,16},{16,8},{24,0},{1,25},{9,17},{17,9},{25,1},{2,26},{10... | collective-permute-start | bytes 49160 | tf_op jit(solution)/shard_map/ppermute | solution.py:407
  35.4 9.4 %collective-permute-start.17 = (bf16[64,128]{1,0:T(8,128)(2,1)S(1)}, bf16[64,128]{1,0:T(8,128)(2,1)S(1)}, u32[]{:S(2)}, u32[]{:S(2)}) collective-permute-start(bf16[64,128]{1,0:T(8,128)(2,1)S(1)} %choose.3.refs_0_), channel_id=1, source_target_pairs={{0,16},{8,24},{16,0},{24,8},{1,17},{9,25},{17,1},{25,9},{2,18},{10... | collective-permute-start | bytes 49160 | tf_op jit(solution)/shard_map/ppermute | solution.py:407
  38.2 6.5 %collective-permute-start.16 = (bf16[64,128]{1,0:T(8,128)(2,1)S(1)}, bf16[64,128]{1,0:T(8,128)(2,1)S(1)}, u32[]{:S(2)}, u32[]{:S(2)}) collective-permute-start(bf16[64,128]{1,0:T(8,128)(2,1)S(1)} %choose.3.refs_0_), channel_id=1, source_target_pairs={{0,8},{8,0},{16,24},{24,16},{1,9},{9,1},{17,25},{25,17},{2,10},{10... | collective-permute-start | bytes 49160 | tf_op jit(solution)/shard_map/ppermute | solution.py:407
  38.7 10.6 %collective-permute-start.7 = (bf16[64,1024]{1,0:T(8,128)(2,1)S(1)}, bf16[64,1024]{1,0:T(8,128)(2,1)S(1)}, u32[]{:S(2)}, u32[]{:S(2)}) collective-permute-start(bf16[64,1024]{1,0:T(8,128)(2,1)S(1)} %add_select_fusion.2), channel_id=1, source_target_pairs={{0,6},{8,14},{16,22},{24,30},{96,102},{104,110},{112,118},{120,126... | collective-permute-start | bytes 393224 | tf_op jit(solution)/shard_map/ppermute | solution.py:404
  42.1 7.9 %collective-permute-start.6 = (bf16[64,1024]{1,0:T(8,128)(2,1)S(1)}, bf16[64,1024]{1,0:T(8,128)(2,1)S(1)}, u32[]{:S(2)}, u32[]{:S(2)}) collective-permute-start(bf16[64,1024]{1,0:T(8,128)(2,1)S(1)} %add_select_fusion.2), channel_id=1, source_target_pairs={{0,4},{8,12},{16,20},{24,28},{96,100},{104,108},{112,116},{120,124... | collective-permute-start | bytes 393224 | tf_op jit(solution)/shard_map/ppermute | solution.py:404
  43.4 6.6 %collective-permute-start.5 = (bf16[64,1024]{1,0:T(8,128)(2,1)S(1)}, bf16[64,1024]{1,0:T(8,128)(2,1)S(1)}, u32[]{:S(2)}, u32[]{:S(2)}) collective-permute-start(bf16[64,1024]{1,0:T(8,128)(2,1)S(1)} %add_select_fusion.2), channel_id=1, source_target_pairs={{0,2},{8,10},{16,18},{24,26},{96,98},{104,106},{112,114},{120,122}... | collective-permute-start | bytes 393224 | tf_op jit(solution)/shard_map/ppermute | solution.py:404
  45.8 6.2 %collective-permute-start.19 = (bf16[144,128]{1,0:T(8,128)(2,1)S(1)}, bf16[144,128]{1,0:T(8,128)(2,1)S(1)}, u32[]{:S(2)}, u32[]{:S(2)}) collective-permute-start(bf16[144,128]{1,0:T(8,128)(2,1)S(1)} %get-tuple-element.46), channel_id=1, source_target_pairs={{0,24},{8,16},{16,8},{24,0},{1,25},{9,17},{17,9},{25,1},{2,26},{10... | collective-permute-start | bytes 110600 | tf_op jit(solution)/shard_map/ppermute | solution.py:407
  47.2 5.5 %collective-permute-start.20 = (bf16[144,128]{1,0:T(8,128)(2,1)S(1)}, bf16[144,128]{1,0:T(8,128)(2,1)S(1)}, u32[]{:S(2)}, u32[]{:S(2)}) collective-permute-start(bf16[144,128]{1,0:T(8,128)(2,1)S(1)} %get-tuple-element.47), channel_id=1, source_target_pairs={{0,16},{8,24},{16,0},{24,8},{1,17},{9,25},{17,1},{25,9},{2,18},{10... | collective-permute-start | bytes 110600 | tf_op jit(solution)/shard_map/ppermute | solution.py:407
  49.3 4.0 %collective-permute-start.21 = (bf16[144,128]{1,0:T(8,128)(2,1)S(1)}, bf16[144,128]{1,0:T(8,128)(2,1)S(1)}, u32[]{:S(2)}, u32[]{:S(2)}) collective-permute-start(bf16[144,128]{1,0:T(8,128)(2,1)S(1)} %get-tuple-element.48), channel_id=1, source_target_pairs={{0,8},{8,0},{16,24},{24,16},{1,9},{9,1},{17,25},{25,17},{2,10},{10... | collective-permute-start | bytes 110600 | tf_op jit(solution)/shard_map/ppermute | solution.py:407
  50.0 10.8 %collective-permute-start.9 = (bf16[64,1024]{1,0:T(8,128)(2,1)S(1)}, bf16[64,1024]{1,0:T(8,128)(2,1)S(1)}, u32[]{:S(2)}, u32[]{:S(2)}) collective-permute-start(bf16[64,1024]{1,0:T(8,128)(2,1)S(1)} %add_select_fusion.1), channel_id=1, source_target_pairs={{96,64},{98,66},{100,68},{102,70},{104,72},{106,74},{108,76},{110,... | collective-permute-start | bytes 393224 | tf_op jit(solution)/shard_map/ppermute | solution.py:404
  50.7 10.2 %collective-permute-start.8 = (bf16[64,1024]{1,0:T(8,128)(2,1)S(1)}, bf16[64,1024]{1,0:T(8,128)(2,1)S(1)}, u32[]{:S(2)}, u32[]{:S(2)}) collective-permute-start(bf16[64,1024]{1,0:T(8,128)(2,1)S(1)} %add_select_fusion.1), channel_id=1, source_target_pairs={{0,32},{2,34},{4,36},{6,38},{8,40},{10,42},{12,44},{14,46},{16,48}... | collective-permute-start | bytes 393224 | tf_op jit(solution)/shard_map/ppermute | solution.py:404
  54.3 12.5 %all-to-all-start.2 = ((bf16[8,80,128]{2,1,0:T(8,128)(2,1)}), bf16[8,80,128]{2,1,0:T(8,128)(2,1)S(1)}, u32[]{:S(2)}, u32[]{:S(2)}) async-start(bf16[8,80,128]{2,1,0:T(8,128)(2,1)} %join_pieces.2), calls=%async_computation.2 | async-start | bytes 327680 | tf_op jit(solution)/shard_map/all_to_all | solution.py:393
  60.9 12.4 %copy-start = (bf16[256,512]{1,0:T(8,128)(2,1)S(1)}, bf16[256,512]{1,0:T(8,128)(2,1)}, u32[]{:S(2)}) copy-start(bf16[256,512]{1,0:T(8,128)(2,1)} %k_ref.3) | copy-start | bytes 786436
  60.9 12.4 %copy-start.1 = (bf16[256,512]{1,0:T(8,128)(2,1)S(1)}, bf16[256,512]{1,0:T(8,128)(2,1)}, u32[]{:S(2)}) copy-start(bf16[256,512]{1,0:T(8,128)(2,1)} %v_ref.3) | copy-start | bytes 786436
  60.9 12.4 %copy-start.2 = (bf16[256,4096]{1,0:T(8,128)(2,1)S(1)}, bf16[256,4096]{1,0:T(8,128)(2,1)}, u32[]{:S(2)}) copy-start(bf16[256,4096]{1,0:T(8,128)(2,1)} %q_ref.1) | copy-start | bytes 6291460
  61.0 12.4 %collective-permute-start.12 = (bf16[64,1024]{1,0:T(8,128)(2,1)S(1)}, bf16[64,1024]{1,0:T(8,128)(2,1)S(1)}, u32[]{:S(2)}, u32[]{:S(2)}) collective-permute-start(bf16[64,1024]{1,0:T(8,128)(2,1)S(1)} %add_select_fusion.refs_0_), channel_id=1, source_target_pairs={{0,24},{8,16},{16,8},{24,0},{1,25},{9,17},{17,9},{25,1},{2,26},{10... | collective-permute-start | bytes 393224 | tf_op jit(solution)/shard_map/ppermute | solution.py:407
  61.9 11.4 %collective-permute-start.11 = (bf16[64,1024]{1,0:T(8,128)(2,1)S(1)}, bf16[64,1024]{1,0:T(8,128)(2,1)S(1)}, u32[]{:S(2)}, u32[]{:S(2)}) collective-permute-start(bf16[64,1024]{1,0:T(8,128)(2,1)S(1)} %add_select_fusion.refs_0_), channel_id=1, source_target_pairs={{0,16},{8,24},{16,0},{24,8},{1,17},{9,25},{17,1},{25,9},{2,18},{10... | collective-permute-start | bytes 393224 | tf_op jit(solution)/shard_map/ppermute | solution.py:407
  64.0 9.3 %collective-permute-start.10 = (bf16[64,1024]{1,0:T(8,128)(2,1)S(1)}, bf16[64,1024]{1,0:T(8,128)(2,1)S(1)}, u32[]{:S(2)}, u32[]{:S(2)}) collective-permute-start(bf16[64,1024]{1,0:T(8,128)(2,1)S(1)} %add_select_fusion.refs_0_), channel_id=1, source_target_pairs={{0,8},{8,0},{16,24},{24,16},{1,9},{9,1},{17,25},{25,17},{2,10},{10... | collective-permute-start | bytes 393224 | tf_op jit(solution)/shard_map/ppermute | solution.py:407
  67.8 12.4 %all-to-all-start.3 = ((bf16[16,64,128]{2,1,0:T(8,128)(2,1)}), bf16[16,64,128]{2,1,0:T(8,128)(2,1)S(1)}, u32[]{:S(2)}, u32[]{:S(2)}) async-start(bf16[16,64,128]{2,1,0:T(8,128)(2,1)} %join_pieces.3), calls=%async_computation.3 | async-start | bytes 524288 | tf_op jit(solution)/shard_map/all_to_all | solution.py:393

commit v9 on v7

--- a/solution.py
+++ b/solution.py
@@ -417,7 +417,7 @@
     moved, lines = lax.optimization_barrier((moved, lines))
     anchor = jnp.where(z == 0, anchor, got[0] + got[1])
     rows = [(to * n_x + i) * n_y for to in (0, 3, 5) for i in range(n_x)]
-    got = [move(anchor, [(p, p + j) for p in rows]) for j in range(1, n_y)]
+    got = [move(anchor, [(p, p + j) for p in rows]) for j in (3, 2, 1)]
     queries = [moved] + [shift_x(moved, i) for i in range(1, n_x)]
 
     partials = request_partials(query_owner, queries, lines, own_rows)

time: 80.8 us -> 80.8 us (level)
  no operation moved by 1% of the time
where the time goes in v9:
time: 80.8 us; the launch traced here: 79.7 us
  starting transfers between devices  61 us (75%)
  Pallas kernels  13 us (16%)
  waiting for transfers between devices  3.21 us (4%)
  between operations  2.4 us (3%)
    all_to_all x4, starting transfers between devices, exchange(): lax.all_to_all(x, axis, split_axis=0, concat_axis=0, axis_index_groups=gr...  28.7 us
    ppermute x10, starting transfers between devices, move(): return lax.ppermute(value, ('z', 'x', 'y'), pairs)  15.3 us
    ppermute x9, starting transfers between devices, shift_x(): lax.ppermute(value, 'x', [(a, (a + count) % n_x) for a in range(n_x)])  13.3 us
    pallas_call x1, Pallas kernels, context_attention(): pl.pallas_call(functools.partial(context_kernel, len(anchor)), out_shape=...  6.78 us
    ppermute x3, starting transfers between devices, local(): lax.ppermute(lines[i], 'y', [(a, (a + i) % n_y) for a in range(n_y)])  3.82 us
    pallas_call x1, Pallas kernels, prepare(): pl.pallas_call(functools.partial(prepare_kernel, n_x, n_y), out_shape=sha...  2.36 us
    pallas_call x2, Pallas kernels, join(): pl.pallas_call(functools.partial(join_kernel, parts_in, keep_code), out_s...  2.04 us
  transfers between devices with their start and end apart: 26, of which 3 were waited for; matrix products, arithmetic and copies ran while one was open for 0% of the time, Pallas kernels for 13%

profile of v9, /device:TPU:2, one launch (start us, length us, event | category | flops | bytes accessed | tf_op | source)
XLA Modules:
  0.0 79.7 jit_solution(416674753689855814)
XLA Ops:
  1.3 2.4 %prepare.1 = (bf16[32,32,128]{2,1,0:T(8,128)(2,1)}, bf16[64,1024]{1,0:T(8,128)(2,1)}, bf16[64,1024]{1,0:T(8,128)(2,1)}, bf16[64,1024]{1,0:T(8,128)(2,1)}, bf16[6...) custom-call(s32[1]{0:T(128)S(6)} %copy.12.len_ref, ...), custom_call_target="tpu_custom_call" | custom-call | flops 262144 | bytes 2621440 | tf_op jit(solution)/shard_map/prepare/pallas_call | solution.py:180
  3.6 7.8 %all-to-all-start = ((bf16[32,32,128]{2,1,0:T(8,128)(2,1)}), bf16[32,32,128]{2,1,0:T(8,128)(2,1)S(1)}, u32[]{:S(2)}, u32[]{:S(2)}) async-start(bf16[32,32,128]{2,1,0:T(8,128)(2,1)} %get-tuple-element.27), calls=%async_computation | async-start | bytes 524288 | tf_op jit(solution)/shard_map/all_to_all | solution.py:386
  11.4 1.3 %collective-permute-start = (bf16[64,1024]{1,0:T(8,128)(2,1)}, bf16[64,1024]{1,0:T(8,128)(2,1)S(1)}, u32[]{:S(2)}, u32[]{:S(2)}) collective-permute-start(bf16[64,1024]{1,0:T(8,128)(2,1)} %get-tuple-element.28), channel_id=1, source_target_pairs={{0,8},{1,9}} | collective-permute-start | bytes 393224 | tf_op jit(solution)/shard_map/ppermute | solution.py:397
  12.7 0.7 collective-permute-start.1
  13.4 0.7 collective-permute-start.2
  14.1 0.9 %collective-permute-start.13 = (bf16[576,128]{1,0:T(8,128)(2,1)}, bf16[576,128]{1,0:T(8,128)(2,1)S(1)}, u32[]{:S(2)}, u32[]{:S(2)}) collective-permute-start(bf16[576,128]{1,0:T(8,128)(2,1)} %get-tuple-element.37), channel_id=1, source_target_pairs={{0,2},{2,4},{4,6},{6,0},{1,3},{3,5},{5,7},{7,1},{8,10},{10,12},{12... | collective-permute-start | bytes 442376 | tf_op jit(solution)/shard_map/ppermute | solution.py:406
  15.0 2.7 %collective-permute-start.14 = (bf16[576,128]{1,0:T(8,128)(2,1)}, bf16[576,128]{1,0:T(8,128)(2,1)S(1)}, u32[]{:S(2)}, u32[]{:S(2)}) collective-permute-start(bf16[576,128]{1,0:T(8,128)(2,1)} %get-tuple-element.38), channel_id=1, source_target_pairs={{0,4},{2,6},{4,0},{6,2},{1,5},{3,7},{5,1},{7,3},{8,12},{10,14},{12... | collective-permute-start | bytes 442376 | tf_op jit(solution)/shard_map/ppermute | solution.py:406
  18.3 1.3 %collective-permute-done = bf16[64,1024]{1,0:T(8,128)(2,1)S(1)} collective-permute-done((bf16[64,1024]{1,0:T(8,128)(2,1)}, bf16[64,1024]{1,0:T(8,128)(2,1)S(1)}, u32[]{:S(2)}, u32[]{:S(2)}) %collective-permute-start) | collective-permute-done | bytes 131104 | tf_op jit(solution)/shard_map/ppermute | solution.py:397
  19.9 0.7 choose.2
  20.5 9.2 %all-to-all-start.1 = ((bf16[8,64,128]{2,1,0:T(8,128)(2,1)}), bf16[8,64,128]{2,1,0:T(8,128)(2,1)S(1)}, u32[]{:S(2)}, u32[]{:S(2)}) async-start(bf16[8,64,128]{2,1,0:T(8,128)(2,1)} %choose.2), calls=%async_computation.1 | async-start | bytes 262144 | tf_op jit(solution)/shard_map/all_to_all | solution.py:386
  29.8 4.4 %collective-permute-start.4 = (bf16[64,1024]{1,0:T(8,128)(2,1)S(1)}, bf16[64,1024]{1,0:T(8,128)(2,1)S(1)}, u32[]{:S(2)}, u32[]{:S(2)}) collective-permute-start(bf16[64,1024]{1,0:T(8,128)(2,1)S(1)} %add_select_fusion.3), channel_id=1, source_target_pairs={{0,160},{8,168},{16,176},{24,184},{1,161},{9,169},{17,177},{25,185}} | collective-permute-start | bytes 393224 | tf_op jit(solution)/shard_map/ppermute | solution.py:397
  34.1 1.6 %collective-permute-start.3 = (bf16[64,1024]{1,0:T(8,128)(2,1)S(1)}, bf16[64,1024]{1,0:T(8,128)(2,1)S(1)}, u32[]{:S(2)}, u32[]{:S(2)}) collective-permute-start(bf16[64,1024]{1,0:T(8,128)(2,1)S(1)} %add_select_fusion.3), channel_id=1, source_target_pairs={{0,96},{8,104},{16,112},{24,120},{1,97},{9,105},{17,113},{25,121}} | collective-permute-start | bytes 393224 | tf_op jit(solution)/shard_map/ppermute | solution.py:397
  35.8 0.8 %collective-permute-start.18 = (bf16[64,128]{1,0:T(8,128)(2,1)S(1)}, bf16[64,128]{1,0:T(8,128)(2,1)S(1)}, u32[]{:S(2)}, u32[]{:S(2)}) collective-permute-start(bf16[64,128]{1,0:T(8,128)(2,1)S(1)} %choose.3.refs_0_), channel_id=1, source_target_pairs={{0,24},{8,0},{16,8},{24,16},{1,25},{9,1},{17,9},{25,17},{2,26},{10... | collective-permute-start | bytes 49160 | tf_op jit(solution)/shard_map/ppermute | solution.py:400
  36.6 2.2 %collective-permute-start.17 = (bf16[64,128]{1,0:T(8,128)(2,1)S(1)}, bf16[64,128]{1,0:T(8,128)(2,1)S(1)}, u32[]{:S(2)}, u32[]{:S(2)}) collective-permute-start(bf16[64,128]{1,0:T(8,128)(2,1)S(1)} %choose.3.refs_0_), channel_id=1, source_target_pairs={{0,16},{8,24},{16,0},{24,8},{1,17},{9,25},{17,1},{25,9},{2,18},{10... | collective-permute-start | bytes 49160 | tf_op jit(solution)/shard_map/ppermute | solution.py:400
  38.8 1.8 %collective-permute-start.16 = (bf16[64,128]{1,0:T(8,128)(2,1)S(1)}, bf16[64,128]{1,0:T(8,128)(2,1)S(1)}, u32[]{:S(2)}, u32[]{:S(2)}) collective-permute-start(bf16[64,128]{1,0:T(8,128)(2,1)S(1)} %choose.3.refs_0_), channel_id=1, source_target_pairs={{0,8},{8,16},{16,24},{24,0},{1,9},{9,17},{17,25},{25,1},{2,10},{10... | collective-permute-start | bytes 49160 | tf_op jit(solution)/shard_map/ppermute | solution.py:400
  40.7 2.1 %collective-permute-start.7 = (bf16[64,1024]{1,0:T(8,128)(2,1)S(1)}, bf16[64,1024]{1,0:T(8,128)(2,1)S(1)}, u32[]{:S(2)}, u32[]{:S(2)}) collective-permute-start(bf16[64,1024]{1,0:T(8,128)(2,1)S(1)} %add_select_fusion.2), channel_id=1, source_target_pairs={{0,2},{8,10},{16,18},{24,26},{96,98},{104,106},{112,114},{120,122}... | collective-permute-start | bytes 393224 | tf_op jit(solution)/shard_map/ppermute | solution.py:397
  42.8 1.3 %collective-permute-start.6 = (bf16[64,1024]{1,0:T(8,128)(2,1)S(1)}, bf16[64,1024]{1,0:T(8,128)(2,1)S(1)}, u32[]{:S(2)}, u32[]{:S(2)}) collective-permute-start(bf16[64,1024]{1,0:T(8,128)(2,1)S(1)} %add_select_fusion.2), channel_id=1, source_target_pairs={{0,4},{8,12},{16,20},{24,28},{96,100},{104,108},{112,116},{120,124... | collective-permute-start | bytes 393224 | tf_op jit(solution)/shard_map/ppermute | solution.py:397
  44.1 1.3 %collective-permute-start.5 = (bf16[64,1024]{1,0:T(8,128)(2,1)S(1)}, bf16[64,1024]{1,0:T(8,128)(2,1)S(1)}, u32[]{:S(2)}, u32[]{:S(2)}) collective-permute-start(bf16[64,1024]{1,0:T(8,128)(2,1)S(1)} %add_select_fusion.2), channel_id=1, source_target_pairs={{0,6},{8,14},{16,22},{24,30},{96,102},{104,110},{112,118},{120,126... | collective-permute-start | bytes 393224 | tf_op jit(solution)/shard_map/ppermute | solution.py:397
  45.5 1.1 %request_partials.1 = (bf16[144,128]{1,0:T(8,128)(2,1)S(1)}, bf16[144,128]{1,0:T(8,128)(2,1)S(1)}, bf16[144,128]{1,0:T(8,128)(2,1)S(1)}, bf16[144,128]{1,0:T(8,128)(2,1)S(1)}) custom-call(s32[1]{0:T(128)S(6)} %copy.13.owner_ref, bf16[64,128]{1,0:T(8,128)(2,1)S(1)} %choose.3.refs_0_, bf16[64,128]{1,0:T(8,128)(2,1)S(1)} %collective-permute-done.16.refs_1_, ...), custom_call_target="tpu_custom_call" | custom-call | flops 3000000000 | bytes 1048576 | tf_op jit(solution)/shard_map/request_partials/pallas_call | solution.py:287
  46.8 1.4 %collective-permute-start.20 = (bf16[144,128]{1,0:T(8,128)(2,1)S(1)}, bf16[144,128]{1,0:T(8,128)(2,1)S(1)}, u32[]{:S(2)}, u32[]{:S(2)}) collective-permute-start(bf16[144,128]{1,0:T(8,128)(2,1)S(1)} %get-tuple-element.47), channel_id=1, source_target_pairs={{0,16},{8,24},{16,0},{24,8},{1,17},{9,25},{17,1},{25,9},{2,18},{10... | collective-permute-start | bytes 110600 | tf_op jit(solution)/shard_map/ppermute | solution.py:400
  48.2 2.4 %collective-permute-start.21 = (bf16[144,128]{1,0:T(8,128)(2,1)S(1)}, bf16[144,128]{1,0:T(8,128)(2,1)S(1)}, u32[]{:S(2)}, u32[]{:S(2)}) collective-permute-start(bf16[144,128]{1,0:T(8,128)(2,1)S(1)} %get-tuple-element.48), channel_id=1, source_target_pairs={{0,8},{8,16},{16,24},{24,0},{1,9},{9,17},{17,25},{25,1},{2,10},{10... | collective-permute-start | bytes 110600 | tf_op jit(solution)/shard_map/ppermute | solution.py:400
  50.6 0.7 collective-permute-start.9
  51.3 1.3 %collective-permute-start.8 = (bf16[64,1024]{1,0:T(8,128)(2,1)S(1)}, bf16[64,1024]{1,0:T(8,128)(2,1)S(1)}, u32[]{:S(2)}, u32[]{:S(2)}) collective-permute-start(bf16[64,1024]{1,0:T(8,128)(2,1)S(1)} %add_select_fusion.1), channel_id=1, source_target_pairs={{0,32},{2,34},{4,36},{6,38},{8,40},{10,42},{12,44},{14,46},{16,48}... | collective-permute-start | bytes 393224 | tf_op jit(solution)/shard_map/ppermute | solution.py:397
  53.0 1.0 %join_pieces.2 = bf16[8,80,128]{2,1,0:T(8,128)(2,1)} custom-call(bf16[144,128]{1,0:T(8,128)(2,1)S(1)} %get-tuple-element.45.refs_0_, bf16[144,128]{1,0:T(8,128)(2,1)S(1)} %collective-permute-done.19.refs_1_, bf16[144,128]{1,0:T(8,128)(2,1)S(1)} %collective-permute-done.20.refs_2_, bf16[144,128]{1,0:T(8,128)(2,1)S(1)} %collective-permute-done.21.refs_3_), custom_call_target="tpu_custom_call" | custom-call | flops 3000000000 | bytes 524288 | tf_op jit(solution)/shard_map/join_pieces/pallas_call | solution.py:345
  54.0 6.0 %all-to-all-start.2 = ((bf16[8,80,128]{2,1,0:T(8,128)(2,1)}), bf16[8,80,128]{2,1,0:T(8,128)(2,1)S(1)}, u32[]{:S(2)}, u32[]{:S(2)}) async-start(bf16[8,80,128]{2,1,0:T(8,128)(2,1)} %join_pieces.2), calls=%async_computation.2 | async-start | bytes 327680 | tf_op jit(solution)/shard_map/all_to_all | solution.py:386
  60.0 2.1 %collective-permute-start.12 = (bf16[64,1024]{1,0:T(8,128)(2,1)S(1)}, bf16[64,1024]{1,0:T(8,128)(2,1)S(1)}, u32[]{:S(2)}, u32[]{:S(2)}) collective-permute-start(bf16[64,1024]{1,0:T(8,128)(2,1)S(1)} %add_select_fusion.refs_0_), channel_id=1, source_target_pairs={{0,24},{8,0},{16,8},{24,16},{1,25},{9,1},{17,9},{25,17},{2,26},{10... | collective-permute-start | bytes 393224 | tf_op jit(solution)/shard_map/ppermute | solution.py:400
  62.2 1.1 %collective-permute-start.11 = (bf16[64,1024]{1,0:T(8,128)(2,1)S(1)}, bf16[64,1024]{1,0:T(8,128)(2,1)S(1)}, u32[]{:S(2)}, u32[]{:S(2)}) collective-permute-start(bf16[64,1024]{1,0:T(8,128)(2,1)S(1)} %add_select_fusion.refs_0_), channel_id=1, source_target_pairs={{0,16},{8,24},{16,0},{24,8},{1,17},{9,25},{17,1},{25,9},{2,18},{10... | collective-permute-start | bytes 393224 | tf_op jit(solution)/shard_map/ppermute | solution.py:400
  63.3 1.1 %collective-permute-start.10 = (bf16[64,1024]{1,0:T(8,128)(2,1)S(1)}, bf16[64,1024]{1,0:T(8,128)(2,1)S(1)}, u32[]{:S(2)}, u32[]{:S(2)}) collective-permute-start(bf16[64,1024]{1,0:T(8,128)(2,1)S(1)} %add_select_fusion.refs_0_), channel_id=1, source_target_pairs={{0,8},{8,16},{16,24},{24,0},{1,9},{9,17},{17,25},{25,1},{2,10},{10... | collective-permute-start | bytes 393224 | tf_op jit(solution)/shard_map/ppermute | solution.py:400
  64.4 1.5 %all-to-all-done.2.refs_0_ = bf16[8,80,128]{2,1,0:T(8,128)(2,1)S(1)} async-done(((bf16[8,80,128]{2,1,0:T(8,128)(2,1)}), bf16[8,80,128]{2,1,0:T(8,128)(2,1)S(1)}, u32[]{:S(2)}, u32[]{:S(2)}) %all-to-all-start.2) | async-done | bytes 163872 | tf_op jit(solution)/shard_map/all_to_all | solution.py:386
  65.9 1.1 %join_pieces.3 = bf16[16,64,128]{2,1,0:T(8,128)(2,1)} custom-call(bf16[8,80,128]{2,1,0:T(8,128)(2,1)S(1)} %all-to-all-done.2.refs_0_), custom_call_target="tpu_custom_call" | custom-call | flops 3000000000 | bytes 524288 | tf_op jit(solution)/shard_map/join_pieces/pallas_call | solution.py:345
  66.9 5.8 %all-to-all-start.3 = ((bf16[16,64,128]{2,1,0:T(8,128)(2,1)}), bf16[16,64,128]{2,1,0:T(8,128)(2,1)S(1)}, u32[]{:S(2)}, u32[]{:S(2)}) async-start(bf16[16,64,128]{2,1,0:T(8,128)(2,1)} %join_pieces.3), calls=%async_computation.3 | async-start | bytes 524288 | tf_op jit(solution)/shard_map/all_to_all | solution.py:386
  72.8 6.8 %context_attention.1 = (bf16[256,4096]{1,0:T(8,128)(2,1)}, bf16[32,4096]{1,0:T(8,128)(2,1)}) custom-call(s32[1]{0:T(128)S(6)} %copy.12.len_ref, bf16[256,4096]{1,0:T(8,128)(2,1)S(1)} %copy-done.2, bf16[256,512]{1,0:T(8,128)(2,1)S(1)} %copy-done, bf16[256,512]{1,0:T(8,128)(2,1)S(1)} %copy-done.1, bf16[64,1024]{1,0:T(8,128)(2,1)S(1)} %add_select_fusion.refs_0_, ...), custom_call_target="tpu_custom_call" | custom-call | flops 2147483648 | bytes 5242880 | tf_op jit(solution)/shard_map/context_attention/pallas_call | solution.py:111
  (42 shorter events, 1.1 us)
Async XLA Ops:
  3.6 26.1 %copy-start.4 = (bf16[64,1024]{1,0:T(8,128)(2,1)S(1)}, bf16[64,1024]{1,0:T(8,128)(2,1)}, u32[]{:S(2)}) copy-start(bf16[64,1024]{1,0:T(8,128)(2,1)} %get-tuple-element.26) | copy-start | bytes 393220
  3.6 16.2 %all-to-all-start = ((bf16[32,32,128]{2,1,0:T(8,128)(2,1)}), bf16[32,32,128]{2,1,0:T(8,128)(2,1)S(1)}, u32[]{:S(2)}, u32[]{:S(2)}) async-start(bf16[32,32,128]{2,1,0:T(8,128)(2,1)} %get-tuple-element.27), calls=%async_computation | async-start | bytes 524288 | tf_op jit(solution)/shard_map/all_to_all | solution.py:386
  11.4 8.2 %collective-permute-start = (bf16[64,1024]{1,0:T(8,128)(2,1)}, bf16[64,1024]{1,0:T(8,128)(2,1)S(1)}, u32[]{:S(2)}, u32[]{:S(2)}) collective-permute-start(bf16[64,1024]{1,0:T(8,128)(2,1)} %get-tuple-element.28), channel_id=1, source_target_pairs={{0,8},{1,9}} | collective-permute-start | bytes 393224 | tf_op jit(solution)/shard_map/ppermute | solution.py:397
  12.7 7.2 %collective-permute-start.1 = (bf16[64,1024]{1,0:T(8,128)(2,1)}, bf16[64,1024]{1,0:T(8,128)(2,1)S(1)}, u32[]{:S(2)}, u32[]{:S(2)}) collective-permute-start(bf16[64,1024]{1,0:T(8,128)(2,1)} %get-tuple-element.29), channel_id=1, source_target_pairs={{0,16},{1,17}} | collective-permute-start | bytes 393224 | tf_op jit(solution)/shard_map/ppermute | solution.py:397
  13.4 6.5 %collective-permute-start.2 = (bf16[64,1024]{1,0:T(8,128)(2,1)}, bf16[64,1024]{1,0:T(8,128)(2,1)S(1)}, u32[]{:S(2)}, u32[]{:S(2)}) collective-permute-start(bf16[64,1024]{1,0:T(8,128)(2,1)} %get-tuple-element.30), channel_id=1, source_target_pairs={{0,24},{1,25}} | collective-permute-start | bytes 393224 | tf_op jit(solution)/shard_map/ppermute | solution.py:397
  14.1 21.7 %collective-permute-start.13 = (bf16[576,128]{1,0:T(8,128)(2,1)}, bf16[576,128]{1,0:T(8,128)(2,1)S(1)}, u32[]{:S(2)}, u32[]{:S(2)}) collective-permute-start(bf16[576,128]{1,0:T(8,128)(2,1)} %get-tuple-element.37), channel_id=1, source_target_pairs={{0,2},{2,4},{4,6},{6,0},{1,3},{3,5},{5,7},{7,1},{8,10},{10,12},{12... | collective-permute-start | bytes 442376 | tf_op jit(solution)/shard_map/ppermute | solution.py:406
  15.0 20.8 %collective-permute-start.14 = (bf16[576,128]{1,0:T(8,128)(2,1)}, bf16[576,128]{1,0:T(8,128)(2,1)S(1)}, u32[]{:S(2)}, u32[]{:S(2)}) collective-permute-start(bf16[576,128]{1,0:T(8,128)(2,1)} %get-tuple-element.38), channel_id=1, source_target_pairs={{0,4},{2,6},{4,0},{6,2},{1,5},{3,7},{5,1},{7,3},{8,12},{10,14},{12... | collective-permute-start | bytes 442376 | tf_op jit(solution)/shard_map/ppermute | solution.py:406
  19.6 16.1 %collective-permute-start.15 = (bf16[576,128]{1,0:T(8,128)(2,1)}, bf16[576,128]{1,0:T(8,128)(2,1)S(1)}, u32[]{:S(2)}, u32[]{:S(2)}) collective-permute-start(bf16[576,128]{1,0:T(8,128)(2,1)} %get-tuple-element.39), channel_id=1, source_target_pairs={{0,6},{2,0},{4,2},{6,4},{1,7},{3,1},{5,3},{7,5},{8,14},{10,8},{12,... | collective-permute-start | bytes 442376 | tf_op jit(solution)/shard_map/ppermute | solution.py:406
  20.5 15.2 %all-to-all-start.1 = ((bf16[8,64,128]{2,1,0:T(8,128)(2,1)}), bf16[8,64,128]{2,1,0:T(8,128)(2,1)S(1)}, u32[]{:S(2)}, u32[]{:S(2)}) async-start(bf16[8,64,128]{2,1,0:T(8,128)(2,1)} %choose.2), calls=%async_computation.1 | async-start | bytes 262144 | tf_op jit(solution)/shard_map/all_to_all | solution.py:386
  29.7 15.7 %copy-start.3 = (bf16[576,128]{1,0:T(8,128)(2,1)S(1)}, bf16[576,128]{1,0:T(8,128)(2,1)}, u32[]{:S(2)}) copy-start(bf16[576,128]{1,0:T(8,128)(2,1)} %get-tuple-element.41.refs_4_) | copy-start | bytes 442372
  29.8 10.9 %collective-permute-start.4 = (bf16[64,1024]{1,0:T(8,128)(2,1)S(1)}, bf16[64,1024]{1,0:T(8,128)(2,1)S(1)}, u32[]{:S(2)}, u32[]{:S(2)}) collective-permute-start(bf16[64,1024]{1,0:T(8,128)(2,1)S(1)} %add_select_fusion.3), channel_id=1, source_target_pairs={{0,160},{8,168},{16,176},{24,184},{1,161},{9,169},{17,177},{25,185}} | collective-permute-start | bytes 393224 | tf_op jit(solution)/shard_map/ppermute | solution.py:397
  34.1 6.5 %collective-permute-start.3 = (bf16[64,1024]{1,0:T(8,128)(2,1)S(1)}, bf16[64,1024]{1,0:T(8,128)(2,1)S(1)}, u32[]{:S(2)}, u32[]{:S(2)}) collective-permute-start(bf16[64,1024]{1,0:T(8,128)(2,1)S(1)} %add_select_fusion.3), channel_id=1, source_target_pairs={{0,96},{8,104},{16,112},{24,120},{1,97},{9,105},{17,113},{25,121}} | collective-permute-start | bytes 393224 | tf_op jit(solution)/shard_map/ppermute | solution.py:397
  35.8 8.3 %collective-permute-start.18 = (bf16[64,128]{1,0:T(8,128)(2,1)S(1)}, bf16[64,128]{1,0:T(8,128)(2,1)S(1)}, u32[]{:S(2)}, u32[]{:S(2)}) collective-permute-start(bf16[64,128]{1,0:T(8,128)(2,1)S(1)} %choose.3.refs_0_), channel_id=1, source_target_pairs={{0,24},{8,0},{16,8},{24,16},{1,25},{9,1},{17,9},{25,17},{2,26},{10... | collective-permute-start | bytes 49160 | tf_op jit(solution)/shard_map/ppermute | solution.py:400
  36.6 8.8 %collective-permute-start.17 = (bf16[64,128]{1,0:T(8,128)(2,1)S(1)}, bf16[64,128]{1,0:T(8,128)(2,1)S(1)}, u32[]{:S(2)}, u32[]{:S(2)}) collective-permute-start(bf16[64,128]{1,0:T(8,128)(2,1)S(1)} %choose.3.refs_0_), channel_id=1, source_target_pairs={{0,16},{8,24},{16,0},{24,8},{1,17},{9,25},{17,1},{25,9},{2,18},{10... | collective-permute-start | bytes 49160 | tf_op jit(solution)/shard_map/ppermute | solution.py:400
  38.8 6.6 %collective-permute-start.16 = (bf16[64,128]{1,0:T(8,128)(2,1)S(1)}, bf16[64,128]{1,0:T(8,128)(2,1)S(1)}, u32[]{:S(2)}, u32[]{:S(2)}) collective-permute-start(bf16[64,128]{1,0:T(8,128)(2,1)S(1)} %choose.3.refs_0_), channel_id=1, source_target_pairs={{0,8},{8,16},{16,24},{24,0},{1,9},{9,17},{17,25},{25,1},{2,10},{10... | collective-permute-start | bytes 49160 | tf_op jit(solution)/shard_map/ppermute | solution.py:400
  40.7 7.5 %collective-permute-start.7 = (bf16[64,1024]{1,0:T(8,128)(2,1)S(1)}, bf16[64,1024]{1,0:T(8,128)(2,1)S(1)}, u32[]{:S(2)}, u32[]{:S(2)}) collective-permute-start(bf16[64,1024]{1,0:T(8,128)(2,1)S(1)} %add_select_fusion.2), channel_id=1, source_target_pairs={{0,2},{8,10},{16,18},{24,26},{96,98},{104,106},{112,114},{120,122}... | collective-permute-start | bytes 393224 | tf_op jit(solution)/shard_map/ppermute | solution.py:397
  42.8 7.8 %collective-permute-start.6 = (bf16[64,1024]{1,0:T(8,128)(2,1)S(1)}, bf16[64,1024]{1,0:T(8,128)(2,1)S(1)}, u32[]{:S(2)}, u32[]{:S(2)}) collective-permute-start(bf16[64,1024]{1,0:T(8,128)(2,1)S(1)} %add_select_fusion.2), channel_id=1, source_target_pairs={{0,4},{8,12},{16,20},{24,28},{96,100},{104,108},{112,116},{120,124... | collective-permute-start | bytes 393224 | tf_op jit(solution)/shard_map/ppermute | solution.py:397
  44.1 6.5 %collective-permute-start.5 = (bf16[64,1024]{1,0:T(8,128)(2,1)S(1)}, bf16[64,1024]{1,0:T(8,128)(2,1)S(1)}, u32[]{:S(2)}, u32[]{:S(2)}) collective-permute-start(bf16[64,1024]{1,0:T(8,128)(2,1)S(1)} %add_select_fusion.2), channel_id=1, source_target_pairs={{0,6},{8,14},{16,22},{24,30},{96,102},{104,110},{112,118},{120,126... | collective-permute-start | bytes 393224 | tf_op jit(solution)/shard_map/ppermute | solution.py:397
  46.5 6.1 %collective-permute-start.19 = (bf16[144,128]{1,0:T(8,128)(2,1)S(1)}, bf16[144,128]{1,0:T(8,128)(2,1)S(1)}, u32[]{:S(2)}, u32[]{:S(2)}) collective-permute-start(bf16[144,128]{1,0:T(8,128)(2,1)S(1)} %get-tuple-element.46), channel_id=1, source_target_pairs={{0,24},{8,0},{16,8},{24,16},{1,25},{9,1},{17,9},{25,17},{2,26},{10... | collective-permute-start | bytes 110600 | tf_op jit(solution)/shard_map/ppermute | solution.py:400
  46.8 5.8 %collective-permute-start.20 = (bf16[144,128]{1,0:T(8,128)(2,1)S(1)}, bf16[144,128]{1,0:T(8,128)(2,1)S(1)}, u32[]{:S(2)}, u32[]{:S(2)}) collective-permute-start(bf16[144,128]{1,0:T(8,128)(2,1)S(1)} %get-tuple-element.47), channel_id=1, source_target_pairs={{0,16},{8,24},{16,0},{24,8},{1,17},{9,25},{17,1},{25,9},{2,18},{10... | collective-permute-start | bytes 110600 | tf_op jit(solution)/shard_map/ppermute | solution.py:400
  48.2 4.8 %collective-permute-start.21 = (bf16[144,128]{1,0:T(8,128)(2,1)S(1)}, bf16[144,128]{1,0:T(8,128)(2,1)S(1)}, u32[]{:S(2)}, u32[]{:S(2)}) collective-permute-start(bf16[144,128]{1,0:T(8,128)(2,1)S(1)} %get-tuple-element.48), channel_id=1, source_target_pairs={{0,8},{8,16},{16,24},{24,0},{1,9},{9,17},{17,25},{25,1},{2,10},{10... | collective-permute-start | bytes 110600 | tf_op jit(solution)/shard_map/ppermute | solution.py:400
  50.6 9.3 %collective-permute-start.9 = (bf16[64,1024]{1,0:T(8,128)(2,1)S(1)}, bf16[64,1024]{1,0:T(8,128)(2,1)S(1)}, u32[]{:S(2)}, u32[]{:S(2)}) collective-permute-start(bf16[64,1024]{1,0:T(8,128)(2,1)S(1)} %add_select_fusion.1), channel_id=1, source_target_pairs={{96,64},{98,66},{100,68},{102,70},{104,72},{106,74},{108,76},{110,... | collective-permute-start | bytes 393224 | tf_op jit(solution)/shard_map/ppermute | solution.py:397
  51.3 8.7 %collective-permute-start.8 = (bf16[64,1024]{1,0:T(8,128)(2,1)S(1)}, bf16[64,1024]{1,0:T(8,128)(2,1)S(1)}, u32[]{:S(2)}, u32[]{:S(2)}) collective-permute-start(bf16[64,1024]{1,0:T(8,128)(2,1)S(1)} %add_select_fusion.1), channel_id=1, source_target_pairs={{0,32},{2,34},{4,36},{6,38},{8,40},{10,42},{12,44},{14,46},{16,48}... | collective-permute-start | bytes 393224 | tf_op jit(solution)/shard_map/ppermute | solution.py:397
  54.0 11.9 %all-to-all-start.2 = ((bf16[8,80,128]{2,1,0:T(8,128)(2,1)}), bf16[8,80,128]{2,1,0:T(8,128)(2,1)S(1)}, u32[]{:S(2)}, u32[]{:S(2)}) async-start(bf16[8,80,128]{2,1,0:T(8,128)(2,1)} %join_pieces.2), calls=%async_computation.2 | async-start | bytes 327680 | tf_op jit(solution)/shard_map/all_to_all | solution.py:386
  60.0 12.7 %copy-start = (bf16[256,512]{1,0:T(8,128)(2,1)S(1)}, bf16[256,512]{1,0:T(8,128)(2,1)}, u32[]{:S(2)}) copy-start(bf16[256,512]{1,0:T(8,128)(2,1)} %k_ref.3) | copy-start | bytes 786436
  60.0 12.7 %copy-start.1 = (bf16[256,512]{1,0:T(8,128)(2,1)S(1)}, bf16[256,512]{1,0:T(8,128)(2,1)}, u32[]{:S(2)}) copy-start(bf16[256,512]{1,0:T(8,128)(2,1)} %v_ref.3) | copy-start | bytes 786436
  60.0 12.7 %copy-start.2 = (bf16[256,4096]{1,0:T(8,128)(2,1)S(1)}, bf16[256,4096]{1,0:T(8,128)(2,1)}, u32[]{:S(2)}) copy-start(bf16[256,4096]{1,0:T(8,128)(2,1)} %q_ref.1) | copy-start | bytes 6291460
  60.0 12.7 %collective-permute-start.12 = (bf16[64,1024]{1,0:T(8,128)(2,1)S(1)}, bf16[64,1024]{1,0:T(8,128)(2,1)S(1)}, u32[]{:S(2)}, u32[]{:S(2)}) collective-permute-start(bf16[64,1024]{1,0:T(8,128)(2,1)S(1)} %add_select_fusion.refs_0_), channel_id=1, source_target_pairs={{0,24},{8,0},{16,8},{24,16},{1,25},{9,1},{17,9},{25,17},{2,26},{10... | collective-permute-start | bytes 393224 | tf_op jit(solution)/shard_map/ppermute | solution.py:400
  62.2 10.5 %collective-permute-start.11 = (bf16[64,1024]{1,0:T(8,128)(2,1)S(1)}, bf16[64,1024]{1,0:T(8,128)(2,1)S(1)}, u32[]{:S(2)}, u32[]{:S(2)}) collective-permute-start(bf16[64,1024]{1,0:T(8,128)(2,1)S(1)} %add_select_fusion.refs_0_), channel_id=1, source_target_pairs={{0,16},{8,24},{16,0},{24,8},{1,17},{9,25},{17,1},{25,9},{2,18},{10... | collective-permute-start | bytes 393224 | tf_op jit(solution)/shard_map/ppermute | solution.py:400
  63.3 9.4 %collective-permute-start.10 = (bf16[64,1024]{1,0:T(8,128)(2,1)S(1)}, bf16[64,1024]{1,0:T(8,128)(2,1)S(1)}, u32[]{:S(2)}, u32[]{:S(2)}) collective-permute-start(bf16[64,1024]{1,0:T(8,128)(2,1)S(1)} %add_select_fusion.refs_0_), channel_id=1, source_target_pairs={{0,8},{8,16},{16,24},{24,0},{1,9},{9,17},{17,25},{25,1},{2,10},{10... | collective-permute-start | bytes 393224 | tf_op jit(solution)/shard_map/ppermute | solution.py:400
  66.9 12.6 %all-to-all-start.3 = ((bf16[16,64,128]{2,1,0:T(8,128)(2,1)}), bf16[16,64,128]{2,1,0:T(8,128)(2,1)S(1)}, u32[]{:S(2)}, u32[]{:S(2)}) async-start(bf16[16,64,128]{2,1,0:T(8,128)(2,1)} %join_pieces.3), calls=%async_computation.3 | async-start | bytes 524288 | tf_op jit(solution)/shard_map/all_to_all | solution.py:386

commit v10 on v9

--- a/solution.py
+++ b/solution.py
@@ -16,6 +16,7 @@
 VMEM_LIMIT = 32 * 1024 * 1024
 STACK = 4
 N_X, N_Y = 4, 4
+PLANES = (4, 2, 1, 7, 5, 6, 3, 0)
 
 
 def place():
@@ -202,7 +203,11 @@
 
 
 def line_kernel(owner_ref, x_ref, o_ref):
-    o_ref[...] = x_ref[x_ref.shape[0] - 1 - lax.div(owner_ref[0], N_X * N_Y)]
+    owner_z = lax.div(owner_ref[0], N_X * N_Y)
+    spot = 0
+    for i, z in enumerate(PLANES):
+        spot = jnp.where(owner_z == z, i, spot)
+    o_ref[...] = x_ref[spot]
 
 
 def choose(kernel, owner, x, shape, flops):
@@ -410,25 +415,25 @@
     moved, got = lax.optimization_barrier((moved, got))
     moved = choose(plane_kernel, query_owner, moved, (n_z,) + piece, 8 * 10**8)
     anchor = jnp.where(x == 0, pieces[0], got[0] + got[1] + got[2])
-    got = [move(anchor, [(i * n_y, (to * n_x + i) * n_y) for i in range(n_x)]) for to in (3, 5)]
-    moved = exchange(moved, "z", down)
+    got = [move(anchor, [(i * n_y, (to * n_x + i) * n_y) for i in range(n_x)]) for to in (6, 3)]
+    moved = exchange(moved, "z", [list(PLANES)])
 
     moved = choose(line_kernel, query_owner, moved, piece, 3 * 10**9)
     moved, lines = lax.optimization_barrier((moved, lines))
     anchor = jnp.where(z == 0, anchor, got[0] + got[1])
-    rows = [(to * n_x + i) * n_y for to in (0, 3, 5) for i in range(n_x)]
+    rows = [(to * n_x + i) * n_y for to in (0, 3, 6) for i in range(n_x)]
     got = [move(anchor, [(p, p + j) for p in rows]) for j in (3, 2, 1)]
     queries = [moved] + [shift_x(moved, i) for i in range(1, n_x)]
 
     partials = request_partials(query_owner, queries, lines, own_rows)
     anchor = jnp.where(y == 0, anchor, got[0] + got[1] + got[2])
     plane = range(n_xy)
-    steps = (((0, 1), (3, 4), (5, 6)), ((3, 2), (5, 7)))
+    steps = (((0, 1), (3, 4), (6, 7)), ((3, 2), (6, 5)))
     got = [move(anchor, [(a * n_xy + p, b * n_xy + p) for a, b in step for p in plane]) for step in steps]
     partials = [partials[0]] + [shift_x(partials[i], n_x - i) for i in range(1, n_x)]
 
     planes = join(partials, n_z, 2, True)
-    anchor = jnp.where((z == 0) | (z == 3) | (z == 5), anchor, got[0] + got[1])
+    anchor = jnp.where((z == 0) | (z == 3) | (z == 6), anchor, got[0] + got[1])
     anchors = [anchor]
     for i in range(1, n_x):
         anchors.append(shift_x(anchor, i))

time: 80.8 us -> 81.9 us (1.014)
  starting transfers between devices: 61 us -> 62.6 us
    all_to_all x4, starting transfers between devices: 28.7 us -> 31.9 us  [exchange(): lax.all_to_all(x, axis, split_axis=0, concat_axis=0, axis_index_groups=gr...]
    ppermute x10, starting transfers between devices: 15.3 us -> 13.1 us  [move(): return lax.ppermute(value, ('z', 'x', 'y'), pairs)]
where the time goes in v10:
time: 81.9 us; the launch traced here: 80.7 us
  starting transfers between devices  62.6 us (76%)
  Pallas kernels  13 us (16%)
  waiting for transfers between devices  2.59 us (3%)
  between operations  2.4 us (3%)
    all_to_all x4, starting transfers between devices, exchange(): lax.all_to_all(x, axis, split_axis=0, concat_axis=0, axis_index_groups=gr...  31.9 us
    ppermute x9, starting transfers between devices, shift_x(): lax.ppermute(value, 'x', [(a, (a + count) % n_x) for a in range(n_x)])  13.9 us
    ppermute x10, starting transfers between devices, move(): return lax.ppermute(value, ('z', 'x', 'y'), pairs)  13.1 us
    pallas_call x1, Pallas kernels, context_attention(): pl.pallas_call(functools.partial(context_kernel, len(anchor)), out_shape=...  6.79 us
    ppermute x3, starting transfers between devices, local(): lax.ppermute(lines[i], 'y', [(a, (a + i) % n_y) for a in range(n_y)])  3.82 us
    pallas_call x1, Pallas kernels, prepare(): pl.pallas_call(functools.partial(prepare_kernel, n_x, n_y), out_shape=sha...  2.36 us
    pallas_call x2, Pallas kernels, join(): pl.pallas_call(functools.partial(join_kernel, parts_in, keep_code), out_s...  2.04 us
  transfers between devices with their start and end apart: 26, of which 3 were waited for; matrix products, arithmetic and copies ran while one was open for 0% of the time, Pallas kernels for 13%

profile of v10, /device:TPU:2, one launch (start us, length us, event | category | flops | bytes accessed | tf_op | source)
XLA Modules:
  0.0 80.7 jit_solution(17417415163513426805)
XLA Ops:
  1.3 2.4 %prepare.1 = (bf16[32,32,128]{2,1,0:T(8,128)(2,1)}, bf16[64,1024]{1,0:T(8,128)(2,1)}, bf16[64,1024]{1,0:T(8,128)(2,1)}, bf16[64,1024]{1,0:T(8,128)(2,1)}, bf16[6...) custom-call(s32[1]{0:T(128)S(6)} %copy.12.len_ref, ...), custom_call_target="tpu_custom_call" | custom-call | flops 262144 | bytes 2621440 | tf_op jit(solution)/shard_map/prepare/pallas_call | solution.py:181
  3.6 7.8 %all-to-all-start = ((bf16[32,32,128]{2,1,0:T(8,128)(2,1)}), bf16[32,32,128]{2,1,0:T(8,128)(2,1)S(1)}, u32[]{:S(2)}, u32[]{:S(2)}) async-start(bf16[32,32,128]{2,1,0:T(8,128)(2,1)} %get-tuple-element.27), calls=%async_computation | async-start | bytes 524288 | tf_op jit(solution)/shard_map/all_to_all | solution.py:391
  11.4 1.3 %collective-permute-start = (bf16[64,1024]{1,0:T(8,128)(2,1)}, bf16[64,1024]{1,0:T(8,128)(2,1)S(1)}, u32[]{:S(2)}, u32[]{:S(2)}) collective-permute-start(bf16[64,1024]{1,0:T(8,128)(2,1)} %get-tuple-element.28), channel_id=1, source_target_pairs={{0,8},{1,9}} | collective-permute-start | bytes 393224 | tf_op jit(solution)/shard_map/ppermute | solution.py:402
  12.7 0.7 collective-permute-start.1
  13.4 0.7 collective-permute-start.2
  14.1 0.9 %collective-permute-start.13 = (bf16[576,128]{1,0:T(8,128)(2,1)}, bf16[576,128]{1,0:T(8,128)(2,1)S(1)}, u32[]{:S(2)}, u32[]{:S(2)}) collective-permute-start(bf16[576,128]{1,0:T(8,128)(2,1)} %get-tuple-element.37), channel_id=1, source_target_pairs={{0,2},{2,4},{4,6},{6,0},{1,3},{3,5},{5,7},{7,1},{8,10},{10,12},{12... | collective-permute-start | bytes 442376 | tf_op jit(solution)/shard_map/ppermute | solution.py:411
  15.0 2.7 %collective-permute-start.14 = (bf16[576,128]{1,0:T(8,128)(2,1)}, bf16[576,128]{1,0:T(8,128)(2,1)S(1)}, u32[]{:S(2)}, u32[]{:S(2)}) collective-permute-start(bf16[576,128]{1,0:T(8,128)(2,1)} %get-tuple-element.38), channel_id=1, source_target_pairs={{0,4},{2,6},{4,0},{6,2},{1,5},{3,7},{5,1},{7,3},{8,12},{10,14},{12... | collective-permute-start | bytes 442376 | tf_op jit(solution)/shard_map/ppermute | solution.py:411
  18.3 1.3 %collective-permute-done = bf16[64,1024]{1,0:T(8,128)(2,1)S(1)} collective-permute-done((bf16[64,1024]{1,0:T(8,128)(2,1)}, bf16[64,1024]{1,0:T(8,128)(2,1)S(1)}, u32[]{:S(2)}, u32[]{:S(2)}) %collective-permute-start) | collective-permute-done | bytes 131104 | tf_op jit(solution)/shard_map/ppermute | solution.py:402
  19.9 0.7 choose.2
  20.5 10.5 %all-to-all-start.1 = ((bf16[8,64,128]{2,1,0:T(8,128)(2,1)}), bf16[8,64,128]{2,1,0:T(8,128)(2,1)S(1)}, u32[]{:S(2)}, u32[]{:S(2)}) async-start(bf16[8,64,128]{2,1,0:T(8,128)(2,1)} %choose.2), calls=%async_computation.1 | async-start | bytes 262144 | tf_op jit(solution)/shard_map/all_to_all | solution.py:391
  31.1 2.6 %collective-permute-start.4 = (bf16[64,1024]{1,0:T(8,128)(2,1)S(1)}, bf16[64,1024]{1,0:T(8,128)(2,1)S(1)}, u32[]{:S(2)}, u32[]{:S(2)}) collective-permute-start(bf16[64,1024]{1,0:T(8,128)(2,1)S(1)} %add_select_fusion.3), channel_id=1, source_target_pairs={{0,96},{8,104},{16,112},{24,120},{1,97},{9,105},{17,113},{25,121}} | collective-permute-start | bytes 393224 | tf_op jit(solution)/shard_map/ppermute | solution.py:402
  33.7 1.3 %collective-permute-start.3 = (bf16[64,1024]{1,0:T(8,128)(2,1)S(1)}, bf16[64,1024]{1,0:T(8,128)(2,1)S(1)}, u32[]{:S(2)}, u32[]{:S(2)}) collective-permute-start(bf16[64,1024]{1,0:T(8,128)(2,1)S(1)} %add_select_fusion.3), channel_id=1, source_target_pairs={{0,192},{8,200},{16,208},{24,216},{1,193},{9,201},{17,209},{25,217}} | collective-permute-start | bytes 393224 | tf_op jit(solution)/shard_map/ppermute | solution.py:402
  35.1 1.1 %collective-permute-start.18 = (bf16[64,128]{1,0:T(8,128)(2,1)S(1)}, bf16[64,128]{1,0:T(8,128)(2,1)S(1)}, u32[]{:S(2)}, u32[]{:S(2)}) collective-permute-start(bf16[64,128]{1,0:T(8,128)(2,1)S(1)} %choose.3.refs_0_), channel_id=1, source_target_pairs={{0,24},{8,0},{16,8},{24,16},{1,25},{9,1},{17,9},{25,17},{2,26},{10... | collective-permute-start | bytes 49160 | tf_op jit(solution)/shard_map/ppermute | solution.py:405
  36.1 1.9 %collective-permute-start.17 = (bf16[64,128]{1,0:T(8,128)(2,1)S(1)}, bf16[64,128]{1,0:T(8,128)(2,1)S(1)}, u32[]{:S(2)}, u32[]{:S(2)}) collective-permute-start(bf16[64,128]{1,0:T(8,128)(2,1)S(1)} %choose.3.refs_0_), channel_id=1, source_target_pairs={{0,16},{8,24},{16,0},{24,8},{1,17},{9,25},{17,1},{25,9},{2,18},{10... | collective-permute-start | bytes 49160 | tf_op jit(solution)/shard_map/ppermute | solution.py:405
  38.1 1.8 %collective-permute-start.16 = (bf16[64,128]{1,0:T(8,128)(2,1)S(1)}, bf16[64,128]{1,0:T(8,128)(2,1)S(1)}, u32[]{:S(2)}, u32[]{:S(2)}) collective-permute-start(bf16[64,128]{1,0:T(8,128)(2,1)S(1)} %choose.3.refs_0_), channel_id=1, source_target_pairs={{0,8},{8,16},{16,24},{24,0},{1,9},{9,17},{17,25},{25,1},{2,10},{10... | collective-permute-start | bytes 49160 | tf_op jit(solution)/shard_map/ppermute | solution.py:405
  39.9 2.0 %collective-permute-start.7 = (bf16[64,1024]{1,0:T(8,128)(2,1)S(1)}, bf16[64,1024]{1,0:T(8,128)(2,1)S(1)}, u32[]{:S(2)}, u32[]{:S(2)}) collective-permute-start(bf16[64,1024]{1,0:T(8,128)(2,1)S(1)} %add_select_fusion.2), channel_id=1, source_target_pairs={{0,2},{8,10},{16,18},{24,26},{96,98},{104,106},{112,114},{120,122}... | collective-permute-start | bytes 393224 | tf_op jit(solution)/shard_map/ppermute | solution.py:402
  42.0 1.3 %collective-permute-start.6 = (bf16[64,1024]{1,0:T(8,128)(2,1)S(1)}, bf16[64,1024]{1,0:T(8,128)(2,1)S(1)}, u32[]{:S(2)}, u32[]{:S(2)}) collective-permute-start(bf16[64,1024]{1,0:T(8,128)(2,1)S(1)} %add_select_fusion.2), channel_id=1, source_target_pairs={{0,4},{8,12},{16,20},{24,28},{96,100},{104,108},{112,116},{120,124... | collective-permute-start | bytes 393224 | tf_op jit(solution)/shard_map/ppermute | solution.py:402
  43.3 1.3 %collective-permute-start.5 = (bf16[64,1024]{1,0:T(8,128)(2,1)S(1)}, bf16[64,1024]{1,0:T(8,128)(2,1)S(1)}, u32[]{:S(2)}, u32[]{:S(2)}) collective-permute-start(bf16[64,1024]{1,0:T(8,128)(2,1)S(1)} %add_select_fusion.2), channel_id=1, source_target_pairs={{0,6},{8,14},{16,22},{24,30},{96,102},{104,110},{112,118},{120,126... | collective-permute-start | bytes 393224 | tf_op jit(solution)/shard_map/ppermute | solution.py:402
  44.6 1.1 %request_partials.1 = (bf16[144,128]{1,0:T(8,128)(2,1)S(1)}, bf16[144,128]{1,0:T(8,128)(2,1)S(1)}, bf16[144,128]{1,0:T(8,128)(2,1)S(1)}, bf16[144,128]{1,0:T(8,128)(2,1)S(1)}) custom-call(s32[1]{0:T(128)S(6)} %copy.13.owner_ref, bf16[64,128]{1,0:T(8,128)(2,1)S(1)} %choose.3.refs_0_, bf16[64,128]{1,0:T(8,128)(2,1)S(1)} %collective-permute-done.16.refs_1_, ...), custom_call_target="tpu_custom_call" | custom-call | flops 3000000000 | bytes 1048576 | tf_op jit(solution)/shard_map/request_partials/pallas_call | solution.py:292
  45.9 2.1 %collective-permute-start.20 = (bf16[144,128]{1,0:T(8,128)(2,1)S(1)}, bf16[144,128]{1,0:T(8,128)(2,1)S(1)}, u32[]{:S(2)}, u32[]{:S(2)}) collective-permute-start(bf16[144,128]{1,0:T(8,128)(2,1)S(1)} %get-tuple-element.47), channel_id=1, source_target_pairs={{0,16},{8,24},{16,0},{24,8},{1,17},{9,25},{17,1},{25,9},{2,18},{10... | collective-permute-start | bytes 110600 | tf_op jit(solution)/shard_map/ppermute | solution.py:405
  48.1 1.9 %collective-permute-start.21 = (bf16[144,128]{1,0:T(8,128)(2,1)S(1)}, bf16[144,128]{1,0:T(8,128)(2,1)S(1)}, u32[]{:S(2)}, u32[]{:S(2)}) collective-permute-start(bf16[144,128]{1,0:T(8,128)(2,1)S(1)} %get-tuple-element.48), channel_id=1, source_target_pairs={{0,8},{8,16},{16,24},{24,0},{1,9},{9,17},{17,25},{25,1},{2,10},{10... | collective-permute-start | bytes 110600 | tf_op jit(solution)/shard_map/ppermute | solution.py:405
  50.0 0.7 collective-permute-start.9
  50.7 1.3 %collective-permute-start.8 = (bf16[64,1024]{1,0:T(8,128)(2,1)S(1)}, bf16[64,1024]{1,0:T(8,128)(2,1)S(1)}, u32[]{:S(2)}, u32[]{:S(2)}) collective-permute-start(bf16[64,1024]{1,0:T(8,128)(2,1)S(1)} %add_select_fusion.1), channel_id=1, source_target_pairs={{0,32},{2,34},{4,36},{6,38},{8,40},{10,42},{12,44},{14,46},{16,48}... | collective-permute-start | bytes 393224 | tf_op jit(solution)/shard_map/ppermute | solution.py:402
  52.2 1.0 %join_pieces.2 = bf16[8,80,128]{2,1,0:T(8,128)(2,1)} custom-call(bf16[144,128]{1,0:T(8,128)(2,1)S(1)} %get-tuple-element.45.refs_0_, bf16[144,128]{1,0:T(8,128)(2,1)S(1)} %collective-permute-done.19.refs_1_, bf16[144,128]{1,0:T(8,128)(2,1)S(1)} %collective-permute-done.20.refs_2_, bf16[144,128]{1,0:T(8,128)(2,1)S(1)} %collective-permute-done.21.refs_3_), custom_call_target="tpu_custom_call" | custom-call | flops 3000000000 | bytes 524288 | tf_op jit(solution)/shard_map/join_pieces/pallas_call | solution.py:350
  53.1 7.8 %all-to-all-start.2 = ((bf16[8,80,128]{2,1,0:T(8,128)(2,1)}), bf16[8,80,128]{2,1,0:T(8,128)(2,1)S(1)}, u32[]{:S(2)}, u32[]{:S(2)}) async-start(bf16[8,80,128]{2,1,0:T(8,128)(2,1)} %join_pieces.2), calls=%async_computation.2 | async-start | bytes 327680 | tf_op jit(solution)/shard_map/all_to_all | solution.py:391
  61.1 1.5 %collective-permute-start.12 = (bf16[64,1024]{1,0:T(8,128)(2,1)S(1)}, bf16[64,1024]{1,0:T(8,128)(2,1)S(1)}, u32[]{:S(2)}, u32[]{:S(2)}) collective-permute-start(bf16[64,1024]{1,0:T(8,128)(2,1)S(1)} %add_select_fusion.refs_0_), channel_id=1, source_target_pairs={{0,24},{8,0},{16,8},{24,16},{1,25},{9,1},{17,9},{25,17},{2,26},{10... | collective-permute-start | bytes 393224 | tf_op jit(solution)/shard_map/ppermute | solution.py:405
  62.5 2.3 %collective-permute-start.11 = (bf16[64,1024]{1,0:T(8,128)(2,1)S(1)}, bf16[64,1024]{1,0:T(8,128)(2,1)S(1)}, u32[]{:S(2)}, u32[]{:S(2)}) collective-permute-start(bf16[64,1024]{1,0:T(8,128)(2,1)S(1)} %add_select_fusion.refs_0_), channel_id=1, source_target_pairs={{0,16},{8,24},{16,0},{24,8},{1,17},{9,25},{17,1},{25,9},{2,18},{10... | collective-permute-start | bytes 393224 | tf_op jit(solution)/shard_map/ppermute | solution.py:405
  64.8 1.0 %collective-permute-start.10 = (bf16[64,1024]{1,0:T(8,128)(2,1)S(1)}, bf16[64,1024]{1,0:T(8,128)(2,1)S(1)}, u32[]{:S(2)}, u32[]{:S(2)}) collective-permute-start(bf16[64,1024]{1,0:T(8,128)(2,1)S(1)} %add_select_fusion.refs_0_), channel_id=1, source_target_pairs={{0,8},{8,16},{16,24},{24,0},{1,9},{9,17},{17,25},{25,1},{2,10},{10... | collective-permute-start | bytes 393224 | tf_op jit(solution)/shard_map/ppermute | solution.py:405
  65.8 1.0 %all-to-all-done.2.refs_0_ = bf16[8,80,128]{2,1,0:T(8,128)(2,1)S(1)} async-done(((bf16[8,80,128]{2,1,0:T(8,128)(2,1)}), bf16[8,80,128]{2,1,0:T(8,128)(2,1)S(1)}, u32[]{:S(2)}, u32[]{:S(2)}) %all-to-all-start.2) | async-done | bytes 163872 | tf_op jit(solution)/shard_map/all_to_all | solution.py:391
  66.9 1.1 %join_pieces.3 = bf16[16,64,128]{2,1,0:T(8,128)(2,1)} custom-call(bf16[8,80,128]{2,1,0:T(8,128)(2,1)S(1)} %all-to-all-done.2.refs_0_), custom_call_target="tpu_custom_call" | custom-call | flops 3000000000 | bytes 524288 | tf_op jit(solution)/shard_map/join_pieces/pallas_call | solution.py:350
  67.9 5.8 %all-to-all-start.3 = ((bf16[16,64,128]{2,1,0:T(8,128)(2,1)}), bf16[16,64,128]{2,1,0:T(8,128)(2,1)S(1)}, u32[]{:S(2)}, u32[]{:S(2)}) async-start(bf16[16,64,128]{2,1,0:T(8,128)(2,1)} %join_pieces.3), calls=%async_computation.3 | async-start | bytes 524288 | tf_op jit(solution)/shard_map/all_to_all | solution.py:391
  73.7 6.8 %context_attention.1 = (bf16[256,4096]{1,0:T(8,128)(2,1)}, bf16[32,4096]{1,0:T(8,128)(2,1)}) custom-call(s32[1]{0:T(128)S(6)} %copy.12.len_ref, bf16[256,4096]{1,0:T(8,128)(2,1)S(1)} %copy-done.2, bf16[256,512]{1,0:T(8,128)(2,1)S(1)} %copy-done, bf16[256,512]{1,0:T(8,128)(2,1)S(1)} %copy-done.1, bf16[64,1024]{1,0:T(8,128)(2,1)S(1)} %add_select_fusion.refs_0_, ...), custom_call_target="tpu_custom_call" | custom-call | flops 2147483648 | bytes 5242880 | tf_op jit(solution)/shard_map/context_attention/pallas_call | solution.py:112
  (42 shorter events, 0.9 us)
Async XLA Ops:
  3.6 27.4 %copy-start.4 = (bf16[64,1024]{1,0:T(8,128)(2,1)S(1)}, bf16[64,1024]{1,0:T(8,128)(2,1)}, u32[]{:S(2)}) copy-start(bf16[64,1024]{1,0:T(8,128)(2,1)} %get-tuple-element.26) | copy-start | bytes 393220
  3.6 16.2 %all-to-all-start = ((bf16[32,32,128]{2,1,0:T(8,128)(2,1)}), bf16[32,32,128]{2,1,0:T(8,128)(2,1)S(1)}, u32[]{:S(2)}, u32[]{:S(2)}) async-start(bf16[32,32,128]{2,1,0:T(8,128)(2,1)} %get-tuple-element.27), calls=%async_computation | async-start | bytes 524288 | tf_op jit(solution)/shard_map/all_to_all | solution.py:391
  11.4 8.2 %collective-permute-start = (bf16[64,1024]{1,0:T(8,128)(2,1)}, bf16[64,1024]{1,0:T(8,128)(2,1)S(1)}, u32[]{:S(2)}, u32[]{:S(2)}) collective-permute-start(bf16[64,1024]{1,0:T(8,128)(2,1)} %get-tuple-element.28), channel_id=1, source_target_pairs={{0,8},{1,9}} | collective-permute-start | bytes 393224 | tf_op jit(solution)/shard_map/ppermute | solution.py:402
  12.7 7.2 %collective-permute-start.1 = (bf16[64,1024]{1,0:T(8,128)(2,1)}, bf16[64,1024]{1,0:T(8,128)(2,1)S(1)}, u32[]{:S(2)}, u32[]{:S(2)}) collective-permute-start(bf16[64,1024]{1,0:T(8,128)(2,1)} %get-tuple-element.29), channel_id=1, source_target_pairs={{0,16},{1,17}} | collective-permute-start | bytes 393224 | tf_op jit(solution)/shard_map/ppermute | solution.py:402
  13.4 6.5 %collective-permute-start.2 = (bf16[64,1024]{1,0:T(8,128)(2,1)}, bf16[64,1024]{1,0:T(8,128)(2,1)S(1)}, u32[]{:S(2)}, u32[]{:S(2)}) collective-permute-start(bf16[64,1024]{1,0:T(8,128)(2,1)} %get-tuple-element.30), channel_id=1, source_target_pairs={{0,24},{1,25}} | collective-permute-start | bytes 393224 | tf_op jit(solution)/shard_map/ppermute | solution.py:402
  14.1 21.0 %collective-permute-start.13 = (bf16[576,128]{1,0:T(8,128)(2,1)}, bf16[576,128]{1,0:T(8,128)(2,1)S(1)}, u32[]{:S(2)}, u32[]{:S(2)}) collective-permute-start(bf16[576,128]{1,0:T(8,128)(2,1)} %get-tuple-element.37), channel_id=1, source_target_pairs={{0,2},{2,4},{4,6},{6,0},{1,3},{3,5},{5,7},{7,1},{8,10},{10,12},{12... | collective-permute-start | bytes 442376 | tf_op jit(solution)/shard_map/ppermute | solution.py:411
  15.0 20.1 %collective-permute-start.14 = (bf16[576,128]{1,0:T(8,128)(2,1)}, bf16[576,128]{1,0:T(8,128)(2,1)S(1)}, u32[]{:S(2)}, u32[]{:S(2)}) collective-permute-start(bf16[576,128]{1,0:T(8,128)(2,1)} %get-tuple-element.38), channel_id=1, source_target_pairs={{0,4},{2,6},{4,0},{6,2},{1,5},{3,7},{5,1},{7,3},{8,12},{10,14},{12... | collective-permute-start | bytes 442376 | tf_op jit(solution)/shard_map/ppermute | solution.py:411
  19.6 15.4 %collective-permute-start.15 = (bf16[576,128]{1,0:T(8,128)(2,1)}, bf16[576,128]{1,0:T(8,128)(2,1)S(1)}, u32[]{:S(2)}, u32[]{:S(2)}) collective-permute-start(bf16[576,128]{1,0:T(8,128)(2,1)} %get-tuple-element.39), channel_id=1, source_target_pairs={{0,6},{2,0},{4,2},{6,4},{1,7},{3,1},{5,3},{7,5},{8,14},{10,8},{12,... | collective-permute-start | bytes 442376 | tf_op jit(solution)/shard_map/ppermute | solution.py:411
  20.5 14.5 %all-to-all-start.1 = ((bf16[8,64,128]{2,1,0:T(8,128)(2,1)}), bf16[8,64,128]{2,1,0:T(8,128)(2,1)S(1)}, u32[]{:S(2)}, u32[]{:S(2)}) async-start(bf16[8,64,128]{2,1,0:T(8,128)(2,1)} %choose.2), calls=%async_computation.1 | async-start | bytes 262144 | tf_op jit(solution)/shard_map/all_to_all | solution.py:391
  31.1 13.5 %copy-start.3 = (bf16[576,128]{1,0:T(8,128)(2,1)S(1)}, bf16[576,128]{1,0:T(8,128)(2,1)}, u32[]{:S(2)}) copy-start(bf16[576,128]{1,0:T(8,128)(2,1)} %get-tuple-element.41.refs_4_) | copy-start | bytes 442372
  31.1 8.8 %collective-permute-start.4 = (bf16[64,1024]{1,0:T(8,128)(2,1)S(1)}, bf16[64,1024]{1,0:T(8,128)(2,1)S(1)}, u32[]{:S(2)}, u32[]{:S(2)}) collective-permute-start(bf16[64,1024]{1,0:T(8,128)(2,1)S(1)} %add_select_fusion.3), channel_id=1, source_target_pairs={{0,96},{8,104},{16,112},{24,120},{1,97},{9,105},{17,113},{25,121}} | collective-permute-start | bytes 393224 | tf_op jit(solution)/shard_map/ppermute | solution.py:402
  33.7 6.2 %collective-permute-start.3 = (bf16[64,1024]{1,0:T(8,128)(2,1)S(1)}, bf16[64,1024]{1,0:T(8,128)(2,1)S(1)}, u32[]{:S(2)}, u32[]{:S(2)}) collective-permute-start(bf16[64,1024]{1,0:T(8,128)(2,1)S(1)} %add_select_fusion.3), channel_id=1, source_target_pairs={{0,192},{8,200},{16,208},{24,216},{1,193},{9,201},{17,209},{25,217}} | collective-permute-start | bytes 393224 | tf_op jit(solution)/shard_map/ppermute | solution.py:402
  35.1 8.2 %collective-permute-start.18 = (bf16[64,128]{1,0:T(8,128)(2,1)S(1)}, bf16[64,128]{1,0:T(8,128)(2,1)S(1)}, u32[]{:S(2)}, u32[]{:S(2)}) collective-permute-start(bf16[64,128]{1,0:T(8,128)(2,1)S(1)} %choose.3.refs_0_), channel_id=1, source_target_pairs={{0,24},{8,0},{16,8},{24,16},{1,25},{9,1},{17,9},{25,17},{2,26},{10... | collective-permute-start | bytes 49160 | tf_op jit(solution)/shard_map/ppermute | solution.py:405
  36.1 8.4 %collective-permute-start.17 = (bf16[64,128]{1,0:T(8,128)(2,1)S(1)}, bf16[64,128]{1,0:T(8,128)(2,1)S(1)}, u32[]{:S(2)}, u32[]{:S(2)}) collective-permute-start(bf16[64,128]{1,0:T(8,128)(2,1)S(1)} %choose.3.refs_0_), channel_id=1, source_target_pairs={{0,16},{8,24},{16,0},{24,8},{1,17},{9,25},{17,1},{25,9},{2,18},{10... | collective-permute-start | bytes 49160 | tf_op jit(solution)/shard_map/ppermute | solution.py:405
  38.1 6.5 %collective-permute-start.16 = (bf16[64,128]{1,0:T(8,128)(2,1)S(1)}, bf16[64,128]{1,0:T(8,128)(2,1)S(1)}, u32[]{:S(2)}, u32[]{:S(2)}) collective-permute-start(bf16[64,128]{1,0:T(8,128)(2,1)S(1)} %choose.3.refs_0_), channel_id=1, source_target_pairs={{0,8},{8,16},{16,24},{24,0},{1,9},{9,17},{17,25},{25,1},{2,10},{10... | collective-permute-start | bytes 49160 | tf_op jit(solution)/shard_map/ppermute | solution.py:405
  39.9 8.1 %collective-permute-start.7 = (bf16[64,1024]{1,0:T(8,128)(2,1)S(1)}, bf16[64,1024]{1,0:T(8,128)(2,1)S(1)}, u32[]{:S(2)}, u32[]{:S(2)}) collective-permute-start(bf16[64,1024]{1,0:T(8,128)(2,1)S(1)} %add_select_fusion.2), channel_id=1, source_target_pairs={{0,2},{8,10},{16,18},{24,26},{96,98},{104,106},{112,114},{120,122}... | collective-permute-start | bytes 393224 | tf_op jit(solution)/shard_map/ppermute | solution.py:402
  42.0 8.0 %collective-permute-start.6 = (bf16[64,1024]{1,0:T(8,128)(2,1)S(1)}, bf16[64,1024]{1,0:T(8,128)(2,1)S(1)}, u32[]{:S(2)}, u32[]{:S(2)}) collective-permute-start(bf16[64,1024]{1,0:T(8,128)(2,1)S(1)} %add_select_fusion.2), channel_id=1, source_target_pairs={{0,4},{8,12},{16,20},{24,28},{96,100},{104,108},{112,116},{120,124... | collective-permute-start | bytes 393224 | tf_op jit(solution)/shard_map/ppermute | solution.py:402
  43.3 6.7 %collective-permute-start.5 = (bf16[64,1024]{1,0:T(8,128)(2,1)S(1)}, bf16[64,1024]{1,0:T(8,128)(2,1)S(1)}, u32[]{:S(2)}, u32[]{:S(2)}) collective-permute-start(bf16[64,1024]{1,0:T(8,128)(2,1)S(1)} %add_select_fusion.2), channel_id=1, source_target_pairs={{0,6},{8,14},{16,22},{24,30},{96,102},{104,110},{112,118},{120,126... | collective-permute-start | bytes 393224 | tf_op jit(solution)/shard_map/ppermute | solution.py:402
  45.7 6.3 %collective-permute-start.19 = (bf16[144,128]{1,0:T(8,128)(2,1)S(1)}, bf16[144,128]{1,0:T(8,128)(2,1)S(1)}, u32[]{:S(2)}, u32[]{:S(2)}) collective-permute-start(bf16[144,128]{1,0:T(8,128)(2,1)S(1)} %get-tuple-element.46), channel_id=1, source_target_pairs={{0,24},{8,0},{16,8},{24,16},{1,25},{9,1},{17,9},{25,17},{2,26},{10... | collective-permute-start | bytes 110600 | tf_op jit(solution)/shard_map/ppermute | solution.py:405
  45.9 6.0 %collective-permute-start.20 = (bf16[144,128]{1,0:T(8,128)(2,1)S(1)}, bf16[144,128]{1,0:T(8,128)(2,1)S(1)}, u32[]{:S(2)}, u32[]{:S(2)}) collective-permute-start(bf16[144,128]{1,0:T(8,128)(2,1)S(1)} %get-tuple-element.47), channel_id=1, source_target_pairs={{0,16},{8,24},{16,0},{24,8},{1,17},{9,25},{17,1},{25,9},{2,18},{10... | collective-permute-start | bytes 110600 | tf_op jit(solution)/shard_map/ppermute | solution.py:405
  48.1 4.1 %collective-permute-start.21 = (bf16[144,128]{1,0:T(8,128)(2,1)S(1)}, bf16[144,128]{1,0:T(8,128)(2,1)S(1)}, u32[]{:S(2)}, u32[]{:S(2)}) collective-permute-start(bf16[144,128]{1,0:T(8,128)(2,1)S(1)} %get-tuple-element.48), channel_id=1, source_target_pairs={{0,8},{8,16},{16,24},{24,0},{1,9},{9,17},{17,25},{25,1},{2,10},{10... | collective-permute-start | bytes 110600 | tf_op jit(solution)/shard_map/ppermute | solution.py:405
  50.0 11.0 %collective-permute-start.9 = (bf16[64,1024]{1,0:T(8,128)(2,1)S(1)}, bf16[64,1024]{1,0:T(8,128)(2,1)S(1)}, u32[]{:S(2)}, u32[]{:S(2)}) collective-permute-start(bf16[64,1024]{1,0:T(8,128)(2,1)S(1)} %add_select_fusion.1), channel_id=1, source_target_pairs={{96,64},{98,66},{100,68},{102,70},{104,72},{106,74},{108,76},{110,... | collective-permute-start | bytes 393224 | tf_op jit(solution)/shard_map/ppermute | solution.py:402
  50.7 10.3 %collective-permute-start.8 = (bf16[64,1024]{1,0:T(8,128)(2,1)S(1)}, bf16[64,1024]{1,0:T(8,128)(2,1)S(1)}, u32[]{:S(2)}, u32[]{:S(2)}) collective-permute-start(bf16[64,1024]{1,0:T(8,128)(2,1)S(1)} %add_select_fusion.1), channel_id=1, source_target_pairs={{0,32},{2,34},{4,36},{6,38},{8,40},{10,42},{12,44},{14,46},{16,48}... | collective-permute-start | bytes 393224 | tf_op jit(solution)/shard_map/ppermute | solution.py:402
  53.1 13.7 %all-to-all-start.2 = ((bf16[8,80,128]{2,1,0:T(8,128)(2,1)}), bf16[8,80,128]{2,1,0:T(8,128)(2,1)S(1)}, u32[]{:S(2)}, u32[]{:S(2)}) async-start(bf16[8,80,128]{2,1,0:T(8,128)(2,1)} %join_pieces.2), calls=%async_computation.2 | async-start | bytes 327680 | tf_op jit(solution)/shard_map/all_to_all | solution.py:391
  61.0 12.7 %copy-start = (bf16[256,512]{1,0:T(8,128)(2,1)S(1)}, bf16[256,512]{1,0:T(8,128)(2,1)}, u32[]{:S(2)}) copy-start(bf16[256,512]{1,0:T(8,128)(2,1)} %k_ref.3) | copy-start | bytes 786436
  61.0 12.7 %copy-start.1 = (bf16[256,512]{1,0:T(8,128)(2,1)S(1)}, bf16[256,512]{1,0:T(8,128)(2,1)}, u32[]{:S(2)}) copy-start(bf16[256,512]{1,0:T(8,128)(2,1)} %v_ref.3) | copy-start | bytes 786436
  61.0 12.7 %copy-start.2 = (bf16[256,4096]{1,0:T(8,128)(2,1)S(1)}, bf16[256,4096]{1,0:T(8,128)(2,1)}, u32[]{:S(2)}) copy-start(bf16[256,4096]{1,0:T(8,128)(2,1)} %q_ref.1) | copy-start | bytes 6291460
  61.1 12.6 %collective-permute-start.12 = (bf16[64,1024]{1,0:T(8,128)(2,1)S(1)}, bf16[64,1024]{1,0:T(8,128)(2,1)S(1)}, u32[]{:S(2)}, u32[]{:S(2)}) collective-permute-start(bf16[64,1024]{1,0:T(8,128)(2,1)S(1)} %add_select_fusion.refs_0_), channel_id=1, source_target_pairs={{0,24},{8,0},{16,8},{24,16},{1,25},{9,1},{17,9},{25,17},{2,26},{10... | collective-permute-start | bytes 393224 | tf_op jit(solution)/shard_map/ppermute | solution.py:405
  62.5 11.2 %collective-permute-start.11 = (bf16[64,1024]{1,0:T(8,128)(2,1)S(1)}, bf16[64,1024]{1,0:T(8,128)(2,1)S(1)}, u32[]{:S(2)}, u32[]{:S(2)}) collective-permute-start(bf16[64,1024]{1,0:T(8,128)(2,1)S(1)} %add_select_fusion.refs_0_), channel_id=1, source_target_pairs={{0,16},{8,24},{16,0},{24,8},{1,17},{9,25},{17,1},{25,9},{2,18},{10... | collective-permute-start | bytes 393224 | tf_op jit(solution)/shard_map/ppermute | solution.py:405
  64.8 8.9 %collective-permute-start.10 = (bf16[64,1024]{1,0:T(8,128)(2,1)S(1)}, bf16[64,1024]{1,0:T(8,128)(2,1)S(1)}, u32[]{:S(2)}, u32[]{:S(2)}) collective-permute-start(bf16[64,1024]{1,0:T(8,128)(2,1)S(1)} %add_select_fusion.refs_0_), channel_id=1, source_target_pairs={{0,8},{8,16},{16,24},{24,0},{1,9},{9,17},{17,25},{25,1},{2,10},{10... | collective-permute-start | bytes 393224 | tf_op jit(solution)/shard_map/ppermute | solution.py:405
  67.9 12.6 %all-to-all-start.3 = ((bf16[16,64,128]{2,1,0:T(8,128)(2,1)}), bf16[16,64,128]{2,1,0:T(8,128)(2,1)S(1)}, u32[]{:S(2)}, u32[]{:S(2)}) async-start(bf16[16,64,128]{2,1,0:T(8,128)(2,1)} %join_pieces.3), calls=%async_computation.3 | async-start | bytes 524288 | tf_op jit(solution)/shard_map/all_to_all | solution.py:391

commit v11 on v9

--- a/solution.py
+++ b/solution.py
@@ -410,25 +410,24 @@
     moved, got = lax.optimization_barrier((moved, got))
     moved = choose(plane_kernel, query_owner, moved, (n_z,) + piece, 8 * 10**8)
     anchor = jnp.where(x == 0, pieces[0], got[0] + got[1] + got[2])
-    got = [move(anchor, [(i * n_y, (to * n_x + i) * n_y) for i in range(n_x)]) for to in (3, 5)]
+    got = [move(anchor, [(i * n_y, (to * n_x + i) * n_y) for i in range(n_x)]) for to in (6, 4, 2)]
     moved = exchange(moved, "z", down)
 
     moved = choose(line_kernel, query_owner, moved, piece, 3 * 10**9)
     moved, lines = lax.optimization_barrier((moved, lines))
-    anchor = jnp.where(z == 0, anchor, got[0] + got[1])
-    rows = [(to * n_x + i) * n_y for to in (0, 3, 5) for i in range(n_x)]
+    anchor = jnp.where(z == 0, anchor, got[0] + got[1] + got[2])
+    rows = [(to * n_x + i) * n_y for to in (0, 2, 4, 6) for i in range(n_x)]
     got = [move(anchor, [(p, p + j) for p in rows]) for j in (3, 2, 1)]
     queries = [moved] + [shift_x(moved, i) for i in range(1, n_x)]
 
     partials = request_partials(query_owner, queries, lines, own_rows)
     anchor = jnp.where(y == 0, anchor, got[0] + got[1] + got[2])
     plane = range(n_xy)
-    steps = (((0, 1), (3, 4), (5, 6)), ((3, 2), (5, 7)))
-    got = [move(anchor, [(a * n_xy + p, b * n_xy + p) for a, b in step for p in plane]) for step in steps]
+    got = move(anchor, [(a * n_xy + p, (a + 1) * n_xy + p) for a in range(0, n_z, 2) for p in plane])
     partials = [partials[0]] + [shift_x(partials[i], n_x - i) for i in range(1, n_x)]
 
     planes = join(partials, n_z, 2, True)
-    anchor = jnp.where((z == 0) | (z == 3) | (z == 5), anchor, got[0] + got[1])
+    anchor = jnp.where(z % 2 == 0, anchor, got)
     anchors = [anchor]
     for i in range(1, n_x):
         anchors.append(shift_x(anchor, i))

time: 80.8 us -> 81.5 us (level)
  transfers between devices with their start and end apart: 26 -> 26, of which waited for: 3 -> 4; matrix products, arithmetic and copies ran while one was open for 0% -> 0% of each run, Pallas kernels for 13% -> 13%
where the time goes in v11:
time: 81.5 us; the launch traced here: 80.3 us
  starting transfers between devices  61.1 us (75%)
  Pallas kernels  13 us (16%)
  waiting for transfers between devices  3.79 us (5%)
  between operations  2.38 us (3%)
    all_to_all x4, starting transfers between devices, exchange(): lax.all_to_all(x, axis, split_axis=0, concat_axis=0, axis_index_groups=gr...  28.5 us
    ppermute x10, starting transfers between devices, move(): return lax.ppermute(value, ('z', 'x', 'y'), pairs)  15.1 us
    ppermute x9, starting transfers between devices, shift_x(): lax.ppermute(value, 'x', [(a, (a + count) % n_x) for a in range(n_x)])  13.7 us
    pallas_call x1, Pallas kernels, context_attention(): pl.pallas_call(functools.partial(context_kernel, len(anchor)), out_shape=...  6.79 us
    ppermute x3, starting transfers between devices, local(): lax.ppermute(lines[i], 'y', [(a, (a + i) % n_y) for a in range(n_y)])  3.82 us
    pallas_call x1, Pallas kernels, prepare(): pl.pallas_call(functools.partial(prepare_kernel, n_x, n_y), out_shape=sha...  2.36 us
    pallas_call x2, Pallas kernels, join(): pl.pallas_call(functools.partial(join_kernel, parts_in, keep_code), out_s...  2.04 us
  transfers between devices with their start and end apart: 26, of which 4 were waited for; matrix products, arithmetic and copies ran while one was open for 0% of the time, Pallas kernels for 13%

profile of v11, /device:TPU:2, one launch (start us, length us, event | category | flops | bytes accessed | tf_op | source)
XLA Modules:
  0.0 80.3 jit_solution(11777281924180369267)
XLA Ops:
  1.3 2.4 %prepare.1 = (bf16[32,32,128]{2,1,0:T(8,128)(2,1)}, bf16[64,1024]{1,0:T(8,128)(2,1)}, bf16[64,1024]{1,0:T(8,128)(2,1)}, bf16[64,1024]{1,0:T(8,128)(2,1)}, bf16[6...) custom-call(s32[1]{0:T(128)S(6)} %copy.12.len_ref, ...), custom_call_target="tpu_custom_call" | custom-call | flops 262144 | bytes 2621440 | tf_op jit(solution)/shard_map/prepare/pallas_call | solution.py:180
  3.6 7.8 %all-to-all-start = ((bf16[32,32,128]{2,1,0:T(8,128)(2,1)}), bf16[32,32,128]{2,1,0:T(8,128)(2,1)S(1)}, u32[]{:S(2)}, u32[]{:S(2)}) async-start(bf16[32,32,128]{2,1,0:T(8,128)(2,1)} %get-tuple-element.27), calls=%async_computation | async-start | bytes 524288 | tf_op jit(solution)/shard_map/all_to_all | solution.py:386
  11.4 1.3 %collective-permute-start = (bf16[64,1024]{1,0:T(8,128)(2,1)}, bf16[64,1024]{1,0:T(8,128)(2,1)S(1)}, u32[]{:S(2)}, u32[]{:S(2)}) collective-permute-start(bf16[64,1024]{1,0:T(8,128)(2,1)} %get-tuple-element.28), channel_id=1, source_target_pairs={{0,8},{1,9}} | collective-permute-start | bytes 393224 | tf_op jit(solution)/shard_map/ppermute | solution.py:397
  12.7 0.7 collective-permute-start.1
  13.4 0.7 collective-permute-start.2
  14.1 0.9 %collective-permute-start.13 = (bf16[576,128]{1,0:T(8,128)(2,1)}, bf16[576,128]{1,0:T(8,128)(2,1)S(1)}, u32[]{:S(2)}, u32[]{:S(2)}) collective-permute-start(bf16[576,128]{1,0:T(8,128)(2,1)} %get-tuple-element.37), channel_id=1, source_target_pairs={{0,2},{2,4},{4,6},{6,0},{1,3},{3,5},{5,7},{7,1},{8,10},{10,12},{12... | collective-permute-start | bytes 442376 | tf_op jit(solution)/shard_map/ppermute | solution.py:406
  15.0 2.7 %collective-permute-start.14 = (bf16[576,128]{1,0:T(8,128)(2,1)}, bf16[576,128]{1,0:T(8,128)(2,1)S(1)}, u32[]{:S(2)}, u32[]{:S(2)}) collective-permute-start(bf16[576,128]{1,0:T(8,128)(2,1)} %get-tuple-element.38), channel_id=1, source_target_pairs={{0,4},{2,6},{4,0},{6,2},{1,5},{3,7},{5,1},{7,3},{8,12},{10,14},{12... | collective-permute-start | bytes 442376 | tf_op jit(solution)/shard_map/ppermute | solution.py:406
  18.3 1.3 %collective-permute-done = bf16[64,1024]{1,0:T(8,128)(2,1)S(1)} collective-permute-done((bf16[64,1024]{1,0:T(8,128)(2,1)}, bf16[64,1024]{1,0:T(8,128)(2,1)S(1)}, u32[]{:S(2)}, u32[]{:S(2)}) %collective-permute-start) | collective-permute-done | bytes 131104 | tf_op jit(solution)/shard_map/ppermute | solution.py:397
  19.9 0.7 choose.2
  20.5 9.2 %all-to-all-start.1 = ((bf16[8,64,128]{2,1,0:T(8,128)(2,1)}), bf16[8,64,128]{2,1,0:T(8,128)(2,1)S(1)}, u32[]{:S(2)}, u32[]{:S(2)}) async-start(bf16[8,64,128]{2,1,0:T(8,128)(2,1)} %choose.2), calls=%async_computation.1 | async-start | bytes 262144 | tf_op jit(solution)/shard_map/all_to_all | solution.py:386
  29.8 4.4 %collective-permute-start.5 = (bf16[64,1024]{1,0:T(8,128)(2,1)S(1)}, bf16[64,1024]{1,0:T(8,128)(2,1)S(1)}, u32[]{:S(2)}, u32[]{:S(2)}) collective-permute-start(bf16[64,1024]{1,0:T(8,128)(2,1)S(1)} %add_select_fusion.2), channel_id=1, source_target_pairs={{0,64},{8,72},{16,80},{24,88},{1,65},{9,73},{17,81},{25,89}} | collective-permute-start | bytes 393224 | tf_op jit(solution)/shard_map/ppermute | solution.py:397
  34.2 1.6 %collective-permute-start.4 = (bf16[64,1024]{1,0:T(8,128)(2,1)S(1)}, bf16[64,1024]{1,0:T(8,128)(2,1)S(1)}, u32[]{:S(2)}, u32[]{:S(2)}) collective-permute-start(bf16[64,1024]{1,0:T(8,128)(2,1)S(1)} %add_select_fusion.2), channel_id=1, source_target_pairs={{0,128},{8,136},{16,144},{24,152},{1,129},{9,137},{17,145},{25,153}} | collective-permute-start | bytes 393224 | tf_op jit(solution)/shard_map/ppermute | solution.py:397
  35.7 1.3 %collective-permute-start.3 = (bf16[64,1024]{1,0:T(8,128)(2,1)S(1)}, bf16[64,1024]{1,0:T(8,128)(2,1)S(1)}, u32[]{:S(2)}, u32[]{:S(2)}) collective-permute-start(bf16[64,1024]{1,0:T(8,128)(2,1)S(1)} %add_select_fusion.2), channel_id=1, source_target_pairs={{0,192},{8,200},{16,208},{24,216},{1,193},{9,201},{17,209},{25,217}} | collective-permute-start | bytes 393224 | tf_op jit(solution)/shard_map/ppermute | solution.py:397
  37.1 0.8 collective-permute-start.18
  37.9 2.2 %collective-permute-start.17 = (bf16[64,128]{1,0:T(8,128)(2,1)S(1)}, bf16[64,128]{1,0:T(8,128)(2,1)S(1)}, u32[]{:S(2)}, u32[]{:S(2)}) collective-permute-start(bf16[64,128]{1,0:T(8,128)(2,1)S(1)} %choose.3.refs_0_), channel_id=1, source_target_pairs={{0,16},{8,24},{16,0},{24,8},{1,17},{9,25},{17,1},{25,9},{2,18},{10... | collective-permute-start | bytes 49160 | tf_op jit(solution)/shard_map/ppermute | solution.py:400
  40.1 1.8 %collective-permute-start.16 = (bf16[64,128]{1,0:T(8,128)(2,1)S(1)}, bf16[64,128]{1,0:T(8,128)(2,1)S(1)}, u32[]{:S(2)}, u32[]{:S(2)}) collective-permute-start(bf16[64,128]{1,0:T(8,128)(2,1)S(1)} %choose.3.refs_0_), channel_id=1, source_target_pairs={{0,8},{8,16},{16,24},{24,0},{1,9},{9,17},{17,25},{25,1},{2,10},{10... | collective-permute-start | bytes 49160 | tf_op jit(solution)/shard_map/ppermute | solution.py:400
  42.0 1.3 %collective-permute-start.8 = (bf16[64,1024]{1,0:T(8,128)(2,1)S(1)}, bf16[64,1024]{1,0:T(8,128)(2,1)S(1)}, u32[]{:S(2)}, u32[]{:S(2)}) collective-permute-start(bf16[64,1024]{1,0:T(8,128)(2,1)S(1)} %add_select_fusion.1), channel_id=1, source_target_pairs={{0,2},{8,10},{16,18},{24,26},{64,66},{72,74},{80,82},{88,90},{128,... | collective-permute-start | bytes 393224 | tf_op jit(solution)/shard_map/ppermute | solution.py:397
  43.3 1.3 %collective-permute-start.7 = (bf16[64,1024]{1,0:T(8,128)(2,1)S(1)}, bf16[64,1024]{1,0:T(8,128)(2,1)S(1)}, u32[]{:S(2)}, u32[]{:S(2)}) collective-permute-start(bf16[64,1024]{1,0:T(8,128)(2,1)S(1)} %add_select_fusion.1), channel_id=1, source_target_pairs={{0,4},{8,12},{16,20},{24,28},{64,68},{72,76},{80,84},{88,92},{128,... | collective-permute-start | bytes 393224 | tf_op jit(solution)/shard_map/ppermute | solution.py:397
  44.6 1.3 %collective-permute-start.6 = (bf16[64,1024]{1,0:T(8,128)(2,1)S(1)}, bf16[64,1024]{1,0:T(8,128)(2,1)S(1)}, u32[]{:S(2)}, u32[]{:S(2)}) collective-permute-start(bf16[64,1024]{1,0:T(8,128)(2,1)S(1)} %add_select_fusion.1), channel_id=1, source_target_pairs={{0,6},{8,14},{16,22},{24,30},{64,70},{72,78},{80,86},{88,94},{128,... | collective-permute-start | bytes 393224 | tf_op jit(solution)/shard_map/ppermute | solution.py:397
  45.9 1.1 %request_partials.1 = (bf16[144,128]{1,0:T(8,128)(2,1)S(1)}, bf16[144,128]{1,0:T(8,128)(2,1)S(1)}, bf16[144,128]{1,0:T(8,128)(2,1)S(1)}, bf16[144,128]{1,0:T(8,128)(2,1)S(1)}) custom-call(s32[1]{0:T(128)S(6)} %copy.13.owner_ref, bf16[64,128]{1,0:T(8,128)(2,1)S(1)} %choose.3.refs_0_, bf16[64,128]{1,0:T(8,128)(2,1)S(1)} %collective-permute-done.16.refs_1_, ...), custom_call_target="tpu_custom_call" | custom-call | flops 3000000000 | bytes 1048576 | tf_op jit(solution)/shard_map/request_partials/pallas_call | solution.py:287
  47.3 1.2 %collective-permute-start.20 = (bf16[144,128]{1,0:T(8,128)(2,1)S(1)}, bf16[144,128]{1,0:T(8,128)(2,1)S(1)}, u32[]{:S(2)}, u32[]{:S(2)}) collective-permute-start(bf16[144,128]{1,0:T(8,128)(2,1)S(1)} %get-tuple-element.47), channel_id=1, source_target_pairs={{0,16},{8,24},{16,0},{24,8},{1,17},{9,25},{17,1},{25,9},{2,18},{10... | collective-permute-start | bytes 110600 | tf_op jit(solution)/shard_map/ppermute | solution.py:400
  48.6 2.5 %collective-permute-start.21 = (bf16[144,128]{1,0:T(8,128)(2,1)S(1)}, bf16[144,128]{1,0:T(8,128)(2,1)S(1)}, u32[]{:S(2)}, u32[]{:S(2)}) collective-permute-start(bf16[144,128]{1,0:T(8,128)(2,1)S(1)} %get-tuple-element.48), channel_id=1, source_target_pairs={{0,8},{8,16},{16,24},{24,0},{1,9},{9,17},{17,25},{25,1},{2,10},{10... | collective-permute-start | bytes 110600 | tf_op jit(solution)/shard_map/ppermute | solution.py:400
  51.1 1.3 %collective-permute-start.9 = (bf16[64,1024]{1,0:T(8,128)(2,1)S(1)}, bf16[64,1024]{1,0:T(8,128)(2,1)S(1)}, u32[]{:S(2)}, u32[]{:S(2)}) collective-permute-start(bf16[64,1024]{1,0:T(8,128)(2,1)S(1)} %add_select_fusion), channel_id=1, source_target_pairs={{0,32},{2,34},{4,36},{6,38},{8,40},{10,42},{12,44},{14,46},{16,48}... | collective-permute-start | bytes 393224 | tf_op jit(solution)/shard_map/ppermute | solution.py:397
  52.8 0.7 collective-permute-done.21.refs_3_
  53.5 1.0 %join_pieces.2 = bf16[8,80,128]{2,1,0:T(8,128)(2,1)} custom-call(bf16[144,128]{1,0:T(8,128)(2,1)S(1)} %get-tuple-element.45.refs_0_, bf16[144,128]{1,0:T(8,128)(2,1)S(1)} %collective-permute-done.19.refs_1_, bf16[144,128]{1,0:T(8,128)(2,1)S(1)} %collective-permute-done.20.refs_2_, bf16[144,128]{1,0:T(8,128)(2,1)S(1)} %collective-permute-done.21.refs_3_), custom_call_target="tpu_custom_call" | custom-call | flops 3000000000 | bytes 524288 | tf_op jit(solution)/shard_map/join_pieces/pallas_call | solution.py:345
  54.5 6.0 %all-to-all-start.2 = ((bf16[8,80,128]{2,1,0:T(8,128)(2,1)}), bf16[8,80,128]{2,1,0:T(8,128)(2,1)S(1)}, u32[]{:S(2)}, u32[]{:S(2)}) async-start(bf16[8,80,128]{2,1,0:T(8,128)(2,1)} %join_pieces.2), calls=%async_computation.2 | async-start | bytes 327680 | tf_op jit(solution)/shard_map/all_to_all | solution.py:386
  60.5 2.6 %collective-permute-start.12 = (bf16[64,1024]{1,0:T(8,128)(2,1)S(1)}, bf16[64,1024]{1,0:T(8,128)(2,1)S(1)}, u32[]{:S(2)}, u32[]{:S(2)}) collective-permute-start(bf16[64,1024]{1,0:T(8,128)(2,1)S(1)} %broadcast_select_fusion.refs_0_), channel_id=1, source_target_pairs={{0,24},{8,0},{16,8},{24,16},{1,25},{9,1},{17,9},{25,17},{2,26},{10... | collective-permute-start | bytes 393224 | tf_op jit(solution)/shard_map/ppermute | solution.py:400
  63.7 1.5 %collective-permute-start.10 = (bf16[64,1024]{1,0:T(8,128)(2,1)S(1)}, bf16[64,1024]{1,0:T(8,128)(2,1)S(1)}, u32[]{:S(2)}, u32[]{:S(2)}) collective-permute-start(bf16[64,1024]{1,0:T(8,128)(2,1)S(1)} %broadcast_select_fusion.refs_0_), channel_id=1, source_target_pairs={{0,8},{8,16},{16,24},{24,0},{1,9},{9,17},{17,25},{25,1},{2,10},{10... | collective-permute-start | bytes 393224 | tf_op jit(solution)/shard_map/ppermute | solution.py:400
  65.2 1.4 %all-to-all-done.2.refs_0_ = bf16[8,80,128]{2,1,0:T(8,128)(2,1)S(1)} async-done(((bf16[8,80,128]{2,1,0:T(8,128)(2,1)}), bf16[8,80,128]{2,1,0:T(8,128)(2,1)S(1)}, u32[]{:S(2)}, u32[]{:S(2)}) %all-to-all-start.2) | async-done | bytes 163872 | tf_op jit(solution)/shard_map/all_to_all | solution.py:386
  66.6 1.1 %join_pieces.3 = bf16[16,64,128]{2,1,0:T(8,128)(2,1)} custom-call(bf16[8,80,128]{2,1,0:T(8,128)(2,1)S(1)} %all-to-all-done.2.refs_0_), custom_call_target="tpu_custom_call" | custom-call | flops 3000000000 | bytes 524288 | tf_op jit(solution)/shard_map/join_pieces/pallas_call | solution.py:345
  67.7 5.6 %all-to-all-start.3 = ((bf16[16,64,128]{2,1,0:T(8,128)(2,1)}), bf16[16,64,128]{2,1,0:T(8,128)(2,1)S(1)}, u32[]{:S(2)}, u32[]{:S(2)}) async-start(bf16[16,64,128]{2,1,0:T(8,128)(2,1)} %join_pieces.3), calls=%async_computation.3 | async-start | bytes 524288 | tf_op jit(solution)/shard_map/all_to_all | solution.py:386
  73.3 6.8 %context_attention.1 = (bf16[256,4096]{1,0:T(8,128)(2,1)}, bf16[32,4096]{1,0:T(8,128)(2,1)}) custom-call(s32[1]{0:T(128)S(6)} %copy.12.len_ref, bf16[256,4096]{1,0:T(8,128)(2,1)S(1)} %copy-done.2, bf16[256,512]{1,0:T(8,128)(2,1)S(1)} %copy-done, bf16[256,512]{1,0:T(8,128)(2,1)S(1)} %copy-done.1, bf16[64,1024]{1,0:T(8,128)(2,1)S(1)} %broadcast_select_fusion.refs_0_, ...), custom_call_target="tpu_custom_call" | custom-call | flops 2147483648 | bytes 5242880 | tf_op jit(solution)/shard_map/context_attention/pallas_call | solution.py:111
  (42 shorter events, 1.8 us)
Async XLA Ops:
  3.6 26.1 %copy-start.4 = (bf16[64,1024]{1,0:T(8,128)(2,1)S(1)}, bf16[64,1024]{1,0:T(8,128)(2,1)}, u32[]{:S(2)}) copy-start(bf16[64,1024]{1,0:T(8,128)(2,1)} %get-tuple-element.26) | copy-start | bytes 393220
  3.6 16.2 %all-to-all-start = ((bf16[32,32,128]{2,1,0:T(8,128)(2,1)}), bf16[32,32,128]{2,1,0:T(8,128)(2,1)S(1)}, u32[]{:S(2)}, u32[]{:S(2)}) async-start(bf16[32,32,128]{2,1,0:T(8,128)(2,1)} %get-tuple-element.27), calls=%async_computation | async-start | bytes 524288 | tf_op jit(solution)/shard_map/all_to_all | solution.py:386
  11.4 8.2 %collective-permute-start = (bf16[64,1024]{1,0:T(8,128)(2,1)}, bf16[64,1024]{1,0:T(8,128)(2,1)S(1)}, u32[]{:S(2)}, u32[]{:S(2)}) collective-permute-start(bf16[64,1024]{1,0:T(8,128)(2,1)} %get-tuple-element.28), channel_id=1, source_target_pairs={{0,8},{1,9}} | collective-permute-start | bytes 393224 | tf_op jit(solution)/shard_map/ppermute | solution.py:397
  12.7 7.2 %collective-permute-start.1 = (bf16[64,1024]{1,0:T(8,128)(2,1)}, bf16[64,1024]{1,0:T(8,128)(2,1)S(1)}, u32[]{:S(2)}, u32[]{:S(2)}) collective-permute-start(bf16[64,1024]{1,0:T(8,128)(2,1)} %get-tuple-element.29), channel_id=1, source_target_pairs={{0,16},{1,17}} | collective-permute-start | bytes 393224 | tf_op jit(solution)/shard_map/ppermute | solution.py:397
  13.4 6.5 %collective-permute-start.2 = (bf16[64,1024]{1,0:T(8,128)(2,1)}, bf16[64,1024]{1,0:T(8,128)(2,1)S(1)}, u32[]{:S(2)}, u32[]{:S(2)}) collective-permute-start(bf16[64,1024]{1,0:T(8,128)(2,1)} %get-tuple-element.30), channel_id=1, source_target_pairs={{0,24},{1,25}} | collective-permute-start | bytes 393224 | tf_op jit(solution)/shard_map/ppermute | solution.py:397
  14.1 21.7 %collective-permute-start.13 = (bf16[576,128]{1,0:T(8,128)(2,1)}, bf16[576,128]{1,0:T(8,128)(2,1)S(1)}, u32[]{:S(2)}, u32[]{:S(2)}) collective-permute-start(bf16[576,128]{1,0:T(8,128)(2,1)} %get-tuple-element.37), channel_id=1, source_target_pairs={{0,2},{2,4},{4,6},{6,0},{1,3},{3,5},{5,7},{7,1},{8,10},{10,12},{12... | collective-permute-start | bytes 442376 | tf_op jit(solution)/shard_map/ppermute | solution.py:406
  15.0 22.1 %collective-permute-start.14 = (bf16[576,128]{1,0:T(8,128)(2,1)}, bf16[576,128]{1,0:T(8,128)(2,1)S(1)}, u32[]{:S(2)}, u32[]{:S(2)}) collective-permute-start(bf16[576,128]{1,0:T(8,128)(2,1)} %get-tuple-element.38), channel_id=1, source_target_pairs={{0,4},{2,6},{4,0},{6,2},{1,5},{3,7},{5,1},{7,3},{8,12},{10,14},{12... | collective-permute-start | bytes 442376 | tf_op jit(solution)/shard_map/ppermute | solution.py:406
  19.6 17.4 %collective-permute-start.15 = (bf16[576,128]{1,0:T(8,128)(2,1)}, bf16[576,128]{1,0:T(8,128)(2,1)S(1)}, u32[]{:S(2)}, u32[]{:S(2)}) collective-permute-start(bf16[576,128]{1,0:T(8,128)(2,1)} %get-tuple-element.39), channel_id=1, source_target_pairs={{0,6},{2,0},{4,2},{6,4},{1,7},{3,1},{5,3},{7,5},{8,14},{10,8},{12,... | collective-permute-start | bytes 442376 | tf_op jit(solution)/shard_map/ppermute | solution.py:406
  20.5 16.5 %all-to-all-start.1 = ((bf16[8,64,128]{2,1,0:T(8,128)(2,1)}), bf16[8,64,128]{2,1,0:T(8,128)(2,1)S(1)}, u32[]{:S(2)}, u32[]{:S(2)}) async-start(bf16[8,64,128]{2,1,0:T(8,128)(2,1)} %choose.2), calls=%async_computation.1 | async-start | bytes 262144 | tf_op jit(solution)/shard_map/all_to_all | solution.py:386
  29.7 16.2 %copy-start.3 = (bf16[576,128]{1,0:T(8,128)(2,1)S(1)}, bf16[576,128]{1,0:T(8,128)(2,1)}, u32[]{:S(2)}) copy-start(bf16[576,128]{1,0:T(8,128)(2,1)} %get-tuple-element.41.refs_4_) | copy-start | bytes 442372
  29.8 10.3 %collective-permute-start.5 = (bf16[64,1024]{1,0:T(8,128)(2,1)S(1)}, bf16[64,1024]{1,0:T(8,128)(2,1)S(1)}, u32[]{:S(2)}, u32[]{:S(2)}) collective-permute-start(bf16[64,1024]{1,0:T(8,128)(2,1)S(1)} %add_select_fusion.2), channel_id=1, source_target_pairs={{0,64},{8,72},{16,80},{24,88},{1,65},{9,73},{17,81},{25,89}} | collective-permute-start | bytes 393224 | tf_op jit(solution)/shard_map/ppermute | solution.py:397
  34.2 7.8 %collective-permute-start.4 = (bf16[64,1024]{1,0:T(8,128)(2,1)S(1)}, bf16[64,1024]{1,0:T(8,128)(2,1)S(1)}, u32[]{:S(2)}, u32[]{:S(2)}) collective-permute-start(bf16[64,1024]{1,0:T(8,128)(2,1)S(1)} %add_select_fusion.2), channel_id=1, source_target_pairs={{0,128},{8,136},{16,144},{24,152},{1,129},{9,137},{17,145},{25,153}} | collective-permute-start | bytes 393224 | tf_op jit(solution)/shard_map/ppermute | solution.py:397
  35.7 6.2 %collective-permute-start.3 = (bf16[64,1024]{1,0:T(8,128)(2,1)S(1)}, bf16[64,1024]{1,0:T(8,128)(2,1)S(1)}, u32[]{:S(2)}, u32[]{:S(2)}) collective-permute-start(bf16[64,1024]{1,0:T(8,128)(2,1)S(1)} %add_select_fusion.2), channel_id=1, source_target_pairs={{0,192},{8,200},{16,208},{24,216},{1,193},{9,201},{17,209},{25,217}} | collective-permute-start | bytes 393224 | tf_op jit(solution)/shard_map/ppermute | solution.py:397
  37.1 7.5 %collective-permute-start.18 = (bf16[64,128]{1,0:T(8,128)(2,1)S(1)}, bf16[64,128]{1,0:T(8,128)(2,1)S(1)}, u32[]{:S(2)}, u32[]{:S(2)}) collective-permute-start(bf16[64,128]{1,0:T(8,128)(2,1)S(1)} %choose.3.refs_0_), channel_id=1, source_target_pairs={{0,24},{8,0},{16,8},{24,16},{1,25},{9,1},{17,9},{25,17},{2,26},{10... | collective-permute-start | bytes 49160 | tf_op jit(solution)/shard_map/ppermute | solution.py:400
  37.9 8.0 %collective-permute-start.17 = (bf16[64,128]{1,0:T(8,128)(2,1)S(1)}, bf16[64,128]{1,0:T(8,128)(2,1)S(1)}, u32[]{:S(2)}, u32[]{:S(2)}) collective-permute-start(bf16[64,128]{1,0:T(8,128)(2,1)S(1)} %choose.3.refs_0_), channel_id=1, source_target_pairs={{0,16},{8,24},{16,0},{24,8},{1,17},{9,25},{17,1},{25,9},{2,18},{10... | collective-permute-start | bytes 49160 | tf_op jit(solution)/shard_map/ppermute | solution.py:400
  40.1 5.8 %collective-permute-start.16 = (bf16[64,128]{1,0:T(8,128)(2,1)S(1)}, bf16[64,128]{1,0:T(8,128)(2,1)S(1)}, u32[]{:S(2)}, u32[]{:S(2)}) collective-permute-start(bf16[64,128]{1,0:T(8,128)(2,1)S(1)} %choose.3.refs_0_), channel_id=1, source_target_pairs={{0,8},{8,16},{16,24},{24,0},{1,9},{9,17},{17,25},{25,1},{2,10},{10... | collective-permute-start | bytes 49160 | tf_op jit(solution)/shard_map/ppermute | solution.py:400
  42.0 6.6 %collective-permute-start.8 = (bf16[64,1024]{1,0:T(8,128)(2,1)S(1)}, bf16[64,1024]{1,0:T(8,128)(2,1)S(1)}, u32[]{:S(2)}, u32[]{:S(2)}) collective-permute-start(bf16[64,1024]{1,0:T(8,128)(2,1)S(1)} %add_select_fusion.1), channel_id=1, source_target_pairs={{0,2},{8,10},{16,18},{24,26},{64,66},{72,74},{80,82},{88,90},{128,... | collective-permute-start | bytes 393224 | tf_op jit(solution)/shard_map/ppermute | solution.py:397
  43.3 7.8 %collective-permute-start.7 = (bf16[64,1024]{1,0:T(8,128)(2,1)S(1)}, bf16[64,1024]{1,0:T(8,128)(2,1)S(1)}, u32[]{:S(2)}, u32[]{:S(2)}) collective-permute-start(bf16[64,1024]{1,0:T(8,128)(2,1)S(1)} %add_select_fusion.1), channel_id=1, source_target_pairs={{0,4},{8,12},{16,20},{24,28},{64,68},{72,76},{80,84},{88,92},{128,... | collective-permute-start | bytes 393224 | tf_op jit(solution)/shard_map/ppermute | solution.py:397
  44.6 6.5 %collective-permute-start.6 = (bf16[64,1024]{1,0:T(8,128)(2,1)S(1)}, bf16[64,1024]{1,0:T(8,128)(2,1)S(1)}, u32[]{:S(2)}, u32[]{:S(2)}) collective-permute-start(bf16[64,1024]{1,0:T(8,128)(2,1)S(1)} %add_select_fusion.1), channel_id=1, source_target_pairs={{0,6},{8,14},{16,22},{24,30},{64,70},{72,78},{80,86},{88,94},{128,... | collective-permute-start | bytes 393224 | tf_op jit(solution)/shard_map/ppermute | solution.py:397
  47.0 5.5 %collective-permute-start.19 = (bf16[144,128]{1,0:T(8,128)(2,1)S(1)}, bf16[144,128]{1,0:T(8,128)(2,1)S(1)}, u32[]{:S(2)}, u32[]{:S(2)}) collective-permute-start(bf16[144,128]{1,0:T(8,128)(2,1)S(1)} %get-tuple-element.46), channel_id=1, source_target_pairs={{0,24},{8,0},{16,8},{24,16},{1,25},{9,1},{17,9},{25,17},{2,26},{10... | collective-permute-start | bytes 110600 | tf_op jit(solution)/shard_map/ppermute | solution.py:400
  47.3 5.5 %collective-permute-start.20 = (bf16[144,128]{1,0:T(8,128)(2,1)S(1)}, bf16[144,128]{1,0:T(8,128)(2,1)S(1)}, u32[]{:S(2)}, u32[]{:S(2)}) collective-permute-start(bf16[144,128]{1,0:T(8,128)(2,1)S(1)} %get-tuple-element.47), channel_id=1, source_target_pairs={{0,16},{8,24},{16,0},{24,8},{1,17},{9,25},{17,1},{25,9},{2,18},{10... | collective-permute-start | bytes 110600 | tf_op jit(solution)/shard_map/ppermute | solution.py:400
  48.6 4.9 %collective-permute-start.21 = (bf16[144,128]{1,0:T(8,128)(2,1)S(1)}, bf16[144,128]{1,0:T(8,128)(2,1)S(1)}, u32[]{:S(2)}, u32[]{:S(2)}) collective-permute-start(bf16[144,128]{1,0:T(8,128)(2,1)S(1)} %get-tuple-element.48), channel_id=1, source_target_pairs={{0,8},{8,16},{16,24},{24,0},{1,9},{9,17},{17,25},{25,1},{2,10},{10... | collective-permute-start | bytes 110600 | tf_op jit(solution)/shard_map/ppermute | solution.py:400
  51.1 9.3 %collective-permute-start.9 = (bf16[64,1024]{1,0:T(8,128)(2,1)S(1)}, bf16[64,1024]{1,0:T(8,128)(2,1)S(1)}, u32[]{:S(2)}, u32[]{:S(2)}) collective-permute-start(bf16[64,1024]{1,0:T(8,128)(2,1)S(1)} %add_select_fusion), channel_id=1, source_target_pairs={{0,32},{2,34},{4,36},{6,38},{8,40},{10,42},{12,44},{14,46},{16,48}... | collective-permute-start | bytes 393224 | tf_op jit(solution)/shard_map/ppermute | solution.py:397
  54.5 12.1 %all-to-all-start.2 = ((bf16[8,80,128]{2,1,0:T(8,128)(2,1)}), bf16[8,80,128]{2,1,0:T(8,128)(2,1)S(1)}, u32[]{:S(2)}, u32[]{:S(2)}) async-start(bf16[8,80,128]{2,1,0:T(8,128)(2,1)} %join_pieces.2), calls=%async_computation.2 | async-start | bytes 327680 | tf_op jit(solution)/shard_map/all_to_all | solution.py:386
  60.5 12.8 %copy-start = (bf16[256,512]{1,0:T(8,128)(2,1)S(1)}, bf16[256,512]{1,0:T(8,128)(2,1)}, u32[]{:S(2)}) copy-start(bf16[256,512]{1,0:T(8,128)(2,1)} %k_ref.3) | copy-start | bytes 786436
  60.5 12.8 %copy-start.1 = (bf16[256,512]{1,0:T(8,128)(2,1)S(1)}, bf16[256,512]{1,0:T(8,128)(2,1)}, u32[]{:S(2)}) copy-start(bf16[256,512]{1,0:T(8,128)(2,1)} %v_ref.3) | copy-start | bytes 786436
  60.5 12.8 %copy-start.2 = (bf16[256,4096]{1,0:T(8,128)(2,1)S(1)}, bf16[256,4096]{1,0:T(8,128)(2,1)}, u32[]{:S(2)}) copy-start(bf16[256,4096]{1,0:T(8,128)(2,1)} %q_ref.1) | copy-start | bytes 6291460
  60.5 12.8 %collective-permute-start.12 = (bf16[64,1024]{1,0:T(8,128)(2,1)S(1)}, bf16[64,1024]{1,0:T(8,128)(2,1)S(1)}, u32[]{:S(2)}, u32[]{:S(2)}) collective-permute-start(bf16[64,1024]{1,0:T(8,128)(2,1)S(1)} %broadcast_select_fusion.refs_0_), channel_id=1, source_target_pairs={{0,24},{8,0},{16,8},{24,16},{1,25},{9,1},{17,9},{25,17},{2,26},{10... | collective-permute-start | bytes 393224 | tf_op jit(solution)/shard_map/ppermute | solution.py:400
  63.1 10.2 %collective-permute-start.11 = (bf16[64,1024]{1,0:T(8,128)(2,1)S(1)}, bf16[64,1024]{1,0:T(8,128)(2,1)S(1)}, u32[]{:S(2)}, u32[]{:S(2)}) collective-permute-start(bf16[64,1024]{1,0:T(8,128)(2,1)S(1)} %broadcast_select_fusion.refs_0_), channel_id=1, source_target_pairs={{0,16},{8,24},{16,0},{24,8},{1,17},{9,25},{17,1},{25,9},{2,18},{10... | collective-permute-start | bytes 393224 | tf_op jit(solution)/shard_map/ppermute | solution.py:400
  63.7 9.6 %collective-permute-start.10 = (bf16[64,1024]{1,0:T(8,128)(2,1)S(1)}, bf16[64,1024]{1,0:T(8,128)(2,1)S(1)}, u32[]{:S(2)}, u32[]{:S(2)}) collective-permute-start(bf16[64,1024]{1,0:T(8,128)(2,1)S(1)} %broadcast_select_fusion.refs_0_), channel_id=1, source_target_pairs={{0,8},{8,16},{16,24},{24,0},{1,9},{9,17},{17,25},{25,1},{2,10},{10... | collective-permute-start | bytes 393224 | tf_op jit(solution)/shard_map/ppermute | solution.py:400
  67.7 12.5 %all-to-all-start.3 = ((bf16[16,64,128]{2,1,0:T(8,128)(2,1)}), bf16[16,64,128]{2,1,0:T(8,128)(2,1)S(1)}, u32[]{:S(2)}, u32[]{:S(2)}) async-start(bf16[16,64,128]{2,1,0:T(8,128)(2,1)} %join_pieces.3), calls=%async_computation.3 | async-start | bytes 524288 | tf_op jit(solution)/shard_map/all_to_all | solution.py:386

commit v12 on v9

--- a/solution.py
+++ b/solution.py
@@ -129,17 +129,20 @@
     )(own_len, q, k, v, *anchor)
 
 
-def mark_kernel(n_x, len_ref, k_ref, v_ref, rk_ref, rv_ref, *o_refs):
+def pieces_kernel(len_ref, k_ref, v_ref, *o_refs):
     rows, width = k_ref.shape
-    own = rk_ref.shape[0]
-    slab = rows // n_x
+    slab = rows // len(o_refs)
     first = jnp.broadcast_to(k_ref[0:1, :], (slab, width))
-    for i, o_ref in enumerate(o_refs[:n_x]):
+    for i, o_ref in enumerate(o_refs):
         span = slice(i * slab, (i + 1) * slab)
         valid = (i * slab + lax.broadcasted_iota(jnp.int32, first.shape, 0)) < len_ref[0]
         o_ref[:, :width] = jnp.where(valid, k_ref[span, :], first)
         o_ref[:, width:] = jnp.where(valid, v_ref[span, :], jnp.full_like(first, MARK))
-    lines = o_refs[n_x:]
+
+
+def mark_kernel(len_ref, k_ref, v_ref, rk_ref, rv_ref, *lines):
+    rows = k_ref.shape[0]
+    own = rk_ref.shape[0]
     valid = lax.broadcasted_iota(jnp.int32, (rows, HEAD_SIZE), 0) < len_ref[0]
     y = lax.axis_index("y")
     for i, o_ref in enumerate(lines):
@@ -165,9 +168,21 @@
                 o_ref[2 * j + c, i * own : (i + 1) * own, :] = rq_ref[:, lane : lane + HEAD_SIZE]
 
 
-def prepare_kernel(n_x, n_y, len_ref, rq_ref, k_ref, v_ref, rk_ref, rv_ref, sent_ref, *o_refs):
+def prepare_kernel(n_x, n_y, len_ref, rq_ref, k_ref, v_ref, rk_ref, rv_ref, sent_ref, *refs):
+    pieces, lines = refs[:n_x], refs[n_x : n_x + n_y]
+    held_ref, sems = refs[n_x + n_y :]
+
+    @pl.when(place() == 0)
+    def _():
+        pieces_kernel(len_ref, k_ref, v_ref, *[held_ref.at[i] for i in range(n_x)])
+        copies = [pltpu.make_async_copy(held_ref.at[i], pieces[i], sems.at[i]) for i in range(n_x)]
+        for copy in copies:
+            copy.start()
+        for copy in copies:
+            copy.wait()
+
     pack_kernel(n_y, rq_ref, sent_ref)
-    mark_kernel(n_x, len_ref, k_ref, v_ref, rk_ref, rv_ref, *o_refs)
+    mark_kernel(len_ref, k_ref, v_ref, rk_ref, rv_ref, *lines)
 
 
 def prepare(own_len, rq, k, v, rk, rv, n_x, n_y):
@@ -181,7 +196,8 @@
         functools.partial(prepare_kernel, n_x, n_y),
         out_shape=shapes,
         in_specs=[pl.BlockSpec(memory_space=pltpu.SMEM)] + [vmem] * 5,
-        out_specs=[vmem] * len(shapes),
+        out_specs=[vmem] + [pl.BlockSpec(memory_space=pl.ANY)] * n_x + [vmem] * n_y,
+        scratch_shapes=[pltpu.VMEM((n_x, rows // n_x, 2 * width), k.dtype), pltpu.SemaphoreType.DMA((n_x,))],
         compiler_params=pltpu.CompilerParams(vmem_limit_bytes=56 * 1024 * 1024),
         cost_estimate=pl.CostEstimate(flops=2**18, bytes_accessed=5 * 2**19, transcendentals=0),
         name="prepare",

time: 80.8 us -> 80.8 us (level)
  no operation moved by 1% of the time
where the time goes in v12:
time: 80.8 us; the launch traced here: 79.7 us
  starting transfers between devices  61.1 us (76%)
  Pallas kernels  12.9 us (16%)
  waiting for transfers between devices  3.21 us (4%)
  between operations  2.42 us (3%)
    all_to_all x4, starting transfers between devices, exchange(): lax.all_to_all(x, axis, split_axis=0, concat_axis=0, axis_index_groups=gr...  28.7 us
    ppermute x10, starting transfers between devices, move(): return lax.ppermute(value, ('z', 'x', 'y'), pairs)  15.3 us
    ppermute x9, starting transfers between devices, shift_x(): lax.ppermute(value, 'x', [(a, (a + count) % n_x) for a in range(n_x)])  13.3 us
    pallas_call x1, Pallas kernels, context_attention(): pl.pallas_call(functools.partial(context_kernel, len(anchor)), out_shape=...  6.78 us
    ppermute x3, starting transfers between devices, local(): lax.ppermute(lines[i], 'y', [(a, (a + i) % n_y) for a in range(n_y)])  3.82 us
    pallas_call x1, Pallas kernels, prepare(): pl.pallas_call(functools.partial(prepare_kernel, n_x, n_y), out_shape=sha...  2.25 us
    pallas_call x2, Pallas kernels, join(): pl.pallas_call(functools.partial(join_kernel, parts_in, keep_code), out_s...  2.04 us
  transfers between devices with their start and end apart: 26, of which 3 were waited for; matrix products, arithmetic and copies ran while one was open for 0% of the time, Pallas kernels for 13%

profile of v12, /device:TPU:2, one launch (start us, length us, event | category | flops | bytes accessed | tf_op | source)
XLA Modules:
  0.0 79.7 jit_solution(2936278387663972424)
XLA Ops:
  1.3 2.2 %prepare.1 = (bf16[32,32,128]{2,1,0:T(8,128)(2,1)}, bf16[64,1024]{1,0:T(8,128)(2,1)}, bf16[64,1024]{1,0:T(8,128)(2,1)}, bf16[64,1024]{1,0:T(8,128)(2,1)}, bf16[6...) custom-call(s32[1]{0:T(128)S(6)} %copy.12.len_ref, ...), custom_call_target="tpu_custom_call" | custom-call | flops 262144 | bytes 2621440 | tf_op jit(solution)/shard_map/prepare/pallas_call | solution.py:195
  3.5 7.8 %all-to-all-start = ((bf16[32,32,128]{2,1,0:T(8,128)(2,1)}), bf16[32,32,128]{2,1,0:T(8,128)(2,1)S(1)}, u32[]{:S(2)}, u32[]{:S(2)}) async-start(bf16[32,32,128]{2,1,0:T(8,128)(2,1)} %get-tuple-element.27), calls=%async_computation | async-start | bytes 524288 | tf_op jit(solution)/shard_map/all_to_all | solution.py:402
  11.3 1.3 %collective-permute-start = (bf16[64,1024]{1,0:T(8,128)(2,1)}, bf16[64,1024]{1,0:T(8,128)(2,1)S(1)}, u32[]{:S(2)}, u32[]{:S(2)}) collective-permute-start(bf16[64,1024]{1,0:T(8,128)(2,1)} %get-tuple-element.28), channel_id=1, source_target_pairs={{0,8},{1,9}} | collective-permute-start | bytes 393224 | tf_op jit(solution)/shard_map/ppermute | solution.py:413
  12.6 0.7 collective-permute-start.1
  13.3 0.7 collective-permute-start.2
  14.0 0.9 %collective-permute-start.13 = (bf16[576,128]{1,0:T(8,128)(2,1)}, bf16[576,128]{1,0:T(8,128)(2,1)S(1)}, u32[]{:S(2)}, u32[]{:S(2)}) collective-permute-start(bf16[576,128]{1,0:T(8,128)(2,1)} %get-tuple-element.37), channel_id=1, source_target_pairs={{0,2},{2,4},{4,6},{6,0},{1,3},{3,5},{5,7},{7,1},{8,10},{10,12},{12... | collective-permute-start | bytes 442376 | tf_op jit(solution)/shard_map/ppermute | solution.py:422
  14.9 2.7 %collective-permute-start.14 = (bf16[576,128]{1,0:T(8,128)(2,1)}, bf16[576,128]{1,0:T(8,128)(2,1)S(1)}, u32[]{:S(2)}, u32[]{:S(2)}) collective-permute-start(bf16[576,128]{1,0:T(8,128)(2,1)} %get-tuple-element.38), channel_id=1, source_target_pairs={{0,4},{2,6},{4,0},{6,2},{1,5},{3,7},{5,1},{7,3},{8,12},{10,14},{12... | collective-permute-start | bytes 442376 | tf_op jit(solution)/shard_map/ppermute | solution.py:422
  18.2 1.3 %collective-permute-done = bf16[64,1024]{1,0:T(8,128)(2,1)S(1)} collective-permute-done((bf16[64,1024]{1,0:T(8,128)(2,1)}, bf16[64,1024]{1,0:T(8,128)(2,1)S(1)}, u32[]{:S(2)}, u32[]{:S(2)}) %collective-permute-start) | collective-permute-done | bytes 131104 | tf_op jit(solution)/shard_map/ppermute | solution.py:413
  19.8 0.7 choose.2
  20.5 9.2 %all-to-all-start.1 = ((bf16[8,64,128]{2,1,0:T(8,128)(2,1)}), bf16[8,64,128]{2,1,0:T(8,128)(2,1)S(1)}, u32[]{:S(2)}, u32[]{:S(2)}) async-start(bf16[8,64,128]{2,1,0:T(8,128)(2,1)} %choose.2), calls=%async_computation.1 | async-start | bytes 262144 | tf_op jit(solution)/shard_map/all_to_all | solution.py:402
  29.7 4.4 %collective-permute-start.4 = (bf16[64,1024]{1,0:T(8,128)(2,1)S(1)}, bf16[64,1024]{1,0:T(8,128)(2,1)S(1)}, u32[]{:S(2)}, u32[]{:S(2)}) collective-permute-start(bf16[64,1024]{1,0:T(8,128)(2,1)S(1)} %add_select_fusion.3), channel_id=1, source_target_pairs={{0,160},{8,168},{16,176},{24,184},{1,161},{9,169},{17,177},{25,185}} | collective-permute-start | bytes 393224 | tf_op jit(solution)/shard_map/ppermute | solution.py:413
  34.1 1.6 %collective-permute-start.3 = (bf16[64,1024]{1,0:T(8,128)(2,1)S(1)}, bf16[64,1024]{1,0:T(8,128)(2,1)S(1)}, u32[]{:S(2)}, u32[]{:S(2)}) collective-permute-start(bf16[64,1024]{1,0:T(8,128)(2,1)S(1)} %add_select_fusion.3), channel_id=1, source_target_pairs={{0,96},{8,104},{16,112},{24,120},{1,97},{9,105},{17,113},{25,121}} | collective-permute-start | bytes 393224 | tf_op jit(solution)/shard_map/ppermute | solution.py:413
  35.7 0.8 %collective-permute-start.18 = (bf16[64,128]{1,0:T(8,128)(2,1)S(1)}, bf16[64,128]{1,0:T(8,128)(2,1)S(1)}, u32[]{:S(2)}, u32[]{:S(2)}) collective-permute-start(bf16[64,128]{1,0:T(8,128)(2,1)S(1)} %choose.3.refs_0_), channel_id=1, source_target_pairs={{0,24},{8,0},{16,8},{24,16},{1,25},{9,1},{17,9},{25,17},{2,26},{10... | collective-permute-start | bytes 49160 | tf_op jit(solution)/shard_map/ppermute | solution.py:416
  36.5 2.2 %collective-permute-start.17 = (bf16[64,128]{1,0:T(8,128)(2,1)S(1)}, bf16[64,128]{1,0:T(8,128)(2,1)S(1)}, u32[]{:S(2)}, u32[]{:S(2)}) collective-permute-start(bf16[64,128]{1,0:T(8,128)(2,1)S(1)} %choose.3.refs_0_), channel_id=1, source_target_pairs={{0,16},{8,24},{16,0},{24,8},{1,17},{9,25},{17,1},{25,9},{2,18},{10... | collective-permute-start | bytes 49160 | tf_op jit(solution)/shard_map/ppermute | solution.py:416
  38.7 1.8 %collective-permute-start.16 = (bf16[64,128]{1,0:T(8,128)(2,1)S(1)}, bf16[64,128]{1,0:T(8,128)(2,1)S(1)}, u32[]{:S(2)}, u32[]{:S(2)}) collective-permute-start(bf16[64,128]{1,0:T(8,128)(2,1)S(1)} %choose.3.refs_0_), channel_id=1, source_target_pairs={{0,8},{8,16},{16,24},{24,0},{1,9},{9,17},{17,25},{25,1},{2,10},{10... | collective-permute-start | bytes 49160 | tf_op jit(solution)/shard_map/ppermute | solution.py:416
  40.6 2.1 %collective-permute-start.7 = (bf16[64,1024]{1,0:T(8,128)(2,1)S(1)}, bf16[64,1024]{1,0:T(8,128)(2,1)S(1)}, u32[]{:S(2)}, u32[]{:S(2)}) collective-permute-start(bf16[64,1024]{1,0:T(8,128)(2,1)S(1)} %add_select_fusion.2), channel_id=1, source_target_pairs={{0,2},{8,10},{16,18},{24,26},{96,98},{104,106},{112,114},{120,122}... | collective-permute-start | bytes 393224 | tf_op jit(solution)/shard_map/ppermute | solution.py:413
  42.7 1.3 %collective-permute-start.6 = (bf16[64,1024]{1,0:T(8,128)(2,1)S(1)}, bf16[64,1024]{1,0:T(8,128)(2,1)S(1)}, u32[]{:S(2)}, u32[]{:S(2)}) collective-permute-start(bf16[64,1024]{1,0:T(8,128)(2,1)S(1)} %add_select_fusion.2), channel_id=1, source_target_pairs={{0,4},{8,12},{16,20},{24,28},{96,100},{104,108},{112,116},{120,124... | collective-permute-start | bytes 393224 | tf_op jit(solution)/shard_map/ppermute | solution.py:413
  44.0 1.3 %collective-permute-start.5 = (bf16[64,1024]{1,0:T(8,128)(2,1)S(1)}, bf16[64,1024]{1,0:T(8,128)(2,1)S(1)}, u32[]{:S(2)}, u32[]{:S(2)}) collective-permute-start(bf16[64,1024]{1,0:T(8,128)(2,1)S(1)} %add_select_fusion.2), channel_id=1, source_target_pairs={{0,6},{8,14},{16,22},{24,30},{96,102},{104,110},{112,118},{120,126... | collective-permute-start | bytes 393224 | tf_op jit(solution)/shard_map/ppermute | solution.py:413
  45.4 1.1 %request_partials.1 = (bf16[144,128]{1,0:T(8,128)(2,1)S(1)}, bf16[144,128]{1,0:T(8,128)(2,1)S(1)}, bf16[144,128]{1,0:T(8,128)(2,1)S(1)}, bf16[144,128]{1,0:T(8,128)(2,1)S(1)}) custom-call(s32[1]{0:T(128)S(6)} %copy.13.owner_ref, bf16[64,128]{1,0:T(8,128)(2,1)S(1)} %choose.3.refs_0_, bf16[64,128]{1,0:T(8,128)(2,1)S(1)} %collective-permute-done.16.refs_1_, ...), custom_call_target="tpu_custom_call" | custom-call | flops 3000000000 | bytes 1048576 | tf_op jit(solution)/shard_map/request_partials/pallas_call | solution.py:303
  46.7 1.4 %collective-permute-start.20 = (bf16[144,128]{1,0:T(8,128)(2,1)S(1)}, bf16[144,128]{1,0:T(8,128)(2,1)S(1)}, u32[]{:S(2)}, u32[]{:S(2)}) collective-permute-start(bf16[144,128]{1,0:T(8,128)(2,1)S(1)} %get-tuple-element.47), channel_id=1, source_target_pairs={{0,16},{8,24},{16,0},{24,8},{1,17},{9,25},{17,1},{25,9},{2,18},{10... | collective-permute-start | bytes 110600 | tf_op jit(solution)/shard_map/ppermute | solution.py:416
  48.1 2.4 %collective-permute-start.21 = (bf16[144,128]{1,0:T(8,128)(2,1)S(1)}, bf16[144,128]{1,0:T(8,128)(2,1)S(1)}, u32[]{:S(2)}, u32[]{:S(2)}) collective-permute-start(bf16[144,128]{1,0:T(8,128)(2,1)S(1)} %get-tuple-element.48), channel_id=1, source_target_pairs={{0,8},{8,16},{16,24},{24,0},{1,9},{9,17},{17,25},{25,1},{2,10},{10... | collective-permute-start | bytes 110600 | tf_op jit(solution)/shard_map/ppermute | solution.py:416
  50.6 0.7 collective-permute-start.9
  51.2 1.3 %collective-permute-start.8 = (bf16[64,1024]{1,0:T(8,128)(2,1)S(1)}, bf16[64,1024]{1,0:T(8,128)(2,1)S(1)}, u32[]{:S(2)}, u32[]{:S(2)}) collective-permute-start(bf16[64,1024]{1,0:T(8,128)(2,1)S(1)} %add_select_fusion.1), channel_id=1, source_target_pairs={{0,32},{2,34},{4,36},{6,38},{8,40},{10,42},{12,44},{14,46},{16,48}... | collective-permute-start | bytes 393224 | tf_op jit(solution)/shard_map/ppermute | solution.py:413
  52.9 1.0 %join_pieces.2 = bf16[8,80,128]{2,1,0:T(8,128)(2,1)} custom-call(bf16[144,128]{1,0:T(8,128)(2,1)S(1)} %get-tuple-element.45.refs_0_, bf16[144,128]{1,0:T(8,128)(2,1)S(1)} %collective-permute-done.19.refs_1_, bf16[144,128]{1,0:T(8,128)(2,1)S(1)} %collective-permute-done.20.refs_2_, bf16[144,128]{1,0:T(8,128)(2,1)S(1)} %collective-permute-done.21.refs_3_), custom_call_target="tpu_custom_call" | custom-call | flops 3000000000 | bytes 524288 | tf_op jit(solution)/shard_map/join_pieces/pallas_call | solution.py:361
  53.9 6.0 %all-to-all-start.2 = ((bf16[8,80,128]{2,1,0:T(8,128)(2,1)}), bf16[8,80,128]{2,1,0:T(8,128)(2,1)S(1)}, u32[]{:S(2)}, u32[]{:S(2)}) async-start(bf16[8,80,128]{2,1,0:T(8,128)(2,1)} %join_pieces.2), calls=%async_computation.2 | async-start | bytes 327680 | tf_op jit(solution)/shard_map/all_to_all | solution.py:402
  60.0 2.1 %collective-permute-start.12 = (bf16[64,1024]{1,0:T(8,128)(2,1)S(1)}, bf16[64,1024]{1,0:T(8,128)(2,1)S(1)}, u32[]{:S(2)}, u32[]{:S(2)}) collective-permute-start(bf16[64,1024]{1,0:T(8,128)(2,1)S(1)} %add_select_fusion.refs_0_), channel_id=1, source_target_pairs={{0,24},{8,0},{16,8},{24,16},{1,25},{9,1},{17,9},{25,17},{2,26},{10... | collective-permute-start | bytes 393224 | tf_op jit(solution)/shard_map/ppermute | solution.py:416
  62.1 1.1 %collective-permute-start.11 = (bf16[64,1024]{1,0:T(8,128)(2,1)S(1)}, bf16[64,1024]{1,0:T(8,128)(2,1)S(1)}, u32[]{:S(2)}, u32[]{:S(2)}) collective-permute-start(bf16[64,1024]{1,0:T(8,128)(2,1)S(1)} %add_select_fusion.refs_0_), channel_id=1, source_target_pairs={{0,16},{8,24},{16,0},{24,8},{1,17},{9,25},{17,1},{25,9},{2,18},{10... | collective-permute-start | bytes 393224 | tf_op jit(solution)/shard_map/ppermute | solution.py:416
  63.2 1.1 %collective-permute-start.10 = (bf16[64,1024]{1,0:T(8,128)(2,1)S(1)}, bf16[64,1024]{1,0:T(8,128)(2,1)S(1)}, u32[]{:S(2)}, u32[]{:S(2)}) collective-permute-start(bf16[64,1024]{1,0:T(8,128)(2,1)S(1)} %add_select_fusion.refs_0_), channel_id=1, source_target_pairs={{0,8},{8,16},{16,24},{24,0},{1,9},{9,17},{17,25},{25,1},{2,10},{10... | collective-permute-start | bytes 393224 | tf_op jit(solution)/shard_map/ppermute | solution.py:416
  64.3 1.5 %all-to-all-done.2.refs_0_ = bf16[8,80,128]{2,1,0:T(8,128)(2,1)S(1)} async-done(((bf16[8,80,128]{2,1,0:T(8,128)(2,1)}), bf16[8,80,128]{2,1,0:T(8,128)(2,1)S(1)}, u32[]{:S(2)}, u32[]{:S(2)}) %all-to-all-start.2) | async-done | bytes 163872 | tf_op jit(solution)/shard_map/all_to_all | solution.py:402
  65.8 1.1 %join_pieces.3 = bf16[16,64,128]{2,1,0:T(8,128)(2,1)} custom-call(bf16[8,80,128]{2,1,0:T(8,128)(2,1)S(1)} %all-to-all-done.2.refs_0_), custom_call_target="tpu_custom_call" | custom-call | flops 3000000000 | bytes 524288 | tf_op jit(solution)/shard_map/join_pieces/pallas_call | solution.py:361
  66.8 5.8 %all-to-all-start.3 = ((bf16[16,64,128]{2,1,0:T(8,128)(2,1)}), bf16[16,64,128]{2,1,0:T(8,128)(2,1)S(1)}, u32[]{:S(2)}, u32[]{:S(2)}) async-start(bf16[16,64,128]{2,1,0:T(8,128)(2,1)} %join_pieces.3), calls=%async_computation.3 | async-start | bytes 524288 | tf_op jit(solution)/shard_map/all_to_all | solution.py:402
  72.7 6.8 %context_attention.1 = (bf16[256,4096]{1,0:T(8,128)(2,1)}, bf16[32,4096]{1,0:T(8,128)(2,1)}) custom-call(s32[1]{0:T(128)S(6)} %copy.12.len_ref, bf16[256,4096]{1,0:T(8,128)(2,1)S(1)} %copy-done.2, bf16[256,512]{1,0:T(8,128)(2,1)S(1)} %copy-done, bf16[256,512]{1,0:T(8,128)(2,1)S(1)} %copy-done.1, bf16[64,1024]{1,0:T(8,128)(2,1)S(1)} %add_select_fusion.refs_0_, ...), custom_call_target="tpu_custom_call" | custom-call | flops 2147483648 | bytes 5242880 | tf_op jit(solution)/shard_map/context_attention/pallas_call | solution.py:111
  (42 shorter events, 1.1 us)
Async XLA Ops:
  3.5 26.1 %copy-start.4 = (bf16[64,1024]{1,0:T(8,128)(2,1)S(1)}, bf16[64,1024]{1,0:T(8,128)(2,1)}, u32[]{:S(2)}) copy-start(bf16[64,1024]{1,0:T(8,128)(2,1)} %get-tuple-element.26) | copy-start | bytes 393220
  3.5 16.2 %all-to-all-start = ((bf16[32,32,128]{2,1,0:T(8,128)(2,1)}), bf16[32,32,128]{2,1,0:T(8,128)(2,1)S(1)}, u32[]{:S(2)}, u32[]{:S(2)}) async-start(bf16[32,32,128]{2,1,0:T(8,128)(2,1)} %get-tuple-element.27), calls=%async_computation | async-start | bytes 524288 | tf_op jit(solution)/shard_map/all_to_all | solution.py:402
  11.3 8.2 %collective-permute-start = (bf16[64,1024]{1,0:T(8,128)(2,1)}, bf16[64,1024]{1,0:T(8,128)(2,1)S(1)}, u32[]{:S(2)}, u32[]{:S(2)}) collective-permute-start(bf16[64,1024]{1,0:T(8,128)(2,1)} %get-tuple-element.28), channel_id=1, source_target_pairs={{0,8},{1,9}} | collective-permute-start | bytes 393224 | tf_op jit(solution)/shard_map/ppermute | solution.py:413
  12.6 7.2 %collective-permute-start.1 = (bf16[64,1024]{1,0:T(8,128)(2,1)}, bf16[64,1024]{1,0:T(8,128)(2,1)S(1)}, u32[]{:S(2)}, u32[]{:S(2)}) collective-permute-start(bf16[64,1024]{1,0:T(8,128)(2,1)} %get-tuple-element.29), channel_id=1, source_target_pairs={{0,16},{1,17}} | collective-permute-start | bytes 393224 | tf_op jit(solution)/shard_map/ppermute | solution.py:413
  13.3 6.5 %collective-permute-start.2 = (bf16[64,1024]{1,0:T(8,128)(2,1)}, bf16[64,1024]{1,0:T(8,128)(2,1)S(1)}, u32[]{:S(2)}, u32[]{:S(2)}) collective-permute-start(bf16[64,1024]{1,0:T(8,128)(2,1)} %get-tuple-element.30), channel_id=1, source_target_pairs={{0,24},{1,25}} | collective-permute-start | bytes 393224 | tf_op jit(solution)/shard_map/ppermute | solution.py:413
  14.0 21.7 %collective-permute-start.13 = (bf16[576,128]{1,0:T(8,128)(2,1)}, bf16[576,128]{1,0:T(8,128)(2,1)S(1)}, u32[]{:S(2)}, u32[]{:S(2)}) collective-permute-start(bf16[576,128]{1,0:T(8,128)(2,1)} %get-tuple-element.37), channel_id=1, source_target_pairs={{0,2},{2,4},{4,6},{6,0},{1,3},{3,5},{5,7},{7,1},{8,10},{10,12},{12... | collective-permute-start | bytes 442376 | tf_op jit(solution)/shard_map/ppermute | solution.py:422
  14.9 20.8 %collective-permute-start.14 = (bf16[576,128]{1,0:T(8,128)(2,1)}, bf16[576,128]{1,0:T(8,128)(2,1)S(1)}, u32[]{:S(2)}, u32[]{:S(2)}) collective-permute-start(bf16[576,128]{1,0:T(8,128)(2,1)} %get-tuple-element.38), channel_id=1, source_target_pairs={{0,4},{2,6},{4,0},{6,2},{1,5},{3,7},{5,1},{7,3},{8,12},{10,14},{12... | collective-permute-start | bytes 442376 | tf_op jit(solution)/shard_map/ppermute | solution.py:422
  19.5 16.1 %collective-permute-start.15 = (bf16[576,128]{1,0:T(8,128)(2,1)}, bf16[576,128]{1,0:T(8,128)(2,1)S(1)}, u32[]{:S(2)}, u32[]{:S(2)}) collective-permute-start(bf16[576,128]{1,0:T(8,128)(2,1)} %get-tuple-element.39), channel_id=1, source_target_pairs={{0,6},{2,0},{4,2},{6,4},{1,7},{3,1},{5,3},{7,5},{8,14},{10,8},{12,... | collective-permute-start | bytes 442376 | tf_op jit(solution)/shard_map/ppermute | solution.py:422
  20.5 15.2 %all-to-all-start.1 = ((bf16[8,64,128]{2,1,0:T(8,128)(2,1)}), bf16[8,64,128]{2,1,0:T(8,128)(2,1)S(1)}, u32[]{:S(2)}, u32[]{:S(2)}) async-start(bf16[8,64,128]{2,1,0:T(8,128)(2,1)} %choose.2), calls=%async_computation.1 | async-start | bytes 262144 | tf_op jit(solution)/shard_map/all_to_all | solution.py:402
  29.7 15.7 %copy-start.3 = (bf16[576,128]{1,0:T(8,128)(2,1)S(1)}, bf16[576,128]{1,0:T(8,128)(2,1)}, u32[]{:S(2)}) copy-start(bf16[576,128]{1,0:T(8,128)(2,1)} %get-tuple-element.41.refs_4_) | copy-start | bytes 442372
  29.7 10.9 %collective-permute-start.4 = (bf16[64,1024]{1,0:T(8,128)(2,1)S(1)}, bf16[64,1024]{1,0:T(8,128)(2,1)S(1)}, u32[]{:S(2)}, u32[]{:S(2)}) collective-permute-start(bf16[64,1024]{1,0:T(8,128)(2,1)S(1)} %add_select_fusion.3), channel_id=1, source_target_pairs={{0,160},{8,168},{16,176},{24,184},{1,161},{9,169},{17,177},{25,185}} | collective-permute-start | bytes 393224 | tf_op jit(solution)/shard_map/ppermute | solution.py:413
  34.1 6.5 %collective-permute-start.3 = (bf16[64,1024]{1,0:T(8,128)(2,1)S(1)}, bf16[64,1024]{1,0:T(8,128)(2,1)S(1)}, u32[]{:S(2)}, u32[]{:S(2)}) collective-permute-start(bf16[64,1024]{1,0:T(8,128)(2,1)S(1)} %add_select_fusion.3), channel_id=1, source_target_pairs={{0,96},{8,104},{16,112},{24,120},{1,97},{9,105},{17,113},{25,121}} | collective-permute-start | bytes 393224 | tf_op jit(solution)/shard_map/ppermute | solution.py:413
  35.7 8.3 %collective-permute-start.18 = (bf16[64,128]{1,0:T(8,128)(2,1)S(1)}, bf16[64,128]{1,0:T(8,128)(2,1)S(1)}, u32[]{:S(2)}, u32[]{:S(2)}) collective-permute-start(bf16[64,128]{1,0:T(8,128)(2,1)S(1)} %choose.3.refs_0_), channel_id=1, source_target_pairs={{0,24},{8,0},{16,8},{24,16},{1,25},{9,1},{17,9},{25,17},{2,26},{10... | collective-permute-start | bytes 49160 | tf_op jit(solution)/shard_map/ppermute | solution.py:416
  36.5 8.8 %collective-permute-start.17 = (bf16[64,128]{1,0:T(8,128)(2,1)S(1)}, bf16[64,128]{1,0:T(8,128)(2,1)S(1)}, u32[]{:S(2)}, u32[]{:S(2)}) collective-permute-start(bf16[64,128]{1,0:T(8,128)(2,1)S(1)} %choose.3.refs_0_), channel_id=1, source_target_pairs={{0,16},{8,24},{16,0},{24,8},{1,17},{9,25},{17,1},{25,9},{2,18},{10... | collective-permute-start | bytes 49160 | tf_op jit(solution)/shard_map/ppermute | solution.py:416
  38.7 6.6 %collective-permute-start.16 = (bf16[64,128]{1,0:T(8,128)(2,1)S(1)}, bf16[64,128]{1,0:T(8,128)(2,1)S(1)}, u32[]{:S(2)}, u32[]{:S(2)}) collective-permute-start(bf16[64,128]{1,0:T(8,128)(2,1)S(1)} %choose.3.refs_0_), channel_id=1, source_target_pairs={{0,8},{8,16},{16,24},{24,0},{1,9},{9,17},{17,25},{25,1},{2,10},{10... | collective-permute-start | bytes 49160 | tf_op jit(solution)/shard_map/ppermute | solution.py:416
  40.6 7.5 %collective-permute-start.7 = (bf16[64,1024]{1,0:T(8,128)(2,1)S(1)}, bf16[64,1024]{1,0:T(8,128)(2,1)S(1)}, u32[]{:S(2)}, u32[]{:S(2)}) collective-permute-start(bf16[64,1024]{1,0:T(8,128)(2,1)S(1)} %add_select_fusion.2), channel_id=1, source_target_pairs={{0,2},{8,10},{16,18},{24,26},{96,98},{104,106},{112,114},{120,122}... | collective-permute-start | bytes 393224 | tf_op jit(solution)/shard_map/ppermute | solution.py:413
  42.7 7.8 %collective-permute-start.6 = (bf16[64,1024]{1,0:T(8,128)(2,1)S(1)}, bf16[64,1024]{1,0:T(8,128)(2,1)S(1)}, u32[]{:S(2)}, u32[]{:S(2)}) collective-permute-start(bf16[64,1024]{1,0:T(8,128)(2,1)S(1)} %add_select_fusion.2), channel_id=1, source_target_pairs={{0,4},{8,12},{16,20},{24,28},{96,100},{104,108},{112,116},{120,124... | collective-permute-start | bytes 393224 | tf_op jit(solution)/shard_map/ppermute | solution.py:413
  44.0 6.5 %collective-permute-start.5 = (bf16[64,1024]{1,0:T(8,128)(2,1)S(1)}, bf16[64,1024]{1,0:T(8,128)(2,1)S(1)}, u32[]{:S(2)}, u32[]{:S(2)}) collective-permute-start(bf16[64,1024]{1,0:T(8,128)(2,1)S(1)} %add_select_fusion.2), channel_id=1, source_target_pairs={{0,6},{8,14},{16,22},{24,30},{96,102},{104,110},{112,118},{120,126... | collective-permute-start | bytes 393224 | tf_op jit(solution)/shard_map/ppermute | solution.py:413
  46.4 6.1 %collective-permute-start.19 = (bf16[144,128]{1,0:T(8,128)(2,1)S(1)}, bf16[144,128]{1,0:T(8,128)(2,1)S(1)}, u32[]{:S(2)}, u32[]{:S(2)}) collective-permute-start(bf16[144,128]{1,0:T(8,128)(2,1)S(1)} %get-tuple-element.46), channel_id=1, source_target_pairs={{0,24},{8,0},{16,8},{24,16},{1,25},{9,1},{17,9},{25,17},{2,26},{10... | collective-permute-start | bytes 110600 | tf_op jit(solution)/shard_map/ppermute | solution.py:416
  46.7 5.8 %collective-permute-start.20 = (bf16[144,128]{1,0:T(8,128)(2,1)S(1)}, bf16[144,128]{1,0:T(8,128)(2,1)S(1)}, u32[]{:S(2)}, u32[]{:S(2)}) collective-permute-start(bf16[144,128]{1,0:T(8,128)(2,1)S(1)} %get-tuple-element.47), channel_id=1, source_target_pairs={{0,16},{8,24},{16,0},{24,8},{1,17},{9,25},{17,1},{25,9},{2,18},{10... | collective-permute-start | bytes 110600 | tf_op jit(solution)/shard_map/ppermute | solution.py:416
  48.1 4.8 %collective-permute-start.21 = (bf16[144,128]{1,0:T(8,128)(2,1)S(1)}, bf16[144,128]{1,0:T(8,128)(2,1)S(1)}, u32[]{:S(2)}, u32[]{:S(2)}) collective-permute-start(bf16[144,128]{1,0:T(8,128)(2,1)S(1)} %get-tuple-element.48), channel_id=1, source_target_pairs={{0,8},{8,16},{16,24},{24,0},{1,9},{9,17},{17,25},{25,1},{2,10},{10... | collective-permute-start | bytes 110600 | tf_op jit(solution)/shard_map/ppermute | solution.py:416
  50.6 9.3 %collective-permute-start.9 = (bf16[64,1024]{1,0:T(8,128)(2,1)S(1)}, bf16[64,1024]{1,0:T(8,128)(2,1)S(1)}, u32[]{:S(2)}, u32[]{:S(2)}) collective-permute-start(bf16[64,1024]{1,0:T(8,128)(2,1)S(1)} %add_select_fusion.1), channel_id=1, source_target_pairs={{96,64},{98,66},{100,68},{102,70},{104,72},{106,74},{108,76},{110,... | collective-permute-start | bytes 393224 | tf_op jit(solution)/shard_map/ppermute | solution.py:413
  51.2 8.7 %collective-permute-start.8 = (bf16[64,1024]{1,0:T(8,128)(2,1)S(1)}, bf16[64,1024]{1,0:T(8,128)(2,1)S(1)}, u32[]{:S(2)}, u32[]{:S(2)}) collective-permute-start(bf16[64,1024]{1,0:T(8,128)(2,1)S(1)} %add_select_fusion.1), channel_id=1, source_target_pairs={{0,32},{2,34},{4,36},{6,38},{8,40},{10,42},{12,44},{14,46},{16,48}... | collective-permute-start | bytes 393224 | tf_op jit(solution)/shard_map/ppermute | solution.py:413
  53.9 11.9 %all-to-all-start.2 = ((bf16[8,80,128]{2,1,0:T(8,128)(2,1)}), bf16[8,80,128]{2,1,0:T(8,128)(2,1)S(1)}, u32[]{:S(2)}, u32[]{:S(2)}) async-start(bf16[8,80,128]{2,1,0:T(8,128)(2,1)} %join_pieces.2), calls=%async_computation.2 | async-start | bytes 327680 | tf_op jit(solution)/shard_map/all_to_all | solution.py:402
  59.9 12.7 %copy-start = (bf16[256,512]{1,0:T(8,128)(2,1)S(1)}, bf16[256,512]{1,0:T(8,128)(2,1)}, u32[]{:S(2)}) copy-start(bf16[256,512]{1,0:T(8,128)(2,1)} %k_ref.3) | copy-start | bytes 786436
  59.9 12.7 %copy-start.1 = (bf16[256,512]{1,0:T(8,128)(2,1)S(1)}, bf16[256,512]{1,0:T(8,128)(2,1)}, u32[]{:S(2)}) copy-start(bf16[256,512]{1,0:T(8,128)(2,1)} %v_ref.3) | copy-start | bytes 786436
  60.0 12.7 %copy-start.2 = (bf16[256,4096]{1,0:T(8,128)(2,1)S(1)}, bf16[256,4096]{1,0:T(8,128)(2,1)}, u32[]{:S(2)}) copy-start(bf16[256,4096]{1,0:T(8,128)(2,1)} %q_ref.1) | copy-start | bytes 6291460
  60.0 12.7 %collective-permute-start.12 = (bf16[64,1024]{1,0:T(8,128)(2,1)S(1)}, bf16[64,1024]{1,0:T(8,128)(2,1)S(1)}, u32[]{:S(2)}, u32[]{:S(2)}) collective-permute-start(bf16[64,1024]{1,0:T(8,128)(2,1)S(1)} %add_select_fusion.refs_0_), channel_id=1, source_target_pairs={{0,24},{8,0},{16,8},{24,16},{1,25},{9,1},{17,9},{25,17},{2,26},{10... | collective-permute-start | bytes 393224 | tf_op jit(solution)/shard_map/ppermute | solution.py:416
  62.1 10.5 %collective-permute-start.11 = (bf16[64,1024]{1,0:T(8,128)(2,1)S(1)}, bf16[64,1024]{1,0:T(8,128)(2,1)S(1)}, u32[]{:S(2)}, u32[]{:S(2)}) collective-permute-start(bf16[64,1024]{1,0:T(8,128)(2,1)S(1)} %add_select_fusion.refs_0_), channel_id=1, source_target_pairs={{0,16},{8,24},{16,0},{24,8},{1,17},{9,25},{17,1},{25,9},{2,18},{10... | collective-permute-start | bytes 393224 | tf_op jit(solution)/shard_map/ppermute | solution.py:416
  63.2 9.4 %collective-permute-start.10 = (bf16[64,1024]{1,0:T(8,128)(2,1)S(1)}, bf16[64,1024]{1,0:T(8,128)(2,1)S(1)}, u32[]{:S(2)}, u32[]{:S(2)}) collective-permute-start(bf16[64,1024]{1,0:T(8,128)(2,1)S(1)} %add_select_fusion.refs_0_), channel_id=1, source_target_pairs={{0,8},{8,16},{16,24},{24,0},{1,9},{9,17},{17,25},{25,1},{2,10},{10... | collective-permute-start | bytes 393224 | tf_op jit(solution)/shard_map/ppermute | solution.py:416
  66.8 12.6 %all-to-all-start.3 = ((bf16[16,64,128]{2,1,0:T(8,128)(2,1)}), bf16[16,64,128]{2,1,0:T(8,128)(2,1)S(1)}, u32[]{:S(2)}, u32[]{:S(2)}) async-start(bf16[16,64,128]{2,1,0:T(8,128)(2,1)} %join_pieces.3), calls=%async_computation.3 | async-start | bytes 524288 | tf_op jit(solution)/shard_map/all_to_all | solution.py:402
